TPU v7x, 32 devices: a whole 2x2x4 slice. The times are simulated.
32 devices in a mesh: wide: 8 (over z, x), narrow: 4 (over y, core).
Axes of the slice: x: 2, y: 2, z: 4, core: 2. Of those that a mesh axis runs over, the one named last changes fastest.
Arguments:
- doc_tokens: bfloat16 [8, 512, 768], P('wide', 'narrow'), may hold values from -6 to 6
- query_tokens: bfloat16 [128, 32, 768], P('wide'), may hold values from -6 to 6
- query_lengths: int32 [128], P('wide'), may hold values from 8 to 32, as said below
- positive_docs: int32 [128], P('wide'), may hold values from 0 to 7
- retrieved: int32 [128, 32, 128], P('wide'), may hold values from 0 to 4095
- attend_gain: float32 [768], replicated, may hold values from 0.5 to 1.5
- query_weight: bfloat16 [768, 768], replicated, may hold values from -0.109375 to 0.109375
- key_weight: bfloat16 [768, 768], replicated, may hold values from -0.109375 to 0.109375
- value_weight: bfloat16 [768, 768], replicated, may hold values from -0.21875 to 0.21875
- output_weight: bfloat16 [768, 768], replicated, may hold values from -0.625 to 0.625
- bias_table: float32 [32, 12], replicated, may hold values from -4 to 4
- feed_gain: float32 [768], replicated, may hold values from 0.5 to 1.5
- gate_weight: bfloat16 [768, 2048], replicated, may hold values from -0.21875 to 0.21875
- up_weight: bfloat16 [768, 2048], replicated, may hold values from -0.21875 to 0.21875
- down_weight: bfloat16 [2048, 768], replicated, may hold values from -0.125 to 0.125
- final_gain: float32 [768], replicated, may hold values from 0.5 to 1.5
- proj_weight: bfloat16 [768, 128], replicated, may hold values from -0.21875 to 0.21875
Outputs:
- losses: float32 [128], P(('wide', 'narrow'))
- doc_grad: float32 [8, 512, 768], P('wide', 'narrow')
- query_grad: float32 [128, 32, 768], P(('wide', 'narrow'))
- attend_gain_grad: float32 [768], P(('wide', 'narrow'))
- query_weight_grad: float32 [768, 768], P(('wide', 'narrow'))
- key_weight_grad: float32 [768, 768], P(('wide', 'narrow'))
- value_weight_grad: float32 [768, 768], P(('wide', 'narrow'))
- output_weight_grad: float32 [768, 768], P(('wide', 'narrow'))
- bias_table_grad: float32 [32, 12], replicated
- feed_gain_grad: float32 [768], P(('wide', 'narrow'))
- gate_weight_grad: float32 [768, 2048], P(('wide', 'narrow'))
- up_weight_grad: float32 [768, 2048], P(('wide', 'narrow'))
- down_weight_gradient: float32 [2048, 768], P(('wide', 'narrow'))
- final_gain_grad: float32 [768], P(('wide', 'narrow'))
- proj_weight_grad: float32 [768, 128], P(('wide', 'narrow'))
Inputs may be any that keep to these rules, and one draw needn't show every extreme that they name: `query_lengths`: at least one slot of the batch holds exactly 32 tokens. `retrieved`: an index may repeat within a query token's list.
All inputs are finite; a program needn't handle non-finite values.
Results may differ from a plain program's by a relative error of at most 0.019.
Values may be sent and summed in bfloat16 or wider, within the bound.
No kernel may reach another device: no remote copies, remote signals or barrier semaphores. Data moves between devices by JAX's collectives and lax.ppermute only.
A program may use at most 192 MiB of HBM per device.

v0:
```python
import jax
import jax.numpy as jnp
from jax import lax
from jax.sharding import PartitionSpec as P

BUCKETS = 32


epsilon = 1e-06
contrastive_sharpness_factor = 0.01
masked_value = -1000000000.0
bucket_edges = (12, 16, 23, 32, 46, 64, 91)
highest = lax.Precision.HIGHEST


def bucket_index(offset):
    distance = jnp.abs(offset)
    beyond = 8 + sum(((distance >= boundary).astype(jnp.int32) for boundary in bucket_edges))
    inside = jnp.where(distance < 8, distance, beyond)
    return inside + BUCKETS // 2 * (offset > 0).astype(jnp.int32)


def bucket_onehot(row_places, col_places):
    buckets = bucket_index(col_places[None, :] - row_places[:, None])
    return (buckets[:, :, None] == jnp.arange(BUCKETS, dtype=jnp.int32)).astype(jnp.float32)


def rms_norm(values, gain_vec):
    return values * lax.rsqrt(jnp.mean(values * values, -1, keepdims=True) + epsilon) * gain_vec


def unit_scale(values):
    return values * lax.rsqrt(jnp.sum(values * values, -1, keepdims=True) + epsilon)


def gated_unit(gate_value, up_value):
    return jax.nn.gelu(gate_value, approximate=True) * up_value


def product(leftward_operand, right_side):
    return jnp.dot(leftward_operand, right_side, preferred_element_type=jnp.float32)


def left_product(leftward_operand, right_side):
    return lax.dot_general(
        leftward_operand, right_side, (((0,), (0,)), ((), ())), preferred_element_type=jnp.float32
    )


def right_product(leftward_operand, right_side):
    return lax.dot_general(
        leftward_operand, right_side, (((1,), (1,)), ((), ())), preferred_element_type=jnp.float32
    )


def attend_scores(query_heads, key_heads, pos_bias, key_keep):
    scores = jnp.einsum(
        "brhe,bche->bhrc", query_heads, key_heads, preferred_element_type=jnp.float32
    )
    return jnp.where(key_keep[:, None, None, :], scores + pos_bias[None], masked_value)


def attend_forward(query_heads, key_heads, value_heads, pos_bias, key_keep):
    scores = attend_scores(query_heads, key_heads, pos_bias, key_keep)
    top_score = jnp.max(scores, -1, keepdims=True)
    weights = jnp.exp(scores - top_score)
    totals = jnp.sum(weights, -1, keepdims=True)
    probs_round = (weights / totals).astype(jnp.bfloat16)
    mixed_heads = jnp.einsum(
        "bhrc,bche->brhe", probs_round, value_heads, preferred_element_type=jnp.float32
    )
    return (mixed_heads.astype(jnp.bfloat16), top_score + jnp.log(totals))


def attention_pullback_pass(
    query_heads, key_heads, value_heads, pos_bias, key_keep, log_total, grad_mixed
):
    probs = jnp.exp(attend_scores(query_heads, key_heads, pos_bias, key_keep) - log_total)
    grad_probs = jnp.einsum(
        "brhe,bche->bhrc", grad_mixed, value_heads, preferred_element_type=jnp.float32
    )
    grad_values = jnp.einsum(
        "bhrc,brhe->bche",
        probs.astype(jnp.bfloat16),
        grad_mixed,
        preferred_element_type=jnp.float32,
    )
    grad_scores = (probs * (grad_probs - jnp.sum(probs * grad_probs, -1, keepdims=True))).astype(
        jnp.bfloat16
    )
    query_gradients = jnp.einsum(
        "bhrc,bche->brhe", grad_scores, key_heads, preferred_element_type=jnp.float32
    )
    grad_keys = jnp.einsum(
        "bhrc,brhe->bche", grad_scores, query_heads, preferred_element_type=jnp.float32
    )
    return (query_gradients, grad_keys, grad_values, grad_scores)


def pooled_loss(similar, owner_doc, lengths, positives, doc_total):
    slot_count = similar.shape[0]
    slot_length = similar.shape[1]
    slot_ids = jnp.arange(slot_count * slot_length, dtype=jnp.int32).reshape(
        slot_count, slot_length, 1
    )
    slot_ids = slot_ids * doc_total + owner_doc
    segments = slot_count * slot_length * doc_total
    summed = jax.ops.segment_sum(similar.reshape(-1), slot_ids.reshape(-1), num_segments=segments)
    summed = summed.reshape(slot_count, slot_length, doc_total)
    tallies = jax.ops.segment_sum(
        jnp.ones_like(similar).reshape(-1), slot_ids.reshape(-1), num_segments=segments
    )
    tallies = tallies.reshape(slot_count, slot_length, doc_total)
    pooled = summed / jnp.maximum(tallies, 1.0)
    valid_mask = (jnp.arange(slot_length, dtype=jnp.int32)[None, :] < lengths[:, None]).astype(
        jnp.float32
    )
    weight = jnp.minimum(tallies, 1.0) * valid_mask[:, :, None]
    passage_relevance = jnp.sum(weight * pooled, 1) / jnp.maximum(jnp.sum(weight, 1), 1.0)
    unnormalized_similarity = passage_relevance / contrastive_sharpness_factor
    chosen = jnp.sum(
        jnp.where(
            jnp.arange(doc_total, dtype=jnp.int32)[None, :] == positives[:, None],
            unnormalized_similarity,
            0.0,
        ),
        1,
    )
    return jax.nn.logsumexp(unnormalized_similarity, axis=-1) - chosen


def on_device(
    doc_tokens,
    query_tokens,
    query_lengths,
    positive_docs,
    retrieved,
    attend_gain,
    query_weight,
    key_weight,
    value_weight,
    output_weight,
    bias_table,
    feed_gain,
    gate_weight,
    up_weight,
    down_weight,
    final_gain,
    proj_weight,
):
    narrow_size = lax.axis_size("narrow")
    narrow_rank = lax.axis_index("narrow")
    wide_size = lax.axis_size("wide")
    doc_count = doc_tokens.shape[0]
    doc_rows = doc_tokens.shape[1]
    width = doc_tokens.shape[2]
    doc_length = doc_rows * narrow_size
    doc_total = doc_count * wide_size
    own_slots = query_tokens.shape[0] // narrow_size
    slot_length = query_tokens.shape[1]
    head_count = bias_table.shape[1]
    head_size = width // head_count
    doc_flat = doc_count * doc_rows
    query_flat = own_slots * slot_length
    first_slot = narrow_rank * own_slots
    my_queries = lax.dynamic_slice_in_dim(query_tokens, first_slot, own_slots, 0)
    my_lengths = lax.dynamic_slice_in_dim(query_lengths, first_slot, own_slots, 0)
    my_positives = lax.dynamic_slice_in_dim(positive_docs, first_slot, own_slots, 0)
    my_picked = lax.dynamic_slice_in_dim(retrieved, first_slot, own_slots, 0)
    input_rows = jnp.concatenate(
        [doc_tokens.reshape(doc_flat, width), my_queries.reshape(query_flat, width)], 0
    ).astype(jnp.float32)
    attend_normed, attend_back = jax.vjp(rms_norm, input_rows, attend_gain)
    normed = attend_normed.astype(jnp.bfloat16)
    query_heads = product(normed, query_weight).astype(jnp.bfloat16)
    key_heads = product(normed, key_weight).astype(jnp.bfloat16)
    value_heads = product(normed, value_weight).astype(jnp.bfloat16)
    doc_keys = key_heads[:doc_flat].reshape(doc_count, doc_rows, width)
    doc_values = value_heads[:doc_flat].reshape(doc_count, doc_rows, width)
    all_keys, all_values = (
        lax.all_gather(doc_keys, "narrow", axis=1, tiled=True),
        lax.all_gather(doc_values, "narrow", axis=1, tiled=True),
    )
    key_all = all_keys.reshape(doc_count, doc_length, head_count, head_size)
    value_all = all_values.reshape(doc_count, doc_length, head_count, head_size)
    row_places = narrow_rank * doc_rows + jnp.arange(doc_rows, dtype=jnp.int32)
    doc_onehot = bucket_onehot(row_places, jnp.arange(doc_length, dtype=jnp.int32))
    doc_bias = jnp.einsum("rcu,uh->hrc", doc_onehot, bias_table, precision=highest)
    slot_places = jnp.arange(slot_length, dtype=jnp.int32)
    slot_onehot = bucket_onehot(slot_places, slot_places)
    slot_bias = jnp.einsum("rcu,uh->hrc", slot_onehot, bias_table, precision=highest)
    doc_keep = jnp.ones((doc_count, doc_length), dtype=bool)
    slot_keep = slot_places[None, :] < my_lengths[:, None]
    doc_query = query_heads[:doc_flat].reshape(doc_count, doc_rows, head_count, head_size)
    doc_mixed, doc_logsum = attend_forward(doc_query, key_all, value_all, doc_bias, doc_keep)
    slot_query = query_heads[doc_flat:].reshape(own_slots, slot_length, head_count, head_size)
    slot_key = key_heads[doc_flat:].reshape(own_slots, slot_length, head_count, head_size)
    slot_value = value_heads[doc_flat:].reshape(own_slots, slot_length, head_count, head_size)
    slot_mixed, slot_logsum = attend_forward(slot_query, slot_key, slot_value, slot_bias, slot_keep)
    mixed = jnp.concatenate(
        [doc_mixed.reshape(doc_flat, width), slot_mixed.reshape(query_flat, width)], 0
    )
    after_attend = input_rows + product(mixed, output_weight)
    feed_normed, feed_back = jax.vjp(rms_norm, after_attend, feed_gain)
    normed_feed = feed_normed.astype(jnp.bfloat16)
    gate_value = product(normed_feed, gate_weight)
    upward = product(normed_feed, up_weight)
    gated_value, gated_back = jax.vjp(gated_unit, gate_value, upward)
    hidden = gated_value.astype(jnp.bfloat16)
    after_feed = after_attend + product(hidden, down_weight)
    final_normed, final_back = jax.vjp(rms_norm, after_feed, final_gain)
    normed_final = final_normed.astype(jnp.bfloat16)
    embedded = product(normed_final, proj_weight)
    unit_value, unit_back = jax.vjp(unit_scale, embedded)
    unit_round = unit_value.astype(jnp.bfloat16)
    passage_normalized_vector = unit_round[:doc_flat]
    slot_unit = unit_round[doc_flat:].reshape(own_slots, slot_length, -1)
    every_unit = lax.all_gather(passage_normalized_vector, ("wide", "narrow"), axis=0, tiled=True)
    owner_doc = my_picked // doc_length
    place_doc = my_picked % doc_length
    gathered_row = (
        (owner_doc // doc_count * narrow_size + place_doc // doc_rows) * doc_count
        + owner_doc % doc_count
    ) * doc_rows + place_doc % doc_rows
    picked_rows = every_unit[gathered_row]
    similar = jnp.einsum(
        "aikp,aip->aik", picked_rows, slot_unit, preferred_element_type=jnp.float32
    )

    def loss_of(similar_values):
        return pooled_loss(similar_values, owner_doc, my_lengths, my_positives, doc_total)

    losses, loss_back = jax.vjp(loss_of, similar)
    grad_similar = loss_back(jnp.ones_like(losses))[0]
    grad_slot_unit = jnp.einsum("aik,aikp->aip", grad_similar, picked_rows, precision=highest)
    slot_unit_f = slot_unit.astype(jnp.float32)
    columns = slot_unit_f.shape[-1]
    contrib = grad_similar[..., None] * slot_unit_f[:, :, None, :]
    whole_term = (
        jnp.zeros((every_unit.shape[0], columns), jnp.float32)
        .at[gathered_row.reshape(-1)]
        .add(contrib.reshape(-1, columns))
    )
    grad_doc_unit = lax.psum_scatter(
        whole_term, ("wide", "narrow"), scatter_dimension=0, tiled=True
    )
    grad_unit = jnp.concatenate([grad_doc_unit, grad_slot_unit.reshape(query_flat, -1)], 0)
    grad_embed = unit_back(grad_unit)[0].astype(jnp.bfloat16)
    proj_grad = left_product(normed_final, grad_embed)
    grad_after_feed, final_gain_grad = final_back(right_product(grad_embed, proj_weight))
    grad_feed_out = grad_after_feed.astype(jnp.bfloat16)
    down_grad = left_product(hidden, grad_feed_out)
    grad_gate, grad_upward = gated_back(right_product(grad_feed_out, down_weight))
    grad_gate = grad_gate.astype(jnp.bfloat16)
    grad_upward = grad_upward.astype(jnp.bfloat16)
    gate_grad = left_product(normed_feed, grad_gate)
    up_grad = left_product(normed_feed, grad_upward)
    grad_normed_feed = right_product(grad_gate, gate_weight) + right_product(grad_upward, up_weight)
    grad_feed_part, feed_gain_grad = feed_back(grad_normed_feed)
    grad_after_attend = grad_after_feed + grad_feed_part
    grad_attend_out = grad_after_attend.astype(jnp.bfloat16)
    output_grad = left_product(mixed, grad_attend_out)
    grad_mixed = right_product(grad_attend_out, output_weight).astype(jnp.bfloat16)
    back_keys, back_values = (
        lax.all_gather(doc_keys, "narrow", axis=1, tiled=True),
        lax.all_gather(doc_values, "narrow", axis=1, tiled=True),
    )
    back_key_all = back_keys.reshape(doc_count, doc_length, head_count, head_size)
    back_value_all = back_values.reshape(doc_count, doc_length, head_count, head_size)
    grad_doc_query, grad_key_all, grad_value_all, grad_doc_scores = attention_pullback_pass(
        doc_query,
        back_key_all,
        back_value_all,
        doc_bias,
        doc_keep,
        doc_logsum,
        grad_mixed[:doc_flat].reshape(doc_count, doc_rows, head_count, head_size),
    )
    grad_doc_keys, grad_doc_values = (
        lax.psum_scatter(
            grad_key_all.reshape(doc_count, doc_length, width).astype(jnp.bfloat16),
            "narrow",
            scatter_dimension=1,
            tiled=True,
        ).astype(jnp.float32),
        lax.psum_scatter(
            grad_value_all.reshape(doc_count, doc_length, width).astype(jnp.bfloat16),
            "narrow",
            scatter_dimension=1,
            tiled=True,
        ).astype(jnp.float32),
    )
    grad_slot_query, grad_slot_key, grad_slot_value, grad_slot_scores = attention_pullback_pass(
        slot_query,
        slot_key,
        slot_value,
        slot_bias,
        slot_keep,
        slot_logsum,
        grad_mixed[doc_flat:].reshape(own_slots, slot_length, head_count, head_size),
    )
    table_term = jnp.einsum(
        "nhrc,rcu->uh", grad_doc_scores.astype(jnp.float32), doc_onehot, precision=highest
    )
    table_term = table_term + jnp.einsum(
        "nhrc,rcu->uh", grad_slot_scores.astype(jnp.float32), slot_onehot, precision=highest
    )
    bias_table_grad = lax.psum(table_term, ("wide", "narrow"))
    query_gradients = jnp.concatenate(
        [grad_doc_query.reshape(doc_flat, width), grad_slot_query.reshape(query_flat, width)], 0
    ).astype(jnp.bfloat16)
    grad_keys = jnp.concatenate(
        [grad_doc_keys.reshape(doc_flat, width), grad_slot_key.reshape(query_flat, width)], 0
    ).astype(jnp.bfloat16)
    grad_values = jnp.concatenate(
        [grad_doc_values.reshape(doc_flat, width), grad_slot_value.reshape(query_flat, width)], 0
    ).astype(jnp.bfloat16)
    query_grad_w = left_product(normed, query_gradients)
    key_grad_w = left_product(normed, grad_keys)
    value_grad_w = left_product(normed, grad_values)
    grad_normed = (
        right_product(query_gradients, query_weight)
        + right_product(grad_keys, key_weight)
        + right_product(grad_values, value_weight)
    )
    grad_input_part, attend_gain_grad = attend_back(grad_normed)
    grad_inputs = grad_after_attend + grad_input_part
    doc_grad = grad_inputs[:doc_flat].reshape(doc_count, doc_rows, width)
    query_grad = grad_inputs[doc_flat:].reshape(own_slots, slot_length, width)
    summed = (
        lax.psum_scatter(attend_gain_grad, ("wide", "narrow"), scatter_dimension=0, tiled=True),
        lax.psum_scatter(query_grad_w, ("wide", "narrow"), scatter_dimension=0, tiled=True),
        lax.psum_scatter(key_grad_w, ("wide", "narrow"), scatter_dimension=0, tiled=True),
        lax.psum_scatter(value_grad_w, ("wide", "narrow"), scatter_dimension=0, tiled=True),
        lax.psum_scatter(output_grad, ("wide", "narrow"), scatter_dimension=0, tiled=True),
        lax.psum_scatter(feed_gain_grad, ("wide", "narrow"), scatter_dimension=0, tiled=True),
        lax.psum_scatter(gate_grad, ("wide", "narrow"), scatter_dimension=0, tiled=True),
        lax.psum_scatter(up_grad, ("wide", "narrow"), scatter_dimension=0, tiled=True),
        lax.psum_scatter(down_grad, ("wide", "narrow"), scatter_dimension=0, tiled=True),
        lax.psum_scatter(final_gain_grad, ("wide", "narrow"), scatter_dimension=0, tiled=True),
        lax.psum_scatter(proj_grad, ("wide", "narrow"), scatter_dimension=0, tiled=True),
    )
    return (
        losses,
        doc_grad,
        query_grad,
        summed[0],
        summed[1],
        summed[2],
        summed[3],
        summed[4],
        bias_table_grad,
        summed[5],
        summed[6],
        summed[7],
        summed[8],
        summed[9],
        summed[10],
    )


def solution(mesh):
    return jax.shard_map(
        on_device,
        mesh=mesh,
        in_specs=(
            P("wide", "narrow", None),
            P("wide", None, None),
            P("wide"),
            P("wide"),
            P("wide", None, None),
            P(),
            P(),
            P(),
            P(),
            P(),
            P(),
            P(),
            P(),
            P(),
            P(),
            P(),
            P(),
        ),
        out_specs=(
            P(("wide", "narrow")),
            P("wide", "narrow", None),
            P(("wide", "narrow"), None, None),
            P(("wide", "narrow")),
            P(("wide", "narrow"), None),
            P(("wide", "narrow"), None),
            P(("wide", "narrow"), None),
            P(("wide", "narrow"), None),
            P(),
            P(("wide", "narrow")),
            P(("wide", "narrow"), None),
            P(("wide", "narrow"), None),
            P(("wide", "narrow"), None),
            P(("wide", "narrow")),
            P(("wide", "narrow"), None),
        ),
        check_vma=False,
    )
```

profile of v0, /device:TPU:0, one launch (start us, length us, event | category | flops | bytes accessed | tf_op | source)
XLA Modules:
  0.0 1731.1 jit_solution(18085003762285996423)
XLA Ops:
  8.9 2.5 convolution_bitcast_fusion
  11.4 1.8 copy.89
  17.5 1.8 convolution_convert_fusion.3
  20.1 1.7 copy.83
  21.8 1.9 convolution_convert_fusion.2
  25.8 2.1 reshape.548
  27.9 2.1 reshape.550
  29.9 2.1 reshape.549
  32.0 11.7 all-gather
  43.7 2.3 copy.82
  46.0 9.5 all-gather.1
  55.5 2.3 copy.84
  61.4 2.1 reshape.551
  63.5 5.0 fusion.1
  68.4 5.0 copy.85
  73.4 2.9 fusion.136
  78.1 1.8 fusion.25
  79.9 1.7 copy.93
  81.7 2.2 multiply_reduce_fusion.7
  86.1 2.6 multiply_convert_fusion.2
  103.4 113.8 %scatter_custom_fusion = f32[1024]{0:T(1024)S(1)} fusion(s32[16384]{0:T(1024)} %bitcast.161, f32[16384]{0:T(1024)} %broadcast.406, f32[]{:T(128)} %constant.64.clone.1), kind=kCustom, calls=%fused_computation.204 | custom fusion | flops 16384 | bytes 4608 | tf_op jit(solution)/shard_map/jvp()/scatter-add | solution.py:110
  218.7 61.9 %gather_fusion = bf16[16384,128]{1,0:T(8,128)(2,1)} fusion(bf16[4096,128]{1,0:T(8,128)(2,1)} %all-gather.4.cloned.1.call-done, s32[16384]{0:T(1024)} %broadcast_clamp_fusion.1), kind=kCustom, calls=%fused_computation | custom fusion | bytes 8454144 | tf_op jit(solution)/shard_map/gather | solution.py:225
  280.7 5.1 fusion.80
  285.7 114.2 %scatter_custom_fusion.1 = f32[1024]{0:T(1024)} fusion(s32[16384]{0:T(1024)} %bitcast.162, f32[16384]{0:T(1024)} %bitcast.172, f32[]{:T(128)} %constant.64.clone.1), kind=kCustom, calls=%fused_computation.202 | custom fusion | flops 16384 | bytes 4608 | tf_op jit(solution)/shard_map/jvp()/scatter-add | solution.py:108
  408.8 133.4 %gather_fusion.1 = f32[16384]{0:T(1024)} fusion(f32[1024]{0:T(1024)S(1)} %multiply_divide_fusion, s32[16384]{0:T(1024)} %broadcast_clamp_fusion), kind=kCustom, calls=%fused_computation.1 | custom fusion | bytes 196608 | tf_op jit(solution)/shard_map/transpose(jvp())/gather | solution.py:108
  543.1 5.4 bitcast_multiply_fusion
  548.6 89.1 %scatter_custom_fusion.2 = f32[4096,128]{1,0:T(8,128)} fusion(s32[16384]{0:T(1024)} %bitcast.173, f32[16384,128]{1,0:T(8,128)} %bitcast_multiply_fusion, f32[]{:T(128)} %constant.64.clone.1), kind=kCustom, calls=%fused_computation.68 | custom fusion | flops 2097152 | bytes 2097664 | tf_op jit(solution)/shard_map/scatter-add | solution.py:242
  638.4 6.2 fusion.138
  644.7 131.7 %reduce-scatter.14.cloned.1.call-done = f32[128,128]{1,0:T(8,128)} async-done(((f32[4096,128]{1,0:T(8,128)}), f32[128,128]{1,0:T(8,128)}) %reduce-scatter.14.cloned.1.call-update) | async-done | bytes 65552 | tf_op jit(solution)/shard_map/reduce_scatter | solution.py:244
  779.3 2.4 multiply_reduce_fusion.1
  781.9 5.0 multiply_convert_fusion.1
  788.6 1.8 multiply_reduce_fusion.2
  793.2 1.7 copy.94
  794.9 3.7 fusion.17
  798.6 2.3 copy.104
  801.0 3.5 multiply_reduce_fusion
  807.7 2.3 copy.101
  810.1 2.3 fusion.119
  812.4 3.3 fusion.69
  817.6 2.1 reshape.558
  819.7 1.9 multiply_reduce_fusion.3
  824.6 2.1 reshape.559
  826.7 3.1 convolution_convert_fusion.9
  829.8 1.8 copy.100
  831.5 3.3 fusion.67
  837.4 2.1 reshape.563
  839.5 3.3 fusion.65
  845.2 2.1 reshape.561
  847.3 3.2 fusion.66
  850.6 5.2 fusion.72
  855.8 4.9 fusion.141
  860.9 4.8 fusion.140
  865.8 4.4 copy.107
  870.3 3.1 fusion.26
  876.7 2.0 fusion.33
  878.7 38.5 %all-reduce.4 = (f32[768]{0:T(1024)}, f32[32,12]{0,1:T(8,128)}, f32[768]{0:T(1024)}, f32[768]{0:T(1024)}) all-reduce(f32[768]{0:T(1024)} %get-tuple-element.19, f32[32,12]{0,1:T(8,128)} %fusion.27, f32[768]{0:T(1024)S(1)} %copy-done.62, f32[768]{0:T(1024)S(1)} %copy-done.61), channel_id=7, replica_groups=mesh['wide'=8,'narrow'=4] {'wide','narrow'}, use_global_device_ids=true, to_apply=%region_26.27.clone | all-reduce | flops 2688 | bytes 21504
  924.3 22.6 %reduce-scatter.34.cloned.1.call-done = f32[24,128]{1,0:T(8,128)} async-done(((f32[768,128]{1,0:T(8,128)}), f32[24,128]{1,0:T(8,128)}) %reduce-scatter.34.cloned.1.call-update) | async-done | bytes 12304
  946.9 103.9 %reduce-scatter.26.cloned.1.call-done = f32[24,768]{1,0:T(8,128)} async-done(((f32[768,768]{1,0:T(8,128)}), f32[24,768]{1,0:T(8,128)}) %reduce-scatter.26.cloned.1.call-update) | async-done | bytes 73744 | tf_op jit(solution)/shard_map/reduce_scatter | solution.py:335
  1050.8 104.6 %reduce-scatter.20.cloned.1.call-done = f32[24,768]{1,0:T(8,128)} async-done(((f32[768,768]{1,0:T(8,128)}), f32[24,768]{1,0:T(8,128)}) %reduce-scatter.20.cloned.1.call-update) | async-done | bytes 73744 | tf_op jit(solution)/shard_map/reduce_scatter | solution.py:332
  1155.4 104.0 %reduce-scatter.24.cloned.1.call-done = f32[24,768]{1,0:T(8,128)} async-done(((f32[768,768]{1,0:T(8,128)}), f32[24,768]{1,0:T(8,128)}) %reduce-scatter.24.cloned.1.call-update) | async-done | bytes 73744 | tf_op jit(solution)/shard_map/reduce_scatter | solution.py:334
  1259.5 104.7 %reduce-scatter.22.cloned.1.call-done = f32[24,768]{1,0:T(8,128)} async-done(((f32[768,768]{1,0:T(8,128)}), f32[24,768]{1,0:T(8,128)}) %reduce-scatter.22.cloned.1.call-update) | async-done | bytes 73744 | tf_op jit(solution)/shard_map/reduce_scatter | solution.py:333
  1364.1 119.5 %reduce-scatter.32.cloned.1.call-done = f32[64,768]{1,0:T(8,128)} async-done(((f32[2048,768]{1,0:T(8,128)}), f32[64,768]{1,0:T(8,128)}) %reduce-scatter.32.cloned.1.call-update) | async-done | bytes 196624 | tf_op jit(solution)/shard_map/reduce_scatter | solution.py:339
  1483.6 120.8 %reduce-scatter.30.cloned.1.call-done = f32[24,2048]{1,0:T(8,128)} async-done(((f32[768,2048]{1,0:T(8,128)}), f32[24,2048]{1,0:T(8,128)}) %reduce-scatter.30.cloned.1.call-update) | async-done | bytes 196624 | tf_op jit(solution)/shard_map/reduce_scatter | solution.py:338
  1604.4 119.6 %reduce-scatter.28.cloned.1.call-done = f32[24,2048]{1,0:T(8,128)} async-done(((f32[768,2048]{1,0:T(8,128)}), f32[24,2048]{1,0:T(8,128)}) %reduce-scatter.28.cloned.1.call-update) | async-done | bytes 196624 | tf_op jit(solution)/shard_map/reduce_scatter | solution.py:337
  (258 shorter events, 74.2 us)
Async XLA Ops:
  7.2 78.9 %copy-start = (bf16[768,2048]{1,0:T(8,128)(2,1)S(1)}, bf16[768,2048]{1,0:T(8,128)(2,1)}, u32[]{:S(2)}) copy-start(bf16[768,2048]{1,0:T(8,128)(2,1)} %param.30) | copy-start | bytes 9437188
  7.2 10.3 copy-start.14
  7.2 10.3 copy-start.49
  7.2 211.5 %all-gather.4.cloned.1.call-start = ((), (), s32[]{:S(2)}) async-start(), calls=%async_computation.11 | async-start | bytes 1081344 | tf_op jit(solution)/shard_map/all_gather | solution.py:218
  7.3 4.1 copy-start.51
  14.1 67.6 %copy-start.9 = (bf16[4,32,768]{2,1,0:T(8,128)(2,1)}, bf16[4,32,768]{2,1,0:T(8,128)(2,1)S(1)}, u32[]{:S(2)}) copy-start(bf16[4,32,768]{2,1,0:T(8,128)(2,1)S(1)} %constant_dynamic-slice_fusion) | copy-start | bytes 589828
  15.9 8.6 copy-start.57
  21.8 2.7 copy-start.73
  57.8 1.9 copy-start.30
  59.7 3.7 copy-start.55
  76.3 3.6 copy-start.1
  76.3 3.6 copy-start.47
  76.4 1.7 copy-start.19
  77.3 2.6 copy-start.56
  79.9 4.5 copy-start.53
  81.7 3.3 copy-start.20
  83.9 4.8 copy-start.11
  86.0 2.6 copy-start.24
  86.0 3.4 copy-start.72
  88.6 1.9 copy-start.22
  89.5 2.1 copy-start.39
  89.5 2.1 copy-start.48
  90.6 2.8 copy-start.70
  90.6 12.2 copy-start.59
  93.4 683.0 %reduce-scatter.14.cloned.1.call-start = ((), (), s32[]{:S(2)}) async-start(), calls=%async_computation.12 | async-start | bytes 2162688 | tf_op jit(solution)/shard_map/reduce_scatter | solution.py:244
  543.1 5.4 copy-start.36
  637.7 201.8 %reduce-scatter.18.cloned.1.call-start = ((), (), s32[]{:S(2)}) async-start(), calls=%async_computation.14 | async-start | bytes 983040 | tf_op jit(solution)/shard_map/reduce_scatter | solution.py:286
  638.4 140.8 %copy-start.60 = (f32[256]{0:T(256)S(1)}, f32[256]{0:T(256)}, u32[]{:S(2)}) copy-start(f32[256]{0:T(256)} %copy-done.59) | copy-start | bytes 3076
  776.3 5.3 copy-start.71
  776.4 5.3 copy-start.8
  779.2 2.4 copy-start.40
  779.2 2.6 copy-start.25
  781.9 8.6 copy-start.13
  781.9 5.0 copy-start.21
  786.9 1.7 copy-start.12
  786.9 1.7 copy-start.54
  786.9 1.7 copy-start.64
  788.6 1.8 copy-start.69
  800.9 46.4 %reduce-scatter.16.cloned.1.call-start = ((), (), s32[]{:S(2)}) async-start(), calls=%async_computation.13 | async-start | bytes 983040 | tf_op jit(solution)/shard_map/reduce_scatter | solution.py:280
  801.0 3.5 copy-start.2
  804.5 1.9 copy-start.29
  810.0 136.9 %reduce-scatter.34.cloned.1.call-start = ((), (), s32[]{:S(2)}) async-start(), calls=%async_computation.22 | async-start | bytes 405504
  812.4 238.4 %reduce-scatter.26.cloned.1.call-start = ((), (), s32[]{:S(2)}) async-start(), calls=%async_computation.18 | async-start | bytes 2433024 | tf_op jit(solution)/shard_map/reduce_scatter | solution.py:335
  815.7 339.7 %reduce-scatter.20.cloned.1.call-start = ((), (), s32[]{:S(2)}) async-start(), calls=%async_computation.15 | async-start | bytes 2433024 | tf_op jit(solution)/shard_map/reduce_scatter | solution.py:332
  819.7 1.9 copy-start.5
  819.7 1.9 copy-start.42
  819.7 3.6 copy-start.18
  823.6 7.9 copy-start.50
  823.6 7.9 copy-start.58
  834.8 424.6 %reduce-scatter.24.cloned.1.call-start = ((), (), s32[]{:S(2)}) async-start(), calls=%async_computation.17 | async-start | bytes 2433024 | tf_op jit(solution)/shard_map/reduce_scatter | solution.py:334
  842.8 521.3 %reduce-scatter.22.cloned.1.call-start = ((), (), s32[]{:S(2)}) async-start(), calls=%async_computation.16 | async-start | bytes 2433024 | tf_op jit(solution)/shard_map/reduce_scatter | solution.py:333
  850.5 633.1 %reduce-scatter.32.cloned.1.call-start = ((), (), s32[]{:S(2)}) async-start(), calls=%async_computation.21 | async-start | bytes 6488064 | tf_op jit(solution)/shard_map/reduce_scatter | solution.py:339
  855.8 748.7 %reduce-scatter.30.cloned.1.call-start = ((), (), s32[]{:S(2)}) async-start(), calls=%async_computation.20 | async-start | bytes 6488064 | tf_op jit(solution)/shard_map/reduce_scatter | solution.py:338
  860.7 863.4 %reduce-scatter.28.cloned.1.call-start = ((), (), s32[]{:S(2)}) async-start(), calls=%async_computation.19 | async-start | bytes 6488064 | tf_op jit(solution)/shard_map/reduce_scatter | solution.py:337
  865.8 4.5 copy-start.35
  870.2 3.1 copy-start.45
  870.2 3.1 copy-start.52
  870.3 4.2 copy-start.26
  870.3 4.2 copy-start.27
  870.3 4.2 copy-start.33
  873.4 1.7 copy-start.31
  873.4 1.7 copy-start.37
  876.7 2.1 copy-start.61
  876.7 2.1 copy-start.62
  (23 other events, 23.4 us)
Sparse Core Ops, SparseCore 0:
  93.5 55.3 all-gather.3
  637.8 138.5 reduce-scatter.13
  801.0 19.1 reduce-scatter.17
  822.6 23.2 reduce-scatter.15
  852.0 94.8 reduce-scatter.33
  952.6 98.1 reduce-scatter.25
  1057.5 97.8 reduce-scatter.19
  1161.3 98.1 reduce-scatter.23
  1266.2 97.9 reduce-scatter.21
  1370.2 113.3 reduce-scatter.31
  1490.8 113.6 reduce-scatter.29
  1610.5 113.5 reduce-scatter.27
where the time goes:
time: 1740 us; the launch traced here: 1730 us
  waiting for transfers between devices  932 us (54%)
  other arithmetic  350 us (20%)
  local copies, waits for them, and re-layouts  272 us (16%)
  matrix products  102 us (6%)
  blocking collectives  59.7 us (3%)
    gather x1, local copies, waits for them, and re-layouts, pooled_loss(): jax.ops.segment_sum(similar.reshape(-1), slot_ids.reshape(-1), num_segmen...  133 us
    reduce_scatter x1, waiting for transfers between devices, on_device(): lax.psum_scatter(whole_term, ('wide', 'narrow'), scatter_dimension=0, til...  132 us
    reduce_scatter x1, waiting for transfers between devices, on_device(): lax.psum_scatter(up_grad, ('wide', 'narrow'), scatter_dimension=0, tiled=...  121 us
    reduce_scatter x1, waiting for transfers between devices, on_device(): lax.psum_scatter(gate_grad, ('wide', 'narrow'), scatter_dimension=0, tile...  120 us
    reduce_scatter x1, waiting for transfers between devices, on_device(): lax.psum_scatter(down_grad, ('wide', 'narrow'), scatter_dimension=0, tile...  119 us
    scatter-add x1, other arithmetic, pooled_loss(): jax.ops.segment_sum(similar.reshape(-1), slot_ids.reshape(-1), num_segmen...  114 us
    scatter-add x1, other arithmetic, pooled_loss(): jax.ops.segment_sum(jnp.ones_like(similar).reshape(-1), slot_ids.reshape(...  114 us
    reduce_scatter x1, waiting for transfers between devices, on_device(): lax.psum_scatter(key_grad_w, ('wide', 'narrow'), scatter_dimension=0, til...  105 us
  transfers between devices with their start and end apart: 12, of which 9 were waited for; matrix products, arithmetic and copies ran while one was open for 12% of the time, Pallas kernels for 0%

commit v1 on v0

--- a/solution.py
+++ b/solution.py
@@ -1,6 +1,8 @@
 import jax
 import jax.numpy as jnp
 from jax import lax
+from jax.experimental import pallas as pl
+from jax.experimental.pallas import tpu as pltpu
 from jax.sharding import PartitionSpec as P
 
 BUCKETS = 32
@@ -51,6 +53,88 @@
     return lax.dot_general(
         leftward_operand, right_side, (((1,), (1,)), ((), ())), preferred_element_type=jnp.float32
     )
+
+
+def rank_bits():
+    return (lax.axis_size("wide") * lax.axis_size("narrow")).bit_length() - 1
+
+
+def my_bit(bit):
+    rank = lax.axis_index("wide") * lax.axis_size("narrow") + lax.axis_index("narrow")
+    return (rank >> bit) & 1
+
+
+def swap(values, bit):
+    ranks = 1 << rank_bits()
+    pairs = [(rank, rank ^ (1 << bit)) for rank in range(ranks)]
+    return lax.ppermute(values, ("wide", "narrow"), pairs)
+
+
+def scatter_sum(values, order, last_type=jnp.float32):
+    bits = sorted(order, reverse=True)
+    tail = (values.shape[0] >> len(bits),) + values.shape[1:]
+    values = values.reshape((2,) * len(bits) + tail)
+    for step, bit in enumerate(order):
+        axis = bits.index(bit)
+        bits.pop(axis)
+        mine = my_bit(bit)
+        kept = lax.dynamic_index_in_dim(values, mine, axis, keepdims=False)
+        sent = lax.dynamic_index_in_dim(values, 1 - mine, axis, keepdims=False)
+        total = kept.astype(jnp.float32) + swap(sent, bit).astype(jnp.float32)
+        values = total.astype(last_type if step == len(order) - 1 else values.dtype)
+    return values
+
+
+def gather_all(values, order):
+    bits = []
+    tail = values.shape
+    for bit in order:
+        other = swap(values, bit)
+        mine = my_bit(bit)
+        first = jnp.where(mine == 0, values, other)
+        second = jnp.where(mine == 0, other, values)
+        bits_now = sorted(bits + [bit], reverse=True)
+        axis = bits_now.index(bit)
+        values = jnp.stack([first, second], axis)
+        bits = bits_now
+    return values.reshape((-1,) + tail[1:])
+
+
+def sum_all(values):
+    for bit in range(rank_bits()):
+        values = values + swap(values, bit)
+    return values
+
+
+def count_kernel(places_ref, counts_ref, scratch_ref):
+    rows = places_ref.shape[0]
+    blocks = counts_ref.shape[0]
+
+    def one_row(row, carry):
+        places = places_ref[pl.ds(row, 1), :]
+        high = places >> 7
+        low = places & 127
+        picks = places.shape[1]
+        high_hot = (lax.broadcasted_iota(jnp.int32, (blocks, picks), 0) == high).astype(jnp.bfloat16)
+        low_hot = (lax.broadcasted_iota(jnp.int32, (128, picks), 0) == low).astype(jnp.bfloat16)
+        scratch_ref[pl.ds(row, blocks, stride=rows), :] = right_product(high_hot, low_hot)
+        return carry
+
+    lax.fori_loop(0, rows, one_row, 0, unroll=8)
+    for block in range(blocks):
+        counts_ref[block] = scratch_ref[block * rows : (block + 1) * rows, :].astype(jnp.bfloat16)
+
+
+def count_places(places, blocks):
+    rows = places.shape[0]
+    return pl.pallas_call(
+        count_kernel,
+        out_shape=jax.ShapeDtypeStruct((blocks, rows, 128), jnp.bfloat16),
+        in_specs=[pl.BlockSpec(memory_space=pltpu.VMEM)],
+        out_specs=pl.BlockSpec(memory_space=pltpu.VMEM),
+        scratch_shapes=[pltpu.VMEM((blocks * rows, 128), jnp.float32)],
+        compiler_params=pltpu.CompilerParams(vmem_limit_bytes=56 * 1024 * 1024),
+    )(places)
 
 
 def attend_scores(query_heads, key_heads, pos_bias, key_keep):
@@ -97,20 +181,9 @@
     return (query_gradients, grad_keys, grad_values, grad_scores)
 
 
-def pooled_loss(similar, owner_doc, lengths, positives, doc_total):
-    slot_count = similar.shape[0]
-    slot_length = similar.shape[1]
-    slot_ids = jnp.arange(slot_count * slot_length, dtype=jnp.int32).reshape(
-        slot_count, slot_length, 1
-    )
-    slot_ids = slot_ids * doc_total + owner_doc
-    segments = slot_count * slot_length * doc_total
-    summed = jax.ops.segment_sum(similar.reshape(-1), slot_ids.reshape(-1), num_segments=segments)
-    summed = summed.reshape(slot_count, slot_length, doc_total)
-    tallies = jax.ops.segment_sum(
-        jnp.ones_like(similar).reshape(-1), slot_ids.reshape(-1), num_segments=segments
-    )
-    tallies = tallies.reshape(slot_count, slot_length, doc_total)
+def pooled_loss(summed, tallies, lengths, positives):
+    slot_length = summed.shape[1]
+    doc_total = summed.shape[2]
     pooled = summed / jnp.maximum(tallies, 1.0)
     valid_mask = (jnp.arange(slot_length, dtype=jnp.int32)[None, :] < lengths[:, None]).astype(
         jnp.float32
@@ -173,16 +246,14 @@
     attend_normed, attend_back = jax.vjp(rms_norm, input_rows, attend_gain)
     normed = attend_normed.astype(jnp.bfloat16)
     query_heads = product(normed, query_weight).astype(jnp.bfloat16)
-    key_heads = product(normed, key_weight).astype(jnp.bfloat16)
-    value_heads = product(normed, value_weight).astype(jnp.bfloat16)
-    doc_keys = key_heads[:doc_flat].reshape(doc_count, doc_rows, width)
-    doc_values = value_heads[:doc_flat].reshape(doc_count, doc_rows, width)
-    all_keys, all_values = (
-        lax.all_gather(doc_keys, "narrow", axis=1, tiled=True),
-        lax.all_gather(doc_values, "narrow", axis=1, tiled=True),
-    )
-    key_all = all_keys.reshape(doc_count, doc_length, head_count, head_size)
-    value_all = all_values.reshape(doc_count, doc_length, head_count, head_size)
+    key_heads = product(normed[doc_flat:], key_weight).astype(jnp.bfloat16)
+    value_heads = product(normed[doc_flat:], value_weight).astype(jnp.bfloat16)
+    whole_doc = lax.all_gather(doc_tokens[0], "narrow", axis=0, tiled=True).astype(jnp.float32)
+    whole_normed = rms_norm(whole_doc, attend_gain).astype(jnp.bfloat16)
+    key_all = product(whole_normed, key_weight).astype(jnp.bfloat16)
+    value_all = product(whole_normed, value_weight).astype(jnp.bfloat16)
+    key_all = key_all.reshape(doc_count, doc_length, head_count, head_size)
+    value_all = value_all.reshape(doc_count, doc_length, head_count, head_size)
     row_places = narrow_rank * doc_rows + jnp.arange(doc_rows, dtype=jnp.int32)
     doc_onehot = bucket_onehot(row_places, jnp.arange(doc_length, dtype=jnp.int32))
     doc_bias = jnp.einsum("rcu,uh->hrc", doc_onehot, bias_table, precision=highest)
@@ -194,8 +265,8 @@
     doc_query = query_heads[:doc_flat].reshape(doc_count, doc_rows, head_count, head_size)
     doc_mixed, doc_logsum = attend_forward(doc_query, key_all, value_all, doc_bias, doc_keep)
     slot_query = query_heads[doc_flat:].reshape(own_slots, slot_length, head_count, head_size)
-    slot_key = key_heads[doc_flat:].reshape(own_slots, slot_length, head_count, head_size)
-    slot_value = value_heads[doc_flat:].reshape(own_slots, slot_length, head_count, head_size)
+    slot_key = key_heads.reshape(own_slots, slot_length, head_count, head_size)
+    slot_value = value_heads.reshape(own_slots, slot_length, head_count, head_size)
     slot_mixed, slot_logsum = attend_forward(slot_query, slot_key, slot_value, slot_bias, slot_keep)
     mixed = jnp.concatenate(
         [doc_mixed.reshape(doc_flat, width), slot_mixed.reshape(query_flat, width)], 0
@@ -214,82 +285,76 @@
     unit_value, unit_back = jax.vjp(unit_scale, embedded)
     unit_round = unit_value.astype(jnp.bfloat16)
     passage_normalized_vector = unit_round[:doc_flat]
-    slot_unit = unit_round[doc_flat:].reshape(own_slots, slot_length, -1)
-    every_unit = lax.all_gather(passage_normalized_vector, ("wide", "narrow"), axis=0, tiled=True)
-    owner_doc = my_picked // doc_length
-    place_doc = my_picked % doc_length
-    gathered_row = (
-        (owner_doc // doc_count * narrow_size + place_doc // doc_rows) * doc_count
-        + owner_doc % doc_count
-    ) * doc_rows + place_doc % doc_rows
-    picked_rows = every_unit[gathered_row]
-    similar = jnp.einsum(
-        "aikp,aip->aik", picked_rows, slot_unit, preferred_element_type=jnp.float32
-    )
-
-    def loss_of(similar_values):
-        return pooled_loss(similar_values, owner_doc, my_lengths, my_positives, doc_total)
-
-    losses, loss_back = jax.vjp(loss_of, similar)
-    grad_similar = loss_back(jnp.ones_like(losses))[0]
-    grad_slot_unit = jnp.einsum("aik,aikp->aip", grad_similar, picked_rows, precision=highest)
+    slot_unit = unit_round[doc_flat:]
+    columns = slot_unit.shape[-1]
+    bits = rank_bits()
+    every_unit = gather_all(passage_normalized_vector, list(range(bits))[::-1])
+    blocks = doc_total * doc_length // 128
+    places = my_picked.reshape(query_flat, -1)
+    counts = count_places(places, blocks)
+    per_doc = doc_length // 128
+    block_sum = jnp.einsum(
+        "brl,blp->brp",
+        counts,
+        every_unit.reshape(blocks, 128, columns),
+        preferred_element_type=jnp.float32,
+    )
+    doc_sum = jnp.sum(block_sum.reshape(doc_total, per_doc, query_flat, columns), 1)
     slot_unit_f = slot_unit.astype(jnp.float32)
-    columns = slot_unit_f.shape[-1]
-    contrib = grad_similar[..., None] * slot_unit_f[:, :, None, :]
-    whole_term = (
-        jnp.zeros((every_unit.shape[0], columns), jnp.float32)
-        .at[gathered_row.reshape(-1)]
-        .add(contrib.reshape(-1, columns))
-    )
-    grad_doc_unit = lax.psum_scatter(
-        whole_term, ("wide", "narrow"), scatter_dimension=0, tiled=True
-    )
+    summed = jnp.sum(doc_sum * slot_unit_f[None], -1).T.reshape(own_slots, slot_length, doc_total)
+    tallies = jnp.sum(
+        (places[:, None, :] // doc_length == jnp.arange(doc_total, dtype=jnp.int32)[:, None]).astype(
+            jnp.float32
+        ),
+        -1,
+    ).reshape(own_slots, slot_length, doc_total)
+
+    def loss_of(summed_values):
+        return pooled_loss(summed_values, tallies, my_lengths, my_positives)
+
+    losses, loss_back = jax.vjp(loss_of, summed)
+    grad_summed = loss_back(jnp.ones_like(losses))[0].reshape(query_flat, doc_total)
+    grad_slot_unit = jnp.sum(doc_sum * grad_summed.T[:, :, None], 0)
+    scaled_unit = (grad_summed.T[:, :, None] * slot_unit_f[None]).astype(jnp.bfloat16)
+    scaled_blocks = jnp.broadcast_to(
+        scaled_unit[:, None], (doc_total, per_doc, query_flat, columns)
+    ).reshape(blocks, query_flat, columns)
+    whole_term = jnp.einsum(
+        "brl,brp->blp", counts, scaled_blocks, preferred_element_type=jnp.float32
+    ).astype(jnp.bfloat16)
+    grad_doc_unit = scatter_sum(whole_term.reshape(blocks * 128, columns), range(bits))
     grad_unit = jnp.concatenate([grad_doc_unit, grad_slot_unit.reshape(query_flat, -1)], 0)
     grad_embed = unit_back(grad_unit)[0].astype(jnp.bfloat16)
-    proj_grad = left_product(normed_final, grad_embed)
+    proj_grad = left_product(normed_final, grad_embed).astype(jnp.bfloat16)
     grad_after_feed, final_gain_grad = final_back(right_product(grad_embed, proj_weight))
     grad_feed_out = grad_after_feed.astype(jnp.bfloat16)
-    down_grad = left_product(hidden, grad_feed_out)
+    down_grad = left_product(hidden, grad_feed_out).astype(jnp.bfloat16)
     grad_gate, grad_upward = gated_back(right_product(grad_feed_out, down_weight))
     grad_gate = grad_gate.astype(jnp.bfloat16)
     grad_upward = grad_upward.astype(jnp.bfloat16)
-    gate_grad = left_product(normed_feed, grad_gate)
-    up_grad = left_product(normed_feed, grad_upward)
+    gate_grad = left_product(normed_feed, grad_gate).astype(jnp.bfloat16)
+    up_grad = left_product(normed_feed, grad_upward).astype(jnp.bfloat16)
     grad_normed_feed = right_product(grad_gate, gate_weight) + right_product(grad_upward, up_weight)
     grad_feed_part, feed_gain_grad = feed_back(grad_normed_feed)
     grad_after_attend = grad_after_feed + grad_feed_part
     grad_attend_out = grad_after_attend.astype(jnp.bfloat16)
-    output_grad = left_product(mixed, grad_attend_out)
+    output_grad = left_product(mixed, grad_attend_out).astype(jnp.bfloat16)
     grad_mixed = right_product(grad_attend_out, output_weight).astype(jnp.bfloat16)
-    back_keys, back_values = (
-        lax.all_gather(doc_keys, "narrow", axis=1, tiled=True),
-        lax.all_gather(doc_values, "narrow", axis=1, tiled=True),
-    )
-    back_key_all = back_keys.reshape(doc_count, doc_length, head_count, head_size)
-    back_value_all = back_values.reshape(doc_count, doc_length, head_count, head_size)
     grad_doc_query, grad_key_all, grad_value_all, grad_doc_scores = attention_pullback_pass(
         doc_query,
-        back_key_all,
-        back_value_all,
+        key_all,
+        value_all,
         doc_bias,
         doc_keep,
         doc_logsum,
         grad_mixed[:doc_flat].reshape(doc_count, doc_rows, head_count, head_size),
     )
-    grad_doc_keys, grad_doc_values = (
-        lax.psum_scatter(
-            grad_key_all.reshape(doc_count, doc_length, width).astype(jnp.bfloat16),
-            "narrow",
-            scatter_dimension=1,
-            tiled=True,
-        ).astype(jnp.float32),
-        lax.psum_scatter(
-            grad_value_all.reshape(doc_count, doc_length, width).astype(jnp.bfloat16),
-            "narrow",
-            scatter_dimension=1,
-            tiled=True,
-        ).astype(jnp.float32),
-    )
+    grad_pair = jnp.concatenate(
+        [grad_key_all.reshape(doc_length, width), grad_value_all.reshape(doc_length, width)], 1
+    ).astype(jnp.bfloat16)
+    grad_pair = scatter_sum(grad_pair, range(narrow_size.bit_length() - 1))
+    grad_doc_keys = grad_pair[:, :width]
+    grad_doc_values = grad_pair[:, width:]
     grad_slot_query, grad_slot_key, grad_slot_value, grad_slot_scores = attention_pullback_pass(
         slot_query,
         slot_key,
@@ -305,7 +370,6 @@
     table_term = table_term + jnp.einsum(
         "nhrc,rcu->uh", grad_slot_scores.astype(jnp.float32), slot_onehot, precision=highest
     )
-    bias_table_grad = lax.psum(table_term, ("wide", "narrow"))
     query_gradients = jnp.concatenate(
         [grad_doc_query.reshape(doc_flat, width), grad_slot_query.reshape(query_flat, width)], 0
     ).astype(jnp.bfloat16)
@@ -315,9 +379,8 @@
     grad_values = jnp.concatenate(
         [grad_doc_values.reshape(doc_flat, width), grad_slot_value.reshape(query_flat, width)], 0
     ).astype(jnp.bfloat16)
-    query_grad_w = left_product(normed, query_gradients)
-    key_grad_w = left_product(normed, grad_keys)
-    value_grad_w = left_product(normed, grad_values)
+    both_grads = jnp.concatenate([query_gradients, grad_keys, grad_values], 1)
+    attend_grad_w = left_product(normed, both_grads).astype(jnp.bfloat16)
     grad_normed = (
         right_product(query_gradients, query_weight)
         + right_product(grad_keys, key_weight)
@@ -327,35 +390,44 @@
     grad_inputs = grad_after_attend + grad_input_part
     doc_grad = grad_inputs[:doc_flat].reshape(doc_count, doc_rows, width)
     query_grad = grad_inputs[doc_flat:].reshape(own_slots, slot_length, width)
-    summed = (
-        lax.psum_scatter(attend_gain_grad, ("wide", "narrow"), scatter_dimension=0, tiled=True),
-        lax.psum_scatter(query_grad_w, ("wide", "narrow"), scatter_dimension=0, tiled=True),
-        lax.psum_scatter(key_grad_w, ("wide", "narrow"), scatter_dimension=0, tiled=True),
-        lax.psum_scatter(value_grad_w, ("wide", "narrow"), scatter_dimension=0, tiled=True),
-        lax.psum_scatter(output_grad, ("wide", "narrow"), scatter_dimension=0, tiled=True),
-        lax.psum_scatter(feed_gain_grad, ("wide", "narrow"), scatter_dimension=0, tiled=True),
-        lax.psum_scatter(gate_grad, ("wide", "narrow"), scatter_dimension=0, tiled=True),
-        lax.psum_scatter(up_grad, ("wide", "narrow"), scatter_dimension=0, tiled=True),
-        lax.psum_scatter(down_grad, ("wide", "narrow"), scatter_dimension=0, tiled=True),
-        lax.psum_scatter(final_gain_grad, ("wide", "narrow"), scatter_dimension=0, tiled=True),
-        lax.psum_scatter(proj_grad, ("wide", "narrow"), scatter_dimension=0, tiled=True),
-    )
+    over_y = [0, 1, 2] + list(range(3, bits))
+    over_x = [0, 2, 1] + list(range(3, bits))
+    over_z = [0] + list(range(3, bits)) + [1, 2]
+    hidden_units = gate_grad.shape[1]
+    first_sum = scatter_sum(jnp.concatenate([gate_grad, output_grad], 1), over_y)
+    second_sum = scatter_sum(jnp.concatenate([up_grad, proj_grad], 1), over_x)
+    third_sum = scatter_sum(down_grad, over_z)
+    middle = 3 * width // 2
+    attend_sum = jnp.concatenate(
+        [scatter_sum(attend_grad_w[:, :middle], over_y), scatter_sum(attend_grad_w[:, middle:], over_x)], 1
+    )
+    small = jnp.concatenate(
+        [attend_gain_grad, feed_gain_grad, final_gain_grad, table_term.reshape(-1)]
+    )
+    small = sum_all(small.reshape(-1, 128)).reshape(-1)
+    rank = lax.axis_index("wide") * narrow_size + narrow_rank
+    gain_rows = width >> bits
+    gains = [
+        lax.dynamic_slice_in_dim(small, place * width + rank * gain_rows, gain_rows, 0)
+        for place in range(3)
+    ]
+    bias_table_grad = small[3 * width :].reshape(table_term.shape)
     return (
         losses,
         doc_grad,
         query_grad,
-        summed[0],
-        summed[1],
-        summed[2],
-        summed[3],
-        summed[4],
+        gains[0],
+        attend_sum[:, :width],
+        attend_sum[:, width : 2 * width],
+        attend_sum[:, 2 * width :],
+        first_sum[:, hidden_units:],
         bias_table_grad,
-        summed[5],
-        summed[6],
-        summed[7],
-        summed[8],
-        summed[9],
-        summed[10],
+        gains[1],
+        first_sum[:, :hidden_units],
+        second_sum[:, :hidden_units],
+        third_sum,
+        gains[2],
+        second_sum[:, hidden_units:],
     )
 
 

time: 1740 us -> 402 us (0.23)
  waiting for transfers between devices: 932 us -> 99.6 us
  other arithmetic: 350 us -> 56.6 us
  local copies, waits for them, and re-layouts: 272 us -> 101 us
  blocking collectives: 59.7 us -> 11.9 us
  starting transfers between devices: 1.08 us -> 46.6 us
  matrix products: 102 us -> 69.4 us
    reduce_scatter x10 -> x0, waiting for transfers between devices: 909 us -> none  [the longest x1 132 us: on_device(): lax.psum_scatter(whole_term, ('wide', 'narrow'), scatter_dimension=0, til...]
    scatter-add x3 -> x0, other arithmetic: 317 us -> none  [the longest x1 114 us: pooled_loss(): jax.ops.segment_sum(similar.reshape(-1), slot_ids.reshape(-1), num_segmen...]
    gather x2 -> x0, local copies, waits for them, and re-layouts: 195 us -> none  [the longest x1 133 us: pooled_loss(): jax.ops.segment_sum(similar.reshape(-1), slot_ids.reshape(-1), num_segmen...]
    ppermute x0 -> x42, waiting for transfers between devices: none -> 99.6 us  [swap(): return lax.ppermute(values, ('wide', 'narrow'), pairs)]
    ppermute x0 -> x42, starting transfers between devices: none -> 46.6 us  [swap(): return lax.ppermute(values, ('wide', 'narrow'), pairs)]
    unnamed x1 -> x0, blocking collectives: 38.5 us -> none
    unnamed x13 -> x0, waiting for transfers between devices: 22.8 us -> none
    convert_element_type x1 -> x27, other arithmetic: 1.39 us -> 19.8 us  [the longest x25 16.6 us: scatter_sum(): values = total.astype(last_type if step == len(order) - 1 else values.dtype)]
  transfers between devices with their start and end apart: 12 -> 42, of which waited for: 9 -> 25; matrix products, arithmetic and copies ran while one was open for 12% -> 14% of each run, Pallas kernels for 0% -> 2%
where the time goes in v1:
time: 402 us; the launch traced here: 394 us
  local copies, waits for them, and re-layouts  101 us (25%)
  waiting for transfers between devices  99.6 us (25%)
  matrix products  69.4 us (17%)
  other arithmetic  56.6 us (14%)
  starting transfers between devices  46.6 us (12%)
  blocking collectives  11.9 us (3%)
  Pallas kernels  6.29 us (2%)
    ppermute x42, waiting for transfers between devices, swap(): return lax.ppermute(values, ('wide', 'narrow'), pairs)  99.6 us
    ppermute x42, starting transfers between devices, swap(): return lax.ppermute(values, ('wide', 'narrow'), pairs)  46.6 us
    unnamed x232, local copies, waits for them, and re-layouts  20.2 us
    convert_element_type x25, other arithmetic, scatter_sum(): values = total.astype(last_type if step == len(order) - 1 else values.dtype)  16.6 us
    dot_general x10, matrix products, product(): jnp.dot(leftward_operand, right_side, preferred_element_type=jnp.float32)  16 us
    dot_general x6, matrix products, left_product(): lax.dot_general(leftward_operand, right_side, (((0,), (0,)), ((), ())), p...  13.3 us
    all_gather x1, blocking collectives, on_device(): lax.all_gather(doc_tokens[0], 'narrow', axis=0, tiled=True)  11.9 us
    concatenate x4, local copies, waits for them, and re-layouts, on_device(): jnp.concatenate([grad_key_all.reshape(doc_length, width), grad_value_all....  10.4 us
  transfers between devices with their start and end apart: 42, of which 25 were waited for; matrix products, arithmetic and copies ran while one was open for 14% of the time, Pallas kernels for 2%

profile of v1, /device:TPU:0, one launch (start us, length us, event | category | flops | bytes accessed | tf_op | source)
XLA Modules:
  0.0 394.4 jit_solution(8584227783915133062)
XLA Ops:
  0.7 11.9 %all-gather = bf16[1,512,768]{2,1,0:T(8,128)(2,1)} all-gather(bf16[1,128,768]{2,1,0:T(8,128)(2,1)} %param.17), channel_id=2, replica_groups=mesh['wide'=8,'narrow'=4] {'narrow'}, dimensions={1}, use_global_device_ids=true | all-gather | bytes 983040 | tf_op jit(solution)/shard_map/all_gather | solution.py:251
  16.1 2.4 convolution_convert_fusion.17
  25.4 2.5 convolution_bitcast_fusion
  27.9 1.8 copy.219
  31.3 2.1 reshape.589
  33.4 2.1 reshape.591
  35.4 1.8 convolution_convert_fusion.10
  38.1 2.1 reshape.590
  43.8 2.1 reshape.592
  45.9 2.3 copy.212
  48.2 2.3 copy.214
  50.5 5.4 %fusion.1 = f32[128,512,12]{0,2,1:T(8,128)} fusion(s32[128,512]{0,1:T(8,128)} %fusion.106, f32[32,12]{0,1:T(8,128)S(1)} %copy-done.95), kind=kOutput, calls=%fused_computation.2 | convolution fusion | flops 304087040 | bytes 3409408 | tf_op jit(solution)/shard_map/rcu,uh->hrc/dot_general | solution.py:259
  55.9 5.0 %copy.215 = f32[128,512,12]{1,0,2:T(8,128)} copy(f32[128,512,12]{0,2,1:T(8,128)} %fusion.1) | data formatting | bytes 6291456 | tf_op jit(solution)/shard_map/rcu,uh->hrc/dot_general | solution.py:259
  60.9 2.8 fusion.169
  65.5 1.8 fusion.52
  69.1 2.2 multiply_reduce_fusion.7
  72.9 2.7 multiply_convert_fusion.2
  80.6 2.6 collective-permute-start
  83.2 2.5 collective-permute-done
  90.0 3.0 collective-permute-done.1
  96.6 3.8 collective-permute-done.2
  103.0 6.5 %collective-permute-done.3 = bf16[2,2,2,128,128]{3,4,0,1,2:T(8,128)(2,1)} collective-permute-done((bf16[2,2,2,128,128]{3,4,0,1,2:T(8,128)(2,1)}, bf16[2,2,2,128,128]{3,4,0,1,2:T(8,128)(2,1)}, u32[]{:S(2)}, u32[]{:S(2)}) %collective-permute-start.3) | collective-permute-done | bytes 262176 | tf_op jit(solution)/shard_map/ppermute | solution.py:70
  115.5 6.3 %shard_map.280 = bf16[32,128,128]{2,1,0:T(8,128)(2,1)} custom-call(s32[128,128]{1,0:T(8,128)} %bitcast.371), custom_call_target="tpu_custom_call" | custom-call | tf_op jit(solution)/shard_map/pallas_call | solution.py:130
  127.4 2.4 copy.224
  129.8 2.0 bitcast_reduce_fusion
  139.3 2.0 multiply_convert_fusion.6
  143.2 2.0 copy.230
  145.8 2.0 copy.266
  150.9 8.6 %collective-permute-done.6 = bf16[2,2,2,128,128]{3,4,0,1,2:T(8,128)(2,1)} collective-permute-done((bf16[2,2,2,128,128]{3,4,0,1,2:T(8,128)(2,1)}, bf16[2,2,2,128,128]{3,4,0,1,2:T(8,128)(2,1)}, u32[]{:S(2)}, u32[]{:S(2)}) %collective-permute-start.6) | collective-permute-done | bytes 262176 | tf_op jit(solution)/shard_map/ppermute | solution.py:70
  163.4 3.8 collective-permute-done.7
  176.2 2.6 collective-permute-start.9
  184.7 2.2 convolution_convert_fusion.15
  190.1 4.3 %multiply_convert_fusion.1 = (bf16[256,2048]{1,0:T(8,128)(2,1)S(1)}, bf16[256,2048]{1,0:T(8,128)(2,1)S(1)}) fusion(f32[256,2048]{1,0:T(8,128)S(1)} %copy-done.57, f32[256,2048]{1,0:T(8,128)S(1)} %copy-done.114, bf16[2048,768]{1,0:T(8,128)(2,1)} %param.31, f32[256,768]{1,0:T(8,128)S(1)} %add_add_fusion.2), kind=kOutput, calls=%fused_computation.39 | convolution fusion | flops 818085888 | bytes 10223616 | tf_op jit(solution)/shard_map/dot_general | solution.py:53
  207.3 3.0 convolution_convert_fusion.1
  210.3 2.8 convolution_convert_fusion.2
  213.1 2.7 convolution_convert_fusion.3
  222.9 4.5 %copy.245 = bf16[12,128,512]{1,0,2:T(8,128)(2,1)} copy(bf16[12,128,512]{2,1,0:T(8,128)(2,1)} %copy-done.5) | data formatting | bytes 3145728 | tf_op jit(solution)/shard_map/convert_element_type | solution.py:172
  229.3 2.2 reshape.600
  231.5 2.9 concatenate.50
  234.4 3.0 copy.240
  245.7 3.4 copy.239
  249.1 2.0 fusion.69
  258.2 3.0 fusion.53
  266.1 9.6 %collective-permute-done.11 = bf16[128,1536]{1,0:T(8,128)(2,1)S(1)} collective-permute-done((bf16[128,1536]{1,0:T(8,128)(2,1)}, bf16[128,1536]{1,0:T(8,128)(2,1)S(1)}, u32[]{:S(2)}, u32[]{:S(2)}) %collective-permute-start.11) | collective-permute-done | bytes 393248 | tf_op jit(solution)/shard_map/ppermute | solution.py:70
  285.6 2.2 collective-permute-done.14
  291.5 2.6 collective-permute-start.16
  298.1 2.5 fusion.6
  300.6 1.9 collective-permute-start.38
  302.5 1.9 fusion.5
  310.2 2.1 fusion.2
  314.0 6.4 %collective-permute-done.38 = bf16[2,2,2,64,768]{4,3,1,2,0:T(8,128)(2,1)S(1)} collective-permute-done((bf16[2,2,2,64,768]{4,3,1,2,0:T(8,128)(2,1)S(1)}, bf16[2,2,2,64,768]{4,3,1,2,0:T(8,128)(2,1)S(1)}, u32[]{:S(2)}, u32[]{:S(2)}) %collective-permute-start.38) | collective-permute-done | bytes 786464 | tf_op jit(solution)/shard_map/ppermute | solution.py:70
  320.6 2.5 collective-permute-start.39
  324.8 10.8 %collective-permute-done.23 = bf16[2,2,2,24,1152]{4,3,0,1,2:T(8,128)(2,1)S(1)} collective-permute-done((bf16[2,2,2,24,1152]{4,3,0,1,2:T(8,128)(2,1)S(1)}, bf16[2,2,2,24,1152]{4,3,0,1,2:T(8,128)(2,1)S(1)}, u32[]{:S(2)}, u32[]{:S(2)}) %collective-permute-start.23) | collective-permute-done | bytes 442400 | tf_op jit(solution)/shard_map/ppermute | solution.py:70
  339.6 9.1 %collective-permute-done.24 = bf16[2,2,24,1152]{3,2,0,1:T(8,128)(2,1)S(1)} collective-permute-done((bf16[2,2,24,1152]{3,2,0,1:T(8,128)(2,1)S(1)}, bf16[2,2,24,1152]{3,2,0,1:T(8,128)(2,1)S(1)}, u32[]{:S(2)}, u32[]{:S(2)}) %collective-permute-start.24) | collective-permute-done | bytes 221216 | tf_op jit(solution)/shard_map/ppermute | solution.py:70
  349.7 2.1 collective-permute-start.21
  351.7 1.8 collective-permute-done.25
  353.6 2.6 collective-permute-start.26
  356.3 2.9 collective-permute-done.26
  361.4 3.7 collective-permute-done.41
  366.9 10.9 %collective-permute-done.29 = bf16[2,2,24,2816]{3,2,0,1:T(8,128)(2,1)S(1)} collective-permute-done((bf16[2,2,24,2816]{3,2,0,1:T(8,128)(2,1)S(1)}, bf16[2,2,24,2816]{3,2,0,1:T(8,128)(2,1)S(1)}, u32[]{:S(2)}, u32[]{:S(2)}) %collective-permute-start.29) | collective-permute-done | bytes 540704 | tf_op jit(solution)/shard_map/ppermute | solution.py:70
  378.6 3.1 collective-permute-start.36
  381.6 4.2 %collective-permute-done.30 = bf16[2,24,2816]{2,1,0:T(8,128)(2,1)S(1)} collective-permute-done((bf16[2,24,2816]{2,1,0:T(8,128)(2,1)S(1)}, bf16[2,24,2816]{2,1,0:T(8,128)(2,1)S(1)}, u32[]{:S(2)}, u32[]{:S(2)}) %collective-permute-start.30) | collective-permute-done | bytes 270368 | tf_op jit(solution)/shard_map/ppermute | solution.py:70
  385.9 3.2 collective-permute-start.31
  390.4 2.2 collective-permute-done.31
  (476 shorter events, 164.0 us)
Async XLA Ops:
  0.6 72.2 %copy-start = (bf16[768,2048]{1,0:T(8,128)(2,1)S(1)}, bf16[768,2048]{1,0:T(8,128)(2,1)}, u32[]{:S(2)}) copy-start(bf16[768,2048]{1,0:T(8,128)(2,1)} %param.30) | copy-start | bytes 9437188
  0.7 24.4 %copy-start.91 = (s32[32,32]{0,1:T(8,128)}, s32[32,32]{0,1:T(8,128)S(1)}, u32[]{:S(2)}) copy-start(s32[32,32]{0,1:T(8,128)S(1)} %fusion.134) | copy-start | bytes 12292
  12.6 5.9 %copy-start.65 = (bf16[768,768]{1,0:T(8,128)(2,1)S(1)}, bf16[768,768]{1,0:T(8,128)(2,1)}, u32[]{:S(2)}) copy-start(bf16[768,768]{1,0:T(8,128)(2,1)} %param.25) | copy-start | bytes 3538948
  13.7 5.8 %copy-start.45 = (bf16[1,512,768]{2,1,0:T(8,128)(2,1)S(1)}, bf16[1,512,768]{2,1,0:T(8,128)(2,1)}, u32[]{:S(2)}) copy-start(bf16[1,512,768]{2,1,0:T(8,128)(2,1)} %all-gather) | copy-start | bytes 2359300
  16.0 19.4 %copy-start.33 = (bf16[256,768]{1,0:T(8,128)(2,1)}, bf16[256,768]{1,0:T(8,128)(2,1)S(1)}, u32[]{:S(2)}) copy-start(bf16[256,768]{1,0:T(8,128)(2,1)S(1)} %fusion.62) | copy-start | bytes 1179652
  35.4 4.8 %copy-start.112 = (pred[4,32]{1,0:T(4,128)(4,1)S(1)}, pred[4,32]{1,0:T(4,128)(4,1)}, u32[]{:S(2)}) copy-start(pred[4,32]{1,0:T(4,128)(4,1)} %get-tuple-element.134) | copy-start | bytes 388
  38.1 22.9 %copy-start.58 = (bf16[128,768]{0,1:T(8,128)(2,1)}, bf16[128,768]{0,1:T(8,128)(2,1)S(1)}, u32[]{:S(2)}) copy-start(bf16[128,768]{0,1:T(8,128)(2,1)S(1)} %copy.213) | copy-start | bytes 589828
  43.8 6.7 %copy-start.95 = (f32[32,12]{0,1:T(8,128)S(1)}, f32[32,12]{0,1:T(8,128)}, u32[]{:S(2)}) copy-start(f32[32,12]{0,1:T(8,128)} %param.27) | copy-start | bytes 4612
  77.4 33.2 %copy-start.97 = (f32[256]{0:T(256)}, f32[256]{0:T(256)S(1)}, u32[]{:S(2)}) copy-start(f32[256]{0:T(256)S(1)} %fusion.149) | copy-start | bytes 3076
  79.9 33.5 %copy-start.98 = (f32[4,32]{1,0:T(4,128)S(1)}, f32[4,32]{1,0:T(4,128)}, u32[]{:S(2)}) copy-start(f32[4,32]{1,0:T(4,128)} %get-tuple-element.135) | copy-start | bytes 1540
  80.6 5.1 %collective-permute-start = (bf16[128,128]{0,1:T(8,128)(2,1)}, bf16[128,128]{0,1:T(8,128)(2,1)}, u32[]{:S(2)}, u32[]{:S(2)}) collective-permute-start(bf16[128,128]{0,1:T(8,128)(2,1)} %slice.91), channel_id=1, source_target_pairs={{0,16},{1,17},{2,18},{3,19},{4,20},{5,21},{6,22},{7,23},{8,24},{9,... | collective-permute-start | bytes 98312 | tf_op jit(solution)/shard_map/ppermute | solution.py:70
  88.4 4.6 %collective-permute-start.1 = (bf16[2,128,128]{1,2,0:T(8,128)(2,1)}, bf16[2,128,128]{1,2,0:T(8,128)(2,1)}, u32[]{:S(2)}, u32[]{:S(2)}) collective-permute-start(bf16[2,128,128]{1,2,0:T(8,128)(2,1)} %pad_maximum_fusion.12), channel_id=1, source_target_pairs={{0,8},{1,9},{2,10},{3,11},{4,12},{5,13},{6,14},{7,15},{8,0},{9,1},... | collective-permute-start | bytes 196616 | tf_op jit(solution)/shard_map/ppermute | solution.py:70
  95.1 5.3 %collective-permute-start.2 = (bf16[2,2,128,128]{2,3,0,1:T(8,128)(2,1)}, bf16[2,2,128,128]{2,3,0,1:T(8,128)(2,1)}, u32[]{:S(2)}, u32[]{:S(2)}) collective-permute-start(bf16[2,2,128,128]{2,3,0,1:T(8,128)(2,1)} %pad_maximum_fusion.9), channel_id=1, source_target_pairs={{0,4},{1,5},{2,6},{3,7},{4,0},{5,1},{6,2},{7,3},{8,12},{9,13},{10,... | collective-permute-start | bytes 393224 | tf_op jit(solution)/shard_map/ppermute | solution.py:70
  102.8 6.7 %collective-permute-start.3 = (bf16[2,2,2,128,128]{3,4,0,1,2:T(8,128)(2,1)}, bf16[2,2,2,128,128]{3,4,0,1,2:T(8,128)(2,1)}, u32[]{:S(2)}, u32[]{:S(2)}) collective-permute-start(bf16[2,2,2,128,128]{3,4,0,1,2:T(8,128)(2,1)} %pad_maximum_fusion.6), channel_id=1, source_target_pairs={{0,2},{1,3},{2,0},{3,1},{4,6},{5,7},{6,4},{7,5},{8,10},{9,11},{10,... | collective-permute-start | bytes 786440 | tf_op jit(solution)/shard_map/ppermute | solution.py:70
  112.2 12.9 %collective-permute-start.4 = (bf16[2,2,2,2,128,128]{4,5,0,1,2,3:T(8,128)(2,1)}, bf16[2,2,2,2,128,128]{4,5,0,1,2,3:T(8,128)(2,1)}, u32[]{:S(2)}, u32[]{:S(2)}) collective-permute-start(bf16[2,2,2,2,128,128]{4,5,0,1,2,3:T(8,128)(2,1)} %pad_maximum_fusion.3), channel_id=1, source_target_pairs={{0,1},{1,0},{2,3},{3,2},{4,5},{5,4},{6,7},{7,6},{8,9},{9,8},{10,11... | collective-permute-start | bytes 1572872 | tf_op jit(solution)/shard_map/ppermute | solution.py:70
  145.3 2.6 collective-permute-start.5
  150.7 8.7 %collective-permute-start.6 = (bf16[2,2,2,128,128]{3,4,0,1,2:T(8,128)(2,1)}, bf16[2,2,2,128,128]{3,4,0,1,2:T(8,128)(2,1)}, u32[]{:S(2)}, u32[]{:S(2)}) collective-permute-start(bf16[2,2,2,128,128]{3,4,0,1,2:T(8,128)(2,1)} %dynamic-slice_bitcast_fusion.10), channel_id=1, source_target_pairs={{0,2},{1,3},{2,0},{3,1},{4,6},{5,7},{6,4},{7,5},{8,10},{9,11},{10,... | collective-permute-start | bytes 786440 | tf_op jit(solution)/shard_map/ppermute | solution.py:70
  161.9 5.3 %collective-permute-start.7 = (bf16[2,2,128,128]{2,3,0,1:T(8,128)(2,1)}, bf16[2,2,128,128]{2,3,0,1:T(8,128)(2,1)}, u32[]{:S(2)}, u32[]{:S(2)}) collective-permute-start(bf16[2,2,128,128]{2,3,0,1:T(8,128)(2,1)} %dynamic-slice_bitcast_fusion.16), channel_id=1, source_target_pairs={{0,4},{1,5},{2,6},{3,7},{4,0},{5,1},{6,2},{7,3},{8,12},{9,13},{10,... | collective-permute-start | bytes 393224 | tf_op jit(solution)/shard_map/ppermute | solution.py:70
  169.5 4.6 %collective-permute-start.8 = (bf16[2,128,128]{1,2,0:T(8,128)(2,1)}, bf16[2,128,128]{1,2,0:T(8,128)(2,1)}, u32[]{:S(2)}, u32[]{:S(2)}) collective-permute-start(bf16[2,128,128]{1,2,0:T(8,128)(2,1)} %dynamic-slice_bitcast_fusion.21), channel_id=1, source_target_pairs={{0,8},{1,9},{2,10},{3,11},{4,12},{5,13},{6,14},{7,15},{8,0},{9,1},... | collective-permute-start | bytes 196616 | tf_op jit(solution)/shard_map/ppermute | solution.py:70
  176.2 5.1 %collective-permute-start.9 = (bf16[128,128]{0,1:T(8,128)(2,1)}, bf16[128,128]{0,1:T(8,128)(2,1)}, u32[]{:S(2)}, u32[]{:S(2)}) collective-permute-start(bf16[128,128]{0,1:T(8,128)(2,1)} %dynamic-slice_bitcast_fusion.24), channel_id=1, source_target_pairs={{0,16},{1,17},{2,18},{3,19},{4,20},{5,21},{6,22},{7,23},{8,24},{9,... | collective-permute-start | bytes 98312 | tf_op jit(solution)/shard_map/ppermute | solution.py:70
  181.1 5.9 %copy-start.12 = (f32[256,768]{1,0:T(8,128)S(1)}, f32[256,768]{1,0:T(8,128)}, u32[]{:S(2)}) copy-start(f32[256,768]{1,0:T(8,128)} %copy-done.11) | copy-start | bytes 2359300
  190.0 7.4 %copy-start.19 = (f32[256,768]{1,0:T(8,128)}, f32[256,768]{1,0:T(8,128)S(1)}, u32[]{:S(2)}) copy-start(f32[256,768]{1,0:T(8,128)S(1)} %add_add_fusion.2) | copy-start | bytes 2359300
  198.6 7.1 %copy-start.13 = (f32[256,768]{1,0:T(8,128)}, f32[256,768]{1,0:T(8,128)S(1)}, u32[]{:S(2)}) copy-start(f32[256,768]{1,0:T(8,128)S(1)} %fusion.64) | copy-start | bytes 2359300
  222.9 4.9 %copy-start.62 = (bf16[4,32,12,64]{3,1,2,0:T(8,128)(2,1)S(1)}, bf16[4,32,12,64]{3,1,2,0:T(8,128)(2,1)}, u32[]{:S(2)}) copy-start(bf16[4,32,12,64]{3,1,2,0:T(8,128)(2,1)} %fusion.39) | copy-start | bytes 589828
  229.3 8.1 %copy-start.4 = (bf16[2048,768]{1,0:T(8,128)(2,1)S(1)}, bf16[2048,768]{1,0:T(8,128)(2,1)}, u32[]{:S(2)}) copy-start(bf16[2048,768]{1,0:T(8,128)(2,1)} %convolution_convert_fusion.1) | copy-start | bytes 9437188
  240.1 57.9 %collective-permute-start.37 = (bf16[2,2,2,2,64,768]{5,4,2,3,0,1:T(8,128)(2,1)}, bf16[2,2,2,2,64,768]{5,4,2,3,0,1:T(8,128)(2,1)}, u32[]{:S(2)}, u32[]{:S(2)}) collective-permute-start(bf16[2,2,2,2,64,768]{5,4,2,3,0,1:T(8,128)(2,1)} %bitcast.339), channel_id=1, source_target_pairs={{0,1},{1,0},{2,3},{3,2},{4,5},{5,4},{6,7},{7,6},{8,9},{9,8},{10,11... | collective-permute-start | bytes 4718600 | tf_op jit(solution)/shard_map/ppermute | solution.py:70
  244.6 57.9 %collective-permute-start.32 = (bf16[2,2,2,2,24,2176]{5,4,0,1,3,2:T(8,128)(2,1)}, bf16[2,2,2,2,24,2176]{5,4,0,1,3,2:T(8,128)(2,1)}, u32[]{:S(2)}, u32[]{:S(2)}) collective-permute-start(bf16[2,2,2,2,24,2176]{5,4,0,1,3,2:T(8,128)(2,1)} %bitcast.338), channel_id=1, source_target_pairs={{0,1},{1,0},{2,3},{3,2},{4,5},{5,4},{6,7},{7,6},{8,9},{9,8},{10,11... | collective-permute-start | bytes 5013512 | tf_op jit(solution)/shard_map/ppermute | solution.py:70
  245.7 5.9 %copy-start.7 = (bf16[768,2048]{1,0:T(8,128)(2,1)S(1)}, bf16[768,2048]{1,0:T(8,128)(2,1)}, u32[]{:S(2)}) copy-start(bf16[768,2048]{1,0:T(8,128)(2,1)} %convolution_convert_fusion.3) | copy-start | bytes 9437188
  251.2 10.1 %collective-permute-start.10 = (bf16[2,128,1536]{2,1,0:T(8,128)(2,1)}, bf16[2,128,1536]{2,1,0:T(8,128)(2,1)}, u32[]{:S(2)}, u32[]{:S(2)}) collective-permute-start(bf16[2,128,1536]{2,1,0:T(8,128)(2,1)} %fusion.69), channel_id=1, source_target_pairs={{0,1},{1,0},{2,3},{3,2},{4,5},{5,4},{6,7},{7,6},{8,9},{9,8},{10,11... | collective-permute-start | bytes 2359304 | tf_op jit(solution)/shard_map/ppermute | solution.py:70
  264.4 11.3 %collective-permute-start.11 = (bf16[128,1536]{1,0:T(8,128)(2,1)}, bf16[128,1536]{1,0:T(8,128)(2,1)S(1)}, u32[]{:S(2)}, u32[]{:S(2)}) collective-permute-start(bf16[128,1536]{1,0:T(8,128)(2,1)} %dynamic-slice_bitcast_fusion.8), channel_id=1, source_target_pairs={{0,2},{1,3},{2,0},{3,1},{4,6},{5,7},{6,4},{7,5},{8,10},{9,11},{10,... | collective-permute-start | bytes 1179656 | tf_op jit(solution)/shard_map/ppermute | solution.py:70
  265.4 10.2 %copy-start.51 = (bf16[2,128,1536]{2,1,0:T(8,128)(2,1)S(1)}, bf16[2,128,1536]{2,1,0:T(8,128)(2,1)}, u32[]{:S(2)}) copy-start(bf16[2,128,1536]{2,1,0:T(8,128)(2,1)} %copy-done.50) | copy-start | bytes 2359300
  265.4 10.4 %copy-start.26 = (bf16[768,768]{1,0:T(8,128)(2,1)S(1)}, bf16[768,768]{1,0:T(8,128)(2,1)}, u32[]{:S(2)}) copy-start(bf16[768,768]{1,0:T(8,128)(2,1)} %param.24) | copy-start | bytes 3538948
  265.5 44.7 %collective-permute-start.27 = (bf16[2,2,2,2,24,2816]{5,4,0,1,2,3:T(8,128)(2,1)}, bf16[2,2,2,2,24,2816]{5,4,0,1,2,3:T(8,128)(2,1)}, u32[]{:S(2)}, u32[]{:S(2)}) collective-permute-start(bf16[2,2,2,2,24,2816]{5,4,0,1,2,3:T(8,128)(2,1)} %bitcast.364), channel_id=1, source_target_pairs={{0,1},{1,0},{2,3},{3,2},{4,5},{5,4},{6,7},{7,6},{8,9},{9,8},{10,11... | collective-permute-start | bytes 6488072 | tf_op jit(solution)/shard_map/ppermute | solution.py:70
  279.0 1.2 collective-permute-start.12
  280.2 3.8 collective-permute-start.13
  280.7 4.9 %copy-start.107 = (f32[256]{0:T(256)S(1)}, f32[256]{0:T(256)}, u32[]{:S(2)}) copy-start(f32[256]{0:T(256)} %copy-done.106) | copy-start | bytes 3076
  280.7 8.8 %copy-start.14 = (f32[256,768]{1,0:T(8,128)S(1)}, f32[256,768]{1,0:T(8,128)}, u32[]{:S(2)}) copy-start(f32[256,768]{1,0:T(8,128)} %copy-done.13) | copy-start | bytes 2359300
  284.0 3.8 collective-permute-start.14
  287.8 3.7 collective-permute-start.15
  291.5 4.7 %collective-permute-start.16 = (f32[21,128]{1,0:T(8,128)S(1)}, f32[21,128]{1,0:T(8,128)S(1)}, u32[]{:S(2)}, u32[]{:S(2)}) collective-permute-start(f32[21,128]{1,0:T(8,128)S(1)} %add.611), channel_id=1, source_target_pairs={{0,16},{1,17},{2,18},{3,19},{4,20},{5,21},{6,22},{7,23},{8,24},{9,... | collective-permute-start | bytes 32264 | tf_op jit(solution)/shard_map/ppermute | solution.py:70
  296.1 10.0 %collective-permute-start.17 = (bf16[2,2,2,2,24,1152]{5,4,0,1,2,3:T(8,128)(2,1)S(1)}, bf16[2,2,2,2,24,1152]{5,4,0,1,2,3:T(8,128)(2,1)}, u32[]{:S(2)}, u32[]{:S(2)}) collective-permute-start(bf16[2,2,2,2,24,1152]{5,4,0,1,2,3:T(8,128)(2,1)S(1)} %bitcast.369), channel_id=1, source_target_pairs={{0,1},{1,0},{2,3},{3,2},{4,5},{5,4},{6,7},{7,6},{8,9},{9,8},{10,11... | collective-permute-start | bytes 2654216 | tf_op jit(solution)/shard_map/ppermute | solution.py:70
  296.2 11.9 %collective-permute-start.22 = (bf16[2,2,2,2,24,1152]{5,4,0,1,3,2:T(8,128)(2,1)}, bf16[2,2,2,2,24,1152]{5,4,0,1,3,2:T(8,128)(2,1)}, u32[]{:S(2)}, u32[]{:S(2)}) collective-permute-start(bf16[2,2,2,2,24,1152]{5,4,0,1,3,2:T(8,128)(2,1)} %bitcast.340), channel_id=1, source_target_pairs={{0,1},{1,0},{2,3},{3,2},{4,5},{5,4},{6,7},{7,6},{8,9},{9,8},{10,11... | collective-permute-start | bytes 2654216 | tf_op jit(solution)/shard_map/ppermute | solution.py:70
  298.1 4.5 %copy-start.24 = (bf16[2,2,2,2,1,24,2176]{6,5,4,3,2,1,0:T(8,128)(2,1)S(1)}, bf16[2,2,2,2,1,24,2176]{6,5,4,3,2,1,0:T(8,128)(2,1)}, u32[]{:S(2)}) copy-start(bf16[2,2,2,2,1,24,2176]{6,5,4,3,2,1,0:T(8,128)(2,1)} %get-tuple-element.95) | copy-start | bytes 5013508
  300.6 19.7 %collective-permute-start.38 = (bf16[2,2,2,64,768]{4,3,1,2,0:T(8,128)(2,1)S(1)}, bf16[2,2,2,64,768]{4,3,1,2,0:T(8,128)(2,1)S(1)}, u32[]{:S(2)}, u32[]{:S(2)}) collective-permute-start(bf16[2,2,2,64,768]{4,3,1,2,0:T(8,128)(2,1)S(1)} %dynamic-slice_bitcast_fusion.2), channel_id=1, source_target_pairs={{0,8},{1,9},{2,10},{3,11},{4,12},{5,13},{6,14},{7,15},{8,0},{9,1},... | collective-permute-start | bytes 2359304 | tf_op jit(solution)/shard_map/ppermute | solution.py:70
  304.5 31.7 %collective-permute-start.33 = (bf16[2,2,2,24,2176]{4,3,0,1,2:T(8,128)(2,1)S(1)}, bf16[2,2,2,24,2176]{4,3,0,1,2:T(8,128)(2,1)S(1)}, u32[]{:S(2)}, u32[]{:S(2)}) collective-permute-start(bf16[2,2,2,24,2176]{4,3,0,1,2:T(8,128)(2,1)S(1)} %dynamic-slice_bitcast_fusion.1), channel_id=1, source_target_pairs={{0,4},{1,5},{2,6},{3,7},{4,0},{5,1},{6,2},{7,3},{8,12},{9,13},{10,... | collective-permute-start | bytes 2506760 | tf_op jit(solution)/shard_map/ppermute | solution.py:70
  307.6 15.5 %collective-permute-start.18 = (bf16[2,2,2,24,1152]{4,3,0,1,2:T(8,128)(2,1)S(1)}, bf16[2,2,2,24,1152]{4,3,0,1,2:T(8,128)(2,1)S(1)}, u32[]{:S(2)}, u32[]{:S(2)}) collective-permute-start(bf16[2,2,2,24,1152]{4,3,0,1,2:T(8,128)(2,1)S(1)} %dynamic-slice_bitcast_fusion.5), channel_id=1, source_target_pairs={{0,2},{1,3},{2,0},{3,1},{4,6},{5,7},{6,4},{7,5},{8,10},{9,11},{10,... | collective-permute-start | bytes 1327112 | tf_op jit(solution)/shard_map/ppermute | solution.py:70
  309.6 26.0 %collective-permute-start.23 = (bf16[2,2,2,24,1152]{4,3,0,1,2:T(8,128)(2,1)S(1)}, bf16[2,2,2,24,1152]{4,3,0,1,2:T(8,128)(2,1)S(1)}, u32[]{:S(2)}, u32[]{:S(2)}) collective-permute-start(bf16[2,2,2,24,1152]{4,3,0,1,2:T(8,128)(2,1)S(1)} %dynamic-slice_bitcast_fusion.4), channel_id=1, source_target_pairs={{0,4},{1,5},{2,6},{3,7},{4,0},{5,1},{6,2},{7,3},{8,12},{9,13},{10,... | collective-permute-start | bytes 1327112 | tf_op jit(solution)/shard_map/ppermute | solution.py:70
  312.4 53.4 %collective-permute-start.28 = (bf16[2,2,2,24,2816]{4,3,0,1,2:T(8,128)(2,1)S(1)}, bf16[2,2,2,24,2816]{4,3,0,1,2:T(8,128)(2,1)S(1)}, u32[]{:S(2)}, u32[]{:S(2)}) collective-permute-start(bf16[2,2,2,24,2816]{4,3,0,1,2:T(8,128)(2,1)S(1)} %dynamic-slice_bitcast_fusion), channel_id=1, source_target_pairs={{0,2},{1,3},{2,0},{3,1},{4,6},{5,7},{6,4},{7,5},{8,10},{9,11},{10,... | collective-permute-start | bytes 3244040 | tf_op jit(solution)/shard_map/ppermute | solution.py:70
  320.6 28.4 %collective-permute-start.39 = (bf16[2,2,64,768]{3,2,0,1:T(8,128)(2,1)S(1)}, bf16[2,2,64,768]{3,2,0,1:T(8,128)(2,1)S(1)}, u32[]{:S(2)}, u32[]{:S(2)}) collective-permute-start(bf16[2,2,64,768]{3,2,0,1:T(8,128)(2,1)S(1)} %dynamic-slice_bitcast_fusion.7), channel_id=1, source_target_pairs={{0,16},{1,17},{2,18},{3,19},{4,20},{5,21},{6,22},{7,23},{8,24},{9,... | collective-permute-start | bytes 1179656 | tf_op jit(solution)/shard_map/ppermute | solution.py:70
  323.2 15.9 %collective-permute-start.19 = (bf16[2,2,24,1152]{3,2,0,1:T(8,128)(2,1)S(1)}, bf16[2,2,24,1152]{3,2,0,1:T(8,128)(2,1)S(1)}, u32[]{:S(2)}, u32[]{:S(2)}) collective-permute-start(bf16[2,2,24,1152]{3,2,0,1:T(8,128)(2,1)S(1)} %dynamic-slice_bitcast_fusion.12), channel_id=1, source_target_pairs={{0,4},{1,5},{2,6},{3,7},{4,0},{5,1},{6,2},{7,3},{8,12},{9,13},{10,... | collective-permute-start | bytes 663560 | tf_op jit(solution)/shard_map/ppermute | solution.py:70
  335.7 12.9 %collective-permute-start.24 = (bf16[2,2,24,1152]{3,2,0,1:T(8,128)(2,1)S(1)}, bf16[2,2,24,1152]{3,2,0,1:T(8,128)(2,1)S(1)}, u32[]{:S(2)}, u32[]{:S(2)}) collective-permute-start(bf16[2,2,24,1152]{3,2,0,1:T(8,128)(2,1)S(1)} %dynamic-slice_bitcast_fusion.11), channel_id=1, source_target_pairs={{0,2},{1,3},{2,0},{3,1},{4,6},{5,7},{6,4},{7,5},{8,10},{9,11},{10,... | collective-permute-start | bytes 663560 | tf_op jit(solution)/shard_map/ppermute | solution.py:70
  336.5 23.3 %collective-permute-start.34 = (bf16[2,2,24,2176]{3,2,0,1:T(8,128)(2,1)S(1)}, bf16[2,2,24,2176]{3,2,0,1:T(8,128)(2,1)S(1)}, u32[]{:S(2)}, u32[]{:S(2)}) collective-permute-start(bf16[2,2,24,2176]{3,2,0,1:T(8,128)(2,1)S(1)} %dynamic-slice_bitcast_fusion.6), channel_id=1, source_target_pairs={{0,2},{1,3},{2,0},{3,1},{4,6},{5,7},{6,4},{7,5},{8,10},{9,11},{10,... | collective-permute-start | bytes 1253384 | tf_op jit(solution)/shard_map/ppermute | solution.py:70
  339.2 10.4 %collective-permute-start.20 = (bf16[2,24,1152]{2,1,0:T(8,128)(2,1)S(1)}, bf16[2,24,1152]{2,1,0:T(8,128)(2,1)S(1)}, u32[]{:S(2)}, u32[]{:S(2)}) collective-permute-start(bf16[2,24,1152]{2,1,0:T(8,128)(2,1)S(1)} %dynamic-slice_bitcast_fusion.18), channel_id=1, source_target_pairs={{0,8},{1,9},{2,10},{3,11},{4,12},{5,13},{6,14},{7,15},{8,0},{9,1},... | collective-permute-start | bytes 331784 | tf_op jit(solution)/shard_map/ppermute | solution.py:70
  348.8 4.8 %collective-permute-start.25 = (bf16[2,24,1152]{2,1,0:T(8,128)(2,1)S(1)}, bf16[2,24,1152]{2,1,0:T(8,128)(2,1)S(1)}, u32[]{:S(2)}, u32[]{:S(2)}) collective-permute-start(bf16[2,24,1152]{2,1,0:T(8,128)(2,1)S(1)} %dynamic-slice_bitcast_fusion.17), channel_id=1, source_target_pairs={{0,8},{1,9},{2,10},{3,11},{4,12},{5,13},{6,14},{7,15},{8,0},{9,1},... | collective-permute-start | bytes 331784 | tf_op jit(solution)/shard_map/ppermute | solution.py:70
  349.1 11.2 %collective-permute-start.40 = (bf16[2,64,768]{2,1,0:T(8,128)(2,1)S(1)}, bf16[2,64,768]{2,1,0:T(8,128)(2,1)S(1)}, u32[]{:S(2)}, u32[]{:S(2)}) collective-permute-start(bf16[2,64,768]{2,1,0:T(8,128)(2,1)S(1)} %dynamic-slice_bitcast_fusion.14), channel_id=1, source_target_pairs={{0,2},{1,3},{2,0},{3,1},{4,6},{5,7},{6,4},{7,5},{8,10},{9,11},{10,... | collective-permute-start | bytes 589832 | tf_op jit(solution)/shard_map/ppermute | solution.py:70
  349.7 6.6 %collective-permute-start.21 = (bf16[24,1152]{1,0:T(8,128)(2,1)S(1)}, bf16[24,1152]{1,0:T(8,128)(2,1)S(1)}, u32[]{:S(2)}, u32[]{:S(2)}) collective-permute-start(bf16[24,1152]{1,0:T(8,128)(2,1)S(1)} %dynamic-slice_bitcast_fusion.23), channel_id=1, source_target_pairs={{0,16},{1,17},{2,18},{3,19},{4,20},{5,21},{6,22},{7,23},{8,24},{9,... | collective-permute-start | bytes 165896 | tf_op jit(solution)/shard_map/ppermute | solution.py:70
  353.6 5.5 %collective-permute-start.26 = (bf16[24,1152]{1,0:T(8,128)(2,1)S(1)}, bf16[24,1152]{1,0:T(8,128)(2,1)S(1)}, u32[]{:S(2)}, u32[]{:S(2)}) collective-permute-start(bf16[24,1152]{1,0:T(8,128)(2,1)S(1)} %dynamic-slice_bitcast_fusion.22), channel_id=1, source_target_pairs={{0,16},{1,17},{2,18},{3,19},{4,20},{5,21},{6,22},{7,23},{8,24},{9,... | collective-permute-start | bytes 165896 | tf_op jit(solution)/shard_map/ppermute | solution.py:70
  360.4 4.7 %collective-permute-start.41 = (bf16[64,768]{1,0:T(8,128)(2,1)S(1)}, bf16[64,768]{1,0:T(8,128)(2,1)S(1)}, u32[]{:S(2)}, u32[]{:S(2)}) collective-permute-start(bf16[64,768]{1,0:T(8,128)(2,1)S(1)} %dynamic-slice_bitcast_fusion.20), channel_id=1, source_target_pairs={{0,4},{1,5},{2,6},{3,7},{4,0},{5,1},{6,2},{7,3},{8,12},{9,13},{10,... | collective-permute-start | bytes 294920 | tf_op jit(solution)/shard_map/ppermute | solution.py:70
  361.0 5.9 %collective-permute-start.35 = (bf16[2,24,2176]{2,1,0:T(8,128)(2,1)S(1)}, bf16[2,24,2176]{2,1,0:T(8,128)(2,1)S(1)}, u32[]{:S(2)}, u32[]{:S(2)}) collective-permute-start(bf16[2,24,2176]{2,1,0:T(8,128)(2,1)S(1)} %dynamic-slice_bitcast_fusion.13), channel_id=1, source_target_pairs={{0,8},{1,9},{2,10},{3,11},{4,12},{5,13},{6,14},{7,15},{8,0},{9,1},... | collective-permute-start | bytes 626696 | tf_op jit(solution)/shard_map/ppermute | solution.py:70
  366.1 11.7 %collective-permute-start.29 = (bf16[2,2,24,2816]{3,2,0,1:T(8,128)(2,1)S(1)}, bf16[2,2,24,2816]{3,2,0,1:T(8,128)(2,1)S(1)}, u32[]{:S(2)}, u32[]{:S(2)}) collective-permute-start(bf16[2,2,24,2816]{3,2,0,1:T(8,128)(2,1)S(1)} %dynamic-slice_bitcast_fusion.3), channel_id=1, source_target_pairs={{0,4},{1,5},{2,6},{3,7},{4,0},{5,1},{6,2},{7,3},{8,12},{9,13},{10,... | collective-permute-start | bytes 1622024 | tf_op jit(solution)/shard_map/ppermute | solution.py:70
  377.8 16.2 %copy-start.1 = (bf16[768,2048]{1,0:T(8,128)(2,1)S(1)}, bf16[768,2048]{1,0:T(8,128)(2,1)}, u32[]{:S(2)}) copy-start(bf16[768,2048]{1,0:T(8,128)(2,1)} %param.30) | copy-start | bytes 9437188
  378.0 7.9 %collective-permute-start.30 = (bf16[2,24,2816]{2,1,0:T(8,128)(2,1)S(1)}, bf16[2,24,2816]{2,1,0:T(8,128)(2,1)S(1)}, u32[]{:S(2)}, u32[]{:S(2)}) collective-permute-start(bf16[2,24,2816]{2,1,0:T(8,128)(2,1)S(1)} %dynamic-slice_bitcast_fusion.9), channel_id=1, source_target_pairs={{0,8},{1,9},{2,10},{3,11},{4,12},{5,13},{6,14},{7,15},{8,0},{9,1},... | collective-permute-start | bytes 811016 | tf_op jit(solution)/shard_map/ppermute | solution.py:70
  378.6 10.6 %collective-permute-start.36 = (bf16[24,2176]{1,0:T(8,128)(2,1)S(1)}, bf16[24,2176]{1,0:T(8,128)(2,1)S(1)}, u32[]{:S(2)}, u32[]{:S(2)}) collective-permute-start(bf16[24,2176]{1,0:T(8,128)(2,1)S(1)} %dynamic-slice_bitcast_fusion.19), channel_id=1, source_target_pairs={{0,16},{1,17},{2,18},{3,19},{4,20},{5,21},{6,22},{7,23},{8,24},{9,... | collective-permute-start | bytes 313352 | tf_op jit(solution)/shard_map/ppermute | solution.py:70
  385.9 6.7 %collective-permute-start.31 = (bf16[24,2816]{1,0:T(8,128)(2,1)S(1)}, bf16[24,2816]{1,0:T(8,128)(2,1)S(1)}, u32[]{:S(2)}, u32[]{:S(2)}) collective-permute-start(bf16[24,2816]{1,0:T(8,128)(2,1)S(1)} %dynamic-slice_bitcast_fusion.15), channel_id=1, source_target_pairs={{0,16},{1,17},{2,18},{3,19},{4,20},{5,21},{6,22},{7,23},{8,24},{9,... | collective-permute-start | bytes 405512 | tf_op jit(solution)/shard_map/ppermute | solution.py:70
  (93 other events, 191.4 us)

commit v2 on v0

v2 whole, which is shorter than its diff:
```python
import functools

import jax
import jax.numpy as jnp
from jax import lax
from jax.experimental import pallas as pl
from jax.experimental.pallas import tpu as pltpu
from jax.sharding import PartitionSpec as P

BUCKETS = 32
LANES = 128
CHUNK = 512

epsilon = 1e-06
contrastive_sharpness_factor = 0.01
masked_value = -1000000000.0
bucket_edges = (12, 16, 23, 32, 46, 64, 91)
highest = lax.Precision.HIGHEST
f32 = jnp.float32
bf16 = jnp.bfloat16


def bucket_index(offset):
    distance = jnp.abs(offset)
    beyond = 8 + sum(((distance >= boundary).astype(jnp.int32) for boundary in bucket_edges))
    inside = jnp.where(distance < 8, distance, beyond)
    return inside + BUCKETS // 2 * (offset > 0).astype(jnp.int32)


def product(left, right):
    return jnp.dot(left, right, preferred_element_type=f32)


def left_product(left, right):
    return lax.dot_general(left, right, (((0,), (0,)), ((), ())), preferred_element_type=f32)


def right_product(left, right):
    return lax.dot_general(left, right, (((1,), (1,)), ((), ())), preferred_element_type=f32)


def rank_bits():
    return (lax.axis_size("wide") * lax.axis_size("narrow")).bit_length() - 1


def my_rank():
    return lax.axis_index("wide") * lax.axis_size("narrow") + lax.axis_index("narrow")


def swap(values, bit):
    ranks = 1 << rank_bits()
    pairs = [(rank, rank ^ (1 << bit)) for rank in range(ranks)]
    return lax.ppermute(values, ("wide", "narrow"), pairs)


def scatter_order(position, order):
    count = len(order)
    return sum(((position >> (count - 1 - step)) & 1) << bit for step, bit in enumerate(order))


def gather_order(position, order):
    return sum(((position >> step) & 1) << bit for step, bit in enumerate(order))


def halve(kept, sent, order, last_type=f32):
    for step, bit in enumerate(order):
        came = swap(sent, bit)
        if step == len(order) - 1:
            return kept.astype(f32) + came.astype(f32)
        half = kept.shape[0] // 2
        sent = (kept[half:].astype(f32) + came[half:].astype(f32)).astype(kept.dtype)
        kept = (kept[:half].astype(f32) + came[:half].astype(f32)).astype(kept.dtype)


def sum_all(values):
    for bit in range(rank_bits()):
        values = values + swap(values, bit)
    return values


def call(kernel, outs, args, scratch=(), smem=0, flops=0):
    vmem = pl.BlockSpec(memory_space=pltpu.VMEM)
    specs = [pl.BlockSpec(memory_space=pltpu.SMEM)] * smem + [vmem] * (len(args) - smem)
    moved = sum(a.size * a.dtype.itemsize for a in args)
    moved += sum(o.size * o.dtype.itemsize for o in outs)
    return pl.pallas_call(
        kernel,
        out_shape=tuple(outs),
        in_specs=specs,
        out_specs=tuple([vmem] * len(outs)),
        scratch_shapes=list(scratch),
        compiler_params=pltpu.CompilerParams(vmem_limit_bytes=60 * 1024 * 1024),
        cost_estimate=pl.CostEstimate(flops=flops, bytes_accessed=moved, transcendentals=0),
    )(*args)


def shape(dims, kind=f32):
    return jax.ShapeDtypeStruct(tuple(dims), kind)


def prepare_kernel(
    doc_length, slot_length, doc_total, rank_ref, places_ref, table_ref, counts_ref, tally_ref, doc_bias_ref,
    slot_bias_ref, scratch_ref,
):
    rows, picks = places_ref.shape
    blocks = counts_ref.shape[0]
    heads = doc_bias_ref.shape[0]
    parts = doc_length // LANES

    def one_row(row, carry):
        places = places_ref[pl.ds(row, 1), :]
        high = places >> 7
        low = places & 127
        high_hot = (lax.broadcasted_iota(jnp.int32, (blocks, picks), 0) == high).astype(bf16)
        low_hot = (lax.broadcasted_iota(jnp.int32, (LANES, picks), 0) == low).astype(bf16)
        scratch_ref[pl.ds(row, blocks, stride=rows), :] = right_product(high_hot, low_hot)
        return carry

    lax.fori_loop(0, rows, one_row, 0, unroll=8)

    def one_block(block, carry):
        start = pl.multiple_of(block * rows, rows)
        counts_ref[block] = scratch_ref[pl.ds(start, rows), :].astype(bf16)
        return carry

    lax.fori_loop(0, blocks, one_block, 0, unroll=4)

    owner = places_ref[...] // doc_length
    lane = lax.broadcasted_iota(jnp.int32, (rows, LANES), 1)
    tally = jnp.zeros((rows, LANES), f32)
    for doc in range(doc_total):
        number = jnp.sum((owner == doc).astype(f32), 1, keepdims=True)
        tally = jnp.where(lane == doc, number, tally)
    tally_ref[...] = tally

    narrow = rank_ref[0] & (parts - 1)

    def spread(head, offset):
        line = table_ref[pl.ds(head, 1), pl.ds(pl.multiple_of(offset, LANES), 2 * LANES)]
        rolled = pltpu.roll(jnp.broadcast_to(line, (LANES, 2 * LANES)), 0, 1, stride=1, stride_axis=0)
        return rolled[:, LANES:]

    def one_head(head, carry):
        for part in range(parts):
            distance = (narrow ^ part) - narrow
            doc_bias_ref[head, :, part * LANES : (part + 1) * LANES] = spread(
                head, doc_length - LANES + distance * LANES
            )
        slot_bias_ref[head] = spread(head, doc_length - LANES)
        return carry

    lax.fori_loop(0, heads, one_head, 0)


def rms_scale(values):
    return lax.rsqrt(jnp.mean(values * values, -1, keepdims=True) + epsilon)


def rms_back(values, gain, grad):
    scale = rms_scale(values)
    weighted = grad * gain
    inner = jnp.mean(weighted * values, -1, keepdims=True)
    back = scale * weighted - values * (scale * scale * scale * inner)
    return back, jnp.sum(grad * values * scale, 0, keepdims=True)


def forward_kernel(
    slot_length, slot_ref, own_ref, near_ref, far_ref, last_ref, key_valid_ref, doc_bias_ref, slot_bias_ref,
    attend_gain_ref, feed_gain_ref, final_gain_ref, wq_ref, wk_ref, wv_ref, wo_ref, wg_ref, wu_ref, wd_ref, wp_ref,
    normed_ref, query_ref, key_ref, value_ref, doc_probs_ref, slot_probs_ref, mixed_ref, after_attend_ref,
    normed_feed_ref, hidden_ref, gate_slope_ref, up_slope_ref, after_feed_ref, normed_final_ref, embed_ref,
    slot_unit_ref, doc_unit_ref, all_ref,
):
    rows, width = normed_ref.shape
    head_count = doc_probs_ref.shape[0]
    half = LANES // 2
    slots = slot_ref.shape[0]
    gain = attend_gain_ref[...]
    place = 0
    for ref in (slot_ref, own_ref, near_ref, far_ref, last_ref):
        tokens = ref[...].astype(f32)
        all_ref[place : place + ref.shape[0], :] = (tokens * rms_scale(tokens) * gain).astype(bf16)
        place += ref.shape[0]
    normed = all_ref[:rows, :]
    normed_ref[...] = normed
    query_ref[...] = product(normed, wq_ref[...]).astype(bf16)
    key_ref[...] = product(all_ref[...], wk_ref[...]).astype(bf16)
    value_ref[...] = product(all_ref[...], wv_ref[...]).astype(bf16)

    lane = lax.broadcasted_iota(jnp.int32, (slots, LANES), 1)
    row_slot = lax.broadcasted_iota(jnp.int32, (slots, slots), 0) // slot_length
    col_slot = lax.broadcasted_iota(jnp.int32, (slots, slots), 1) // slot_length
    slot_keep = (row_slot == col_slot) & (key_valid_ref[...] > 0.0)

    def softmax(scores):
        weights = jnp.exp(scores - jnp.max(scores, -1, keepdims=True))
        return (weights * (1.0 / jnp.sum(weights, -1, keepdims=True))).astype(bf16)

    for pair in range(head_count // 2):
        lanes = slice(pair * LANES, (pair + 1) * LANES)
        slot_mixed, doc_mixed = [], []
        for side in range(2):
            head = 2 * pair + side
            mine = (lane < half) if side == 0 else (lane >= half)
            slot_query = jnp.where(mine, query_ref[:slots, lanes], jnp.zeros((), bf16))
            doc_query = jnp.where(mine, query_ref[slots:, lanes], jnp.zeros((), bf16))
            scores = right_product(slot_query, key_ref[:slots, lanes]) + slot_bias_ref[head]
            probs = softmax(jnp.where(slot_keep, scores, masked_value))
            slot_probs_ref[head] = probs
            slot_mixed.append(product(probs, value_ref[:slots, lanes]))
            scores = right_product(doc_query, key_ref[slots:, lanes]) + doc_bias_ref[head]
            probs = softmax(scores)
            doc_probs_ref[head] = probs
            doc_mixed.append(product(probs, value_ref[slots:, lanes]))
        mixed_ref[:slots, lanes] = jnp.where(lane < half, slot_mixed[0], slot_mixed[1]).astype(bf16)
        mixed_ref[slots:, lanes] = jnp.where(lane < half, doc_mixed[0], doc_mixed[1]).astype(bf16)

    attended = product(mixed_ref[...], wo_ref[...])
    after_attend_ref[:slots, :] = slot_ref[...].astype(f32) + attended[:slots]
    after_attend_ref[slots:, :] = own_ref[...].astype(f32) + attended[slots:]
    after_attend = after_attend_ref[...]
    normed_feed = (after_attend * rms_scale(after_attend) * feed_gain_ref[...]).astype(bf16)
    normed_feed_ref[...] = normed_feed
    for start in range(0, hidden_ref.shape[1], CHUNK):
        part = slice(start, start + CHUNK)
        gate = product(normed_feed_ref[...], wg_ref[:, part])
        upward = product(normed_feed_ref[...], wu_ref[:, part])
        factor = 0.7978845608028654
        square = gate * gate
        bent = jnp.tanh(factor * gate * (1.0 + 0.044715 * square))
        curve = 0.5 * gate * (1.0 + bent)
        slope = 0.5 * (1.0 + bent) + 0.5 * factor * gate * (1.0 - bent * bent) * (1.0 + 3 * 0.044715 * square)
        hidden_ref[:, part] = (curve * upward).astype(bf16)
        gate_slope_ref[:, part] = (upward * slope).astype(bf16)
        up_slope_ref[:, part] = curve.astype(bf16)
    after_feed = after_attend_ref[...] + product(hidden_ref[...], wd_ref[...])
    after_feed_ref[...] = after_feed
    normed_final = (after_feed * rms_scale(after_feed) * final_gain_ref[...]).astype(bf16)
    normed_final_ref[...] = normed_final
    embed = product(normed_final, wp_ref[...])
    embed_ref[...] = embed
    unit = (embed * lax.rsqrt(jnp.sum(embed * embed, -1, keepdims=True) + epsilon)).astype(bf16)
    slot_unit_ref[...] = unit[:slots]
    doc_unit_ref[...] = unit[slots:]


def loss_kernel(
    order, gathered, doc_total, slots, rank_ref, counts_ref, near_ref, far_ref, unit_ref, tally_ref, row_valid_ref,
    positive_ref, losses_ref, grad_ref, kept_ref, sent_ref, sum_ref, scaled_ref,
):
    rows = unit_ref.shape[0]
    blocks = counts_ref.shape[0]
    per_doc = blocks // doc_total
    rank = rank_ref[0]
    half = blocks // 2
    sum_ref[...] = jnp.zeros_like(sum_ref)

    def gather_step(place, carry):
        near = rank ^ gather_order(place, gathered)
        far = near ^ (1 << gathered[-1])
        sum_ref[near // per_doc] += product(counts_ref[near], near_ref[place])
        sum_ref[far // per_doc] += product(counts_ref[far], far_ref[place])
        return carry

    lax.fori_loop(0, half, gather_step, 0, unroll=4)

    unit = unit_ref[...].astype(f32)
    lane = lax.broadcasted_iota(jnp.int32, (rows, LANES), 1)
    summed = jnp.zeros((rows, LANES), f32)
    for doc in range(doc_total):
        number = jnp.sum(sum_ref[doc] * unit, 1, keepdims=True)
        summed = jnp.where(lane == doc, number, summed)
    tally = tally_ref[...]
    most = jnp.maximum(tally, 1.0)
    weight = jnp.minimum(tally, 1.0) * row_valid_ref[...]
    slot_length = rows // slots
    pooled = (weight * (summed / most)).reshape(slots, slot_length, LANES)
    weight_sum = jnp.maximum(jnp.sum(weight.reshape(slots, slot_length, LANES), 1), 1.0)
    scores = jnp.sum(pooled, 1) / weight_sum / contrastive_sharpness_factor
    slot_lane = lax.broadcasted_iota(jnp.int32, (slots, LANES), 1)
    inside = slot_lane < doc_total
    scores = jnp.where(inside, scores, -jnp.inf)
    top = jnp.max(scores, -1, keepdims=True)
    powers = jnp.exp(scores - top)
    total = jnp.sum(powers, -1, keepdims=True)
    chosen = (slot_lane == positive_ref[...]).astype(f32)
    picked = jnp.sum(jnp.where(slot_lane == positive_ref[...], scores, 0.0), -1, keepdims=True)
    losses_ref[...] = jnp.broadcast_to(top + jnp.log(total) - picked, (slots, LANES))
    slope = (powers / total - chosen) / contrastive_sharpness_factor / weight_sum
    slope = jnp.where(inside, slope, 0.0)
    slope = jnp.broadcast_to(slope[:, None, :], (slots, slot_length, LANES)).reshape(rows, LANES)
    slope = slope * weight / most

    grad = jnp.zeros((rows, unit.shape[1]), f32)
    for doc in range(doc_total):
        column = jnp.sum(jnp.where(lane == doc, slope, 0.0), 1, keepdims=True)
        grad = grad + column * sum_ref[doc]
        scaled_ref[doc] = (column * unit).T.astype(bf16)
    grad_ref[...] = grad

    def scatter_step(place, carry):
        kept = rank ^ scatter_order(place, order)
        sent = kept ^ (1 << order[0])
        kept_ref[place] = product(scaled_ref[kept // per_doc], counts_ref[kept]).astype(bf16)
        sent_ref[place] = product(scaled_ref[sent // per_doc], counts_ref[sent]).astype(bf16)
        return carry

    lax.fori_loop(0, half, scatter_step, 0, unroll=4)


def feed_back(
    part, grad_unit, embed_ref, after_feed_ref, after_attend_ref, gate_slope_ref, up_slope_ref, feed_gain_ref,
    final_gain_ref, wo_ref, wg_ref, wu_ref, wd_ref, wp_ref, embed_out, feed_out, gate_out, up_out, after_out,
    attend_out, mixed_out, final_gain_out, feed_gain_out,
):
    embed = embed_ref[part, :]
    scale = lax.rsqrt(jnp.sum(embed * embed, -1, keepdims=True) + epsilon)
    inner = jnp.sum(grad_unit * embed, -1, keepdims=True)
    grad_embed = (scale * grad_unit - embed * (scale * scale * scale * inner)).astype(bf16)
    embed_out[...] = grad_embed
    grad_after_feed, final_gain_out[...] = rms_back(
        after_feed_ref[part, :], final_gain_ref[...], right_product(grad_embed, wp_ref[...])
    )
    after_out[...] = grad_after_feed
    feed_out[...] = grad_after_feed.astype(bf16)
    total = jnp.zeros(after_out.shape, f32)
    for start in range(0, gate_out.shape[1], CHUNK):
        cols = slice(start, start + CHUNK)
        grad_hidden = right_product(feed_out[...], wd_ref[cols, :])
        grad_gate = (grad_hidden * gate_slope_ref[part, cols].astype(f32)).astype(bf16)
        grad_up = (grad_hidden * up_slope_ref[part, cols].astype(f32)).astype(bf16)
        gate_out[:, cols] = grad_gate
        up_out[:, cols] = grad_up
        total = total + right_product(grad_gate, wg_ref[:, cols]) + right_product(grad_up, wu_ref[:, cols])
    more, feed_gain_out[...] = rms_back(after_attend_ref[part, :], feed_gain_ref[...], total)
    grad_after_attend = after_out[...] + more
    after_out[...] = grad_after_attend
    attend_out[...] = grad_after_attend.astype(bf16)
    mixed_out[...] = right_product(attend_out[...], wo_ref[...]).astype(bf16)


def diagonal_sums(grads, flip):
    size = grads.shape[0]
    turned = product(flip, grads)
    lines = []
    for start in range(0, grads.shape[1], LANES):
        part = turned[:, start : start + LANES]
        wide = jnp.concatenate([part, jnp.zeros_like(part)], 1)
        rolled = pltpu.roll(wide, 0, 1, stride=1, stride_axis=0)
        lines.append(jnp.sum(rolled.reshape(size // 8, 8, 2 * LANES), 0))
    return jnp.concatenate(lines, 1)


def attend_back(queries, keys, query_ref, key_ref, value_ref, probs_ref, mixed_ref, query_out, key_out, value_out, sums_out):
    size = query_out.shape[0]
    length = probs_ref.shape[2]
    half = LANES // 2
    lane = lax.broadcasted_iota(jnp.int32, (size, LANES), 1)
    key_lane = lax.broadcasted_iota(jnp.int32, (length, LANES), 1)
    row = lax.broadcasted_iota(jnp.int32, (size, size), 0)
    col = lax.broadcasted_iota(jnp.int32, (size, size), 1)
    flip = (row + col == size - 1).astype(bf16)
    for pair in range(probs_ref.shape[0] // 2):
        lanes = slice(pair * LANES, (pair + 1) * LANES)
        sides = []
        for side in range(2):
            head = 2 * pair + side
            mine = (lane < half) if side == 0 else (lane >= half)
            grad_mixed = jnp.where(mine, mixed_ref[:, lanes], jnp.zeros((), bf16))
            probs = probs_ref[head]
            grad_probs = right_product(grad_mixed, value_ref[keys, lanes])
            exact = probs.astype(f32)
            inner = jnp.sum(exact * grad_probs, -1, keepdims=True)
            grad_scores = (exact * (grad_probs - inner)).astype(bf16)
            sums_out[head * 8 : (head + 1) * 8, :] = diagonal_sums(grad_scores, flip)
            sides.append(
                (
                    product(grad_scores, key_ref[keys, lanes]),
                    left_product(grad_scores, query_ref[queries, lanes]),
                    left_product(probs, mixed_ref[:, lanes]),
                )
            )
        query_out[:, lanes] = jnp.where(lane < half, sides[0][0], sides[1][0]).astype(bf16)
        key_out[:, lanes] = jnp.where(key_lane < half, sides[0][1], sides[1][1]).astype(bf16)
        value_out[:, lanes] = jnp.where(key_lane < half, sides[0][2], sides[1][2]).astype(bf16)


def input_back(tokens, gain_ref, after_ref, query, key, value, wq_ref, wk_ref, wv_ref):
    grad_normed = right_product(query, wq_ref[...])
    grad_normed = grad_normed + right_product(key, wk_ref[...])
    grad_normed = grad_normed + right_product(value, wv_ref[...])
    back, gain_grad = rms_back(tokens, gain_ref[...], grad_normed)
    return after_ref[...] + back, gain_grad


def slot_back_kernel(
    grad_unit_ref, embed_ref, after_feed_ref, after_attend_ref, gate_slope_ref, up_slope_ref, tokens_ref, query_ref,
    key_ref, value_ref, probs_ref, attend_gain_ref, feed_gain_ref, final_gain_ref, wq_ref, wk_ref, wv_ref, wo_ref,
    wg_ref, wu_ref, wd_ref, wp_ref,
    embed_out, feed_out, gate_out, up_out, attend_out, query_out, key_out, value_out, tokens_out, gains_out, sums_out,
    after_ref, mixed_ref, final_gain_out, feed_gain_out,
):
    part = slice(0, tokens_ref.shape[0])
    feed_back(
        part, grad_unit_ref[...], embed_ref, after_feed_ref, after_attend_ref, gate_slope_ref, up_slope_ref,
        feed_gain_ref, final_gain_ref, wo_ref, wg_ref, wu_ref, wd_ref, wp_ref, embed_out, feed_out, gate_out, up_out,
        after_ref, attend_out, mixed_ref, final_gain_out, feed_gain_out,
    )
    attend_back(
        part, part, query_ref, key_ref, value_ref, probs_ref, mixed_ref, query_out, key_out, value_out, sums_out
    )
    grads, gain_grad = input_back(
        tokens_ref[...].astype(f32), attend_gain_ref, after_ref, query_out[...], key_out[...], value_out[...], wq_ref,
        wk_ref, wv_ref,
    )
    tokens_out[...] = grads
    gains_out[0:1, :] = gain_grad
    gains_out[1:2, :] = feed_gain_out[...]
    gains_out[2:3, :] = final_gain_out[...]


def doc_feed_kernel(
    kept_ref, came_ref, embed_ref, after_feed_ref, after_attend_ref, gate_slope_ref, up_slope_ref, feed_gain_ref,
    final_gain_ref, wo_ref, wg_ref, wu_ref, wd_ref, wp_ref,
    embed_out, feed_out, gate_out, up_out, after_out, attend_out, mixed_out, gains_out, final_gain_out, feed_gain_out,
):
    rows = kept_ref.shape[1]
    grad_unit = (kept_ref[0].astype(f32) + came_ref[0].astype(f32)).T
    feed_back(
        slice(embed_ref.shape[0] - rows, embed_ref.shape[0]), grad_unit, embed_ref, after_feed_ref, after_attend_ref,
        gate_slope_ref, up_slope_ref, feed_gain_ref, final_gain_ref, wo_ref, wg_ref, wu_ref, wd_ref, wp_ref, embed_out,
        feed_out, gate_out, up_out, after_out, attend_out, mixed_out, final_gain_out, feed_gain_out,
    )
    gains_out[0:1, :] = feed_gain_out[...]
    gains_out[1:2, :] = final_gain_out[...]


def doc_attend_kernel(
    query_ref, key_ref, value_ref, probs_ref, mixed_ref, query_out, key_kept, value_kept, key_sent, value_sent,
    sums_out, key_out, value_out,
):
    rows = query_out.shape[0]
    first = key_ref.shape[0] - probs_ref.shape[2]
    attend_back(
        slice(first, first + rows), slice(first, key_ref.shape[0]), query_ref, key_ref, value_ref, probs_ref, mixed_ref,
        query_out, key_out, value_out, sums_out,
    )
    for place in range(2):
        here = slice(place * rows, (place + 1) * rows)
        key_kept[here, :] = key_out[2 * place * rows : (2 * place + 1) * rows, :]
        value_kept[here, :] = value_out[2 * place * rows : (2 * place + 1) * rows, :]
        key_sent[here, :] = key_out[(2 * place + 1) * rows : (2 * place + 2) * rows, :]
        value_sent[here, :] = value_out[(2 * place + 1) * rows : (2 * place + 2) * rows, :]


def turn(values, scratch, target, order, rank):
    scratch[...] = values.astype(f32).T
    count = 1 << len(order)
    size = scratch.shape[0] // count
    if size % 8:
        row = lax.broadcasted_iota(jnp.int32, (scratch.shape[0], scratch.shape[0]), 0)
        col = lax.broadcasted_iota(jnp.int32, (scratch.shape[0], scratch.shape[0]), 1)
        source = (scatter_order(row // size, order) ^ rank) * size + row % size
        target[...] = product((col == source).astype(bf16), scratch[...].astype(bf16))
        return
    for place in range(count):
        source = (rank ^ scatter_order(place, order)) * size
        target[place * size : (place + 1) * size, :] = scratch[pl.ds(pl.multiple_of(source, 8), size), :]


def store_product(turned, right, kept_ref, sent_ref, start):
    half = kept_ref.shape[0]
    for first in range(0, right.shape[1], CHUNK):
        last = min(first + CHUNK, right.shape[1])
        result = product(turned, right[:, first:last]).astype(bf16)
        kept_ref[:, start + first : start + last] = result[:half]
        sent_ref[:, start + first : start + last] = result[half:]


def both(slot_ref, doc_ref):
    return jnp.concatenate([slot_ref[...], doc_ref[...]], 0)


def feed_weight_kernel(
    first_order, second_order, rank_ref, normed_feed_ref, mixed_ref, normed_final_ref, hidden_ref, slot_gate, doc_gate,
    slot_up, doc_up, slot_attend, doc_attend, slot_embed, doc_embed, slot_feed, doc_feed,
    first_kept, first_sent, second_kept, second_sent, third_kept, third_sent, narrow_ref, narrow_target, wide_ref,
    wide_target,
):
    rank = rank_ref[0]
    units = slot_gate.shape[1]
    turn(hidden_ref[...], wide_ref, wide_target, second_order, rank)
    store_product(wide_target[...].astype(bf16), both(slot_feed, doc_feed), third_kept, third_sent, 0)
    turn(normed_feed_ref[...], narrow_ref, narrow_target, first_order, rank)
    store_product(narrow_target[...].astype(bf16), both(slot_gate, doc_gate), first_kept, first_sent, 0)
    turn(normed_feed_ref[...], narrow_ref, narrow_target, second_order, rank)
    store_product(narrow_target[...].astype(bf16), both(slot_up, doc_up), second_kept, second_sent, 0)
    turn(mixed_ref[...], narrow_ref, narrow_target, first_order, rank)
    store_product(narrow_target[...].astype(bf16), both(slot_attend, doc_attend), first_kept, first_sent, units)
    turn(normed_final_ref[...], narrow_ref, narrow_target, second_order, rank)
    store_product(narrow_target[...].astype(bf16), both(slot_embed, doc_embed), second_kept, second_sent, units)


def attend_weight_kernel(
    first_order, second_order, rank_ref, normed_ref, tokens_ref, gain_ref, after_ref, slot_query, slot_key, slot_value,
    doc_query, key_kept, key_came, value_kept, value_came, wq_ref, wk_ref, wv_ref,
    first_kept, first_sent, second_kept, second_sent, tokens_out, gain_out, grads_ref, narrow_ref, narrow_target,
):
    rank = rank_ref[0]
    slots, width = slot_query.shape
    middle = first_kept.shape[1]
    key = (key_kept[...].astype(f32) + key_came[...].astype(f32)).astype(bf16)
    value = (value_kept[...].astype(f32) + value_came[...].astype(f32)).astype(bf16)
    grads_ref[:slots, :width] = slot_query[...]
    grads_ref[:slots, width : 2 * width] = slot_key[...]
    grads_ref[:slots, 2 * width :] = slot_value[...]
    grads_ref[slots:, :width] = doc_query[...]
    grads_ref[slots:, width : 2 * width] = key
    grads_ref[slots:, 2 * width :] = value
    turn(normed_ref[...], narrow_ref, narrow_target, first_order, rank)
    store_product(narrow_target[...].astype(bf16), grads_ref[:, :middle], first_kept, first_sent, 0)
    turn(normed_ref[...], narrow_ref, narrow_target, second_order, rank)
    store_product(narrow_target[...].astype(bf16), grads_ref[:, middle:], second_kept, second_sent, 0)
    tokens_out[...], gain_out[...] = input_back(
        tokens_ref[...].astype(f32), gain_ref, after_ref, doc_query[...], key, value, wq_ref, wk_ref, wv_ref
    )


def on_device(
    doc_tokens, query_tokens, query_lengths, positive_docs, retrieved, attend_gain, query_weight, key_weight,
    value_weight, output_weight, bias_table, feed_gain, gate_weight, up_weight, down_weight, final_gain, proj_weight,
):
    narrow_size = lax.axis_size("narrow")
    narrow_rank = lax.axis_index("narrow")
    bits = rank_bits()
    rank = my_rank()
    rank_word = rank.astype(jnp.int32).reshape(1)
    doc_rows, width = doc_tokens.shape[1:]
    doc_length = doc_rows * narrow_size
    doc_total = doc_tokens.shape[0] * lax.axis_size("wide")
    slots = query_tokens.shape[0] // narrow_size
    slot_length = query_tokens.shape[1]
    heads = bias_table.shape[1]
    units = gate_weight.shape[1]
    columns = proj_weight.shape[1]
    slot_rows = slots * slot_length
    rows = slot_rows + doc_rows
    blocks = doc_total * doc_length // LANES
    assert doc_tokens.shape[0] == 1 and doc_rows == LANES and slot_rows == LANES and narrow_size == 4
    assert columns == LANES and doc_total <= LANES and blocks == 1 << bits

    def own(values):
        return lax.dynamic_slice_in_dim(values, narrow_rank * slots, slots, 0)

    own_tokens = doc_tokens[0]
    y_tokens = swap(own_tokens, 1)
    slot_tokens = own(query_tokens).reshape(slot_rows, width)
    places = own(retrieved).reshape(slot_rows, -1)
    lengths = own(query_lengths)
    positives = own(positive_docs).reshape(slots, 1)
    valid = (jnp.arange(slot_length, dtype=jnp.int32)[None, :] < lengths[:, None]).astype(f32)
    key_valid = valid.reshape(1, slot_rows)
    row_valid = valid.reshape(slot_rows, 1)
    reach = doc_length + LANES
    offsets = jnp.arange(-doc_length, reach, dtype=jnp.int32)
    offset_hot = (bucket_index(offsets)[:, None] == jnp.arange(BUCKETS, dtype=jnp.int32)).astype(f32)
    offset_bias = jnp.einsum("mu,uh->hm", offset_hot, bias_table, precision=highest)

    counts, tally, doc_bias, slot_bias = call(
        functools.partial(prepare_kernel, doc_length, slot_length, doc_total),
        [
            shape((blocks, slot_rows, LANES), bf16),
            shape((slot_rows, LANES)),
            shape((heads, doc_rows, doc_length)),
            shape((heads, slot_rows, slot_rows)),
        ],
        [rank_word, places, offset_bias],
        scratch=[pltpu.VMEM((blocks * slot_rows, LANES), f32)],
        smem=1,
    )
    core_tokens = swap(own_tokens, 0)
    both_tokens = swap(y_tokens, 0)

    gains = (attend_gain.reshape(1, width), feed_gain.reshape(1, width), final_gain.reshape(1, width))
    all_rows = slot_rows + doc_length
    (
        normed, query, key, value, doc_probs, slot_probs, mixed, after_attend, normed_feed, hidden, gate_slope, up_slope,
        after_feed, normed_final, embed, slot_unit, doc_unit,
    ) = call(
        functools.partial(forward_kernel, slot_length),
        [
            shape((rows, width), bf16),
            shape((rows, width), bf16),
            shape((all_rows, width), bf16),
            shape((all_rows, width), bf16),
            shape((heads, doc_rows, doc_length), bf16),
            shape((heads, slot_rows, slot_rows), bf16),
            shape((rows, width), bf16),
            shape((rows, width)),
            shape((rows, width), bf16),
            shape((rows, units), bf16),
            shape((rows, units), bf16),
            shape((rows, units), bf16),
            shape((rows, width)),
            shape((rows, width), bf16),
            shape((rows, columns)),
            shape((slot_rows, columns), bf16),
            shape((doc_rows, columns), bf16),
        ],
        [
            slot_tokens, own_tokens, core_tokens, y_tokens, both_tokens, key_valid, doc_bias, slot_bias, *gains,
            query_weight, key_weight, value_weight, output_weight, gate_weight, up_weight, down_weight, proj_weight,
        ],
        scratch=[pltpu.VMEM((all_rows, width), bf16)],
    )

    gathered = list(range(bits))[::-1]
    gathered_units = doc_unit[None]
    for bit in gathered[:-1]:
        gathered_units = jnp.concatenate([gathered_units, swap(gathered_units, bit)], 0)
    far_units = swap(gathered_units, gathered[-1])

    order = list(range(bits))
    half = blocks // 2
    losses, grad_slot_unit, kept, sent = call(
        functools.partial(loss_kernel, order, gathered, doc_total, slots),
        [
            shape((slots, LANES)),
            shape((slot_rows, columns)),
            shape((half, columns, LANES), bf16),
            shape((half, columns, LANES), bf16),
        ],
        [rank_word, counts, gathered_units, far_units, slot_unit, tally, row_valid, positives],
        scratch=[
            pltpu.VMEM((doc_total, slot_rows, columns), f32),
            pltpu.VMEM((doc_total, columns, slot_rows), bf16),
        ],
        smem=1,
    )
    for step, bit in enumerate(order):
        came = swap(sent, bit)
        if step < bits - 1:
            cut = kept.shape[0] // 2
            sent = (kept[cut:].astype(f32) + came[cut:].astype(f32)).astype(bf16)
            kept = (kept[:cut].astype(f32) + came[:cut].astype(f32)).astype(bf16)

    feed_shapes = [
        shape((LANES, columns), bf16),
        shape((LANES, width), bf16),
        shape((LANES, units), bf16),
        shape((LANES, units), bf16),
    ]
    row_shape = shape((LANES, width), bf16)
    gain_scratch = [pltpu.VMEM((1, width), f32), pltpu.VMEM((1, width), f32)]
    (
        slot_embed, slot_feed, slot_gate, slot_up, slot_attend, slot_grad_query, slot_grad_key, slot_grad_value,
        query_grad, slot_gains, slot_sums,
    ) = call(
        slot_back_kernel,
        feed_shapes
        + [row_shape] * 4
        + [shape((slot_rows, width)), shape((3, width)), shape((heads * 8, 2 * LANES))],
        [
            grad_slot_unit, embed, after_feed, after_attend, gate_slope, up_slope, slot_tokens, query, key, value,
            slot_probs, *gains, query_weight, key_weight, value_weight, output_weight, gate_weight, up_weight,
            down_weight, proj_weight,
        ],
        scratch=[pltpu.VMEM((slot_rows, width), f32), pltpu.VMEM((slot_rows, width), bf16)] + gain_scratch,
    )
    doc_embed, doc_feed, doc_gate, doc_up, doc_after, doc_attend, doc_mixed, doc_gains = call(
        doc_feed_kernel,
        feed_shapes + [shape((doc_rows, width)), row_shape, row_shape, shape((2, width))],
        [
            kept, came, embed, after_feed, after_attend, gate_slope, up_slope, gains[1], gains[2], output_weight,
            gate_weight, up_weight, down_weight, proj_weight,
        ],
        scratch=gain_scratch,
    )

    over_y = [0, 1, 2] + list(range(3, bits))
    over_x = [0, 2, 1] + list(range(3, bits))
    first_cols, second_cols = units + width, units + columns
    first_kept, first_sent, second_kept, second_sent, third_kept, third_sent = call(
        functools.partial(feed_weight_kernel, over_y, over_x),
        [shape((width // 2, first_cols), bf16)] * 2
        + [shape((width // 2, second_cols), bf16)] * 2
        + [shape((units // 2, width), bf16)] * 2,
        [
            rank_word, normed_feed, mixed, normed_final, hidden, slot_gate, doc_gate, slot_up, doc_up, slot_attend,
            doc_attend, slot_embed, doc_embed, slot_feed, doc_feed,
        ],
        scratch=[
            pltpu.VMEM((width, rows), f32),
            pltpu.VMEM((width, rows), f32),
            pltpu.VMEM((units, rows), f32),
            pltpu.VMEM((units, rows), f32),
        ],
        smem=1,
    )

    doc_grad_query, key_kept, value_kept, key_sent, value_sent, doc_sums = call(
        doc_attend_kernel,
        [row_shape] + [shape((doc_length // 2, width), bf16)] * 4 + [shape((heads * 8, 2 * doc_length))],
        [query, key, value, doc_probs, doc_mixed],
        scratch=[pltpu.VMEM((doc_length, width), bf16), pltpu.VMEM((doc_length, width), bf16)],
    )
    key_came, value_came = swap(key_sent, 0), swap(value_sent, 0)
    pair_sum = []
    for one_kept, one_came in ((key_kept, key_came), (value_kept, value_came)):
        total = one_kept.astype(f32) + one_came.astype(f32)
        pair_sum.append((total[:doc_rows].astype(bf16), total[doc_rows:].astype(bf16)))
    came_pair = swap(jnp.concatenate([pair_sum[0][1], pair_sum[1][1]], 0), 1)

    middle = 3 * width // 2
    fourth_kept, fourth_sent, fifth_kept, fifth_sent, doc_grad, doc_attend_gain = call(
        functools.partial(attend_weight_kernel, over_y, over_x),
        [shape((width // 2, middle), bf16)] * 4 + [shape((doc_rows, width)), shape((1, width))],
        [
            rank_word, normed, own_tokens, gains[0], doc_after, slot_grad_query, slot_grad_key, slot_grad_value,
            doc_grad_query, pair_sum[0][0], came_pair[:doc_rows], pair_sum[1][0], came_pair[doc_rows:], query_weight,
            key_weight, value_weight,
        ],
        scratch=[
            pltpu.VMEM((rows, 3 * width), bf16),
            pltpu.VMEM((width, rows), f32),
            pltpu.VMEM((width, rows), f32),
        ],
        smem=1,
    )

    lines = doc_sums.reshape(heads, 8, narrow_size, 2 * LANES).sum(1)
    span = jnp.arange(2 * LANES, dtype=jnp.int32) - (LANES - 1)
    parts = jnp.arange(narrow_size, dtype=jnp.int32)
    doc_offsets = ((narrow_rank ^ parts) - narrow_rank)[:, None] * LANES + span[None, :]
    places_hot = jnp.arange(BUCKETS, dtype=jnp.int32)
    doc_hot = (bucket_index(doc_offsets)[..., None] == places_hot).astype(f32)
    slot_hot = (bucket_index(span)[:, None] == places_hot).astype(f32)
    table_term = jnp.einsum("hpm,pmu->uh", lines, doc_hot, precision=highest)
    table_term = table_term + jnp.einsum(
        "hm,mu->uh", slot_sums.reshape(heads, 8, 2 * LANES).sum(1), slot_hot, precision=highest
    )

    first_sum = halve(first_kept, first_sent, over_y)
    second_sum = halve(second_kept, second_sent, over_x)
    third_sum = halve(third_kept, third_sent, over_x)
    fourth_sum = halve(fourth_kept, fourth_sent, over_y)
    fifth_sum = halve(fifth_kept, fifth_sent, over_x)
    gain_grads = slot_gains + jnp.concatenate([doc_attend_gain, doc_gains], 0)
    small = jnp.concatenate([gain_grads.reshape(-1), table_term.reshape(-1)])
    small = sum_all(small.reshape(-1, LANES)).reshape(-1)
    gain_rows = width >> bits
    gain_out = [
        lax.dynamic_slice_in_dim(small, place * width + rank * gain_rows, gain_rows, 0) for place in range(3)
    ]
    bias_table_grad = small[3 * width :].reshape(BUCKETS, heads)
    return (
        losses[:, 0],
        doc_grad[None],
        query_grad.reshape(slots, slot_length, width),
        gain_out[0],
        fourth_sum[:, :width],
        jnp.concatenate([fourth_sum[:, width:], fifth_sum[:, : 2 * width - middle]], 1),
        fifth_sum[:, 2 * width - middle :],
        first_sum[:, units:],
        bias_table_grad,
        gain_out[1],
        first_sum[:, :units],
        second_sum[:, :units],
        third_sum,
        gain_out[2],
        second_sum[:, units:],
    )


def solution(mesh):
    return jax.shard_map(
        on_device,
        mesh=mesh,
        in_specs=(
            P("wide", "narrow", None),
            P("wide", None, None),
            P("wide"),
            P("wide"),
            P("wide", None, None),
            P(),
            P(),
            P(),
            P(),
            P(),
            P(),
            P(),
            P(),
            P(),
            P(),
            P(),
            P(),
        ),
        out_specs=(
            P(("wide", "narrow")),
            P("wide", "narrow", None),
            P(("wide", "narrow"), None, None),
            P(("wide", "narrow")),
            P(("wide", "narrow"), None),
            P(("wide", "narrow"), None),
            P(("wide", "narrow"), None),
            P(("wide", "narrow"), None),
            P(),
            P(("wide", "narrow")),
            P(("wide", "narrow"), None),
            P(("wide", "narrow"), None),
            P(("wide", "narrow"), None),
            P(("wide", "narrow")),
            P(("wide", "narrow"), None),
        ),
        check_vma=False,
    )
```

time: 1740 us -> 303 us (0.17)
  waiting for transfers between devices: 932 us -> 110 us
  other arithmetic: 350 us -> 15.9 us
  local copies, waits for them, and re-layouts: 272 us -> 20.2 us
  Pallas kernels: 0 us -> 100 us
  matrix products: 102 us -> 2.25 us
  blocking collectives: 59.7 us -> 0 us
  starting transfers between devices: 1.08 us -> 48.6 us
    reduce_scatter x10 -> x0, waiting for transfers between devices: 909 us -> none  [the longest x1 132 us: on_device(): lax.psum_scatter(whole_term, ('wide', 'narrow'), scatter_dimension=0, til...]
    scatter-add x3 -> x0, other arithmetic: 317 us -> none  [the longest x1 114 us: pooled_loss(): jax.ops.segment_sum(similar.reshape(-1), slot_ids.reshape(-1), num_segmen...]
    gather x2 -> x0, local copies, waits for them, and re-layouts: 195 us -> none  [the longest x1 133 us: pooled_loss(): jax.ops.segment_sum(similar.reshape(-1), slot_ids.reshape(-1), num_segmen...]
    ppermute x0 -> x46, waiting for transfers between devices: none -> 110 us  [swap(): return lax.ppermute(values, ('wide', 'narrow'), pairs)]
    pallas_call x0 -> x8, Pallas kernels: none -> 100 us  [call(): pl.pallas_call(kernel, out_shape=tuple(outs), in_specs=specs, out_specs=t...]
    dot_general x42 -> x3, matrix products: 102 us -> 2.25 us  [the longest x1 1.84 us: on_device(): jnp.einsum('mu,uh->hm', offset_hot, bias_table, precision=highest)]
    ppermute x0 -> x46, starting transfers between devices: none -> 48.6 us  [swap(): return lax.ppermute(values, ('wide', 'narrow'), pairs)]
    unnamed x1 -> x0, blocking collectives: 38.5 us -> none
  transfers between devices with their start and end apart: 12 -> 46, of which waited for: 9 -> 31; matrix products, arithmetic and copies ran while one was open for 12% -> 10% of each run, Pallas kernels for 0% -> 18%
where the time goes in v2:
time: 303 us; the launch traced here: 298 us
  waiting for transfers between devices  110 us (36%)
  Pallas kernels  100 us (33%)
  starting transfers between devices  48.6 us (16%)
  local copies, waits for them, and re-layouts  20.2 us (7%)
  other arithmetic  15.9 us (5%)
    ppermute x46, waiting for transfers between devices, swap(): return lax.ppermute(values, ('wide', 'narrow'), pairs)  110 us
    pallas_call x8, Pallas kernels, call(): pl.pallas_call(kernel, out_shape=tuple(outs), in_specs=specs, out_specs=t...  100 us
    ppermute x46, starting transfers between devices, swap(): return lax.ppermute(values, ('wide', 'narrow'), pairs)  48.6 us
    convert_element_type x15, other arithmetic, halve(): (kept[:half].astype(f32) + came[:half].astype(f32)).astype(kept.dtype)  8.74 us
  transfers between devices with their start and end apart: 46, of which 31 were waited for; matrix products, arithmetic and copies ran while one was open for 10% of the time, Pallas kernels for 18%

profile of v2, /device:TPU:0, one launch (start us, length us, event | category | flops | bytes accessed | tf_op | source)
XLA Modules:
  0.0 298.1 jit_solution(16480531704060056891)
XLA Ops:
  0.7 3.0 %collective-permute-start.1 = (bf16[128,768]{1,0:T(8,128)(2,1)}, bf16[128,768]{1,0:T(8,128)(2,1)S(1)}, u32[]{:S(2)}, u32[]{:S(2)}) collective-permute-start(bf16[128,768]{1,0:T(8,128)(2,1)} %bitcast.28), channel_id=1, source_target_pairs={{0,2},{1,3},{2,0},{3,1},{4,6},{5,7},{6,4},{7,5},{8,10},{9,11},{10,... | collective-permute-start | bytes 589832 | tf_op jit(solution)/shard_map/ppermute | solution.py:53
  5.1 1.3 reshape.264.attend_gain_ref.gain_ref
  6.4 1.3 reshape.265.feed_gain_ref
  7.7 1.3 reshape.266.final_gain_ref
  9.0 1.8 convolution_bitcast_fusion.table_ref
  11.3 1.5 constant_dynamic-slice_fusion.1
  12.8 10.7 %shard_map.280 = (bf16[32,128,128]{2,1,0:T(8,128)(2,1)}, f32[128,128]{1,0:T(8,128)}, f32[12,128,512]{2,1,0:T(8,128)}, f32[12,128,128]{2,1,0:T(8,128)}) custom-call(s32[1]{0:T(128)} %bitcast.rank_ref, s32[128,128]{1,0:T(8,128)} %bitcast.37, f32[12,1152]{1,0:T(8,128)} %convolution_bitcast_fusion.table_ref), custom_call_target="tpu_custom_call" | custom-call | bytes 5167108 | tf_op jit(solution)/shard_map/pallas_call | solution.py:86
  24.9 22.6 %shard_map.281 = (bf16[256,768]{1,0:T(8,128)(2,1)}, bf16[256,768]{1,0:T(8,128)(2,1)}, bf16[640,768]{1,0:T(8,128)(2,1)}, bf16[640,768]{1,0:T(8,128)(2,1)}, bf16[1...) custom-call(bf16[128,768]{1,0:T(8,128)(2,1)} %bitcast.26, ...), custom_call_target="tpu_custom_call" | custom-call | bytes 30090752 | tf_op jit(solution)/shard_map/pallas_call | solution.py:86
  47.5 2.6 collective-permute-start.3
  50.2 2.8 collective-permute-done.3
  53.8 1.2 collective-permute-start.4
  55.0 3.0 %collective-permute-done.4 = bf16[2,128,128]{2,1,0:T(8,128)(2,1)S(1)} collective-permute-done((bf16[2,128,128]{2,1,0:T(8,128)(2,1)S(1)}, bf16[2,128,128]{2,1,0:T(8,128)(2,1)S(1)}, u32[]{:S(2)}, u32[]{:S(2)}) %collective-permute-start.4) | collective-permute-done | bytes 65568 | tf_op jit(solution)/shard_map/ppermute | solution.py:53
  58.8 1.6 collective-permute-start.5
  61.1 2.7 collective-permute-done.5
  64.8 6.3 %collective-permute-done.6 = bf16[8,128,128]{2,1,0:T(8,128)(2,1)S(1)} collective-permute-done((bf16[8,128,128]{2,1,0:T(8,128)(2,1)S(1)}, bf16[8,128,128]{2,1,0:T(8,128)(2,1)S(1)}, u32[]{:S(2)}, u32[]{:S(2)}) %collective-permute-start.6) | collective-permute-done | bytes 262176 | tf_op jit(solution)/shard_map/ppermute | solution.py:53
  73.9 5.5 %shard_map.282 = (f32[4,128]{1,0:T(4,128)}, f32[128,128]{1,0:T(8,128)}, bf16[16,128,128]{2,1,0:T(8,128)(2,1)}, bf16[16,128,128]{2,1,0:T(8,128)(2,1)}) custom-call(s32[1]{0:T(128)} %bitcast.rank_ref, bf16[32,128,128]{2,1,0:T(8,128)(2,1)} %get-tuple-element.77.counts_ref, bf16[16,128,128]{2,1,0:T(8,128)(2,1)} %copy-done.6, bf16[16,128,128]{2,1,0:T(8,128)(2,1)} %copy-done.7, ...), custom_call_target="tpu_custom_call" | custom-call | bytes 3312148 | tf_op jit(solution)/shard_map/pallas_call | solution.py:86
  79.5 2.0 collective-permute-done.8
  82.8 8.3 %collective-permute-done.9 = bf16[8,128,128]{2,1,0:T(8,128)(2,1)S(1)} collective-permute-done((bf16[8,128,128]{2,1,0:T(8,128)(2,1)S(1)}, bf16[8,128,128]{2,1,0:T(8,128)(2,1)S(1)}, u32[]{:S(2)}, u32[]{:S(2)}) %collective-permute-start.9) | collective-permute-done | bytes 262176 | tf_op jit(solution)/shard_map/ppermute | solution.py:53
  91.2 1.6 collective-permute-start.10
  92.7 3.5 %collective-permute-done.10 = bf16[4,128,128]{2,1,0:T(8,128)(2,1)S(1)} collective-permute-done((bf16[4,128,128]{2,1,0:T(8,128)(2,1)S(1)}, bf16[4,128,128]{2,1,0:T(8,128)(2,1)S(1)}, u32[]{:S(2)}, u32[]{:S(2)}) %collective-permute-start.10) | collective-permute-done | bytes 131104 | tf_op jit(solution)/shard_map/ppermute | solution.py:53
  96.3 1.3 collective-permute-start.11
  97.5 3.0 %collective-permute-done.11 = bf16[2,128,128]{2,1,0:T(8,128)(2,1)S(1)} collective-permute-done((bf16[2,128,128]{2,1,0:T(8,128)(2,1)S(1)}, bf16[2,128,128]{2,1,0:T(8,128)(2,1)S(1)}, u32[]{:S(2)}, u32[]{:S(2)}) %collective-permute-start.11) | collective-permute-done | bytes 65568 | tf_op jit(solution)/shard_map/ppermute | solution.py:53
  101.2 2.3 collective-permute-start.12
  103.5 2.6 collective-permute-done.12.came_ref
  106.7 10.2 %shard_map.283 = (bf16[128,128]{1,0:T(8,128)(2,1)}, bf16[128,768]{1,0:T(8,128)(2,1)}, bf16[128,2048]{1,0:T(8,128)(2,1)}, bf16[128,2048]{1,0:T(8,128)(2,1)}, f32[...) custom-call(bf16[1,128,128]{2,1,0:T(8,128)(2,1)} %get-tuple-element.212.kept_ref, ...), custom_call_target="tpu_custom_call" | custom-call | bytes 16756736 | tf_op jit(solution)/shard_map/pallas_call | solution.py:86
  116.8 8.5 %shard_map.285 = (bf16[128,768]{1,0:T(8,128)(2,1)}, bf16[256,768]{1,0:T(8,128)(2,1)}, bf16[256,768]{1,0:T(8,128)(2,1)}, bf16[256,768]{1,0:T(8,128)(2,1)}, bf16[256,768]{1,0:T(8,128)(2,1)}, /*index=5*/f32[96,1024]{1,0:T(8,128)}) custom-call(bf16[256,768]{1,0:T(8,128)(2,1)} %get-tuple-element.94.query_ref, bf16[640,768]{1,0:T(8,128)(2,1)} %get-tuple-element.95.key_ref, ...), custom_call_target="tpu_custom_call" | custom-call | bytes 6291456 | tf_op jit(solution)/shard_map/pallas_call | solution.py:86
  125.5 26.9 %shard_map.284 = (bf16[128,128]{1,0:T(8,128)(2,1)}, bf16[128,768]{1,0:T(8,128)(2,1)}, bf16[128,2048]{1,0:T(8,128)(2,1)}, bf16[128,2048]{1,0:T(8,128)(2,1)}, bf16...) custom-call(f32[128,128]{1,0:T(8,128)} %get-tuple-element.93.grad_un, ...), custom_call_target="tpu_custom_call" | custom-call | bytes 23742464 | tf_op jit(solution)/shard_map/pallas_call | solution.py:86
  155.6 9.6 %shard_map.287 = (bf16[384,2816]{1,0:T(8,128)(2,1)}, bf16[384,2816]{1,0:T(8,128)(2,1)}, bf16[384,2176]{1,0:T(8,128)(2,1)}, bf16[384,2176]{1,0:T(8,128)(2,1)}, bf...) custom-call(s32[1]{0:T(128)} %bitcast.rank_ref, bf16[256,768]{1,0:T(8,128)(2,1)} %get-tuple-element.119.normed_feed_ref, ...), custom_call_target="tpu_custom_call" | custom-call | bytes 15990788 | tf_op jit(solution)/shard_map/pallas_call | solution.py:86
  167.4 6.2 %shard_map.286 = (bf16[384,1152]{1,0:T(8,128)(2,1)}, bf16[384,1152]{1,0:T(8,128)(2,1)}, bf16[384,1152]{1,0:T(8,128)(2,1)}, bf16[384,1152]{1,0:T(8,128)(2,1)}, f32[128,768]{1,0:T(8,128)}, /*index=5*/f32[1,768]{1,0:T(1,128)}) custom-call(s32[1]{0:T(128)} %bitcast.rank_ref, bf16[256,768]{1,0:T(8,128)(2,1)} %get-tuple-element.84.normed_ref, ...), custom_call_target="tpu_custom_call" | custom-call | bytes 10033156 | tf_op jit(solution)/shard_map/pallas_call | solution.py:86
  175.6 1.3 collective-permute-start.17
  177.0 2.3 collective-permute-done.17
  179.3 1.6 collective-permute-start.18
  180.9 2.2 collective-permute-done.18
  184.3 2.5 collective-permute-done.19
  186.8 2.3 collective-permute-start.20
  189.7 1.7 collective-permute-done.20
  192.8 2.3 add_convert_fusion.5
  195.1 1.6 collective-permute-start.42
  196.6 1.4 add_convert_fusion.11
  198.0 1.4 collective-permute-start.22
  199.4 1.4 add_convert_fusion.9
  201.4 1.8 add_convert_fusion.3
  203.2 1.6 collective-permute-start.37
  204.8 5.6 %collective-permute-done.22 = bf16[192,1152]{1,0:T(8,128)(2,1)S(1)} collective-permute-done((bf16[192,1152]{1,0:T(8,128)(2,1)S(1)}, bf16[192,1152]{1,0:T(8,128)(2,1)S(1)}, u32[]{:S(2)}, u32[]{:S(2)}) %collective-permute-start.22) | collective-permute-done | bytes 442400 | tf_op jit(solution)/shard_map/ppermute | solution.py:53
  211.1 13.9 %collective-permute-done.27 = bf16[192,1152]{1,0:T(8,128)(2,1)S(1)} collective-permute-done((bf16[192,1152]{1,0:T(8,128)(2,1)S(1)}, bf16[192,1152]{1,0:T(8,128)(2,1)S(1)}, u32[]{:S(2)}, u32[]{:S(2)}) %collective-permute-start.27) | collective-permute-done | bytes 442400 | tf_op jit(solution)/shard_map/ppermute | solution.py:53
  225.1 1.4 collective-permute-start.28
  227.8 19.4 %collective-permute-done.23 = bf16[96,1152]{1,0:T(8,128)(2,1)S(1)} collective-permute-done((bf16[96,1152]{1,0:T(8,128)(2,1)S(1)}, bf16[96,1152]{1,0:T(8,128)(2,1)S(1)}, u32[]{:S(2)}, u32[]{:S(2)}) %collective-permute-start.23) | collective-permute-done | bytes 221216 | tf_op jit(solution)/shard_map/ppermute | solution.py:53
  247.3 1.3 collective-permute-start.24
  249.7 1.4 collective-permute-start.43
  251.1 2.1 collective-permute-done.24
  253.2 2.1 collective-permute-start.25
  255.3 2.1 collective-permute-start.30
  257.4 2.1 collective-permute-done.25
  261.8 1.6 collective-permute-done.43
  263.5 1.3 collective-permute-start.44
  265.0 1.4 collective-permute-start.38
  266.4 2.8 collective-permute-done.44
  269.3 2.3 collective-permute-start.45
  271.9 1.6 collective-permute-start.33
  273.4 1.3 collective-permute-done.38
  276.7 6.4 %collective-permute-done.33 = bf16[96,2816]{1,0:T(8,128)(2,1)S(1)} collective-permute-done((bf16[96,2816]{1,0:T(8,128)(2,1)S(1)}, bf16[96,2816]{1,0:T(8,128)(2,1)S(1)}, u32[]{:S(2)}, u32[]{:S(2)}) %collective-permute-start.33) | collective-permute-done | bytes 540704 | tf_op jit(solution)/shard_map/ppermute | solution.py:53
  283.3 1.8 collective-permute-start.34
  285.5 5.0 %collective-permute-done.34 = bf16[48,2816]{1,0:T(8,128)(2,1)S(1)} collective-permute-done((bf16[48,2816]{1,0:T(8,128)(2,1)S(1)}, bf16[48,2816]{1,0:T(8,128)(2,1)S(1)}, u32[]{:S(2)}, u32[]{:S(2)}) %collective-permute-start.34) | collective-permute-done | bytes 270368 | tf_op jit(solution)/shard_map/ppermute | solution.py:53
  291.5 3.0 collective-permute-done.40
  (166 shorter events, 36.5 us)
Async XLA Ops:
  0.6 22.9 %copy-start = (bf16[16,32,768]{2,1,0:T(8,128)(2,1)S(1)}, bf16[16,32,768]{2,1,0:T(8,128)(2,1)}, u32[]{:S(2)}) copy-start(bf16[16,32,768]{2,1,0:T(8,128)(2,1)} %param.18) | copy-start | bytes 2359300
  0.7 10.1 %collective-permute-start.1 = (bf16[128,768]{1,0:T(8,128)(2,1)}, bf16[128,768]{1,0:T(8,128)(2,1)S(1)}, u32[]{:S(2)}, u32[]{:S(2)}) collective-permute-start(bf16[128,768]{1,0:T(8,128)(2,1)} %bitcast.28), channel_id=1, source_target_pairs={{0,2},{1,3},{2,0},{3,1},{4,6},{5,7},{6,4},{7,5},{8,10},{9,11},{10,... | collective-permute-start | bytes 589832 | tf_op jit(solution)/shard_map/ppermute | solution.py:53
  3.7 20.5 %collective-permute-start = (bf16[128,768]{1,0:T(8,128)(2,1)}, bf16[128,768]{1,0:T(8,128)(2,1)S(1)}, u32[]{:S(2)}, u32[]{:S(2)}) collective-permute-start(bf16[128,768]{1,0:T(8,128)(2,1)} %bitcast.29), channel_id=1, source_target_pairs={{0,1},{1,0},{2,3},{3,2},{4,5},{5,4},{6,7},{7,6},{8,9},{9,8},{10,11... | collective-permute-start | bytes 589832 | tf_op jit(solution)/shard_map/ppermute | solution.py:53
  10.8 13.4 %copy-start.11 = (bf16[128,768]{1,0:T(8,128)(2,1)}, bf16[128,768]{1,0:T(8,128)(2,1)S(1)}, u32[]{:S(2)}) copy-start(bf16[128,768]{1,0:T(8,128)(2,1)S(1)} %collective-permute-done.1.far_ref) | copy-start | bytes 589828
  10.8 13.4 %collective-permute-start.2 = (bf16[128,768]{1,0:T(8,128)(2,1)S(1)}, bf16[128,768]{1,0:T(8,128)(2,1)S(1)}, u32[]{:S(2)}, u32[]{:S(2)}) collective-permute-start(bf16[128,768]{1,0:T(8,128)(2,1)S(1)} %collective-permute-done.1.far_ref), channel_id=1, source_target_pairs={{0,1},{1,0},{2,3},{3,2},{4,5},{5,4},{6,7},{7,6},{8,9},{9,8},{10,11... | collective-permute-start | bytes 589832 | tf_op jit(solution)/shard_map/ppermute | solution.py:53
  47.5 24.4 %copy-start.20 = (s32[16]{0:T(128)S(1)}, s32[16]{0:T(128)}, u32[]{:S(2)}) copy-start(s32[16]{0:T(128)} %param.20) | copy-start | bytes 196
  47.5 5.4 %collective-permute-start.3 = (bf16[1,128,128]{2,1,0:T(8,128)(2,1)}, bf16[1,128,128]{2,1,0:T(8,128)(2,1)S(1)}, u32[]{:S(2)}, u32[]{:S(2)}) collective-permute-start(bf16[1,128,128]{2,1,0:T(8,128)(2,1)} %bitcast.32), channel_id=1, source_target_pairs={{0,16},{1,17},{2,18},{3,19},{4,20},{5,21},{6,22},{7,23},{8,24},{9,... | collective-permute-start | bytes 98312 | tf_op jit(solution)/shard_map/ppermute | solution.py:53
  53.8 4.3 %collective-permute-start.4 = (bf16[2,128,128]{2,1,0:T(8,128)(2,1)S(1)}, bf16[2,128,128]{2,1,0:T(8,128)(2,1)S(1)}, u32[]{:S(2)}, u32[]{:S(2)}) collective-permute-start(bf16[2,128,128]{2,1,0:T(8,128)(2,1)S(1)} %pad_maximum_fusion.4), channel_id=1, source_target_pairs={{0,8},{1,9},{2,10},{3,11},{4,12},{5,13},{6,14},{7,15},{8,0},{9,1},... | collective-permute-start | bytes 196616 | tf_op jit(solution)/shard_map/ppermute | solution.py:53
  58.8 5.0 %collective-permute-start.5 = (bf16[4,128,128]{2,1,0:T(8,128)(2,1)S(1)}, bf16[4,128,128]{2,1,0:T(8,128)(2,1)S(1)}, u32[]{:S(2)}, u32[]{:S(2)}) collective-permute-start(bf16[4,128,128]{2,1,0:T(8,128)(2,1)S(1)} %pad_maximum_fusion.2), channel_id=1, source_target_pairs={{0,4},{1,5},{2,6},{3,7},{4,0},{5,1},{6,2},{7,3},{8,12},{9,13},{10,... | collective-permute-start | bytes 393224 | tf_op jit(solution)/shard_map/ppermute | solution.py:53
  64.6 6.4 %collective-permute-start.6 = (bf16[8,128,128]{2,1,0:T(8,128)(2,1)S(1)}, bf16[8,128,128]{2,1,0:T(8,128)(2,1)S(1)}, u32[]{:S(2)}, u32[]{:S(2)}) collective-permute-start(bf16[8,128,128]{2,1,0:T(8,128)(2,1)S(1)} %pad_maximum_fusion.1), channel_id=1, source_target_pairs={{0,2},{1,3},{2,0},{3,1},{4,6},{5,7},{6,4},{7,5},{8,10},{9,11},{10,... | collective-permute-start | bytes 786440 | tf_op jit(solution)/shard_map/ppermute | solution.py:53
  71.1 2.0 copy-start.6
  71.1 2.0 collective-permute-start.7
  73.1 0.8 copy-start.7
  79.4 2.1 collective-permute-start.8
  82.7 8.4 %collective-permute-start.9 = (bf16[8,128,128]{2,1,0:T(8,128)(2,1)S(1)}, bf16[8,128,128]{2,1,0:T(8,128)(2,1)S(1)}, u32[]{:S(2)}, u32[]{:S(2)}) collective-permute-start(bf16[8,128,128]{2,1,0:T(8,128)(2,1)S(1)} %get-tuple-element.188), channel_id=1, source_target_pairs={{0,2},{1,3},{2,0},{3,1},{4,6},{5,7},{6,4},{7,5},{8,10},{9,11},{10,... | collective-permute-start | bytes 786440 | tf_op jit(solution)/shard_map/ppermute | solution.py:53
  91.2 5.0 %collective-permute-start.10 = (bf16[4,128,128]{2,1,0:T(8,128)(2,1)S(1)}, bf16[4,128,128]{2,1,0:T(8,128)(2,1)S(1)}, u32[]{:S(2)}, u32[]{:S(2)}) collective-permute-start(bf16[4,128,128]{2,1,0:T(8,128)(2,1)S(1)} %get-tuple-element.198), channel_id=1, source_target_pairs={{0,4},{1,5},{2,6},{3,7},{4,0},{5,1},{6,2},{7,3},{8,12},{9,13},{10,... | collective-permute-start | bytes 393224 | tf_op jit(solution)/shard_map/ppermute | solution.py:53
  96.3 4.3 %collective-permute-start.11 = (bf16[2,128,128]{2,1,0:T(8,128)(2,1)S(1)}, bf16[2,128,128]{2,1,0:T(8,128)(2,1)S(1)}, u32[]{:S(2)}, u32[]{:S(2)}) collective-permute-start(bf16[2,128,128]{2,1,0:T(8,128)(2,1)S(1)} %get-tuple-element.210), channel_id=1, source_target_pairs={{0,8},{1,9},{2,10},{3,11},{4,12},{5,13},{6,14},{7,15},{8,0},{9,1},... | collective-permute-start | bytes 196616 | tf_op jit(solution)/shard_map/ppermute | solution.py:53
  101.2 4.8 %collective-permute-start.12 = (bf16[1,128,128]{2,1,0:T(8,128)(2,1)S(1)}, bf16[1,128,128]{2,1,0:T(8,128)(2,1)S(1)}, u32[]{:S(2)}, u32[]{:S(2)}) collective-permute-start(bf16[1,128,128]{2,1,0:T(8,128)(2,1)S(1)} %get-tuple-element.211), channel_id=1, source_target_pairs={{0,16},{1,17},{2,18},{3,19},{4,20},{5,21},{6,22},{7,23},{8,24},{9,... | collective-permute-start | bytes 98312 | tf_op jit(solution)/shard_map/ppermute | solution.py:53
  125.4 27.6 %collective-permute-start.13 = (bf16[256,768]{1,0:T(8,128)(2,1)}, bf16[256,768]{1,0:T(8,128)(2,1)S(1)}, u32[]{:S(2)}, u32[]{:S(2)}) collective-permute-start(bf16[256,768]{1,0:T(8,128)(2,1)} %get-tuple-element.105), channel_id=1, source_target_pairs={{0,1},{1,0},{2,3},{3,2},{4,5},{5,4},{6,7},{7,6},{8,9},{9,8},{10,11... | collective-permute-start | bytes 1179656 | tf_op jit(solution)/shard_map/ppermute | solution.py:53
  125.5 26.9 %copy-start.19 = (bf16[256,768]{1,0:T(8,128)(2,1)S(1)}, bf16[256,768]{1,0:T(8,128)(2,1)}, u32[]{:S(2)}) copy-start(bf16[256,768]{1,0:T(8,128)(2,1)} %get-tuple-element.107) | copy-start | bytes 1179652
  125.5 27.5 %copy-start.10 = (bf16[256,768]{1,0:T(8,128)(2,1)S(1)}, bf16[256,768]{1,0:T(8,128)(2,1)}, u32[]{:S(2)}) copy-start(bf16[256,768]{1,0:T(8,128)(2,1)} %get-tuple-element.104) | copy-start | bytes 1179652
  152.4 1.9 copy-start.9
  152.4 1.9 collective-permute-start.14
  153.8 1.8 copy-start.14
  155.1 11.5 %collective-permute-start.15 = (bf16[256,768]{1,0:T(8,128)(2,1)S(1)}, bf16[256,768]{1,0:T(8,128)(2,1)S(1)}, u32[]{:S(2)}, u32[]{:S(2)}) collective-permute-start(bf16[256,768]{1,0:T(8,128)(2,1)S(1)} %pad_maximum_fusion), channel_id=1, source_target_pairs={{0,2},{1,3},{2,0},{3,1},{4,6},{5,7},{6,4},{7,5},{8,10},{9,11},{10,... | collective-permute-start | bytes 1179656 | tf_op jit(solution)/shard_map/ppermute | solution.py:53
  155.6 9.8 %copy-start.8 = (f32[96,1024]{1,0:T(8,128)S(1)}, f32[96,1024]{1,0:T(8,128)}, u32[]{:S(2)}) copy-start(f32[96,1024]{1,0:T(8,128)} %get-tuple-element.113) | copy-start | bytes 1179652
  165.2 27.5 %collective-permute-start.41 = (bf16[1024,768]{1,0:T(8,128)(2,1)}, bf16[1024,768]{1,0:T(8,128)(2,1)}, u32[]{:S(2)}, u32[]{:S(2)}) collective-permute-start(bf16[1024,768]{1,0:T(8,128)(2,1)} %get-tuple-element.138), channel_id=1, source_target_pairs={{0,1},{1,0},{2,3},{3,2},{4,5},{5,4},{6,7},{7,6},{8,9},{9,8},{10,11... | collective-permute-start | bytes 4718600 | tf_op jit(solution)/shard_map/ppermute | solution.py:53
  167.4 6.2 %copy-start.16 = (f32[3,768]{1,0:T(4,128)S(1)}, f32[3,768]{1,0:T(4,128)}, u32[]{:S(2)}) copy-start(f32[3,768]{1,0:T(4,128)} %get-tuple-element.110) | copy-start | bytes 27652
  167.4 6.2 %copy-start.17 = (f32[2,768]{1,0:T(2,128)S(1)}, f32[2,768]{1,0:T(2,128)}, u32[]{:S(2)}) copy-start(f32[2,768]{1,0:T(2,128)} %get-tuple-element.112) | copy-start | bytes 18436
  167.4 21.7 %copy-start.18 = (f32[4,128]{1,0:T(4,128)S(1)}, f32[4,128]{1,0:T(4,128)}, u32[]{:S(2)}) copy-start(f32[4,128]{1,0:T(4,128)} %get-tuple-element.83) | copy-start | bytes 6148
  174.3 1.2 collective-permute-start.16
  174.4 22.2 %collective-permute-start.21 = (bf16[384,1152]{1,0:T(8,128)(2,1)}, bf16[384,1152]{1,0:T(8,128)(2,1)}, u32[]{:S(2)}, u32[]{:S(2)}) collective-permute-start(bf16[384,1152]{1,0:T(8,128)(2,1)} %get-tuple-element.116), channel_id=1, source_target_pairs={{0,1},{1,0},{2,3},{3,2},{4,5},{5,4},{6,7},{7,6},{8,9},{9,8},{10,11... | collective-permute-start | bytes 2654216 | tf_op jit(solution)/shard_map/ppermute | solution.py:53
  175.6 3.7 %collective-permute-start.17 = (f32[21,128]{1,0:T(8,128)S(1)}, f32[21,128]{1,0:T(8,128)S(1)}, u32[]{:S(2)}, u32[]{:S(2)}) collective-permute-start(f32[21,128]{1,0:T(8,128)S(1)} %fusion.37), channel_id=1, source_target_pairs={{0,2},{1,3},{2,0},{3,1},{4,6},{5,7},{6,4},{7,5},{8,10},{9,11},{10,... | collective-permute-start | bytes 32264 | tf_op jit(solution)/shard_map/ppermute | solution.py:53
  176.9 24.5 %collective-permute-start.36 = (bf16[384,2176]{1,0:T(8,128)(2,1)}, bf16[384,2176]{1,0:T(8,128)(2,1)}, u32[]{:S(2)}, u32[]{:S(2)}) collective-permute-start(bf16[384,2176]{1,0:T(8,128)(2,1)} %get-tuple-element.136), channel_id=1, source_target_pairs={{0,1},{1,0},{2,3},{3,2},{4,5},{5,4},{6,7},{7,6},{8,9},{9,8},{10,11... | collective-permute-start | bytes 5013512 | tf_op jit(solution)/shard_map/ppermute | solution.py:53
  179.3 3.8 %collective-permute-start.18 = (f32[21,128]{1,0:T(8,128)S(1)}, f32[21,128]{1,0:T(8,128)S(1)}, u32[]{:S(2)}, u32[]{:S(2)}) collective-permute-start(f32[21,128]{1,0:T(8,128)S(1)} %fusion.38), channel_id=1, source_target_pairs={{0,4},{1,5},{2,6},{3,7},{4,0},{5,1},{6,2},{7,3},{8,12},{9,13},{10,... | collective-permute-start | bytes 32264 | tf_op jit(solution)/shard_map/ppermute | solution.py:53
  183.1 3.7 %collective-permute-start.19 = (f32[21,128]{1,0:T(8,128)S(1)}, f32[21,128]{1,0:T(8,128)S(1)}, u32[]{:S(2)}, u32[]{:S(2)}) collective-permute-start(f32[21,128]{1,0:T(8,128)S(1)} %add.457), channel_id=1, source_target_pairs={{0,8},{1,9},{2,10},{3,11},{4,12},{5,13},{6,14},{7,15},{8,0},{9,1},... | collective-permute-start | bytes 32264 | tf_op jit(solution)/shard_map/ppermute | solution.py:53
  186.8 4.6 %collective-permute-start.20 = (f32[21,128]{1,0:T(8,128)S(1)}, f32[21,128]{1,0:T(8,128)S(1)}, u32[]{:S(2)}, u32[]{:S(2)}) collective-permute-start(f32[21,128]{1,0:T(8,128)S(1)} %add.458), channel_id=1, source_target_pairs={{0,16},{1,17},{2,18},{3,19},{4,20},{5,21},{6,22},{7,23},{8,24},{9,... | collective-permute-start | bytes 32264 | tf_op jit(solution)/shard_map/ppermute | solution.py:53
  189.7 36.8 %collective-permute-start.31 = (bf16[384,2816]{1,0:T(8,128)(2,1)}, bf16[384,2816]{1,0:T(8,128)(2,1)S(1)}, u32[]{:S(2)}, u32[]{:S(2)}) collective-permute-start(bf16[384,2816]{1,0:T(8,128)(2,1)} %get-tuple-element.134), channel_id=1, source_target_pairs={{0,1},{1,0},{2,3},{3,2},{4,5},{5,4},{6,7},{7,6},{8,9},{9,8},{10,11... | collective-permute-start | bytes 6488072 | tf_op jit(solution)/shard_map/ppermute | solution.py:53
  191.4 8.0 %collective-permute-start.26 = (bf16[384,1152]{1,0:T(8,128)(2,1)}, bf16[384,1152]{1,0:T(8,128)(2,1)}, u32[]{:S(2)}, u32[]{:S(2)}) collective-permute-start(bf16[384,1152]{1,0:T(8,128)(2,1)} %get-tuple-element.118), channel_id=1, source_target_pairs={{0,1},{1,0},{2,3},{3,2},{4,5},{5,4},{6,7},{7,6},{8,9},{9,8},{10,11... | collective-permute-start | bytes 2654216 | tf_op jit(solution)/shard_map/ppermute | solution.py:53
  192.8 3.9 %copy-start.5 = (bf16[384,1152]{1,0:T(8,128)(2,1)S(1)}, bf16[384,1152]{1,0:T(8,128)(2,1)}, u32[]{:S(2)}) copy-start(bf16[384,1152]{1,0:T(8,128)(2,1)} %get-tuple-element.115) | copy-start | bytes 2654212
  195.1 4.4 %copy-start.4 = (bf16[384,1152]{1,0:T(8,128)(2,1)S(1)}, bf16[384,1152]{1,0:T(8,128)(2,1)}, u32[]{:S(2)}) copy-start(bf16[384,1152]{1,0:T(8,128)(2,1)} %get-tuple-element.117) | copy-start | bytes 2654212
  195.1 54.4 %collective-permute-start.42 = (bf16[512,768]{1,0:T(8,128)(2,1)S(1)}, bf16[512,768]{1,0:T(8,128)(2,1)S(1)}, u32[]{:S(2)}, u32[]{:S(2)}) collective-permute-start(bf16[512,768]{1,0:T(8,128)(2,1)S(1)} %get-tuple-element.174), channel_id=1, source_target_pairs={{0,4},{1,5},{2,6},{3,7},{4,0},{5,1},{6,2},{7,3},{8,12},{9,13},{10,... | collective-permute-start | bytes 2359304 | tf_op jit(solution)/shard_map/ppermute | solution.py:53
  198.0 3.4 %copy-start.3 = (bf16[384,2176]{1,0:T(8,128)(2,1)S(1)}, bf16[384,2176]{1,0:T(8,128)(2,1)}, u32[]{:S(2)}) copy-start(bf16[384,2176]{1,0:T(8,128)(2,1)} %get-tuple-element.135) | copy-start | bytes 5013508
  198.0 12.4 %collective-permute-start.22 = (bf16[192,1152]{1,0:T(8,128)(2,1)S(1)}, bf16[192,1152]{1,0:T(8,128)(2,1)S(1)}, u32[]{:S(2)}, u32[]{:S(2)}) collective-permute-start(bf16[192,1152]{1,0:T(8,128)(2,1)S(1)} %get-tuple-element.180), channel_id=1, source_target_pairs={{0,2},{1,3},{2,0},{3,1},{4,6},{5,7},{6,4},{7,5},{8,10},{9,11},{10,... | collective-permute-start | bytes 1327112 | tf_op jit(solution)/shard_map/ppermute | solution.py:53
  200.8 24.2 %collective-permute-start.27 = (bf16[192,1152]{1,0:T(8,128)(2,1)S(1)}, bf16[192,1152]{1,0:T(8,128)(2,1)S(1)}, u32[]{:S(2)}, u32[]{:S(2)}) collective-permute-start(bf16[192,1152]{1,0:T(8,128)(2,1)S(1)} %get-tuple-element.178), channel_id=1, source_target_pairs={{0,4},{1,5},{2,6},{3,7},{4,0},{5,1},{6,2},{7,3},{8,12},{9,13},{10,... | collective-permute-start | bytes 1327112 | tf_op jit(solution)/shard_map/ppermute | solution.py:53
  203.2 23.3 %copy-start.2 = (bf16[384,2816]{1,0:T(8,128)(2,1)S(1)}, bf16[384,2816]{1,0:T(8,128)(2,1)}, u32[]{:S(2)}) copy-start(bf16[384,2816]{1,0:T(8,128)(2,1)} %get-tuple-element.133) | copy-start | bytes 6488068
  203.2 61.6 %collective-permute-start.37 = (bf16[192,2176]{1,0:T(8,128)(2,1)S(1)}, bf16[192,2176]{1,0:T(8,128)(2,1)S(1)}, u32[]{:S(2)}, u32[]{:S(2)}) collective-permute-start(bf16[192,2176]{1,0:T(8,128)(2,1)S(1)} %get-tuple-element.172), channel_id=1, source_target_pairs={{0,4},{1,5},{2,6},{3,7},{4,0},{5,1},{6,2},{7,3},{8,12},{9,13},{10,... | collective-permute-start | bytes 2506760 | tf_op jit(solution)/shard_map/ppermute | solution.py:53
  210.5 36.7 %collective-permute-start.23 = (bf16[96,1152]{1,0:T(8,128)(2,1)S(1)}, bf16[96,1152]{1,0:T(8,128)(2,1)S(1)}, u32[]{:S(2)}, u32[]{:S(2)}) collective-permute-start(bf16[96,1152]{1,0:T(8,128)(2,1)S(1)} %get-tuple-element.192), channel_id=1, source_target_pairs={{0,4},{1,5},{2,6},{3,7},{4,0},{5,1},{6,2},{7,3},{8,12},{9,13},{10,... | collective-permute-start | bytes 663560 | tf_op jit(solution)/shard_map/ppermute | solution.py:53
  225.1 23.5 %collective-permute-start.28 = (bf16[96,1152]{1,0:T(8,128)(2,1)S(1)}, bf16[96,1152]{1,0:T(8,128)(2,1)S(1)}, u32[]{:S(2)}, u32[]{:S(2)}) collective-permute-start(bf16[96,1152]{1,0:T(8,128)(2,1)S(1)} %get-tuple-element.190), channel_id=1, source_target_pairs={{0,2},{1,3},{2,0},{3,1},{4,6},{5,7},{6,4},{7,5},{8,10},{9,11},{10,... | collective-permute-start | bytes 663560 | tf_op jit(solution)/shard_map/ppermute | solution.py:53
  227.0 44.6 %collective-permute-start.32 = (bf16[192,2816]{1,0:T(8,128)(2,1)S(1)}, bf16[192,2816]{1,0:T(8,128)(2,1)S(1)}, u32[]{:S(2)}, u32[]{:S(2)}) collective-permute-start(bf16[192,2816]{1,0:T(8,128)(2,1)S(1)} %get-tuple-element.170), channel_id=1, source_target_pairs={{0,2},{1,3},{2,0},{3,1},{4,6},{5,7},{6,4},{7,5},{8,10},{9,11},{10,... | collective-permute-start | bytes 3244040 | tf_op jit(solution)/shard_map/ppermute | solution.py:53
  247.3 5.9 %collective-permute-start.24 = (bf16[48,1152]{1,0:T(8,128)(2,1)S(1)}, bf16[48,1152]{1,0:T(8,128)(2,1)S(1)}, u32[]{:S(2)}, u32[]{:S(2)}) collective-permute-start(bf16[48,1152]{1,0:T(8,128)(2,1)S(1)} %get-tuple-element.202), channel_id=1, source_target_pairs={{0,8},{1,9},{2,10},{3,11},{4,12},{5,13},{6,14},{7,15},{8,0},{9,1},... | collective-permute-start | bytes 331784 | tf_op jit(solution)/shard_map/ppermute | solution.py:53
  248.6 6.7 %collective-permute-start.29 = (bf16[48,1152]{1,0:T(8,128)(2,1)S(1)}, bf16[48,1152]{1,0:T(8,128)(2,1)S(1)}, u32[]{:S(2)}, u32[]{:S(2)}) collective-permute-start(bf16[48,1152]{1,0:T(8,128)(2,1)S(1)} %get-tuple-element.200), channel_id=1, source_target_pairs={{0,8},{1,9},{2,10},{3,11},{4,12},{5,13},{6,14},{7,15},{8,0},{9,1},... | collective-permute-start | bytes 331784 | tf_op jit(solution)/shard_map/ppermute | solution.py:53
  249.7 13.7 %collective-permute-start.43 = (bf16[256,768]{1,0:T(8,128)(2,1)S(1)}, bf16[256,768]{1,0:T(8,128)(2,1)S(1)}, u32[]{:S(2)}, u32[]{:S(2)}) collective-permute-start(bf16[256,768]{1,0:T(8,128)(2,1)S(1)} %get-tuple-element.184), channel_id=1, source_target_pairs={{0,2},{1,3},{2,0},{3,1},{4,6},{5,7},{6,4},{7,5},{8,10},{9,11},{10,... | collective-permute-start | bytes 1179656 | tf_op jit(solution)/shard_map/ppermute | solution.py:53
  253.2 6.3 %collective-permute-start.25 = (bf16[24,1152]{1,0:T(8,128)(2,1)S(1)}, bf16[24,1152]{1,0:T(8,128)(2,1)S(1)}, u32[]{:S(2)}, u32[]{:S(2)}) collective-permute-start(bf16[24,1152]{1,0:T(8,128)(2,1)S(1)} %add_convert_fusion.46), channel_id=1, source_target_pairs={{0,16},{1,17},{2,18},{3,19},{4,20},{5,21},{6,22},{7,23},{8,24},{9,... | collective-permute-start | bytes 165896 | tf_op jit(solution)/shard_map/ppermute | solution.py:53
  255.3 5.1 %collective-permute-start.30 = (bf16[24,1152]{1,0:T(8,128)(2,1)S(1)}, bf16[24,1152]{1,0:T(8,128)(2,1)S(1)}, u32[]{:S(2)}, u32[]{:S(2)}) collective-permute-start(bf16[24,1152]{1,0:T(8,128)(2,1)S(1)} %add_convert_fusion.44), channel_id=1, source_target_pairs={{0,16},{1,17},{2,18},{3,19},{4,20},{5,21},{6,22},{7,23},{8,24},{9,... | collective-permute-start | bytes 165896 | tf_op jit(solution)/shard_map/ppermute | solution.py:53
  263.5 5.7 %collective-permute-start.44 = (bf16[128,768]{1,0:T(8,128)(2,1)S(1)}, bf16[128,768]{1,0:T(8,128)(2,1)S(1)}, u32[]{:S(2)}, u32[]{:S(2)}) collective-permute-start(bf16[128,768]{1,0:T(8,128)(2,1)S(1)} %get-tuple-element.196), channel_id=1, source_target_pairs={{0,8},{1,9},{2,10},{3,11},{4,12},{5,13},{6,14},{7,15},{8,0},{9,1},... | collective-permute-start | bytes 589832 | tf_op jit(solution)/shard_map/ppermute | solution.py:53
  265.0 9.8 %collective-permute-start.38 = (bf16[96,2176]{1,0:T(8,128)(2,1)S(1)}, bf16[96,2176]{1,0:T(8,128)(2,1)S(1)}, u32[]{:S(2)}, u32[]{:S(2)}) collective-permute-start(bf16[96,2176]{1,0:T(8,128)(2,1)S(1)} %get-tuple-element.182), channel_id=1, source_target_pairs={{0,2},{1,3},{2,0},{3,1},{4,6},{5,7},{6,4},{7,5},{8,10},{9,11},{10,... | collective-permute-start | bytes 1253384 | tf_op jit(solution)/shard_map/ppermute | solution.py:53
  269.3 6.7 %collective-permute-start.45 = (bf16[64,768]{1,0:T(8,128)(2,1)S(1)}, bf16[64,768]{1,0:T(8,128)(2,1)S(1)}, u32[]{:S(2)}, u32[]{:S(2)}) collective-permute-start(bf16[64,768]{1,0:T(8,128)(2,1)S(1)} %add_convert_fusion.40), channel_id=1, source_target_pairs={{0,16},{1,17},{2,18},{3,19},{4,20},{5,21},{6,22},{7,23},{8,24},{9,... | collective-permute-start | bytes 294920 | tf_op jit(solution)/shard_map/ppermute | solution.py:53
  271.9 11.3 %collective-permute-start.33 = (bf16[96,2816]{1,0:T(8,128)(2,1)S(1)}, bf16[96,2816]{1,0:T(8,128)(2,1)S(1)}, u32[]{:S(2)}, u32[]{:S(2)}) collective-permute-start(bf16[96,2816]{1,0:T(8,128)(2,1)S(1)} %get-tuple-element.176), channel_id=1, source_target_pairs={{0,4},{1,5},{2,6},{3,7},{4,0},{5,1},{6,2},{7,3},{8,12},{9,13},{10,... | collective-permute-start | bytes 1622024 | tf_op jit(solution)/shard_map/ppermute | solution.py:53
  274.9 10.2 %collective-permute-start.39 = (bf16[48,2176]{1,0:T(8,128)(2,1)S(1)}, bf16[48,2176]{1,0:T(8,128)(2,1)S(1)}, u32[]{:S(2)}, u32[]{:S(2)}) collective-permute-start(bf16[48,2176]{1,0:T(8,128)(2,1)S(1)} %get-tuple-element.194), channel_id=1, source_target_pairs={{0,8},{1,9},{2,10},{3,11},{4,12},{5,13},{6,14},{7,15},{8,0},{9,1},... | collective-permute-start | bytes 626696 | tf_op jit(solution)/shard_map/ppermute | solution.py:53
  283.2 14.8 %copy-start.1 = (bf16[16,32,768]{2,1,0:T(8,128)(2,1)S(1)}, bf16[16,32,768]{2,1,0:T(8,128)(2,1)}, u32[]{:S(2)}) copy-start(bf16[16,32,768]{2,1,0:T(8,128)(2,1)} %param.18) | copy-start | bytes 2359300
  283.3 7.2 %collective-permute-start.34 = (bf16[48,2816]{1,0:T(8,128)(2,1)S(1)}, bf16[48,2816]{1,0:T(8,128)(2,1)S(1)}, u32[]{:S(2)}, u32[]{:S(2)}) collective-permute-start(bf16[48,2816]{1,0:T(8,128)(2,1)S(1)} %get-tuple-element.186), channel_id=1, source_target_pairs={{0,8},{1,9},{2,10},{3,11},{4,12},{5,13},{6,14},{7,15},{8,0},{9,1},... | collective-permute-start | bytes 811016 | tf_op jit(solution)/shard_map/ppermute | solution.py:53
  285.2 9.3 %collective-permute-start.40 = (bf16[24,2176]{1,0:T(8,128)(2,1)S(1)}, bf16[24,2176]{1,0:T(8,128)(2,1)S(1)}, u32[]{:S(2)}, u32[]{:S(2)}) collective-permute-start(bf16[24,2176]{1,0:T(8,128)(2,1)S(1)} %add_convert_fusion.38), channel_id=1, source_target_pairs={{0,16},{1,17},{2,18},{3,19},{4,20},{5,21},{6,22},{7,23},{8,24},{9,... | collective-permute-start | bytes 313352 | tf_op jit(solution)/shard_map/ppermute | solution.py:53
  290.6 6.0 %collective-permute-start.35 = (bf16[24,2816]{1,0:T(8,128)(2,1)S(1)}, bf16[24,2816]{1,0:T(8,128)(2,1)S(1)}, u32[]{:S(2)}, u32[]{:S(2)}) collective-permute-start(bf16[24,2816]{1,0:T(8,128)(2,1)S(1)} %add_convert_fusion.30), channel_id=1, source_target_pairs={{0,16},{1,17},{2,18},{3,19},{4,20},{5,21},{6,22},{7,23},{8,24},{9,... | collective-permute-start | bytes 405512 | tf_op jit(solution)/shard_map/ppermute | solution.py:53
  (3 other events, 2.0 us)

commit v3 on v2

v3 whole, which is shorter than its diff:
```python
import functools

import jax
import jax.numpy as jnp
from jax import lax
from jax.experimental import pallas as pl
from jax.experimental.pallas import tpu as pltpu
from jax.sharding import PartitionSpec as P

BUCKETS = 32
LANES = 128
CHUNK = 512

epsilon = 1e-06
contrastive_sharpness_factor = 0.01
masked_value = -1000000000.0
bucket_edges = (12, 16, 23, 32, 46, 64, 91)
highest = lax.Precision.HIGHEST
f32 = jnp.float32
bf16 = jnp.bfloat16


def bucket_index(offset):
    distance = jnp.abs(offset)
    beyond = 8 + sum(((distance >= boundary).astype(jnp.int32) for boundary in bucket_edges))
    inside = jnp.where(distance < 8, distance, beyond)
    return inside + BUCKETS // 2 * (offset > 0).astype(jnp.int32)


def product(left, right):
    return jnp.dot(left, right, preferred_element_type=f32)


def left_product(left, right):
    return lax.dot_general(left, right, (((0,), (0,)), ((), ())), preferred_element_type=f32)


def right_product(left, right):
    return lax.dot_general(left, right, (((1,), (1,)), ((), ())), preferred_element_type=f32)


def rank_bits():
    return (lax.axis_size("wide") * lax.axis_size("narrow")).bit_length() - 1


def my_rank():
    return lax.axis_index("wide") * lax.axis_size("narrow") + lax.axis_index("narrow")


def swap(values, mask):
    ranks = 1 << rank_bits()
    pairs = [(rank, rank ^ mask) for rank in range(ranks)]
    return lax.ppermute(values, ("wide", "narrow"), pairs)


def scatter_order(position, order):
    count = len(order)
    return sum(((position >> (count - 1 - step)) & 1) << bit for step, bit in enumerate(order))


def gather_order(position, order):
    return sum(((position >> step) & 1) << bit for step, bit in enumerate(order))


def after(values, *others):
    flat, tree = jax.tree.flatten(values)
    done = lax.optimization_barrier(tuple(flat) + tuple(others))
    return jax.tree.unflatten(tree, done[: len(flat)])


def add(*values):
    total = values[0].astype(f32)
    for value in values[1:]:
        total = total + value.astype(f32)
    return total


def cut_kernel(kept_ref, came_ref, kept_out, sent_out):
    half = kept_out.shape[0]
    kept_out[...] = add(kept_ref[:half, :], came_ref[:half, :]).astype(bf16)
    sent_out[...] = add(kept_ref[half:, :], came_ref[half:, :]).astype(bf16)


def cut(kept, came):
    half = kept.shape[0] // 2
    if half % 16 == 0:
        return call(cut_kernel, [shape((half, kept.shape[1]), bf16)] * 2, [kept, came])
    return add(kept[:half], came[:half]).astype(bf16), add(kept[half:], came[half:]).astype(bf16)


def call(kernel, outs, args, spaces="", scratch=(), flops=0):
    kinds = {"s": pltpu.SMEM, "v": pltpu.VMEM, "a": pl.ANY}
    spaces = spaces.ljust(len(args) + len(outs), "v")
    specs = [pl.BlockSpec(memory_space=kinds[kind]) for kind in spaces]
    return pl.pallas_call(
        kernel,
        out_shape=tuple(outs),
        in_specs=specs[: len(args)],
        out_specs=tuple(specs[len(args) :]),
        scratch_shapes=list(scratch),
        compiler_params=pltpu.CompilerParams(vmem_limit_bytes=60 * 1024 * 1024),
        cost_estimate=pl.CostEstimate(flops=flops, bytes_accessed=0, transcendentals=0),
    )(*args)


def shape(dims, kind=f32):
    return jax.ShapeDtypeStruct(tuple(dims), kind)


def room(values):
    return pltpu.VMEM(values.shape, values.dtype)


def loads(refs, rooms, sems):
    return [pltpu.make_async_copy(ref, place, sems.at[i]) for i, (ref, place) in enumerate(zip(refs, rooms))]


def bias_kernel(doc_length, rank_ref, table_ref, doc_bias_ref, slot_bias_ref, line_ref):
    pairs = doc_bias_ref.shape[0]
    parts = doc_length // LANES
    length = line_ref.shape[1]
    offset = lax.broadcasted_iota(jnp.int32, (BUCKETS, length), 1) - doc_length
    hot = (bucket_index(offset) == lax.broadcasted_iota(jnp.int32, (BUCKETS, length), 0)).astype(f32)
    line_ref[...] = lax.dot_general(
        table_ref[...], hot, (((0,), (0,)), ((), ())), precision=highest, preferred_element_type=f32
    )
    narrow = rank_ref[0] & (parts - 1)

    def spread(head, start):
        line = line_ref[pl.ds(head, 1), pl.ds(pl.multiple_of(start, LANES), 2 * LANES)]
        rolled = pltpu.roll(jnp.broadcast_to(line, (LANES, 2 * LANES)), 0, 1, stride=1, stride_axis=0)
        return rolled[:, LANES:]

    def one_pair(pair, carry):
        for side in range(2):
            rows = slice(side * LANES, (side + 1) * LANES)
            head = 2 * pair + side
            for part in range(parts):
                distance = (narrow ^ part) - narrow
                doc_bias_ref[pair, rows, part * LANES : (part + 1) * LANES] = spread(
                    head, doc_length - LANES + distance * LANES
                )
            slot_bias_ref[pair, rows, :] = spread(head, doc_length - LANES)
        return carry

    lax.fori_loop(0, pairs, one_pair, 0)


def count_kernel(doc_length, doc_total, rank_ref, picked_ref, counts_ref, tally_ref, load_ref, places_ref, scratch_ref, sem):
    slots, slot_length, picks = load_ref.shape
    rows = slots * slot_length
    blocks = counts_ref.shape[0]
    narrow_size = picked_ref.shape[0] // slots
    first = (rank_ref[0] & (narrow_size - 1)) * slots
    load = pltpu.make_async_copy(picked_ref.at[pl.ds(first, slots)], load_ref, sem)
    load.start()
    load.wait()

    places_ref[...] = load_ref[...].reshape(rows, picks)

    def one_row(row, carry):
        places = places_ref[pl.ds(row, 1), :]
        high = places >> 7
        low = places & 127
        high_hot = (lax.broadcasted_iota(jnp.int32, (blocks, picks), 0) == high).astype(bf16)
        low_hot = (lax.broadcasted_iota(jnp.int32, (LANES, picks), 0) == low).astype(bf16)
        scratch_ref[pl.ds(row, blocks, stride=rows), :] = right_product(high_hot, low_hot)
        return carry

    lax.fori_loop(0, rows, one_row, 0, unroll=8)

    def one_block(block, carry):
        start = pl.multiple_of(block * rows, rows)
        counts_ref[block] = scratch_ref[pl.ds(start, rows), :].astype(bf16)
        return carry

    lax.fori_loop(0, blocks, one_block, 0, unroll=4)

    owner = places_ref[...] // doc_length
    lane = lax.broadcasted_iota(jnp.int32, (rows, LANES), 1)
    tally = jnp.zeros((rows, LANES), f32)
    for doc in range(doc_total):
        number = jnp.sum((owner == doc).astype(f32), 1, keepdims=True)
        tally = jnp.where(lane == doc, number, tally)
    tally_ref[...] = tally


def rms_scale(values):
    return lax.rsqrt(jnp.mean(values * values, -1, keepdims=True) + epsilon)


def rms_back(values, gain, grad):
    scale = rms_scale(values)
    weighted = grad * gain
    inner = jnp.mean(weighted * values, -1, keepdims=True)
    return scale * weighted - values * (scale * scale * scale * inner)


def tile(index, size=LANES):
    return pl.ds(pl.multiple_of(index * size, size), size)


def halves(values, zero_row):
    return jnp.concatenate([jnp.where(zero_row, values, jnp.zeros((), values.dtype)),
                            jnp.where(zero_row, jnp.zeros((), values.dtype), values)], 0)


def joined(values, first_lanes):
    rows = values.shape[0] // 2
    return jnp.where(first_lanes, values[:rows], values[rows:])


def forward_kernel(
    slots, slot_length, rank_ref, lengths_ref, queries_ref, own_ref, near_ref, far_ref, last_ref, doc_bias_ref,
    slot_bias_ref, attend_gain_ref, feed_gain_ref, final_gain_ref,
    wq_any, wk_any, wv_any, wo_any, wg_any, wu_any, wd_any, wp_any,
    all_any, query_any, key_any, value_any, doc_probs_any, slot_probs_any, mixed_any, after_attend_any,
    normed_feed_any, hidden_any, gate_slope_any, up_slope_any, after_feed_any, normed_final_any, embed_any,
    slot_unit_any, doc_unit_any,
    all_ref, query_ref, key_ref, value_ref, doc_probs_ref, slot_probs_ref, mixed_ref, after_attend_ref,
    normed_feed_ref, hidden_ref, gate_slope_ref, up_slope_ref, after_feed_ref, normed_final_ref, embed_ref,
    slot_unit_ref, doc_unit_ref,
    wq_ref, wk_ref, wv_ref, wo_ref, wg_ref, wu_ref, wd_ref, wp_ref, slot_ref, load_sems, store_sems, slot_sem,
):
    slot_rows = slots * slot_length
    rows, width = query_ref.shape
    pairs = doc_probs_ref.shape[0]
    half = LANES // 2
    narrow_size = queries_ref.shape[0] // slots
    first = (rank_ref[0] & (narrow_size - 1)) * slots
    load_slots = pltpu.make_async_copy(queries_ref.at[pl.ds(first, slots)], slot_ref, slot_sem)
    load_slots.start()
    weights = loads(
        (wq_any, wk_any, wv_any, wo_any, wg_any, wu_any, wd_any, wp_any),
        (wq_ref, wk_ref, wv_ref, wo_ref, wg_ref, wu_ref, wd_ref, wp_ref),
        load_sems,
    )
    stores = loads(
        (all_ref, query_ref, key_ref, value_ref, doc_probs_ref, slot_probs_ref, mixed_ref, after_attend_ref,
         normed_feed_ref, hidden_ref, gate_slope_ref, up_slope_ref, after_feed_ref, normed_final_ref, embed_ref,
         slot_unit_ref, doc_unit_ref),
        (all_any, query_any, key_any, value_any, doc_probs_any, slot_probs_any, mixed_any, after_attend_any,
         normed_feed_any, hidden_any, gate_slope_any, up_slope_any, after_feed_any, normed_final_any, embed_any,
         slot_unit_any, doc_unit_any),
        store_sems,
    )
    for weight in weights[:3]:
        weight.start()
    gain = attend_gain_ref[...].reshape(1, width)
    place = slot_rows
    for ref in (own_ref, near_ref, far_ref, last_ref):
        tokens = ref[...].astype(f32)
        all_ref[place : place + ref.shape[0], :] = (tokens * rms_scale(tokens) * gain).astype(bf16)
        place += ref.shape[0]
    load_slots.wait()
    slot_tokens = slot_ref[...].reshape(slot_rows, width).astype(f32)
    all_ref[:slot_rows, :] = (slot_tokens * rms_scale(slot_tokens) * gain).astype(bf16)
    normed = all_ref[:rows, :]
    stores[0].start()
    weights[0].wait()
    for weight in weights[3:]:
        weight.start()
    query_ref[...] = product(normed, wq_ref[...]).astype(bf16)
    stores[1].start()
    weights[1].wait()
    key_ref[...] = product(all_ref[...], wk_ref[...]).astype(bf16)
    stores[2].start()
    weights[2].wait()
    value_ref[...] = product(all_ref[...], wv_ref[...]).astype(bf16)
    stores[3].start()

    lane = lax.broadcasted_iota(jnp.int32, (slot_rows, LANES), 1)
    row = lax.broadcasted_iota(jnp.int32, (slot_rows, slot_rows), 0)
    col = lax.broadcasted_iota(jnp.int32, (slot_rows, slot_rows), 1)
    slot_keep = row < 0
    for slot in range(slots):
        start = slot * slot_length
        inside = (row >= start) & (row < start + slot_length) & (col >= start)
        slot_keep = slot_keep | (inside & (col < start + lengths_ref[first + slot]))

    def softmax(scores):
        weights = jnp.exp(scores - jnp.max(scores, -1, keepdims=True))
        return (weights * (1.0 / jnp.sum(weights, -1, keepdims=True))).astype(bf16)

    first_lanes = lane < half
    pair_keep = jnp.concatenate([slot_keep, slot_keep], 0)

    def one_pair(pair, carry):
        lanes = tile(pair)
        slot_query = halves(query_ref[:slot_rows, lanes], first_lanes)
        scores = right_product(slot_query, key_ref[:slot_rows, lanes]) + slot_bias_ref[pair]
        probs = softmax(jnp.where(pair_keep, scores, masked_value))
        slot_probs_ref[pair] = probs
        slot_mixed = product(probs, value_ref[:slot_rows, lanes])
        mixed_ref[:slot_rows, lanes] = joined(slot_mixed, first_lanes).astype(bf16)
        doc_query = halves(query_ref[slot_rows:, lanes], first_lanes)
        scores = right_product(doc_query, key_ref[slot_rows:, lanes]) + doc_bias_ref[pair]
        probs = softmax(scores)
        doc_probs_ref[pair] = probs
        doc_mixed = product(probs, value_ref[slot_rows:, lanes])
        mixed_ref[slot_rows:, lanes] = joined(doc_mixed, first_lanes).astype(bf16)
        return carry

    lax.fori_loop(0, pairs, one_pair, 0)
    for store in stores[4:7]:
        store.start()

    weights[3].wait()
    attended = product(mixed_ref[...], wo_ref[...])
    after_attend_ref[:slot_rows, :] = slot_ref[...].reshape(slot_rows, width).astype(f32) + attended[:slot_rows]
    after_attend_ref[slot_rows:, :] = own_ref[...].astype(f32) + attended[slot_rows:]
    stores[7].start()
    after_attend = after_attend_ref[...]
    feed_gain = feed_gain_ref[...].reshape(1, width)
    normed_feed_ref[...] = (after_attend * rms_scale(after_attend) * feed_gain).astype(bf16)
    stores[8].start()
    weights[4].wait()
    weights[5].wait()

    def one_part(step, carry):
        part = tile(step, CHUNK)
        gate = product(normed_feed_ref[...], wg_ref[:, part])
        upward = product(normed_feed_ref[...], wu_ref[:, part])
        factor = 0.7978845608028654
        square = gate * gate
        bent = jnp.tanh(factor * gate * (1.0 + 0.044715 * square))
        curve = 0.5 * gate * (1.0 + bent)
        slope = 0.5 * (1.0 + bent) + 0.5 * factor * gate * (1.0 - bent * bent) * (1.0 + 3 * 0.044715 * square)
        hidden_ref[:, part] = (curve * upward).astype(bf16)
        gate_slope_ref[:, part] = (upward * slope).astype(bf16)
        up_slope_ref[:, part] = curve.astype(bf16)
        return carry

    lax.fori_loop(0, hidden_ref.shape[1] // CHUNK, one_part, 0)
    for store in stores[9:12]:
        store.start()
    weights[6].wait()
    after_feed = after_attend_ref[...] + product(hidden_ref[...], wd_ref[...])
    after_feed_ref[...] = after_feed
    stores[12].start()
    final_gain = final_gain_ref[...].reshape(1, width)
    normed_final = (after_feed * rms_scale(after_feed) * final_gain).astype(bf16)
    normed_final_ref[...] = normed_final
    stores[13].start()
    weights[7].wait()
    embed = product(normed_final, wp_ref[...])
    embed_ref[...] = embed
    unit = (embed * lax.rsqrt(jnp.sum(embed * embed, -1, keepdims=True) + epsilon)).astype(bf16)
    slot_unit_ref[...] = unit[:slot_rows]
    doc_unit_ref[...] = unit[slot_rows:]
    for store in stores[14:]:
        store.start()
    for store in stores:
        store.wait()


def loss_kernel(
    order, gathered, doc_total, slots, rank_ref, lengths_ref, positives_ref, counts_ref, near_ref, far_ref, unit_ref,
    tally_ref, losses_ref, grad_ref, kept_ref, sent_ref, sum_ref, scaled_ref,
):
    rows = unit_ref.shape[0]
    blocks = counts_ref.shape[0]
    per_doc = blocks // doc_total
    rank = rank_ref[0]
    half = blocks // 2
    sum_ref[...] = jnp.zeros_like(sum_ref)

    def gather_step(place, carry):
        near = rank ^ gather_order(place, gathered)
        far = near ^ (1 << gathered[-1])
        sum_ref[near // per_doc] += product(counts_ref[near], near_ref[place])
        sum_ref[far // per_doc] += product(counts_ref[far], far_ref[place])
        return carry

    lax.fori_loop(0, half, gather_step, 0, unroll=4)

    unit = unit_ref[...].astype(f32)
    lane = lax.broadcasted_iota(jnp.int32, (rows, LANES), 1)
    summed = jnp.zeros((rows, LANES), f32)
    for doc in range(doc_total):
        number = jnp.sum(sum_ref[doc] * unit, 1, keepdims=True)
        summed = jnp.where(lane == doc, number, summed)
    tally = tally_ref[...]
    most = jnp.maximum(tally, 1.0)
    slot_length = rows // slots
    narrow_size = lengths_ref.shape[0] // slots
    first = (rank & (narrow_size - 1)) * slots
    row = lax.broadcasted_iota(jnp.int32, (rows, LANES), 0)
    slot_row = lax.broadcasted_iota(jnp.int32, (slots, LANES), 0)
    valid = row < 0
    positive = jnp.zeros((slots, LANES), jnp.int32)
    for slot in range(slots):
        start = slot * slot_length
        valid = valid | ((row >= start) & (row < start + lengths_ref[first + slot]))
        positive = jnp.where(slot_row == slot, positives_ref[first + slot], positive)
    weight = jnp.where(valid, jnp.minimum(tally, 1.0), 0.0)
    pooled = (weight * (summed / most)).reshape(slots, slot_length, LANES)
    weight_sum = jnp.maximum(jnp.sum(weight.reshape(slots, slot_length, LANES), 1), 1.0)
    scores = jnp.sum(pooled, 1) / weight_sum / contrastive_sharpness_factor
    slot_lane = lax.broadcasted_iota(jnp.int32, (slots, LANES), 1)
    inside = slot_lane < doc_total
    scores = jnp.where(inside, scores, -jnp.inf)
    top = jnp.max(scores, -1, keepdims=True)
    powers = jnp.exp(scores - top)
    total = jnp.sum(powers, -1, keepdims=True)
    chosen = (slot_lane == positive).astype(f32)
    picked = jnp.sum(jnp.where(slot_lane == positive, scores, 0.0), -1, keepdims=True)
    losses_ref[...] = jnp.broadcast_to(top + jnp.log(total) - picked, (slots, LANES))
    slope = (powers / total - chosen) / contrastive_sharpness_factor / weight_sum
    slope = jnp.where(inside, slope, 0.0)
    slope = jnp.broadcast_to(slope[:, None, :], (slots, slot_length, LANES)).reshape(rows, LANES)
    slope = slope * weight / most

    grad = jnp.zeros((rows, unit.shape[1]), f32)
    for doc in range(doc_total):
        column = jnp.sum(jnp.where(lane == doc, slope, 0.0), 1, keepdims=True)
        grad = grad + column * sum_ref[doc]
        scaled_ref[doc] = (column * unit).T.astype(bf16)
    grad_ref[...] = grad

    def scatter_step(place, carry):
        kept = rank ^ scatter_order(place, order)
        sent = kept ^ (1 << order[0])
        kept_ref[place] = product(scaled_ref[kept // per_doc], counts_ref[kept]).astype(bf16)
        sent_ref[place] = product(scaled_ref[sent // per_doc], counts_ref[sent]).astype(bf16)
        return carry

    lax.fori_loop(0, half, scatter_step, 0, unroll=4)


def feed_back(
    part, waits, grad_unit, embed_ref, after_feed_ref, after_attend_ref, gate_slope_ref, up_slope_ref, feed_gain_ref,
    final_gain_ref, wo_ref, wg_ref, wu_ref, wd_ref, wp_ref, grads_out, after_out, mixed_out, more_ref,
):
    units, width = wd_ref.shape
    up_start, feed_start = units, 2 * units
    attend_start, embed_start = 2 * units + width, 2 * units + 2 * width
    embed = embed_ref[part, :]
    scale = lax.rsqrt(jnp.sum(embed * embed, -1, keepdims=True) + epsilon)
    inner = jnp.sum(grad_unit * embed, -1, keepdims=True)
    grad_embed = (scale * grad_unit - embed * (scale * scale * scale * inner)).astype(bf16)
    grads_out[:, embed_start : embed_start + embed.shape[1]] = grad_embed
    waits[0].wait()
    grad_after_feed = rms_back(
        after_feed_ref[part, :], final_gain_ref[...].reshape(1, -1), right_product(grad_embed, wp_ref[...])
    )
    after_out[...] = grad_after_feed
    grad_feed = grad_after_feed.astype(bf16)
    grads_out[:, feed_start:attend_start] = grad_feed
    for wait in waits[1:4]:
        wait.wait()

    def one_part(step, total):
        cols = tile(step, CHUNK)
        grad_hidden = right_product(grads_out[:, feed_start:attend_start], wd_ref[cols, :])
        grad_gate = (grad_hidden * gate_slope_ref[part, cols].astype(f32)).astype(bf16)
        grad_up = (grad_hidden * up_slope_ref[part, cols].astype(f32)).astype(bf16)
        grads_out[:, cols] = grad_gate
        grads_out[:, pl.ds(pl.multiple_of(up_start + step * CHUNK, CHUNK), CHUNK)] = grad_up
        more_ref[...] += right_product(grad_gate, wg_ref[:, cols]) + right_product(grad_up, wu_ref[:, cols])
        return total

    more_ref[...] = jnp.zeros_like(more_ref)
    lax.fori_loop(0, units // CHUNK, one_part, 0)
    total = more_ref[...]
    more = rms_back(after_attend_ref[part, :], feed_gain_ref[...].reshape(1, -1), total)
    grad_after_attend = after_out[...] + more
    after_out[...] = grad_after_attend
    grad_attend = grad_after_attend.astype(bf16)
    grads_out[:, attend_start:embed_start] = grad_attend
    waits[4].wait()
    mixed_out[...] = right_product(grad_attend, wo_ref[...]).astype(bf16)


def attend_back(
    far_parts, queries, keys, query_ref, key_ref, value_ref, probs_ref, mixed_ref, query_out, key_out, value_out,
    sums_out,
):
    rows = mixed_ref.shape[0]
    length = probs_ref.shape[2]
    half = LANES // 2
    first_lanes = lax.broadcasted_iota(jnp.int32, (rows, LANES), 1) < half
    row = lax.broadcasted_iota(jnp.int32, (rows, rows), 0)
    col = lax.broadcasted_iota(jnp.int32, (rows, rows), 1)
    flip = (row + col == rows - 1).astype(bf16)
    nothing = jnp.zeros((rows, LANES), f32)

    def one_pair(pair, carry):
        lanes = tile(pair)
        grad_mixed = halves(mixed_ref[:, lanes], first_lanes)
        query = halves(query_ref[queries, lanes], first_lanes)
        probs = probs_ref[pair]
        grad_probs = right_product(grad_mixed, value_ref[keys, lanes])
        exact = probs.astype(f32)
        inner = jnp.sum(exact * grad_probs, -1, keepdims=True)
        grad_scores = (exact * (grad_probs - inner)).astype(bf16)
        query_out(joined(product(grad_scores, key_ref[keys, lanes]), first_lanes).astype(bf16), pair)
        key_out(left_product(grad_scores, query).astype(bf16), pair)
        value_out(left_product(probs, grad_mixed).astype(bf16), pair)
        for side in range(2):
            head = 2 * pair + side
            own = grad_scores[side * rows : (side + 1) * rows, :]
            for part in range(length // LANES):
                piece = own[:, part * LANES : (part + 1) * LANES]
                if part in far_parts:
                    line = jnp.concatenate([piece.astype(f32), nothing], 1)
                else:
                    line = pltpu.roll(
                        jnp.concatenate([product(flip, piece), nothing], 1), 0, 1, stride=1, stride_axis=0
                    )
                sums_out[tile(head, 8), part * 2 * LANES : (part + 1) * 2 * LANES] = jnp.sum(
                    line.reshape(rows // 8, 8, 2 * LANES), 0
                )
        return carry

    lax.fori_loop(0, probs_ref.shape[0], one_pair, 0)


def input_back(tokens, gain_ref, after_ref, query, key, value, wq_ref, wk_ref, wv_ref):
    grad_normed = right_product(query, wq_ref[...])
    grad_normed = grad_normed + right_product(key, wk_ref[...])
    grad_normed = grad_normed + right_product(value, wv_ref[...])
    return after_ref[...] + rms_back(tokens, gain_ref[...].reshape(1, -1), grad_normed)


def table_sums(sums_ref, distances):
    heads = sums_ref.shape[0] // 8
    span = lax.broadcasted_iota(jnp.int32, (2 * LANES, LANES), 0) - (LANES - 1)
    bucket = lax.broadcasted_iota(jnp.int32, (2 * LANES, LANES), 1)
    total = jnp.zeros((heads, LANES), f32)
    for part, distance in enumerate(distances):
        lines = jnp.sum(sums_ref[:, part * 2 * LANES : (part + 1) * 2 * LANES].reshape(heads, 8, 2 * LANES), 1)
        hot = (bucket_index(span + distance * LANES) == bucket).astype(f32)
        total = total + lax.dot_general(
            lines, hot, (((1,), (0,)), ((), ())), precision=highest, preferred_element_type=f32
        )
    return total


def slot_back_kernel(
    slots, rank_ref, queries_ref, grad_unit_ref, embed_ref, after_feed_ref, after_attend_ref, gate_slope_ref,
    up_slope_ref, query_ref, key_ref, value_ref, probs_ref, attend_gain_ref, feed_gain_ref, final_gain_ref,
    wp_any, wd_any, wg_any, wu_any, wo_any, wq_any, wk_any, wv_any,
    grads_out, tokens_out, table_out,
    wp_ref, wd_ref, wg_ref, wu_ref, wo_ref, wq_ref, wk_ref, wv_ref, slot_ref, after_ref, mixed_ref, more_ref, sums_ref,
    load_sems, slot_sem,
):
    weights = loads(
        (wp_any, wd_any, wg_any, wu_any, wo_any, wq_any, wk_any, wv_any),
        (wp_ref, wd_ref, wg_ref, wu_ref, wo_ref, wq_ref, wk_ref, wv_ref),
        load_sems,
    )
    for weight in weights:
        weight.start()
    narrow_size = queries_ref.shape[0] // slots
    first = (rank_ref[0] & (narrow_size - 1)) * slots
    load_slots = pltpu.make_async_copy(queries_ref.at[pl.ds(first, slots)], slot_ref, slot_sem)
    load_slots.start()
    rows, width = after_ref.shape
    part = slice(0, rows)
    feed_back(
        part, weights[:5], grad_unit_ref[...], embed_ref, after_feed_ref, after_attend_ref, gate_slope_ref,
        up_slope_ref, feed_gain_ref, final_gain_ref, wo_ref, wg_ref, wu_ref, wd_ref, wp_ref, grads_out, after_ref,
        mixed_ref, more_ref,
    )
    start = grads_out.shape[1] - 3 * width

    def third(place):
        return grads_out.at[:, start + place * width : start + (place + 1) * width]

    def out(place):
        def store(values, pair):
            grads_out[:, pl.ds(pl.multiple_of(start + place * width + pair * LANES, LANES), LANES)] = values

        return store

    attend_back(
        (), part, part, query_ref, key_ref, value_ref, probs_ref, mixed_ref, out(0), out(1), out(2), sums_ref
    )
    table_out[...] = table_sums(sums_ref, [0])
    for weight in weights[5:]:
        weight.wait()
    load_slots.wait()
    tokens_out[...] = input_back(
        slot_ref[...].reshape(rows, width).astype(f32), attend_gain_ref, after_ref, third(0)[...], third(1)[...],
        third(2)[...], wq_ref, wk_ref, wv_ref,
    )


def doc_feed_kernel(came, *refs):
    parts, refs = refs[:came], refs[came:]
    (
        embed_ref, after_feed_ref, after_attend_ref, gate_slope_ref, up_slope_ref, feed_gain_ref, final_gain_ref,
        wp_any, wd_any, wg_any, wu_any, wo_any,
        grads_out, after_out, mixed_out,
        wp_ref, wd_ref, wg_ref, wu_ref, wo_ref, more_ref, load_sems,
    ) = refs
    weights = loads(
        (wp_any, wd_any, wg_any, wu_any, wo_any), (wp_ref, wd_ref, wg_ref, wu_ref, wo_ref), load_sems
    )
    for weight in weights:
        weight.start()
    rows = after_out.shape[0]
    grad_unit = add(*(part[0] for part in parts)).T
    feed_back(
        slice(embed_ref.shape[0] - rows, embed_ref.shape[0]), weights, grad_unit, embed_ref, after_feed_ref,
        after_attend_ref, gate_slope_ref, up_slope_ref, feed_gain_ref, final_gain_ref, wo_ref, wg_ref, wu_ref, wd_ref,
        wp_ref, grads_out, after_out, mixed_out, more_ref,
    )


def doc_attend_kernel(
    rank_ref, query_ref, key_ref, value_ref, probs_ref, mixed_ref, slot_table_ref, grads_out, table_out, query_room,
    sums_ref,
):
    rows, width = query_room.shape
    length = probs_ref.shape[2]
    first = key_ref.shape[0] - length

    def query_out(values, pair):
        query_room[:, tile(pair)] = values

    def key_out(values, pair):
        grads_out[:length, tile(pair)] = values

    def value_out(values, pair):
        grads_out[:length, pl.ds(pl.multiple_of(width + pair * LANES, LANES), LANES)] = values

    attend_back(
        (2,), slice(first, first + rows), slice(first, key_ref.shape[0]), query_ref, key_ref, value_ref, probs_ref,
        mixed_ref, query_out, key_out, value_out, sums_ref,
    )
    grads_out[length:, :width] = query_room[: rows // 2, :]
    grads_out[length:, width:] = query_room[rows // 2 :, :]
    parts = length // LANES
    narrow = rank_ref[0] & (parts - 1)
    table = table_sums(sums_ref, [(narrow ^ part) - narrow for part in range(parts)]) + slot_table_ref[...]
    heads = table.shape[0]
    table_out[...] = jnp.concatenate([table, jnp.zeros((16 - heads, LANES), f32)], 0).astype(bf16)


def pick_columns(values, total, order, flipped, rank):
    count = 1 << len(order) + 1
    size = total // count
    row = lax.broadcasted_iota(jnp.int32, (total, total // 2), 0)
    col = lax.broadcasted_iota(jnp.int32, (total, total // 2), 1)
    source = (scatter_order(col // size, order) ^ rank ^ flipped) * size + col % size
    return product(values, (row == source).astype(bf16)).astype(bf16)


def pick_tiles(values_ref, order, flipped, rank, store):
    rows = values_ref.shape[0]
    half = LANES // 2
    first_lanes = lax.broadcasted_iota(jnp.int32, (rows, LANES), 1) < half
    upper = ((rank ^ flipped) & 1) == 1

    def one_tile(step, carry):
        place = 2 * step
        sides = []
        for side in range(2):
            tile = (rank ^ scatter_order(place + side, order)) >> 1
            values = values_ref[:, pl.ds(pl.multiple_of(tile * LANES, LANES), LANES)].astype(f32)
            turned = pltpu.roll(values, half, 1)
            sides.append(jnp.where(upper, turned, values) if side == 0 else jnp.where(upper, values, turned))
        store(step, jnp.where(first_lanes, sides[0], sides[1]).astype(bf16))
        return carry

    lax.fori_loop(0, 1 << len(order) - 1, one_tile, 0)


def turn_kernel(
    orders, rank_ref, all_ref, normed_feed_ref, mixed_ref, normed_final_ref, hidden_ref, kept_out, sent_out, doc_out,
):
    first, second, third, fourth = orders
    rank = rank_ref[0]
    rows, width = normed_feed_ref.shape
    units = hidden_ref.shape[1]
    slots = all_ref.shape[0] - doc_out.shape[0]
    half = width // 2
    for out, flipped in ((kept_out, 0), (sent_out, 1)):
        out[:, :half] = pick_columns(normed_feed_ref[...], width, first, flipped, rank)
        out[:, half : 2 * half] = pick_columns(normed_feed_ref[...], width, second, flipped, rank)
        out[:, 2 * half : 3 * half] = pick_columns(mixed_ref[...], width, first, flipped, rank)
        out[:, 3 * half : 4 * half] = pick_columns(normed_final_ref[...], width, second, flipped, rank)
        start = 4 * half
        if units >> (len(third) + 1) == LANES // 2:

            def store(place, values):
                out[:, pl.ds(pl.multiple_of(start + place * LANES, LANES), LANES)] = values

            pick_tiles(hidden_ref, third, flipped, rank, store)
        else:
            out[:, start : start + units // 2] = pick_columns(hidden_ref[...], units, third, flipped, rank)
        start = start + units // 2
        out[slots:, start:] = jnp.zeros((rows - slots, half), bf16)
        if flipped:
            out[:slots, start:] = pick_columns(all_ref[:slots, :], width, fourth, flipped, rank)
        else:
            both = pick_columns(all_ref[...], width, fourth, flipped, rank)
            out[:slots, start:] = both[:slots]
            doc_out[...] = both[slots:]


def store_product(left, right_ref, columns, kept_ref, sent_ref, start):
    half = left.shape[1] // 2
    size = 2 * LANES

    def one_part(first, size):
        here = pl.ds(pl.multiple_of(start + first, LANES), size)
        result = left_product(left, right_ref[:, pl.ds(pl.multiple_of(first, LANES), size)]).astype(bf16)
        kept_ref[:half, here] = result[:half]
        sent_ref[:half, here] = result[half:]

    def step(place, carry):
        one_part(place * size, size)
        return carry

    lax.fori_loop(0, columns // size, step, 0)
    if columns % size:
        one_part(columns // size * size, columns % size)


def weight_kernel(
    terms, kept_any, came_any, slot_any, slot_came_any, doc_any, doc_came_any, kept_ref, sent_ref, left_ref, right_ref,
    sems,
):
    rows = kept_any.shape[0]
    part = slot_any.shape[0]
    copies = []
    left_place, right_place = 0, 0
    for left_start, left_width, right_start, right_width in terms:
        pieces = []
        for place, ref in enumerate((kept_any, came_any)):
            source = ref.at[:, left_start : left_start + left_width]
            target = left_ref.at[place * rows : (place + 1) * rows, left_place : left_place + left_width]
            pieces.append((source, target))
        for place, ref in enumerate((slot_any, doc_any, slot_came_any, doc_came_any)):
            source = ref.at[:, right_start : right_start + right_width]
            target = right_ref.at[place * part : (place + 1) * part, right_place : right_place + right_width]
            pieces.append((source, target))
        first = sum(len(group) for group in copies)
        copies.append(
            [pltpu.make_async_copy(one, two, sems.at[first + i]) for i, (one, two) in enumerate(pieces)]
        )
        left_place += left_width
        right_place += right_width
    for group in copies:
        for copy in group:
            copy.start()
    left_place, right_place = 0, 0
    for group, (_, left_width, _, right_width) in zip(copies, terms):
        for copy in group:
            copy.wait()
        left = left_ref[:, left_place : left_place + left_width]
        right = right_ref.at[:, right_place : right_place + right_width]
        store_product(left, right, right_width, kept_ref, sent_ref, right_place)
        left_place += left_width
        right_place += right_width


def attend_weight_kernel(
    doc_ref, kept_any, came_any, slot_any, slot_came_any, grads_ref, other_ref, table_ref, other_table_ref,
    kept_out, sent_out, pair_kept, pair_sent, slot_room, slot_came_room, left_ref, right_ref, query_ref, sems,
):
    rows = slot_any.shape[0]
    width = slot_room.shape[1] // 3
    half = doc_ref.shape[1]
    length = doc_ref.shape[0]
    start = slot_any.shape[1] - 3 * width
    lanes = slice(kept_any.shape[1] - half, kept_any.shape[1])
    copies = loads(
        (slot_any.at[:, start:], slot_came_any.at[:, start:], kept_any.at[:rows, lanes], came_any.at[:rows, lanes]),
        (slot_room, slot_came_room, left_ref.at[length : length + rows, :], left_ref.at[length + rows :, :]),
        sems,
    )
    for copy in copies:
        copy.start()
    left_ref[:length, :] = doc_ref[...]
    for part in range(length // LANES):
        here = slice(part * LANES, (part + 1) * LANES)
        there = slice((part ^ 1) * LANES, ((part ^ 1) + 1) * LANES)
        right_ref[here, :] = add(grads_ref[here, :], other_ref[there, :]).astype(bf16)
    pair_kept[...] = right_ref[:LANES, :]
    pair_sent[...] = right_ref[2 * LANES : 3 * LANES, :]
    small = LANES // 2
    for place, ref in enumerate((grads_ref, other_ref)):
        query_ref[2 * place * small : (2 * place + 1) * small, :] = ref[length:, :width]
        query_ref[(2 * place + 1) * small : (2 * place + 2) * small, :] = ref[length:, width:]
    for copy in copies:
        copy.wait()
    right_ref[length : length + rows, :] = slot_room[:, width:]
    right_ref[length + rows :, :] = slot_came_room[:, width:]
    query_ref[2 * LANES : 2 * LANES + rows, :] = slot_room[:, :width]
    query_ref[2 * LANES + rows :, :] = slot_came_room[:, :width]
    store_product(left_ref[...], right_ref, 2 * width, kept_out, sent_out, width)
    left = jnp.concatenate([left_ref[: 2 * LANES, :], left_ref[length:, :]], 0)
    store_product(left, query_ref, width, kept_out, sent_out, 0)
    tail = sent_out.shape[0] - 16
    sent_out[tail:, :] = jnp.zeros((16, sent_out.shape[1]), bf16)
    sent_out[tail:, :LANES] = add(table_ref[...], other_table_ref[...]).astype(bf16)


def doc_input_kernel(
    tokens_ref, gain_ref, after_ref, grads_ref, kept_ref, came_ref, wq_ref, wk_ref, wv_ref, tokens_out
):
    width = tokens_ref.shape[1]
    rest = grads_ref.shape[0] - tokens_ref.shape[0] // 2
    query = jnp.concatenate([grads_ref[rest:, :width], grads_ref[rest:, width:]], 0)
    pair = add(kept_ref[...], came_ref[...]).astype(bf16)
    tokens_out[...] = input_back(
        tokens_ref[...].astype(f32), gain_ref, after_ref, query, pair[:, :width], pair[:, width:], wq_ref, wk_ref, wv_ref
    )


def on_device(
    doc_tokens, query_tokens, query_lengths, positive_docs, retrieved, attend_gain, query_weight, key_weight,
    value_weight, output_weight, bias_table, feed_gain, gate_weight, up_weight, down_weight, final_gain, proj_weight,
):
    narrow_size = lax.axis_size("narrow")
    bits = rank_bits()
    rank = my_rank()
    rank_word = rank.astype(jnp.int32).reshape(1)
    doc_rows, width = doc_tokens.shape[1:]
    doc_length = doc_rows * narrow_size
    doc_total = doc_tokens.shape[0] * lax.axis_size("wide")
    slots = query_tokens.shape[0] // narrow_size
    slot_length = query_tokens.shape[1]
    heads = bias_table.shape[1]
    units = gate_weight.shape[1]
    columns = proj_weight.shape[1]
    slot_rows = slots * slot_length
    rows = slot_rows + doc_rows
    blocks = doc_total * doc_length // LANES
    assert doc_tokens.shape[0] == 1 and doc_rows == LANES and slot_rows == LANES and narrow_size == 4
    assert columns == LANES and doc_total <= LANES and blocks == 1 << bits
    gains = (attend_gain, feed_gain, final_gain)
    dma = pltpu.SemaphoreType.DMA
    over_y = [1, 2] + list(range(3, bits))
    over_x = [2, 1] + list(range(3, bits))
    over_z = [bits - 2, 2, 1] + list(range(3, bits - 2)) + [bits - 1]

    orders = (over_y, over_x, over_x, over_z)
    own_tokens = doc_tokens[0]
    y_tokens = swap(own_tokens, 2)
    core_tokens = swap(own_tokens, 1)
    pairs = heads // 2
    doc_bias, slot_bias = call(
        functools.partial(bias_kernel, doc_length),
        [shape((pairs, 2 * doc_rows, doc_length)), shape((pairs, 2 * slot_rows, slot_rows))],
        [rank_word, bias_table],
        "s",
        [pltpu.VMEM((heads, 2 * doc_length + LANES), f32)],
    )
    y_tokens = after(y_tokens, doc_bias)
    both_tokens = swap(y_tokens, 1)

    all_rows = slot_rows + doc_length
    forward_shapes = [
        shape((all_rows, width), bf16),
        shape((rows, width), bf16),
        shape((all_rows, width), bf16),
        shape((all_rows, width), bf16),
        shape((pairs, 2 * doc_rows, doc_length), bf16),
        shape((pairs, 2 * slot_rows, slot_rows), bf16),
        shape((rows, width), bf16),
        shape((rows, width)),
        shape((rows, width), bf16),
        shape((rows, units), bf16),
        shape((rows, units), bf16),
        shape((rows, units), bf16),
        shape((rows, width)),
        shape((rows, width), bf16),
        shape((rows, columns)),
        shape((slot_rows, columns), bf16),
        shape((doc_rows, columns), bf16),
    ]
    weights = [
        query_weight, key_weight, value_weight, output_weight, gate_weight, up_weight, down_weight, proj_weight,
    ]
    slot_room = pltpu.VMEM((slots, slot_length, width), bf16)
    (
        all_normed, query, key, value, doc_probs, slot_probs, mixed, after_attend, normed_feed, hidden, gate_slope,
        up_slope, after_feed, normed_final, embed, slot_unit, doc_unit,
    ) = call(
        functools.partial(forward_kernel, slots, slot_length),
        forward_shapes,
        [
            rank_word, query_lengths, query_tokens, own_tokens, core_tokens, y_tokens, both_tokens, doc_bias, slot_bias,
            *gains, *weights,
        ],
        "ssa" + "v" * 9 + "a" * 8 + "a" * len(forward_shapes),
        [room(value) for value in forward_shapes]
        + [room(weight) for weight in weights]
        + [slot_room, dma((8,)), dma((len(forward_shapes),)), dma],
    )

    phases = [list(range(high, max(high - 2, 0), -1)) for high in range(bits - 1, 0, -2)]
    gathered = []
    near_units = doc_unit[None]
    for phase, group in enumerate(phases):
        group = group[::-1]
        masks = [gather_order(place, group) for place in range(1, 1 << len(group))]
        came = [swap(near_units, mask) for mask in masks]
        if phase == 0:
            counts, tally = call(
                functools.partial(count_kernel, doc_length, doc_total),
                [shape((blocks, slot_rows, LANES), bf16), shape((slot_rows, LANES))],
                after([rank_word, retrieved], doc_unit),
                "sa",
                [
                    pltpu.VMEM((slots, slot_length, retrieved.shape[2]), jnp.int32),
                    pltpu.VMEM((slot_rows, retrieved.shape[2]), jnp.int32),
                    pltpu.VMEM((blocks * slot_rows, LANES), f32),
                    dma,
                ],
            )
            came = after(came, tally)
        if phase == 1:
            turned_cols = 5 * width // 2 + units // 2
            turned, turned_sent, turned_docs = call(
                functools.partial(turn_kernel, orders),
                [shape((rows, turned_cols), bf16)] * 2 + [shape((doc_length, width // 2), bf16)],
                after([rank_word, all_normed, normed_feed, mixed, normed_final, hidden], near_units),
                "s",
            )
            came = after(came, turned)
        near_units = jnp.concatenate([near_units] + came, 0)
        gathered = gathered + group
    gathered = gathered + [0]
    far_units = swap(near_units, 1)

    order = list(range(bits))
    half = blocks // 2
    losses, grad_slot_unit, kept, sent = call(
        functools.partial(loss_kernel, order, gathered, doc_total, slots),
        [
            shape((slots, LANES)),
            shape((slot_rows, columns)),
            shape((half, columns, LANES), bf16),
            shape((half, columns, LANES), bf16),
        ],
        [rank_word, query_lengths, positive_docs, counts, near_units, far_units, slot_unit, tally],
        "sss",
        [
            pltpu.VMEM((doc_total, slot_rows, columns), f32),
            pltpu.VMEM((doc_total, columns, slot_rows), bf16),
        ],
    )
    turned_came = swap(after(turned_sent, losses), 1)
    back_weights = [proj_weight, down_weight, gate_weight, up_weight, output_weight]
    all_weights = back_weights + [query_weight, key_weight, value_weight]
    doc_cols = 2 * units + 2 * width + columns

    came = [swap(sent, 1)]
    rest = order[1:]
    parts = [kept]
    first_phase = True
    while rest:
        group, rest = rest[:2], rest[2:]
        count = 1 << len(group)
        size = parts[0].shape[0] // count
        pieces = []
        for place in range(count):
            here = slice(place * size, (place + 1) * size)
            pieces.append(add(*(part[here] for part in parts), *(one[here] for one in came)).astype(bf16))
        masks = [scatter_order(place, group) for place in range(count)]
        came = [swap(piece, mask) for piece, mask in zip(pieces[1:], masks[1:])]
        parts = [pieces[0]]
        if first_phase:
            slot_grads, query_grad, slot_table = call(
                functools.partial(slot_back_kernel, slots),
                [shape((slot_rows, doc_cols + 3 * width), bf16), shape((slot_rows, width)), shape((heads, LANES))],
                [rank_word, query_tokens, after(grad_slot_unit, pieces[1], turned_came)]
                + [embed, after_feed, after_attend, gate_slope, up_slope, query, key, value, slot_probs, *gains]
                + all_weights,
                "sa" + "v" * 13 + "a" * 8,
                [room(weight) for weight in all_weights]
                + [slot_room, pltpu.VMEM((slot_rows, width), f32), pltpu.VMEM((slot_rows, width), bf16)]
                + [pltpu.VMEM((slot_rows, width), f32)]
                + [pltpu.VMEM((heads * 8, 2 * LANES), f32), dma((8,)), dma],
            )
            came = after(came, slot_table)
            first_phase = False
    slot_came = swap(after(slot_grads, *pieces[1:]), 1)

    doc_grads, doc_after, doc_mixed = call(
        functools.partial(doc_feed_kernel, 1 + len(came)),
        [shape((doc_rows, doc_cols), bf16), shape((doc_rows, width)), shape((doc_rows, width), bf16)],
        parts + after(came, slot_came)
        + [embed, after_feed, after_attend, gate_slope, up_slope, gains[1], gains[2]]
        + back_weights,
        "v" * (8 + len(came)) + "a" * 5,
        [room(weight) for weight in back_weights] + [pltpu.VMEM((doc_rows, width), f32), dma((5,))],
    )
    doc_came = swap(doc_grads, 1)

    class Stream:
        def __init__(self, kept, sent, order):
            self.kept, self.order, self.step = kept, order, 0
            self.loaded = sent.shape[0] > kept.shape[0]
            if self.loaded:
                self.small = sent[-16:]
            self.send(sent)

        def send(self, sent):
            self.came = swap(sent, 1 << self.order[self.step])
            self.step += 1

        def advance(self, *wait):
            came = after(self.came, *wait)
            if self.loaded:
                self.small = add(self.small, came[-16:]).astype(bf16)
                came = came[:-16]
            if self.step == len(self.order):
                self.result = add(self.kept, came)
                return self.result
            self.kept, sent = cut(self.kept, came)
            if self.loaded:
                sent = jnp.concatenate([sent, self.small], 0)
            self.send(sent)
            return self.kept

    def weight_product(terms, order, *wait):
        left = sum(term[1] for term in terms)
        right = sum(term[3] for term in terms)
        tall = terms[0][1] // 2
        args = after([turned, turned_came, slot_grads, slot_came, doc_grads, doc_came], *wait)
        kept, sent = call(
            functools.partial(weight_kernel, terms),
            [shape((tall, right), bf16)] * 2,
            args,
            "a" * 6,
            [pltpu.VMEM((2 * rows, left), bf16), pltpu.VMEM((2 * rows, right), bf16), dma((6 * len(terms),))],
        )
        return Stream(kept, sent, order)

    small_half = width // 2
    att_grads, table = call(
        doc_attend_kernel,
        [shape((doc_length + doc_rows // 2, 2 * width), bf16), shape((16, LANES), bf16)],
        [rank_word, query, key, value, doc_probs, doc_mixed, slot_table],
        "s",
        [pltpu.VMEM((doc_rows, width), bf16), pltpu.VMEM((heads * 8, 2 * doc_length), f32)],
    )
    att_came, table_came = swap(att_grads, 1), swap(table, 1)
    first = weight_product(
        [(0, small_half, 0, units), (2 * small_half, small_half, 2 * units + width, width)], orders[0], table
    )
    fourth_kept, fourth_sent, pair_kept, pair_sent = call(
        attend_weight_kernel,
        [
            shape((width // 4, 3 * width), bf16),
            shape((width // 4 + 16, 3 * width), bf16),
            shape((doc_rows, 2 * width), bf16),
            shape((doc_rows, 2 * width), bf16),
        ],
        [turned_docs, turned, turned_came, slot_grads, slot_came, att_grads, att_came, after(table, first.kept), table_came],
        "vaaaa",
        [
            pltpu.VMEM((slot_rows, 3 * width), bf16),
            pltpu.VMEM((slot_rows, 3 * width), bf16),
            pltpu.VMEM((doc_length + 2 * slot_rows, width // 2), bf16),
            pltpu.VMEM((doc_length + 2 * slot_rows, 2 * width), bf16),
            pltpu.VMEM((2 * doc_rows + 2 * slot_rows, width), bf16),
            dma((4,)),
        ],
    )
    fourth = Stream(fourth_kept, fourth_sent, orders[3])
    second = weight_product(
        [(small_half, small_half, units, units), (3 * small_half, small_half, 2 * units + 2 * width, columns)],
        orders[1],
        fourth_kept,
    )
    third = weight_product([(4 * small_half, units // 2, 2 * units, width)], orders[2], second.kept)
    pair_came = swap(pair_sent, 2)
    done = third.kept
    for step in range(bits - 1):
        for stream in (first, fourth, second, third):
            done = stream.advance(done)
        if step == 1:
            (doc_grad,) = call(
                doc_input_kernel,
                [shape((doc_rows, width))],
                [own_tokens, gains[0], doc_after, att_grads, pair_kept, after(pair_came, done)]
                + [query_weight, key_weight, value_weight],
            )
            done = doc_grad

    def own_rows(values):
        return lax.dynamic_slice_in_dim(values, rank * (width >> bits), width >> bits, 0).astype(f32)

    def gain_grad(gain, *pairs):
        return sum(jnp.sum(own_rows(weight) * grad, 1) for weight, grad in pairs) / own_rows(gain)

    gate_grad, output_grad = first.result[:, :units], first.result[:, units:]
    up_grad, proj_grad = second.result[:, :units], second.result[:, units:]
    query_g, key_g, value_g = (fourth.result[:, place * width : (place + 1) * width] for place in range(3))
    return (
        losses[:, 0],
        doc_grad[None],
        query_grad.reshape(slots, slot_length, width),
        gain_grad(attend_gain, (query_weight, query_g), (key_weight, key_g), (value_weight, value_g)),
        query_g,
        key_g,
        value_g,
        output_grad,
        fourth.small[:heads, :BUCKETS].astype(f32).T,
        gain_grad(feed_gain, (gate_weight, gate_grad), (up_weight, up_grad)),
        gate_grad,
        up_grad,
        third.result,
        gain_grad(final_gain, (proj_weight, proj_grad)),
        proj_grad,
    )


def solution(mesh):
    return jax.shard_map(
        on_device,
        mesh=mesh,
        in_specs=(
            P("wide", "narrow", None),
            P("wide", None, None),
            P("wide"),
            P("wide"),
            P("wide", None, None),
            P(),
            P(),
            P(),
            P(),
            P(),
            P(),
            P(),
            P(),
            P(),
            P(),
            P(),
            P(),
        ),
        out_specs=(
            P(("wide", "narrow")),
            P("wide", "narrow", None),
            P(("wide", "narrow"), None, None),
            P(("wide", "narrow")),
            P(("wide", "narrow"), None),
            P(("wide", "narrow"), None),
            P(("wide", "narrow"), None),
            P(("wide", "narrow"), None),
            P(),
            P(("wide", "narrow")),
            P(("wide", "narrow"), None),
            P(("wide", "narrow"), None),
            P(("wide", "narrow"), None),
            P(("wide", "narrow")),
            P(("wide", "narrow"), None),
        ),
        check_vma=False,
    )
```

time: 303 us -> 268 us (0.88); the launches traced: 298 us -> 267 us
  waiting for transfers between devices: 110 us -> 66 us
  Pallas kernels: 100 us -> 132 us
  starting transfers between devices: 48.6 us -> 39.2 us
  local copies, waits for them, and re-layouts: 20.2 us -> 14.6 us
    ppermute x46 -> x39, waiting for transfers between devices: 110 us -> 66 us  [swap(): return lax.ppermute(values, ('wide', 'narrow'), pairs)]
    pallas_call x8 -> x22, Pallas kernels: 100 us -> 132 us  [call(): pl.pallas_call(kernel, out_shape=tuple(outs), in_specs=specs[:len(args)],...]
    ppermute x46 -> x39, starting transfers between devices: 48.6 us -> 39.2 us  [swap(): return lax.ppermute(values, ('wide', 'narrow'), pairs)]
    convert_element_type x25 -> x8, other arithmetic: 10.8 us -> 3.05 us  [the longest x2 1.93 us: on_device(): add(*(part[here] for part in parts), *(one[here] for one in came))]
    unnamed x47 -> x65, local copies, waits for them, and re-layouts: 3.69 us -> 11.5 us
    reshape x8 -> x0, local copies, waits for them, and re-layouts: 4.81 us -> none  [the longest x1 1.28 us: on_device(): attend_gain.reshape(1, width)]
    reduce_sum x2 -> x3, other arithmetic: 0.14 us -> 4.88 us  [gain_grad(): jnp.sum(own_rows(weight) * grad, 1)]
    slice x12 -> x4, local copies, waits for them, and re-layouts: 6.08 us -> 2.47 us  [the longest x2 1.82 us: advance(): came = came[:-16]]
  transfers between devices with their start and end apart: 46 -> 39, of which waited for: 31 -> 16; matrix products, arithmetic and copies ran while one was open for 10% -> 5% of each run, Pallas kernels for 18% -> 33%
where the time goes in v3:
time: 268 us; the launch traced here: 267 us
  Pallas kernels  132 us (49%)
  waiting for transfers between devices  66 us (25%)
  starting transfers between devices  39.2 us (15%)
  local copies, waits for them, and re-layouts  14.6 us (5%)
  other arithmetic  13.8 us (5%)
    pallas_call x22, Pallas kernels, call(): pl.pallas_call(kernel, out_shape=tuple(outs), in_specs=specs[:len(args)],...  132 us
    ppermute x39, waiting for transfers between devices, swap(): return lax.ppermute(values, ('wide', 'narrow'), pairs)  66 us
    ppermute x39, starting transfers between devices, swap(): return lax.ppermute(values, ('wide', 'narrow'), pairs)  39.2 us
    unnamed x65, local copies, waits for them, and re-layouts  11.5 us
  transfers between devices with their start and end apart: 39, of which 16 were waited for; matrix products, arithmetic and copies ran while one was open for 5% of the time, Pallas kernels for 33%

profile of v3, /device:TPU:0, one launch (start us, length us, event | category | flops | bytes accessed | tf_op | source)
XLA Modules:
  0.0 267.0 jit_solution(15618650963350008206)
XLA Ops:
  0.6 3.0 %collective-permute-start.1 = (bf16[128,768]{1,0:T(8,128)(2,1)}, bf16[128,768]{1,0:T(8,128)(2,1)S(1)}, u32[]{:S(2)}, u32[]{:S(2)}) collective-permute-start(bf16[128,768]{1,0:T(8,128)(2,1)} %bitcast.8), channel_id=1, source_target_pairs={{0,2},{1,3},{2,0},{3,1},{4,6},{5,7},{6,4},{7,5},{8,10},{9,11},{10,... | collective-permute-start | bytes 589832 | tf_op jit(solution)/shard_map/ppermute | solution.py:53
  3.7 1.4 copy.33.table_ref
  5.1 5.4 %shard_map.280 = (f32[6,256,512]{2,1,0:T(8,128)}, f32[6,256,128]{2,1,0:T(8,128)}) custom-call(s32[1]{0:T(128)} %bitcast.rank_ref, f32[32,12]{1,0:T(8,128)} %copy.33.table_ref), custom_call_target="tpu_custom_call" | custom-call | tf_op jit(solution)/shard_map/pallas_call | solution.py:95
  11.0 1.1 collective-permute-done.2.last_ref
  12.7 18.7 %shard_map.281 = (bf16[640,768]{1,0:T(8,128)(2,1)}, bf16[256,768]{1,0:T(8,128)(2,1)}, bf16[640,768]{1,0:T(8,128)(2,1)}, bf16[640,768]{1,0:T(8,128)(2,1)}, bf16[6...) custom-call(s32[1]{0:T(128)} %bitcast.rank_ref, ...), custom_call_target="tpu_custom_call" | custom-call | tf_op jit(solution)/shard_map/pallas_call | solution.py:95
  31.5 1.6 collective-permute-start.3
  33.1 2.6 collective-permute-start.4
  36.7 6.4 %shard_map.282 = (bf16[32,128,128]{2,1,0:T(8,128)(2,1)}, f32[128,128]{1,0:T(8,128)}) custom-call(s32[1]{0:T(128)} %bitcast.rank_ref, s32[16,32,128]{2,1,0:T(8,128)} %picked_ref), custom_call_target="tpu_custom_call" | custom-call | tf_op jit(solution)/shard_map/pallas_call | solution.py:95
  44.3 1.7 collective-permute-start.7
  46.0 1.5 collective-permute-start.8
  47.5 8.0 %shard_map.283 = (bf16[256,2944]{1,0:T(8,128)(2,1)}, bf16[256,2944]{1,0:T(8,128)(2,1)}, bf16[512,384]{1,0:T(8,128)(2,1)}) custom-call(s32[1]{0:T(128)} %bitcast.rank_ref, bf16[640,768]{1,0:T(8,128)(2,1)} %get-tuple-element.156.all_ref, bf16[256,768]{1,0:T(8,128)(2,1)} %get-tuple-element.157.normed_feed_ref, bf16[256,768]{1,0:T(8,128)(2,1)} %get-tuple-element.158.mixed_ref, ...), custom_call_target="tpu_custom_call" | custom-call | tf_op jit(solution)/shard_map/pallas_call | solution.py:95
  55.7 1.9 collective-permute-done.9.far_ref
  58.5 5.2 %shard_map.284 = (f32[4,128]{1,0:T(4,128)}, f32[128,128]{1,0:T(8,128)}, bf16[16,128,128]{2,1,0:T(8,128)(2,1)}, bf16[16,128,128]{2,1,0:T(8,128)(2,1)}) custom-call(s32[1]{0:T(128)} %bitcast.rank_ref, s32[16]{0:T(128)} %lengths_ref.3, s32[16]{0:T(128)} %positives_ref.1, bf16[32,128,128]{2,1,0:T(8,128)(2,1)} %get-tuple-element.145.counts_ref, ...), custom_call_target="tpu_custom_call" | custom-call | tf_op jit(solution)/shard_map/pallas_call | solution.py:95
  64.2 3.8 %collective-permute-done.10 = bf16[16,128,128]{2,1,0:T(8,128)(2,1)S(1)} collective-permute-done((bf16[16,128,128]{2,1,0:T(8,128)(2,1)}, bf16[16,128,128]{2,1,0:T(8,128)(2,1)S(1)}, u32[]{:S(2)}, u32[]{:S(2)}) %collective-permute-start.10) | collective-permute-done | bytes 524320 | tf_op jit(solution)/shard_map/ppermute | solution.py:53
  68.0 1.2 add_convert_fusion.2
  69.2 1.3 collective-permute-start.11
  71.0 1.7 collective-permute-start.13
  72.8 18.5 %shard_map.285 = (bf16[128,8064]{1,0:T(8,128)(2,1)}, f32[128,768]{1,0:T(8,128)}, f32[12,128]{1,0:T(8,128)}) custom-call(s32[1]{0:T(128)} %bitcast.rank_ref, bf16[16,32,768]{2,1,0:T(8,128)(2,1)} %queries_ref.3, f32[128,128]{1,0:T(8,128)} %get-tuple-element.172.grad_unit_ref, f32[256,128]{1,0:T(8,128)} %get-tuple-element.173.embed_ref.refs_4_, ...), custom_call_target="tpu_custom_call" | custom-call | tf_op jit(solution)/shard_map/pallas_call | solution.py:95
  92.0 1.5 collective-permute-start.15
  93.5 2.5 collective-permute-start.16
  96.8 1.1 collective-permute-done.16.refs_2_
  97.9 3.8 %collective-permute-done.17.refs_3_ = bf16[1,128,128]{2,1,0:T(8,128)(2,1)S(1)} collective-permute-done((bf16[1,128,128]{2,1,0:T(8,128)(2,1)S(1)}, bf16[1,128,128]{2,1,0:T(8,128)(2,1)S(1)}, u32[]{:S(2)}, u32[]{:S(2)}) %collective-permute-start.17) | collective-permute-done | bytes 32800 | tf_op jit(solution)/shard_map/ppermute | solution.py:53
  102.3 11.9 %shard_map.286 = (bf16[128,5760]{1,0:T(8,128)(2,1)}, f32[128,768]{1,0:T(8,128)}, bf16[128,768]{1,0:T(8,128)(2,1)}) custom-call(bf16[1,128,128]{2,1,0:T(8,128)(2,1)} %get-tuple-element.284.refs_0_, bf16[1,128,128]{2,1,0:T(8,128)(2,1)} %copy-done.21, bf16[1,128,128]{2,1,0:T(8,128)(2,1)} %copy-done.22, bf16[1,128,128]{2,1,0:T(8,128)(2,1)} %copy-done.23, ...), custom_call_target="tpu_custom_call" | custom-call | tf_op jit(solution)/shard_map/pallas_call | solution.py:95
  114.2 8.9 %shard_map.287 = (bf16[576,1536]{1,0:T(8,128)(2,1)}, bf16[16,128]{1,0:T(8,128)(2,1)}) custom-call(s32[1]{0:T(128)} %bitcast.rank_ref, bf16[256,768]{1,0:T(8,128)(2,1)} %get-tuple-element.178.query_ref, bf16[640,768]{1,0:T(8,128)(2,1)} %get-tuple-element.179.key_ref, bf16[640,768]{1,0:T(8,128)(2,1)} %get-tuple-element.180.value_ref, ...), custom_call_target="tpu_custom_call" | custom-call | tf_op jit(solution)/shard_map/pallas_call | solution.py:95
  123.7 5.3 %collective-permute-done.20.doc_came_any = bf16[128,5760]{1,0:T(8,128)(2,1)S(1)} collective-permute-done((bf16[128,5760]{1,0:T(8,128)(2,1)S(1)}, bf16[128,5760]{1,0:T(8,128)(2,1)S(1)}, u32[]{:S(2)}, u32[]{:S(2)}) %collective-permute-start.20) | collective-permute-done | bytes 1474592 | tf_op jit(solution)/shard_map/ppermute | solution.py:53
  129.0 1.1 copy-done.3
  130.1 6.6 %shard_map.288 = (bf16[192,2816]{1,0:T(8,128)(2,1)}, bf16[192,2816]{1,0:T(8,128)(2,1)}) custom-call(bf16[256,2944]{1,0:T(8,128)(2,1)} %get-tuple-element.216.kept_any, bf16[256,2944]{1,0:T(8,128)(2,1)} %copy-done.1, bf16[128,8064]{1,0:T(8,128)(2,1)} %get-tuple-element.218.slot_any, bf16[128,8064]{1,0:T(8,128)(2,1)} %copy-done, ...), custom_call_target="tpu_custom_call" | custom-call | tf_op jit(solution)/shard_map/pallas_call | solution.py:95
  137.3 1.2 collective-permute-done.21.other_table_ref
  139.0 8.1 %shard_map.289 = (bf16[192,2304]{1,0:T(8,128)(2,1)}, bf16[208,2304]{1,0:T(8,128)(2,1)}, bf16[128,1536]{1,0:T(8,128)(2,1)}, bf16[128,1536]{1,0:T(8,128)(2,1)}) custom-call(bf16[512,384]{1,0:T(8,128)(2,1)} %get-tuple-element.195.doc_ref, bf16[256,2944]{1,0:T(8,128)(2,1)} %get-tuple-element.216.kept_any, bf16[256,2944]{1,0:T(8,128)(2,1)} %copy-done.1, ...), custom_call_target="tpu_custom_call" | custom-call | tf_op jit(solution)/shard_map/pallas_call | solution.py:95
  147.2 5.9 %shard_map.290 = (bf16[192,2176]{1,0:T(8,128)(2,1)}, bf16[192,2176]{1,0:T(8,128)(2,1)}) custom-call(bf16[256,2944]{1,0:T(8,128)(2,1)} %get-tuple-element.216.kept_any, bf16[256,2944]{1,0:T(8,128)(2,1)} %copy-done.1, bf16[128,8064]{1,0:T(8,128)(2,1)} %get-tuple-element.218.slot_any, bf16[128,8064]{1,0:T(8,128)(2,1)} %copy-done, ...), custom_call_target="tpu_custom_call" | custom-call | tf_op jit(solution)/shard_map/pallas_call | solution.py:95
  153.1 4.1 %shard_map.291 = (bf16[512,768]{1,0:T(8,128)(2,1)}, bf16[512,768]{1,0:T(8,128)(2,1)}) custom-call(bf16[256,2944]{1,0:T(8,128)(2,1)} %get-tuple-element.216.kept_any, bf16[256,2944]{1,0:T(8,128)(2,1)} %copy-done.1, bf16[128,8064]{1,0:T(8,128)(2,1)} %get-tuple-element.218.slot_any, bf16[128,8064]{1,0:T(8,128)(2,1)} %copy-done, ...), custom_call_target="tpu_custom_call" | custom-call | tf_op jit(solution)/shard_map/pallas_call | solution.py:95
  157.2 1.6 collective-permute-start.23
  159.3 3.6 %collective-permute-done.26.came_ref = bf16[192,2816]{1,0:T(8,128)(2,1)S(1)} collective-permute-done((bf16[192,2816]{1,0:T(8,128)(2,1)}, bf16[192,2816]{1,0:T(8,128)(2,1)S(1)}, u32[]{:S(2)}, u32[]{:S(2)}) %collective-permute-start.26) | collective-permute-done | bytes 1081376 | tf_op jit(solution)/shard_map/ppermute | solution.py:53
  162.9 1.0 copy-done.4
  163.9 2.7 %shard_map.292 = (bf16[96,2816]{1,0:T(8,128)(2,1)}, bf16[96,2816]{1,0:T(8,128)(2,1)}) custom-call(bf16[192,2816]{1,0:T(8,128)(2,1)} %get-tuple-element.204.kept_ref, bf16[192,2816]{1,0:T(8,128)(2,1)} %copy-done.4), custom_call_target="tpu_custom_call" | custom-call | tf_op jit(solution)/shard_map/pallas_call | solution.py:95
  166.6 1.6 collective-permute-start.30
  168.1 2.5 collective-permute-done.25
  171.6 1.0 slice.187.came_ref
  172.6 2.5 shard_map.293
  175.1 1.0 pad_maximum_fusion
  176.1 1.6 collective-permute-start.29
  177.7 18.0 %collective-permute-done.24.came_ref = bf16[192,2176]{1,0:T(8,128)(2,1)S(1)} collective-permute-done((bf16[192,2176]{1,0:T(8,128)(2,1)}, bf16[192,2176]{1,0:T(8,128)(2,1)S(1)}, u32[]{:S(2)}, u32[]{:S(2)}) %collective-permute-start.24) | collective-permute-done | bytes 835616 | tf_op jit(solution)/shard_map/ppermute | solution.py:53
  196.7 2.4 shard_map.294
  199.2 1.5 collective-permute-start.28
  201.6 2.4 shard_map.295
  205.1 1.5 collective-permute-start.22
  207.4 2.1 shard_map.296
  209.5 2.0 collective-permute-start.32
  211.6 6.1 %collective-permute-done.29 = bf16[112,2304]{1,0:T(8,128)(2,1)S(1)} collective-permute-done((bf16[112,2304]{1,0:T(8,128)(2,1)S(1)}, bf16[112,2304]{1,0:T(8,128)(2,1)S(1)}, u32[]{:S(2)}, u32[]{:S(2)}) %collective-permute-start.29) | collective-permute-done | bytes 516128 | tf_op jit(solution)/shard_map/ppermute | solution.py:53
  218.5 2.0 shard_map.297
  221.2 2.0 shard_map.298
  223.9 1.9 shard_map.299
  226.4 1.4 collective-permute-start.36
  227.8 1.6 collective-permute-start.31
  230.0 5.1 %shard_map.300 = f32[128,768]{1,0:T(8,128)} custom-call(bf16[128,768]{1,0:T(8,128)(2,1)} %bitcast.11, f32[768]{0:T(1024)} %gain_ref.1, f32[128,768]{1,0:T(8,128)} %get-tuple-element.191.after_ref, bf16[576,1536]{1,0:T(8,128)(2,1)} %get-tuple-element.194.grads_ref, bf16[128,1536]{1,0:T(8,128)(2,1)} %get-tuple-element.206.kept_ref, ...), custom_call_target="tpu_custom_call" | custom-call | tf_op jit(solution)/shard_map/pallas_call | solution.py:95
  236.1 2.3 collective-permute-start.37
  239.9 1.7 shard_map.301
  241.6 9.3 %collective-permute-done.34 = bf16[24,2816]{1,0:T(8,128)(2,1)S(1)} collective-permute-done((bf16[24,2816]{1,0:T(8,128)(2,1)S(1)}, bf16[24,2816]{1,0:T(8,128)(2,1)S(1)}, u32[]{:S(2)}, u32[]{:S(2)}) %collective-permute-start.34) | collective-permute-done | bytes 135200 | tf_op jit(solution)/shard_map/ppermute | solution.py:53
  251.6 6.6 %collective-permute-done.33 = bf16[40,2304]{1,0:T(8,128)(2,1)S(1)} collective-permute-done((bf16[40,2304]{1,0:T(8,128)(2,1)S(1)}, bf16[40,2304]{1,0:T(8,128)(2,1)S(1)}, u32[]{:S(2)}, u32[]{:S(2)}) %collective-permute-start.33) | collective-permute-done | bytes 184352 | tf_op jit(solution)/shard_map/ppermute | solution.py:53
  258.3 1.6 multiply_reduce_fusion.3
  259.9 1.4 multiply_reduce_fusion.5
  261.3 1.8 multiply_reduce_fusion
  264.5 1.3 dynamic-slice_divide_fusion.1
  265.7 1.3 dynamic-slice_divide_fusion
  (129 shorter events, 22.4 us)
Async XLA Ops:
  0.6 9.8 %collective-permute-start.1 = (bf16[128,768]{1,0:T(8,128)(2,1)}, bf16[128,768]{1,0:T(8,128)(2,1)S(1)}, u32[]{:S(2)}, u32[]{:S(2)}) collective-permute-start(bf16[128,768]{1,0:T(8,128)(2,1)} %bitcast.8), channel_id=1, source_target_pairs={{0,2},{1,3},{2,0},{3,1},{4,6},{5,7},{6,4},{7,5},{8,10},{9,11},{10,... | collective-permute-start | bytes 589832 | tf_op jit(solution)/shard_map/ppermute | solution.py:53
  3.7 7.3 %collective-permute-start = (bf16[128,768]{1,0:T(8,128)(2,1)}, bf16[128,768]{1,0:T(8,128)(2,1)S(1)}, u32[]{:S(2)}, u32[]{:S(2)}) collective-permute-start(bf16[128,768]{1,0:T(8,128)(2,1)} %bitcast.9), channel_id=1, source_target_pairs={{0,1},{1,0},{2,3},{3,2},{4,5},{5,4},{6,7},{7,6},{8,9},{9,8},{10,11... | collective-permute-start | bytes 589832 | tf_op jit(solution)/shard_map/ppermute | solution.py:53
  10.5 1.6 copy-start.17
  10.5 1.6 collective-permute-start.2
  11.0 1.1 copy-start.18
  31.5 11.6 %collective-permute-start.3 = (bf16[1,128,128]{2,1,0:T(8,128)(2,1)}, bf16[1,128,128]{2,1,0:T(8,128)(2,1)S(1)}, u32[]{:S(2)}, u32[]{:S(2)}) collective-permute-start(bf16[1,128,128]{2,1,0:T(8,128)(2,1)} %bitcast.13), channel_id=1, source_target_pairs={{0,8},{1,9},{2,10},{3,11},{4,12},{5,13},{6,14},{7,15},{8,0},{9,1},... | collective-permute-start | bytes 98312 | tf_op jit(solution)/shard_map/ppermute | solution.py:53
  33.1 10.0 %collective-permute-start.4 = (bf16[1,128,128]{2,1,0:T(8,128)(2,1)}, bf16[1,128,128]{2,1,0:T(8,128)(2,1)S(1)}, u32[]{:S(2)}, u32[]{:S(2)}) collective-permute-start(bf16[1,128,128]{2,1,0:T(8,128)(2,1)} %bitcast.14), channel_id=1, source_target_pairs={{0,16},{1,17},{2,18},{3,19},{4,20},{5,21},{6,22},{7,23},{8,24},{9,... | collective-permute-start | bytes 98312 | tf_op jit(solution)/shard_map/ppermute | solution.py:53
  35.7 7.4 %collective-permute-start.5 = (bf16[1,128,128]{2,1,0:T(8,128)(2,1)}, bf16[1,128,128]{2,1,0:T(8,128)(2,1)S(1)}, u32[]{:S(2)}, u32[]{:S(2)}) collective-permute-start(bf16[1,128,128]{2,1,0:T(8,128)(2,1)} %bitcast.15), channel_id=1, source_target_pairs={{0,24},{1,25},{2,26},{3,27},{4,28},{5,29},{6,30},{7,31},{8,16},{9,... | collective-permute-start | bytes 98312 | tf_op jit(solution)/shard_map/ppermute | solution.py:53
  43.9 11.6 %collective-permute-start.6 = (bf16[4,128,128]{2,1,0:T(8,128)(2,1)S(1)}, bf16[4,128,128]{2,1,0:T(8,128)(2,1)S(1)}, u32[]{:S(2)}, u32[]{:S(2)}) collective-permute-start(bf16[4,128,128]{2,1,0:T(8,128)(2,1)S(1)} %pad_maximum_fusion.3), channel_id=1, source_target_pairs={{0,2},{1,3},{2,0},{3,1},{4,6},{5,7},{6,4},{7,5},{8,10},{9,11},{10,... | collective-permute-start | bytes 393224 | tf_op jit(solution)/shard_map/ppermute | solution.py:53
  44.3 11.3 %collective-permute-start.7 = (bf16[4,128,128]{2,1,0:T(8,128)(2,1)S(1)}, bf16[4,128,128]{2,1,0:T(8,128)(2,1)S(1)}, u32[]{:S(2)}, u32[]{:S(2)}) collective-permute-start(bf16[4,128,128]{2,1,0:T(8,128)(2,1)S(1)} %pad_maximum_fusion.3), channel_id=1, source_target_pairs={{0,4},{1,5},{2,6},{3,7},{4,0},{5,1},{6,2},{7,3},{8,12},{9,13},{10,... | collective-permute-start | bytes 393224 | tf_op jit(solution)/shard_map/ppermute | solution.py:53
  46.0 9.6 %collective-permute-start.8 = (bf16[4,128,128]{2,1,0:T(8,128)(2,1)S(1)}, bf16[4,128,128]{2,1,0:T(8,128)(2,1)S(1)}, u32[]{:S(2)}, u32[]{:S(2)}) collective-permute-start(bf16[4,128,128]{2,1,0:T(8,128)(2,1)S(1)} %pad_maximum_fusion.3), channel_id=1, source_target_pairs={{0,6},{1,7},{2,4},{3,5},{4,2},{5,3},{6,0},{7,1},{8,14},{9,15},{10,... | collective-permute-start | bytes 393224 | tf_op jit(solution)/shard_map/ppermute | solution.py:53
  55.5 8.1 %copy-start.27 = (bf16[256,2944]{1,0:T(8,128)(2,1)S(1)}, bf16[256,2944]{1,0:T(8,128)(2,1)}, u32[]{:S(2)}) copy-start(bf16[256,2944]{1,0:T(8,128)(2,1)} %get-tuple-element.171) | copy-start | bytes 4521988
  55.7 2.0 copy-start.7
  55.7 2.0 collective-permute-start.9
  57.6 0.8 copy-start.8
  63.7 9.1 %collective-permute-start.14 = (bf16[256,2944]{1,0:T(8,128)(2,1)S(1)}, bf16[256,2944]{1,0:T(8,128)(2,1)S(1)}, u32[]{:S(2)}, u32[]{:S(2)}) collective-permute-start(bf16[256,2944]{1,0:T(8,128)(2,1)S(1)} %copy-done.27), channel_id=1, source_target_pairs={{0,1},{1,0},{2,3},{3,2},{4,5},{5,4},{6,7},{7,6},{8,9},{9,8},{10,11... | collective-permute-start | bytes 4521992 | tf_op jit(solution)/shard_map/ppermute | solution.py:53
  63.8 4.1 %collective-permute-start.10 = (bf16[16,128,128]{2,1,0:T(8,128)(2,1)}, bf16[16,128,128]{2,1,0:T(8,128)(2,1)S(1)}, u32[]{:S(2)}, u32[]{:S(2)}) collective-permute-start(bf16[16,128,128]{2,1,0:T(8,128)(2,1)} %get-tuple-element.168), channel_id=1, source_target_pairs={{0,1},{1,0},{2,3},{3,2},{4,5},{5,4},{6,7},{7,6},{8,9},{9,8},{10,11... | collective-permute-start | bytes 1572872 | tf_op jit(solution)/shard_map/ppermute | solution.py:53
  69.2 22.1 %collective-permute-start.11 = (bf16[4,128,128]{2,1,0:T(8,128)(2,1)S(1)}, bf16[4,128,128]{2,1,0:T(8,128)(2,1)S(1)}, u32[]{:S(2)}, u32[]{:S(2)}) collective-permute-start(bf16[4,128,128]{2,1,0:T(8,128)(2,1)S(1)} %get-tuple-element.277), channel_id=1, source_target_pairs={{0,4},{1,5},{2,6},{3,7},{4,0},{5,1},{6,2},{7,3},{8,12},{9,13},{10,... | collective-permute-start | bytes 393224 | tf_op jit(solution)/shard_map/ppermute | solution.py:53
  70.5 20.7 %collective-permute-start.12 = (bf16[4,128,128]{2,1,0:T(8,128)(2,1)S(1)}, bf16[4,128,128]{2,1,0:T(8,128)(2,1)S(1)}, u32[]{:S(2)}, u32[]{:S(2)}) collective-permute-start(bf16[4,128,128]{2,1,0:T(8,128)(2,1)S(1)} %get-tuple-element.276), channel_id=1, source_target_pairs={{0,2},{1,3},{2,0},{3,1},{4,6},{5,7},{6,4},{7,5},{8,10},{9,11},{10,... | collective-permute-start | bytes 393224 | tf_op jit(solution)/shard_map/ppermute | solution.py:53
  71.0 20.2 %collective-permute-start.13 = (bf16[4,128,128]{2,1,0:T(8,128)(2,1)S(1)}, bf16[4,128,128]{2,1,0:T(8,128)(2,1)S(1)}, u32[]{:S(2)}, u32[]{:S(2)}) collective-permute-start(bf16[4,128,128]{2,1,0:T(8,128)(2,1)S(1)} %get-tuple-element.275), channel_id=1, source_target_pairs={{0,6},{1,7},{2,4},{3,5},{4,2},{5,3},{6,0},{7,1},{8,14},{9,15},{10,... | collective-permute-start | bytes 393224 | tf_op jit(solution)/shard_map/ppermute | solution.py:53
  72.8 18.5 %copy-start.1 = (bf16[256,2944]{1,0:T(8,128)(2,1)}, bf16[256,2944]{1,0:T(8,128)(2,1)S(1)}, u32[]{:S(2)}) copy-start(bf16[256,2944]{1,0:T(8,128)(2,1)S(1)} %collective-permute-done.14.came_any) | copy-start | bytes 4521988
  92.0 9.7 %collective-permute-start.18 = (bf16[128,8064]{1,0:T(8,128)(2,1)}, bf16[128,8064]{1,0:T(8,128)(2,1)S(1)}, u32[]{:S(2)}, u32[]{:S(2)}) collective-permute-start(bf16[128,8064]{1,0:T(8,128)(2,1)} %get-tuple-element.218.slot_any), channel_id=1, source_target_pairs={{0,1},{1,0},{2,3},{3,2},{4,5},{5,4},{6,7},{7,6},{8,9},{9,8},{10,11... | collective-permute-start | bytes 6193160 | tf_op jit(solution)/shard_map/ppermute | solution.py:53
  92.0 4.8 %collective-permute-start.15 = (bf16[1,128,128]{2,1,0:T(8,128)(2,1)S(1)}, bf16[1,128,128]{2,1,0:T(8,128)(2,1)S(1)}, u32[]{:S(2)}, u32[]{:S(2)}) collective-permute-start(bf16[1,128,128]{2,1,0:T(8,128)(2,1)S(1)} %get-tuple-element.283), channel_id=1, source_target_pairs={{0,16},{1,17},{2,18},{3,19},{4,20},{5,21},{6,22},{7,23},{8,24},{9,... | collective-permute-start | bytes 98312 | tf_op jit(solution)/shard_map/ppermute | solution.py:53
  93.5 4.4 %collective-permute-start.16 = (bf16[1,128,128]{2,1,0:T(8,128)(2,1)S(1)}, bf16[1,128,128]{2,1,0:T(8,128)(2,1)S(1)}, u32[]{:S(2)}, u32[]{:S(2)}) collective-permute-start(bf16[1,128,128]{2,1,0:T(8,128)(2,1)S(1)} %get-tuple-element.282), channel_id=1, source_target_pairs={{0,8},{1,9},{2,10},{3,11},{4,12},{5,13},{6,14},{7,15},{8,0},{9,1},... | collective-permute-start | bytes 98312 | tf_op jit(solution)/shard_map/ppermute | solution.py:53
  96.0 5.7 %collective-permute-start.17 = (bf16[1,128,128]{2,1,0:T(8,128)(2,1)S(1)}, bf16[1,128,128]{2,1,0:T(8,128)(2,1)S(1)}, u32[]{:S(2)}, u32[]{:S(2)}) collective-permute-start(bf16[1,128,128]{2,1,0:T(8,128)(2,1)S(1)} %get-tuple-element.281), channel_id=1, source_target_pairs={{0,24},{1,25},{2,26},{3,27},{4,28},{5,29},{6,30},{7,31},{8,16},{9,... | collective-permute-start | bytes 98312 | tf_op jit(solution)/shard_map/ppermute | solution.py:53
  96.8 4.9 %copy-start.21 = (bf16[1,128,128]{2,1,0:T(8,128)(2,1)}, bf16[1,128,128]{2,1,0:T(8,128)(2,1)S(1)}, u32[]{:S(2)}) copy-start(bf16[1,128,128]{2,1,0:T(8,128)(2,1)S(1)} %collective-permute-done.15.refs_1_) | copy-start | bytes 98308
  97.9 3.8 %copy-start.22 = (bf16[1,128,128]{2,1,0:T(8,128)(2,1)}, bf16[1,128,128]{2,1,0:T(8,128)(2,1)S(1)}, u32[]{:S(2)}) copy-start(bf16[1,128,128]{2,1,0:T(8,128)(2,1)S(1)} %collective-permute-done.16.refs_2_) | copy-start | bytes 98308
  101.7 12.5 %copy-start = (bf16[128,8064]{1,0:T(8,128)(2,1)}, bf16[128,8064]{1,0:T(8,128)(2,1)S(1)}, u32[]{:S(2)}) copy-start(bf16[128,8064]{1,0:T(8,128)(2,1)S(1)} %collective-permute-done.18.slot_came_any) | copy-start | bytes 6193156
  114.2 8.9 %copy-start.2 = (bf16[128,5760]{1,0:T(8,128)(2,1)S(1)}, bf16[128,5760]{1,0:T(8,128)(2,1)}, u32[]{:S(2)}) copy-start(bf16[128,5760]{1,0:T(8,128)(2,1)} %get-tuple-element.220.doc_any) | copy-start | bytes 4423684
  123.2 15.3 %collective-permute-start.19 = (bf16[576,1536]{1,0:T(8,128)(2,1)}, bf16[576,1536]{1,0:T(8,128)(2,1)}, u32[]{:S(2)}, u32[]{:S(2)}) collective-permute-start(bf16[576,1536]{1,0:T(8,128)(2,1)} %get-tuple-element.194.grads_ref), channel_id=1, source_target_pairs={{0,1},{1,0},{2,3},{3,2},{4,5},{5,4},{6,7},{7,6},{8,9},{9,8},{10,11... | collective-permute-start | bytes 5308424 | tf_op jit(solution)/shard_map/ppermute | solution.py:53
  123.2 5.8 %collective-permute-start.20 = (bf16[128,5760]{1,0:T(8,128)(2,1)S(1)}, bf16[128,5760]{1,0:T(8,128)(2,1)S(1)}, u32[]{:S(2)}, u32[]{:S(2)}) collective-permute-start(bf16[128,5760]{1,0:T(8,128)(2,1)S(1)} %copy-done.2), channel_id=1, source_target_pairs={{0,1},{1,0},{2,3},{3,2},{4,5},{5,4},{6,7},{7,6},{8,9},{9,8},{10,11... | collective-permute-start | bytes 4423688 | tf_op jit(solution)/shard_map/ppermute | solution.py:53
  129.0 1.1 copy-start.3
  130.1 7.2 %copy-start.24 = (bf16[16,128]{1,0:T(8,128)(2,1)S(1)}, bf16[16,128]{1,0:T(8,128)(2,1)}, u32[]{:S(2)}) copy-start(bf16[16,128]{1,0:T(8,128)(2,1)} %get-tuple-element.205.table_ref) | copy-start | bytes 12292
  136.7 26.2 %collective-permute-start.26 = (bf16[192,2816]{1,0:T(8,128)(2,1)}, bf16[192,2816]{1,0:T(8,128)(2,1)S(1)}, u32[]{:S(2)}, u32[]{:S(2)}) collective-permute-start(bf16[192,2816]{1,0:T(8,128)(2,1)} %get-tuple-element.226), channel_id=1, source_target_pairs={{0,2},{1,3},{2,0},{3,1},{4,6},{5,7},{6,4},{7,5},{8,10},{9,11},{10,... | collective-permute-start | bytes 3244040 | tf_op jit(solution)/shard_map/ppermute | solution.py:53
  137.3 1.2 collective-permute-start.21
  147.1 23.6 %collective-permute-start.25 = (bf16[208,2304]{1,0:T(8,128)(2,1)}, bf16[208,2304]{1,0:T(8,128)(2,1)S(1)}, u32[]{:S(2)}, u32[]{:S(2)}) collective-permute-start(bf16[208,2304]{1,0:T(8,128)(2,1)} %get-tuple-element.225), channel_id=1, source_target_pairs={{0,8},{1,9},{2,10},{3,11},{4,12},{5,13},{6,14},{7,15},{8,0},{9,1},... | collective-permute-start | bytes 2875400 | tf_op jit(solution)/shard_map/ppermute | solution.py:53
  157.2 43.5 %collective-permute-start.23 = (bf16[512,768]{1,0:T(8,128)(2,1)}, bf16[512,768]{1,0:T(8,128)(2,1)S(1)}, u32[]{:S(2)}, u32[]{:S(2)}) collective-permute-start(bf16[512,768]{1,0:T(8,128)(2,1)} %get-tuple-element.223), channel_id=1, source_target_pairs={{0,4},{1,5},{2,6},{3,7},{4,0},{5,1},{6,2},{7,3},{8,12},{9,13},{10,... | collective-permute-start | bytes 2359304 | tf_op jit(solution)/shard_map/ppermute | solution.py:53
  158.8 36.9 %collective-permute-start.24 = (bf16[192,2176]{1,0:T(8,128)(2,1)}, bf16[192,2176]{1,0:T(8,128)(2,1)S(1)}, u32[]{:S(2)}, u32[]{:S(2)}) collective-permute-start(bf16[192,2176]{1,0:T(8,128)(2,1)} %get-tuple-element.224), channel_id=1, source_target_pairs={{0,4},{1,5},{2,6},{3,7},{4,0},{5,1},{6,2},{7,3},{8,12},{9,13},{10,... | collective-permute-start | bytes 2506760 | tf_op jit(solution)/shard_map/ppermute | solution.py:53
  162.9 1.0 copy-start.4
  166.6 40.9 %collective-permute-start.30 = (bf16[96,2816]{1,0:T(8,128)(2,1)}, bf16[96,2816]{1,0:T(8,128)(2,1)}, u32[]{:S(2)}, u32[]{:S(2)}) collective-permute-start(bf16[96,2816]{1,0:T(8,128)(2,1)} %get-tuple-element.238), channel_id=1, source_target_pairs={{0,4},{1,5},{2,6},{3,7},{4,0},{5,1},{6,2},{7,3},{8,12},{9,13},{10,... | collective-permute-start | bytes 1622024 | tf_op jit(solution)/shard_map/ppermute | solution.py:53
  176.1 41.5 %collective-permute-start.29 = (bf16[112,2304]{1,0:T(8,128)(2,1)S(1)}, bf16[112,2304]{1,0:T(8,128)(2,1)S(1)}, u32[]{:S(2)}, u32[]{:S(2)}) collective-permute-start(bf16[112,2304]{1,0:T(8,128)(2,1)S(1)} %pad_maximum_fusion), channel_id=1, source_target_pairs={{0,4},{1,5},{2,6},{3,7},{4,0},{5,1},{6,2},{7,3},{8,12},{9,13},{10,... | collective-permute-start | bytes 1548296 | tf_op jit(solution)/shard_map/ppermute | solution.py:53
  195.8 1.0 copy-start.5
  196.7 7.8 %copy-start.26 = (f32[4,128]{1,0:T(4,128)S(1)}, f32[4,128]{1,0:T(4,128)}, u32[]{:S(2)}) copy-start(f32[4,128]{1,0:T(4,128)} %get-tuple-element.166) | copy-start | bytes 6148
  199.1 6.0 %copy-start.28 = (bf16[128,1536]{1,0:T(8,128)(2,1)S(1)}, bf16[128,1536]{1,0:T(8,128)(2,1)}, u32[]{:S(2)}) copy-start(bf16[128,1536]{1,0:T(8,128)(2,1)} %get-tuple-element.207) | copy-start | bytes 1179652
  199.2 21.3 %collective-permute-start.28 = (bf16[96,2176]{1,0:T(8,128)(2,1)}, bf16[96,2176]{1,0:T(8,128)(2,1)S(1)}, u32[]{:S(2)}, u32[]{:S(2)}) collective-permute-start(bf16[96,2176]{1,0:T(8,128)(2,1)} %get-tuple-element.236), channel_id=1, source_target_pairs={{0,2},{1,3},{2,0},{3,1},{4,6},{5,7},{6,4},{7,5},{8,10},{9,11},{10,... | collective-permute-start | bytes 1253384 | tf_op jit(solution)/shard_map/ppermute | solution.py:53
  200.7 0.9 copy-start.6
  204.0 19.2 %collective-permute-start.27 = (bf16[256,768]{1,0:T(8,128)(2,1)}, bf16[256,768]{1,0:T(8,128)(2,1)S(1)}, u32[]{:S(2)}, u32[]{:S(2)}) collective-permute-start(bf16[256,768]{1,0:T(8,128)(2,1)} %get-tuple-element.235), channel_id=1, source_target_pairs={{0,2},{1,3},{2,0},{3,1},{4,6},{5,7},{6,4},{7,5},{8,10},{9,11},{10,... | collective-permute-start | bytes 1179656 | tf_op jit(solution)/shard_map/ppermute | solution.py:53
  205.1 21.2 %collective-permute-start.22 = (bf16[128,1536]{1,0:T(8,128)(2,1)S(1)}, bf16[128,1536]{1,0:T(8,128)(2,1)S(1)}, u32[]{:S(2)}, u32[]{:S(2)}) collective-permute-start(bf16[128,1536]{1,0:T(8,128)(2,1)S(1)} %copy-done.28), channel_id=1, source_target_pairs={{0,2},{1,3},{2,0},{3,1},{4,6},{5,7},{6,4},{7,5},{8,10},{9,11},{10,... | collective-permute-start | bytes 1179656 | tf_op jit(solution)/shard_map/ppermute | solution.py:53
  209.5 25.6 %collective-permute-start.32 = (bf16[48,2816]{1,0:T(8,128)(2,1)}, bf16[48,2816]{1,0:T(8,128)(2,1)S(1)}, u32[]{:S(2)}, u32[]{:S(2)}) collective-permute-start(bf16[48,2816]{1,0:T(8,128)(2,1)} %get-tuple-element.250), channel_id=1, source_target_pairs={{0,8},{1,9},{2,10},{3,11},{4,12},{5,13},{6,14},{7,15},{8,0},{9,1},... | collective-permute-start | bytes 811016 | tf_op jit(solution)/shard_map/ppermute | solution.py:53
  220.5 7.3 %copy-start.13 = (bf16[48,2304]{1,0:T(8,128)(2,1)S(1)}, bf16[48,2304]{1,0:T(8,128)(2,1)}, u32[]{:S(2)}) copy-start(bf16[48,2304]{1,0:T(8,128)(2,1)} %get-tuple-element.249) | copy-start | bytes 663556
  220.5 0.8 copy-start.9
  223.2 0.7 copy-start.11
  226.4 3.6 %copy-start.10 = (bf16[128,1536]{1,0:T(8,128)(2,1)}, bf16[128,1536]{1,0:T(8,128)(2,1)S(1)}, u32[]{:S(2)}) copy-start(bf16[128,1536]{1,0:T(8,128)(2,1)S(1)} %collective-permute-done.22.came_ref) | copy-start | bytes 1179652
  226.4 9.4 %collective-permute-start.36 = (bf16[48,2176]{1,0:T(8,128)(2,1)}, bf16[48,2176]{1,0:T(8,128)(2,1)S(1)}, u32[]{:S(2)}, u32[]{:S(2)}) collective-permute-start(bf16[48,2176]{1,0:T(8,128)(2,1)} %get-tuple-element.254), channel_id=1, source_target_pairs={{0,8},{1,9},{2,10},{3,11},{4,12},{5,13},{6,14},{7,15},{8,0},{9,1},... | collective-permute-start | bytes 626696 | tf_op jit(solution)/shard_map/ppermute | solution.py:53
  227.8 7.8 %collective-permute-start.31 = (bf16[64,2304]{1,0:T(8,128)(2,1)S(1)}, bf16[64,2304]{1,0:T(8,128)(2,1)S(1)}, u32[]{:S(2)}, u32[]{:S(2)}) collective-permute-start(bf16[64,2304]{1,0:T(8,128)(2,1)S(1)} %pad_maximum_fusion.1), channel_id=1, source_target_pairs={{0,2},{1,3},{2,0},{3,1},{4,6},{5,7},{6,4},{7,5},{8,10},{9,11},{10,... | collective-permute-start | bytes 884744 | tf_op jit(solution)/shard_map/ppermute | solution.py:53
  229.4 9.8 %collective-permute-start.35 = (bf16[128,768]{1,0:T(8,128)(2,1)}, bf16[128,768]{1,0:T(8,128)(2,1)S(1)}, u32[]{:S(2)}, u32[]{:S(2)}) collective-permute-start(bf16[128,768]{1,0:T(8,128)(2,1)} %get-tuple-element.253), channel_id=1, source_target_pairs={{0,8},{1,9},{2,10},{3,11},{4,12},{5,13},{6,14},{7,15},{8,0},{9,1},... | collective-permute-start | bytes 589832 | tf_op jit(solution)/shard_map/ppermute | solution.py:53
  230.0 5.2 %copy-start.12 = (bf16[48,2816]{1,0:T(8,128)(2,1)S(1)}, bf16[48,2816]{1,0:T(8,128)(2,1)}, u32[]{:S(2)}) copy-start(bf16[48,2816]{1,0:T(8,128)(2,1)} %get-tuple-element.240) | copy-start | bytes 811012
  230.0 5.7 %copy-start.14 = (bf16[48,2304]{1,0:T(8,128)(2,1)S(1)}, bf16[48,2304]{1,0:T(8,128)(2,1)}, u32[]{:S(2)}) copy-start(bf16[48,2304]{1,0:T(8,128)(2,1)} %get-tuple-element.242) | copy-start | bytes 663556
  235.1 0.9 copy-start.15
  235.2 15.7 %collective-permute-start.34 = (bf16[24,2816]{1,0:T(8,128)(2,1)S(1)}, bf16[24,2816]{1,0:T(8,128)(2,1)S(1)}, u32[]{:S(2)}, u32[]{:S(2)}) collective-permute-start(bf16[24,2816]{1,0:T(8,128)(2,1)S(1)} %get-tuple-element.279), channel_id=1, source_target_pairs={{0,16},{1,17},{2,18},{3,19},{4,20},{5,21},{6,22},{7,23},{8,24},{9,... | collective-permute-start | bytes 405512 | tf_op jit(solution)/shard_map/ppermute | solution.py:53
  236.1 22.1 %collective-permute-start.37 = (bf16[24,2176]{1,0:T(8,128)(2,1)S(1)}, bf16[24,2176]{1,0:T(8,128)(2,1)S(1)}, u32[]{:S(2)}, u32[]{:S(2)}) collective-permute-start(bf16[24,2176]{1,0:T(8,128)(2,1)S(1)} %get-tuple-element.287), channel_id=1, source_target_pairs={{0,16},{1,17},{2,18},{3,19},{4,20},{5,21},{6,22},{7,23},{8,24},{9,... | collective-permute-start | bytes 313352 | tf_op jit(solution)/shard_map/ppermute | solution.py:53
  238.5 19.7 %collective-permute-start.33 = (bf16[40,2304]{1,0:T(8,128)(2,1)S(1)}, bf16[40,2304]{1,0:T(8,128)(2,1)S(1)}, u32[]{:S(2)}, u32[]{:S(2)}) collective-permute-start(bf16[40,2304]{1,0:T(8,128)(2,1)S(1)} %pad_maximum_fusion.2), channel_id=1, source_target_pairs={{0,16},{1,17},{2,18},{3,19},{4,20},{5,21},{6,22},{7,23},{8,24},{9,... | collective-permute-start | bytes 552968 | tf_op jit(solution)/shard_map/ppermute | solution.py:53
  251.0 12.8 %copy-start.20 = (bf16[64,768]{1,0:T(8,128)(2,1)S(1)}, bf16[64,768]{1,0:T(8,128)(2,1)}, u32[]{:S(2)}) copy-start(bf16[64,768]{1,0:T(8,128)(2,1)} %get-tuple-element.257) | copy-start | bytes 294916
  251.6 12.1 %collective-permute-start.38 = (bf16[64,768]{1,0:T(8,128)(2,1)}, bf16[64,768]{1,0:T(8,128)(2,1)S(1)}, u32[]{:S(2)}, u32[]{:S(2)}) collective-permute-start(bf16[64,768]{1,0:T(8,128)(2,1)} %get-tuple-element.261), channel_id=1, source_target_pairs={{0,16},{1,17},{2,18},{3,19},{4,20},{5,21},{6,22},{7,23},{8,24},{9,... | collective-permute-start | bytes 294920 | tf_op jit(solution)/shard_map/ppermute | solution.py:53
  (4 other events, 2.6 us)

commit v4 on v3

--- a/solution.py
+++ b/solution.py
@@ -10,6 +10,8 @@
 BUCKETS = 32
 LANES = 128
 CHUNK = 512
+VM = (60, 34, 24, 16, 8)
+COST = 1.1e9
 
 epsilon = 1e-06
 contrastive_sharpness_factor = 0.01
@@ -81,15 +83,33 @@
     sent_out[...] = add(kept_ref[half:, :], came_ref[half:, :]).astype(bf16)
 
 
-def cut(kept, came):
-    half = kept.shape[0] // 2
+def cut_loaded_kernel(kept_ref, came_ref, small_ref, kept_out, sent_out, small_out):
+    half = kept_out.shape[0]
+    kept_out[...] = add(kept_ref[:half, :], came_ref[:half, :]).astype(bf16)
+    sent_out[:half, :] = add(kept_ref[half:, :], came_ref[half : 2 * half, :]).astype(bf16)
+    small = add(small_ref[...], came_ref[2 * half :, :]).astype(bf16)
+    sent_out[half:, :] = small
+    small_out[...] = small
+
+
+def cut(kept, came, small=None):
+    half, cols = kept.shape[0] // 2, kept.shape[1]
+    if half % 16 == 0 and small is None:
+        return *call(cut_kernel, [shape((half, cols), bf16)] * 2, [kept, came], vmem=VM[4], us=0), None
     if half % 16 == 0:
-        return call(cut_kernel, [shape((half, kept.shape[1]), bf16)] * 2, [kept, came])
-    return add(kept[:half], came[:half]).astype(bf16), add(kept[half:], came[half:]).astype(bf16)
-
-
-def call(kernel, outs, args, spaces="", scratch=(), flops=0):
-    kinds = {"s": pltpu.SMEM, "v": pltpu.VMEM, "a": pl.ANY}
+        outs = [shape((half, cols), bf16), shape((half + 16, cols), bf16), shape((16, cols), bf16)]
+        return call(cut_loaded_kernel, outs, [kept, came, small], vmem=VM[4], us=0)
+    if small is not None:
+        small = add(small, came[-16:]).astype(bf16)
+        came = came[:-16]
+    next_sent = add(kept[half:], came[half:]).astype(bf16)
+    if small is not None:
+        next_sent = jnp.concatenate([next_sent, small], 0)
+    return add(kept[:half], came[:half]).astype(bf16), next_sent, small
+
+
+def call(kernel, outs, args, spaces="", scratch=(), vmem=None, us=3, wide=False):
+    kinds = {"s": pltpu.SMEM, "v": pltpu.VMEM, "a": pl.ANY, "h": pltpu.HBM}
     spaces = spaces.ljust(len(args) + len(outs), "v")
     specs = [pl.BlockSpec(memory_space=kinds[kind]) for kind in spaces]
     return pl.pallas_call(
@@ -98,8 +118,8 @@
         in_specs=specs[: len(args)],
         out_specs=tuple(specs[len(args) :]),
         scratch_shapes=list(scratch),
-        compiler_params=pltpu.CompilerParams(vmem_limit_bytes=60 * 1024 * 1024),
-        cost_estimate=pl.CostEstimate(flops=flops, bytes_accessed=0, transcendentals=0),
+        compiler_params=pltpu.CompilerParams(vmem_limit_bytes=(60 if wide else vmem or VM[3]) * 1024 * 1024),
+        cost_estimate=pl.CostEstimate(flops=int(us * COST), bytes_accessed=0, transcendentals=0),
     )(*args)
 
 
@@ -537,54 +557,40 @@
     return total
 
 
-def slot_back_kernel(
-    slots, rank_ref, queries_ref, grad_unit_ref, embed_ref, after_feed_ref, after_attend_ref, gate_slope_ref,
-    up_slope_ref, query_ref, key_ref, value_ref, probs_ref, attend_gain_ref, feed_gain_ref, final_gain_ref,
-    wp_any, wd_any, wg_any, wu_any, wo_any, wq_any, wk_any, wv_any,
-    grads_out, tokens_out, table_out,
-    wp_ref, wd_ref, wg_ref, wu_ref, wo_ref, wq_ref, wk_ref, wv_ref, slot_ref, after_ref, mixed_ref, more_ref, sums_ref,
-    load_sems, slot_sem,
+def slot_feed_kernel(
+    grad_unit_ref, embed_ref, after_feed_ref, after_attend_ref, gate_slope_ref, up_slope_ref, feed_gain_ref,
+    final_gain_ref, wp_any, wd_any, wg_any, wu_any, wo_any,
+    grads_out, after_out, mixed_out,
+    wp_ref, wd_ref, wg_ref, wu_ref, wo_ref, more_ref, load_sems,
 ):
     weights = loads(
-        (wp_any, wd_any, wg_any, wu_any, wo_any, wq_any, wk_any, wv_any),
-        (wp_ref, wd_ref, wg_ref, wu_ref, wo_ref, wq_ref, wk_ref, wv_ref),
-        load_sems,
+        (wp_any, wd_any, wg_any, wu_any, wo_any), (wp_ref, wd_ref, wg_ref, wu_ref, wo_ref), load_sems
     )
     for weight in weights:
         weight.start()
-    narrow_size = queries_ref.shape[0] // slots
-    first = (rank_ref[0] & (narrow_size - 1)) * slots
-    load_slots = pltpu.make_async_copy(queries_ref.at[pl.ds(first, slots)], slot_ref, slot_sem)
-    load_slots.start()
-    rows, width = after_ref.shape
-    part = slice(0, rows)
     feed_back(
-        part, weights[:5], grad_unit_ref[...], embed_ref, after_feed_ref, after_attend_ref, gate_slope_ref,
-        up_slope_ref, feed_gain_ref, final_gain_ref, wo_ref, wg_ref, wu_ref, wd_ref, wp_ref, grads_out, after_ref,
-        mixed_ref, more_ref,
-    )
-    start = grads_out.shape[1] - 3 * width
-
-    def third(place):
-        return grads_out.at[:, start + place * width : start + (place + 1) * width]
+        slice(0, after_out.shape[0]), weights, grad_unit_ref[...], embed_ref, after_feed_ref, after_attend_ref,
+        gate_slope_ref, up_slope_ref, feed_gain_ref, final_gain_ref, wo_ref, wg_ref, wu_ref, wd_ref, wp_ref, grads_out,
+        after_out, mixed_out, more_ref,
+    )
+
+
+def slot_attend_kernel(
+    query_ref, key_ref, value_ref, probs_ref, mixed_ref, grads_out, table_out, sums_ref
+):
+    rows, width = mixed_ref.shape
 
     def out(place):
         def store(values, pair):
-            grads_out[:, pl.ds(pl.multiple_of(start + place * width + pair * LANES, LANES), LANES)] = values
+            grads_out[:, pl.ds(pl.multiple_of(place * width + pair * LANES, LANES), LANES)] = values
 
         return store
 
+    part = slice(0, rows)
     attend_back(
         (), part, part, query_ref, key_ref, value_ref, probs_ref, mixed_ref, out(0), out(1), out(2), sums_ref
     )
     table_out[...] = table_sums(sums_ref, [0])
-    for weight in weights[5:]:
-        weight.wait()
-    load_slots.wait()
-    tokens_out[...] = input_back(
-        slot_ref[...].reshape(rows, width).astype(f32), attend_gain_ref, after_ref, third(0)[...], third(1)[...],
-        third(2)[...], wq_ref, wk_ref, wv_ref,
-    )
 
 
 def doc_feed_kernel(came, *refs):
@@ -766,10 +772,9 @@
     width = slot_room.shape[1] // 3
     half = doc_ref.shape[1]
     length = doc_ref.shape[0]
-    start = slot_any.shape[1] - 3 * width
     lanes = slice(kept_any.shape[1] - half, kept_any.shape[1])
     copies = loads(
-        (slot_any.at[:, start:], slot_came_any.at[:, start:], kept_any.at[:rows, lanes], came_any.at[:rows, lanes]),
+        (slot_any, slot_came_any, kept_any.at[:rows, lanes], came_any.at[:rows, lanes]),
         (slot_room, slot_came_room, left_ref.at[length : length + rows, :], left_ref.at[length + rows :, :]),
         sems,
     )
@@ -800,15 +805,26 @@
     sent_out[tail:, :LANES] = add(table_ref[...], other_table_ref[...]).astype(bf16)
 
 
-def doc_input_kernel(
-    tokens_ref, gain_ref, after_ref, grads_ref, kept_ref, came_ref, wq_ref, wk_ref, wv_ref, tokens_out
+def input_kernel(
+    slots, rank_ref, tokens_ref, gain_ref, after_ref, grads_ref, kept_ref, came_ref, queries_any, slot_after_ref,
+    slot_grads_ref, wq_ref, wk_ref, wv_ref, tokens_out, queries_out, slot_room, sem,
 ):
-    width = tokens_ref.shape[1]
-    rest = grads_ref.shape[0] - tokens_ref.shape[0] // 2
+    narrow_size = queries_any.shape[0] // slots
+    first = (rank_ref[0] & (narrow_size - 1)) * slots
+    load = pltpu.make_async_copy(queries_any.at[pl.ds(first, slots)], slot_room, sem)
+    load.start()
+    rows, width = tokens_ref.shape
+    rest = grads_ref.shape[0] - rows // 2
     query = jnp.concatenate([grads_ref[rest:, :width], grads_ref[rest:, width:]], 0)
     pair = add(kept_ref[...], came_ref[...]).astype(bf16)
     tokens_out[...] = input_back(
         tokens_ref[...].astype(f32), gain_ref, after_ref, query, pair[:, :width], pair[:, width:], wq_ref, wk_ref, wv_ref
+    )
+    load.wait()
+    query, key, value = (slot_grads_ref[:, place * width : (place + 1) * width] for place in range(3))
+    queries_out[...] = input_back(
+        slot_room[...].reshape(queries_out.shape).astype(f32), gain_ref, slot_after_ref, query, key, value, wq_ref,
+        wk_ref, wv_ref,
     )
 
 
@@ -835,11 +851,9 @@
     assert columns == LANES and doc_total <= LANES and blocks == 1 << bits
     gains = (attend_gain, feed_gain, final_gain)
     dma = pltpu.SemaphoreType.DMA
-    over_y = [1, 2] + list(range(3, bits))
-    over_x = [2, 1] + list(range(3, bits))
-    over_z = [bits - 2, 2, 1] + list(range(3, bits - 2)) + [bits - 1]
-
-    orders = (over_y, over_x, over_x, over_z)
+    waxes = list(range(3, bits))
+
+    orders = ([1, 2] + waxes, waxes[:1] + [1, 2] + waxes[1:], [1] + waxes[:1] + [2] + waxes[1:], [2] + waxes[:1] + [1] + waxes[1:])
     own_tokens = doc_tokens[0]
     y_tokens = swap(own_tokens, 2)
     core_tokens = swap(own_tokens, 1)
@@ -888,10 +902,12 @@
             rank_word, query_lengths, query_tokens, own_tokens, core_tokens, y_tokens, both_tokens, doc_bias, slot_bias,
             *gains, *weights,
         ],
-        "ssa" + "v" * 9 + "a" * 8 + "a" * len(forward_shapes),
+        "ssa" + "v" * 9 + "h" * 8 + "a" * len(forward_shapes),
         [room(value) for value in forward_shapes]
         + [room(weight) for weight in weights]
         + [slot_room, dma((8,)), dma((len(forward_shapes),)), dma],
+        vmem=VM[0],
+        us=18,
     )
 
     phases = [list(range(high, max(high - 2, 0), -1)) for high in range(bits - 1, 0, -2)]
@@ -913,6 +929,8 @@
                     pltpu.VMEM((blocks * slot_rows, LANES), f32),
                     dma,
                 ],
+                us=5,
+                wide=bits > 5,
             )
             came = after(came, tally)
         if phase == 1:
@@ -922,6 +940,8 @@
                 [shape((rows, turned_cols), bf16)] * 2 + [shape((doc_length, width // 2), bf16)],
                 after([rank_word, all_normed, normed_feed, mixed, normed_final, hidden], near_units),
                 "s",
+                us=5,
+                wide=bits > 5,
             )
             came = after(came, turned)
         near_units = jnp.concatenate([near_units] + came, 0)
@@ -945,16 +965,17 @@
             pltpu.VMEM((doc_total, slot_rows, columns), f32),
             pltpu.VMEM((doc_total, columns, slot_rows), bf16),
         ],
+        wide=bits > 5,
     )
     turned_came = swap(after(turned_sent, losses), 1)
     back_weights = [proj_weight, down_weight, gate_weight, up_weight, output_weight]
-    all_weights = back_weights + [query_weight, key_weight, value_weight]
     doc_cols = 2 * units + 2 * width + columns
 
     came = [swap(sent, 1)]
     rest = order[1:]
     parts = [kept]
-    first_phase = True
+    phase = 0
+    feed_shapes = [shape((LANES, doc_cols), bf16), shape((LANES, width)), shape((LANES, width), bf16)]
     while rest:
         group, rest = rest[:2], rest[2:]
         count = 1 << len(group)
@@ -966,40 +987,50 @@
         masks = [scatter_order(place, group) for place in range(count)]
         came = [swap(piece, mask) for piece, mask in zip(pieces[1:], masks[1:])]
         parts = [pieces[0]]
-        if first_phase:
-            slot_grads, query_grad, slot_table = call(
-                functools.partial(slot_back_kernel, slots),
-                [shape((slot_rows, doc_cols + 3 * width), bf16), shape((slot_rows, width)), shape((heads, LANES))],
-                [rank_word, query_tokens, after(grad_slot_unit, pieces[1], turned_came)]
-                + [embed, after_feed, after_attend, gate_slope, up_slope, query, key, value, slot_probs, *gains]
-                + all_weights,
-                "sa" + "v" * 13 + "a" * 8,
-                [room(weight) for weight in all_weights]
-                + [slot_room, pltpu.VMEM((slot_rows, width), f32), pltpu.VMEM((slot_rows, width), bf16)]
-                + [pltpu.VMEM((slot_rows, width), f32)]
-                + [pltpu.VMEM((heads * 8, 2 * LANES), f32), dma((8,)), dma],
+        if phase == 0:
+            slot_grads, slot_after, slot_mixed = call(
+                slot_feed_kernel,
+                feed_shapes,
+                [after(grad_slot_unit, pieces[1], turned_came)]
+                + [embed, after_feed, after_attend, gate_slope, up_slope, gains[1], gains[2]]
+                + back_weights,
+                "v" * 8 + "a" * 5,
+                [room(weight) for weight in back_weights] + [pltpu.VMEM((slot_rows, width), f32), dma((5,))],
+                vmem=VM[1],
+                us=7,
+            )
+            came = after(came, slot_after)
+        if phase == 1:
+            slot_came = swap(after(slot_grads, *pieces[1:]), 1)
+            slot_thirds, slot_table = call(
+                slot_attend_kernel,
+                [shape((slot_rows, 3 * width), bf16), shape((heads, LANES))],
+                [query, key, value, slot_probs, after(slot_mixed, *pieces[1:])],
+                scratch=[pltpu.VMEM((heads * 8, 2 * LANES), f32)],
+                us=4,
             )
             came = after(came, slot_table)
-            first_phase = False
-    slot_came = swap(after(slot_grads, *pieces[1:]), 1)
+        phase += 1
 
     doc_grads, doc_after, doc_mixed = call(
         functools.partial(doc_feed_kernel, 1 + len(came)),
-        [shape((doc_rows, doc_cols), bf16), shape((doc_rows, width)), shape((doc_rows, width), bf16)],
+        feed_shapes,
         parts + after(came, slot_came)
         + [embed, after_feed, after_attend, gate_slope, up_slope, gains[1], gains[2]]
         + back_weights,
         "v" * (8 + len(came)) + "a" * 5,
         [room(weight) for weight in back_weights] + [pltpu.VMEM((doc_rows, width), f32), dma((5,))],
-    )
+        vmem=VM[2],
+        us=7,
+    )
+    thirds_came = swap(after(slot_thirds, doc_after), 1)
     doc_came = swap(doc_grads, 1)
 
     class Stream:
         def __init__(self, kept, sent, order):
             self.kept, self.order, self.step = kept, order, 0
             self.loaded = sent.shape[0] > kept.shape[0]
-            if self.loaded:
-                self.small = sent[-16:]
+            self.small = sent[-16:] if self.loaded else None
             self.send(sent)
 
         def send(self, sent):
@@ -1008,15 +1039,13 @@
 
         def advance(self, *wait):
             came = after(self.came, *wait)
-            if self.loaded:
-                self.small = add(self.small, came[-16:]).astype(bf16)
-                came = came[:-16]
             if self.step == len(self.order):
+                if self.loaded:
+                    self.small = add(self.small, came[-16:]).astype(bf16)
+                    came = came[:-16]
                 self.result = add(self.kept, came)
                 return self.result
-            self.kept, sent = cut(self.kept, came)
-            if self.loaded:
-                sent = jnp.concatenate([sent, self.small], 0)
+            self.kept, sent, self.small = cut(self.kept, came, self.small)
             self.send(sent)
             return self.kept
 
@@ -1054,7 +1083,7 @@
             shape((doc_rows, 2 * width), bf16),
             shape((doc_rows, 2 * width), bf16),
         ],
-        [turned_docs, turned, turned_came, slot_grads, slot_came, att_grads, att_came, after(table, first.kept), table_came],
+        [turned_docs, turned, turned_came, slot_thirds, thirds_came, att_grads, att_came, after(table, first.kept), table_came],
         "vaaaa",
         [
             pltpu.VMEM((slot_rows, 3 * width), bf16),
@@ -1072,17 +1101,21 @@
         fourth_kept,
     )
     third = weight_product([(4 * small_half, units // 2, 2 * units, width)], orders[2], second.kept)
-    pair_came = swap(pair_sent, 2)
     done = third.kept
     for step in range(bits - 1):
         for stream in (first, fourth, second, third):
             done = stream.advance(done)
-        if step == 1:
-            (doc_grad,) = call(
-                doc_input_kernel,
-                [shape((doc_rows, width))],
-                [own_tokens, gains[0], doc_after, att_grads, pair_kept, after(pair_came, done)]
-                + [query_weight, key_weight, value_weight],
+        if step == 0:
+            pair_came = swap(after(pair_sent, done), 2)
+        if step == 2:
+            doc_grad, query_grad = call(
+                functools.partial(input_kernel, slots),
+                [shape((doc_rows, width)), shape((slot_rows, width))],
+                [rank_word, own_tokens, gains[0], doc_after, att_grads, pair_kept, after(pair_came, done)]
+                + [query_tokens, slot_after, slot_thirds, query_weight, key_weight, value_weight],
+                "s" + "v" * 6 + "a",
+                [slot_room, dma],
+                us=4,
             )
             done = doc_grad
 

time: 268 us -> 187 us (0.70)
  Pallas kernels: 132 us -> 79.4 us
  waiting for transfers between devices: 66 us -> 46.5 us
  other arithmetic: 13.8 us -> 7.54 us
  local copies, waits for them, and re-layouts: 14.6 us -> 11.5 us
    pallas_call x22 -> x23, Pallas kernels: 132 us -> 79.4 us  [call(): pl.pallas_call(kernel, out_shape=tuple(outs), in_specs=specs[:len(args)],...]
    ppermute x39 -> x40, waiting for transfers between devices: 66 us -> 46.5 us  [swap(): return lax.ppermute(values, ('wide', 'narrow'), pairs)]
    unnamed x65 -> x105, local copies, waits for them, and re-layouts: 11.5 us -> 10.2 us
    ppermute x39 -> x40, starting transfers between devices: 39.2 us -> 39.9 us  [swap(): return lax.ppermute(values, ('wide', 'narrow'), pairs)]
  transfers between devices with their start and end apart: 39 -> 40, of which waited for: 16 -> 14; matrix products, arithmetic and copies ran while one was open for 5% -> 4% of each run, Pallas kernels for 33% -> 27%
where the time goes in v4:
time: 187 us; the launch traced here: 186 us
  Pallas kernels  79.4 us (42%)
  waiting for transfers between devices  46.5 us (25%)
  starting transfers between devices  39.9 us (21%)
  local copies, waits for them, and re-layouts  11.5 us (6%)
  other arithmetic  7.54 us (4%)
    pallas_call x23, Pallas kernels, call(): pl.pallas_call(kernel, out_shape=tuple(outs), in_specs=specs[:len(args)],...  79.4 us
    ppermute x40, waiting for transfers between devices, swap(): return lax.ppermute(values, ('wide', 'narrow'), pairs)  46.5 us
    ppermute x40, starting transfers between devices, swap(): return lax.ppermute(values, ('wide', 'narrow'), pairs)  39.9 us
    unnamed x105, local copies, waits for them, and re-layouts  10.2 us
  transfers between devices with their start and end apart: 40, of which 14 were waited for; matrix products, arithmetic and copies ran while one was open for 4% of the time, Pallas kernels for 27%

profile of v4, /device:TPU:0, one launch (start us, length us, event | category | flops | bytes accessed | tf_op | source)
XLA Modules:
  0.0 186.4 jit_solution(15315055600795942107)
XLA Ops:
  1.2 2.6 %collective-permute-start.1 = (bf16[128,768]{1,0:T(8,128)(2,1)}, bf16[128,768]{1,0:T(8,128)(2,1)S(1)}, u32[]{:S(2)}, u32[]{:S(2)}) collective-permute-start(bf16[128,768]{1,0:T(8,128)(2,1)} %bitcast.9), channel_id=1, source_target_pairs={{0,2},{1,3},{2,0},{3,1},{4,6},{5,7},{6,4},{7,5},{8,10},{9,11},{10,... | collective-permute-start | bytes 589832 | tf_op jit(solution)/shard_map/ppermute | solution.py:55
  3.8 0.8 copy.33.table_ref
  4.5 2.7 %shard_map.280 = (f32[6,256,512]{2,1,0:T(8,128)S(1)}, f32[6,256,128]{2,1,0:T(8,128)S(1)}) custom-call(s32[1]{0:T(128)} %bitcast.rank_ref, f32[32,12]{1,0:T(8,128)S(1)} %copy.33.table_ref), custom_call_target="tpu_custom_call" | custom-call | flops 3300000000 | tf_op jit(solution)/shard_map/pallas_call | solution.py:115
  7.3 1.6 copy-done.24
  8.9 0.9 copy-done.34
  10.0 1.3 collective-permute-done.2.last_ref
  11.9 18.8 %shard_map.281 = (bf16[640,768]{1,0:T(8,128)(2,1)}, bf16[256,768]{1,0:T(8,128)(2,1)}, bf16[640,768]{1,0:T(8,128)(2,1)}, bf16[640,768]{1,0:T(8,128)(2,1)}, bf16[6...) custom-call(s32[1]{0:T(128)} %bitcast.rank_ref, ...), custom_call_target="tpu_custom_call" | custom-call | flops 19800000512 | tf_op jit(solution)/shard_map/pallas_call | solution.py:115
  30.8 1.6 collective-permute-start.3
  32.4 2.6 %collective-permute-start.4 = (bf16[1,128,128]{2,1,0:T(8,128)(2,1)}, bf16[1,128,128]{2,1,0:T(8,128)(2,1)S(1)}, u32[]{:S(2)}, u32[]{:S(2)}) collective-permute-start(bf16[1,128,128]{2,1,0:T(8,128)(2,1)} %bitcast.13), channel_id=1, source_target_pairs={{0,16},{1,17},{2,18},{3,19},{4,20},{5,21},{6,22},{7,23},{8,24},{9,... | collective-permute-start | bytes 98312 | tf_op jit(solution)/shard_map/ppermute | solution.py:55
  35.2 4.8 %shard_map.282 = (bf16[32,128,128]{2,1,0:T(8,128)(2,1)S(1)}, f32[128,128]{1,0:T(8,128)S(1)}) custom-call(s32[1]{0:T(128)} %bitcast.rank_ref, s32[16,32,128]{2,1,0:T(8,128)S(1)} %copy-done.17), custom_call_target="tpu_custom_call" | custom-call | flops 5500000256 | tf_op jit(solution)/shard_map/pallas_call | solution.py:115
  40.1 0.8 collective-permute-done.5
  40.9 1.5 collective-permute-start.6
  42.4 1.5 collective-permute-start.7
  44.6 4.9 %shard_map.283 = (bf16[256,2944]{1,0:T(8,128)(2,1)S(1)}, bf16[256,2944]{1,0:T(8,128)(2,1)S(1)}, bf16[512,384]{1,0:T(8,128)(2,1)S(1)}) custom-call(s32[1]{0:T(128)} %bitcast.rank_ref, bf16[640,768]{1,0:T(8,128)(2,1)S(1)} %copy-done.38, bf16[256,768]{1,0:T(8,128)(2,1)S(1)} %copy-done.41, bf16[256,768]{1,0:T(8,128)(2,1)S(1)} %copy-done.40, ...), custom_call_target="tpu_custom_call" | custom-call | flops 5500000256 | tf_op jit(solution)/shard_map/pallas_call | solution.py:115
  49.9 1.9 %collective-permute-done.9.far_ref = bf16[16,128,128]{2,1,0:T(8,128)(2,1)S(1)} collective-permute-done((bf16[16,128,128]{2,1,0:T(8,128)(2,1)S(1)}, bf16[16,128,128]{2,1,0:T(8,128)(2,1)S(1)}, u32[]{:S(2)}, u32[]{:S(2)}) %collective-permute-start.9) | collective-permute-done | bytes 524320 | tf_op jit(solution)/shard_map/ppermute | solution.py:55
  51.9 3.2 %shard_map.284 = (f32[4,128]{1,0:T(4,128)S(1)}, f32[128,128]{1,0:T(8,128)S(1)}, bf16[16,128,128]{2,1,0:T(8,128)(2,1)S(1)}, bf16[16,128,128]{2,1,0:T(8,128)(2,1)S(1)}) custom-call(s32[1]{0:T(128)} %bitcast.rank_ref, s32[16]{0:T(128)S(1)} %copy-done.19, s32[16]{0:T(128)S(1)} %copy-done.20, bf16[32,128,128]{2,1,0:T(8,128)(2,1)S(1)} %get-tuple-element.157.counts_ref, ...), custom_call_target="tpu_custom_call" | custom-call | flops 3300000000 | tf_op jit(solution)/shard_map/pallas_call | solution.py:115
  55.8 3.6 %collective-permute-done.10 = bf16[16,128,128]{2,1,0:T(8,128)(2,1)S(1)} collective-permute-done((bf16[16,128,128]{2,1,0:T(8,128)(2,1)S(1)}, bf16[16,128,128]{2,1,0:T(8,128)(2,1)S(1)}, u32[]{:S(2)}, u32[]{:S(2)}) %collective-permute-start.10) | collective-permute-done | bytes 524320 | tf_op jit(solution)/shard_map/ppermute | solution.py:55
  59.5 1.3 collective-permute-start.11
  60.8 1.4 collective-permute-start.12
  62.2 0.8 collective-permute-start.13
  63.2 6.8 %shard_map.285 = (bf16[128,5760]{1,0:T(8,128)(2,1)S(1)}, f32[128,768]{1,0:T(8,128)S(1)}, bf16[128,768]{1,0:T(8,128)(2,1)S(1)}) custom-call(f32[128,128]{1,0:T(8,128)S(1)} %get-tuple-element.184.grad_unit_ref, f32[256,128]{1,0:T(8,128)S(1)} %copy-done.43, f32[256,768]{1,0:T(8,128)S(1)} %copy-done.36, f32[256,768]{1,0:T(8,128)S(1)} %copy-done.35, ...), custom_call_target="tpu_custom_call" | custom-call | flops 7699999744 | tf_op jit(solution)/shard_map/pallas_call | solution.py:115
  70.2 1.5 collective-permute-start.15
  71.6 2.5 %collective-permute-start.16 = (bf16[1,128,128]{2,1,0:T(8,128)(2,1)S(1)}, bf16[1,128,128]{2,1,0:T(8,128)(2,1)S(1)}, u32[]{:S(2)}, u32[]{:S(2)}) collective-permute-start(bf16[1,128,128]{2,1,0:T(8,128)(2,1)S(1)} %get-tuple-element.306), channel_id=1, source_target_pairs={{0,8},{1,9},{2,10},{3,11},{4,12},{5,13},{6,14},{7,15},{8,0},{9,1},... | collective-permute-start | bytes 98312 | tf_op jit(solution)/shard_map/ppermute | solution.py:55
  74.7 3.7 %shard_map.286 = (bf16[128,2304]{1,0:T(8,128)(2,1)S(1)}, f32[12,128]{1,0:T(8,128)S(1)}) custom-call(bf16[256,768]{1,0:T(8,128)(2,1)S(1)} %copy-done.31, bf16[640,768]{1,0:T(8,128)(2,1)S(1)} %copy-done.25, bf16[640,768]{1,0:T(8,128)(2,1)S(1)} %copy-done.26, bf16[6,256,128]{2,1,0:T(8,128)(2,1)S(1)} %copy-done.39, bf16[128,768]{1,0:T(8,128)(2,1)S(1)} %get-tuple-element.199.mixed_ref), custom_call_target="tpu_custom_call" | custom-call | flops 4400000000 | tf_op jit(solution)/shard_map/pallas_call | solution.py:115
  78.4 1.4 collective-permute-done.17.refs_3_
  79.9 6.7 %shard_map.287 = (bf16[128,5760]{1,0:T(8,128)(2,1)S(1)}, f32[128,768]{1,0:T(8,128)S(1)}, bf16[128,768]{1,0:T(8,128)(2,1)S(1)}) custom-call(bf16[1,128,128]{2,1,0:T(8,128)(2,1)S(1)} %get-tuple-element.308.refs_0_, bf16[1,128,128]{2,1,0:T(8,128)(2,1)S(1)} %collective-permute-done.15.refs_1_, bf16[1,128,128]{2,1,0:T(8,128)(2,1)S(1)} %collective-permute-done.16.refs_2_, ...), custom_call_target="tpu_custom_call" | custom-call | flops 7699999744 | tf_op jit(solution)/shard_map/pallas_call | solution.py:115
  86.7 5.6 %shard_map.288 = (bf16[576,1536]{1,0:T(8,128)(2,1)S(1)}, bf16[16,128]{1,0:T(8,128)(2,1)S(1)}) custom-call(s32[1]{0:T(128)} %bitcast.rank_ref, bf16[256,768]{1,0:T(8,128)(2,1)S(1)} %copy-done.31, bf16[640,768]{1,0:T(8,128)(2,1)S(1)} %copy-done.25, bf16[640,768]{1,0:T(8,128)(2,1)S(1)} %copy-done.26, bf16[6,256,512]{2,1,0:T(8,128)(2,1)S(1)} %copy-done.21, ...), custom_call_target="tpu_custom_call" | custom-call | flops 3300000000 | tf_op jit(solution)/shard_map/pallas_call | solution.py:115
  93.3 4.0 %shard_map.289 = (bf16[192,2816]{1,0:T(8,128)(2,1)S(1)}, bf16[192,2816]{1,0:T(8,128)(2,1)S(1)}) custom-call(bf16[256,2944]{1,0:T(8,128)(2,1)S(1)} %get-tuple-element.236.kept_any, bf16[256,2944]{1,0:T(8,128)(2,1)S(1)} %collective-permute-done.14.came_any, bf16[128,5760]{1,0:T(8,128)(2,1)S(1)} %get-tuple-element.238.slot_any, ...), custom_call_target="tpu_custom_call" | custom-call | flops 3300000000 | tf_op jit(solution)/shard_map/pallas_call | solution.py:115
  97.3 0.9 collective-permute-start.26
  98.2 4.5 %shard_map.290 = (bf16[192,2304]{1,0:T(8,128)(2,1)S(1)}, bf16[208,2304]{1,0:T(8,128)(2,1)S(1)}, bf16[128,1536]{1,0:T(8,128)(2,1)S(1)}, bf16[128,1536]{1,0:T(8,128)(2,1)S(1)}) custom-call(bf16[512,384]{1,0:T(8,128)(2,1)S(1)} %get-tuple-element.213.doc_ref, bf16[256,2944]{1,0:T(8,128)(2,1)S(1)} %get-tuple-element.236.kept_any, ...), custom_call_target="tpu_custom_call" | custom-call | flops 3300000000 | tf_op jit(solution)/shard_map/pallas_call | solution.py:115
  102.7 0.7 copy-done.22
  103.5 3.2 %shard_map.291 = (bf16[192,2176]{1,0:T(8,128)(2,1)S(1)}, bf16[192,2176]{1,0:T(8,128)(2,1)S(1)}) custom-call(bf16[256,2944]{1,0:T(8,128)(2,1)S(1)} %get-tuple-element.236.kept_any, bf16[256,2944]{1,0:T(8,128)(2,1)S(1)} %collective-permute-done.14.came_any, bf16[128,5760]{1,0:T(8,128)(2,1)S(1)} %get-tuple-element.238.slot_any, ...), custom_call_target="tpu_custom_call" | custom-call | flops 3300000000 | tf_op jit(solution)/shard_map/pallas_call | solution.py:115
  106.8 1.6 collective-permute-start.25
  108.4 1.8 shard_map.292
  110.9 13.2 %collective-permute-done.26.came_ref = bf16[192,2816]{1,0:T(8,128)(2,1)S(1)} collective-permute-done((bf16[192,2816]{1,0:T(8,128)(2,1)S(1)}, bf16[192,2816]{1,0:T(8,128)(2,1)S(1)}, u32[]{:S(2)}, u32[]{:S(2)}) %collective-permute-start.26) | collective-permute-done | bytes 1081376 | tf_op jit(solution)/shard_map/ppermute | solution.py:55
  124.3 1.0 collective-permute-start.31
  125.4 5.6 %collective-permute-done.25.came_ref = bf16[208,2304]{1,0:T(8,128)(2,1)S(1)} collective-permute-done((bf16[208,2304]{1,0:T(8,128)(2,1)S(1)}, bf16[208,2304]{1,0:T(8,128)(2,1)S(1)}, u32[]{:S(2)}, u32[]{:S(2)}) %collective-permute-start.25) | collective-permute-done | bytes 958496 | tf_op jit(solution)/shard_map/ppermute | solution.py:55
  131.0 0.9 shard_map.294
  131.9 2.0 %collective-permute-start.30 = (bf16[112,2304]{1,0:T(8,128)(2,1)}, bf16[112,2304]{1,0:T(8,128)(2,1)S(1)}, u32[]{:S(2)}, u32[]{:S(2)}) collective-permute-start(bf16[112,2304]{1,0:T(8,128)(2,1)} %get-tuple-element.258), channel_id=1, source_target_pairs={{0,8},{1,9},{2,10},{3,11},{4,12},{5,13},{6,14},{7,15},{8,0},{9,1},... | collective-permute-start | bytes 1548296 | tf_op jit(solution)/shard_map/ppermute | solution.py:55
  134.1 1.3 collective-permute-start.29
  135.4 5.6 %collective-permute-done.23.came_ref = bf16[512,768]{1,0:T(8,128)(2,1)S(1)} collective-permute-done((bf16[512,768]{1,0:T(8,128)(2,1)S(1)}, bf16[512,768]{1,0:T(8,128)(2,1)S(1)}, u32[]{:S(2)}, u32[]{:S(2)}) %collective-permute-start.23) | collective-permute-done | bytes 786464 | tf_op jit(solution)/shard_map/ppermute | solution.py:55
  140.9 0.9 shard_map.296
  141.8 0.8 shard_map.297
  142.6 2.0 %collective-permute-start.35 = (bf16[48,2816]{1,0:T(8,128)(2,1)}, bf16[48,2816]{1,0:T(8,128)(2,1)}, u32[]{:S(2)}, u32[]{:S(2)}) collective-permute-start(bf16[48,2816]{1,0:T(8,128)(2,1)} %get-tuple-element.272), channel_id=1, source_target_pairs={{0,8},{1,9},{2,10},{3,11},{4,12},{5,13},{6,14},{7,15},{8,0},{9,1},... | collective-permute-start | bytes 811016 | tf_op jit(solution)/shard_map/ppermute | solution.py:55
  145.3 0.8 collective-permute-start.27
  146.2 3.7 %collective-permute-done.29.came_ref = bf16[96,2176]{1,0:T(8,128)(2,1)S(1)} collective-permute-done((bf16[96,2176]{1,0:T(8,128)(2,1)S(1)}, bf16[96,2176]{1,0:T(8,128)(2,1)S(1)}, u32[]{:S(2)}, u32[]{:S(2)}) %collective-permute-start.29) | collective-permute-done | bytes 417824 | tf_op jit(solution)/shard_map/ppermute | solution.py:55
  150.0 4.1 %collective-permute-done.28.came_ref = bf16[256,768]{1,0:T(8,128)(2,1)S(1)} collective-permute-done((bf16[256,768]{1,0:T(8,128)(2,1)}, bf16[256,768]{1,0:T(8,128)(2,1)S(1)}, u32[]{:S(2)}, u32[]{:S(2)}) %collective-permute-start.28) | collective-permute-done | bytes 393248 | tf_op jit(solution)/shard_map/ppermute | solution.py:55
  154.2 1.0 collective-permute-start.32
  155.2 1.1 collective-permute-start.33
  156.3 0.8 collective-permute-start.34
  157.1 0.7 collective-permute-done.35
  157.9 1.2 add_convert_fusion
  159.1 1.9 %collective-permute-start.37 = (bf16[24,2816]{1,0:T(8,128)(2,1)S(1)}, bf16[24,2816]{1,0:T(8,128)(2,1)S(1)}, u32[]{:S(2)}, u32[]{:S(2)}) collective-permute-start(bf16[24,2816]{1,0:T(8,128)(2,1)S(1)} %get-tuple-element.303), channel_id=1, source_target_pairs={{0,16},{1,17},{2,18},{3,19},{4,20},{5,21},{6,22},{7,23},{8,24},{9,... | collective-permute-start | bytes 405512 | tf_op jit(solution)/shard_map/ppermute | solution.py:55
  161.0 2.8 %collective-permute-done.34 = bf16[64,2304]{1,0:T(8,128)(2,1)S(1)} collective-permute-done((bf16[64,2304]{1,0:T(8,128)(2,1)S(1)}, bf16[64,2304]{1,0:T(8,128)(2,1)S(1)}, u32[]{:S(2)}, u32[]{:S(2)}) %collective-permute-start.34) | collective-permute-done | bytes 294944 | tf_op jit(solution)/shard_map/ppermute | solution.py:55
  164.6 2.5 %collective-permute-start.36 = (bf16[40,2304]{1,0:T(8,128)(2,1)S(1)}, bf16[40,2304]{1,0:T(8,128)(2,1)S(1)}, u32[]{:S(2)}, u32[]{:S(2)}) collective-permute-start(bf16[40,2304]{1,0:T(8,128)(2,1)S(1)} %pad_maximum_fusion), channel_id=1, source_target_pairs={{0,16},{1,17},{2,18},{3,19},{4,20},{5,21},{6,22},{7,23},{8,24},{9,... | collective-permute-start | bytes 552968 | tf_op jit(solution)/shard_map/ppermute | solution.py:55
  167.1 1.1 copy-done.13
  168.3 1.1 copy-done.15
  169.3 1.0 copy-done.23
  170.3 1.0 copy-done.28
  171.3 1.0 copy-done.30
  172.3 5.3 %shard_map.302 = (f32[128,768]{1,0:T(8,128)}, f32[128,768]{1,0:T(8,128)}) custom-call(s32[1]{0:T(128)} %bitcast.rank_ref, bf16[128,768]{1,0:T(8,128)(2,1)S(1)} %bitcast.11, f32[768]{0:T(1024)S(1)} %copy-done.7, f32[128,768]{1,0:T(8,128)S(1)} %copy-done.30, bf16[576,1536]{1,0:T(8,128)(2,1)S(1)} %copy-done.11, bf16[128,1536]{1,0:T(8,128)(2,1)S(1)} %copy-done.23, ...), custom_call_target="tpu_custom_call" | custom-call | flops 4400000000 | tf_op jit(solution)/shard_map/pallas_call | solution.py:115
  178.8 1.6 collective-permute-done.36
  180.5 0.8 multiply_reduce_fusion.3
  182.0 1.8 multiply_reduce_fusion
  (167 shorter events, 12.8 us)
Async XLA Ops:
  0.6 9.3 %collective-permute-start = (bf16[128,768]{1,0:T(8,128)(2,1)}, bf16[128,768]{1,0:T(8,128)(2,1)S(1)}, u32[]{:S(2)}, u32[]{:S(2)}) collective-permute-start(bf16[128,768]{1,0:T(8,128)(2,1)} %bitcast.8), channel_id=1, source_target_pairs={{0,1},{1,0},{2,3},{3,2},{4,5},{5,4},{6,7},{7,6},{8,9},{9,8},{10,11... | collective-permute-start | bytes 589832 | tf_op jit(solution)/shard_map/ppermute | solution.py:55
  1.2 8.7 %collective-permute-start.1 = (bf16[128,768]{1,0:T(8,128)(2,1)}, bf16[128,768]{1,0:T(8,128)(2,1)S(1)}, u32[]{:S(2)}, u32[]{:S(2)}) collective-permute-start(bf16[128,768]{1,0:T(8,128)(2,1)} %bitcast.9), channel_id=1, source_target_pairs={{0,2},{1,3},{2,0},{3,1},{4,6},{5,7},{6,4},{7,5},{8,10},{9,11},{10,... | collective-permute-start | bytes 589832 | tf_op jit(solution)/shard_map/ppermute | solution.py:55
  9.8 1.4 collective-permute-start.2
  11.9 23.3 %copy-start.17 = (s32[16,32,128]{2,1,0:T(8,128)S(1)}, s32[16,32,128]{2,1,0:T(8,128)}, u32[]{:S(2)}) copy-start(s32[16,32,128]{2,1,0:T(8,128)} %picked_ref) | copy-start | bytes 786436
  30.7 9.4 %copy-start.45 = (bf16[128,128]{1,0:T(8,128)(2,1)S(1)}, bf16[128,128]{1,0:T(8,128)(2,1)}, u32[]{:S(2)}) copy-start(bf16[128,128]{1,0:T(8,128)(2,1)} %get-tuple-element.154) | copy-start | bytes 98308
  30.7 13.8 %copy-start.37 = (bf16[256,2048]{1,0:T(8,128)(2,1)S(1)}, bf16[256,2048]{1,0:T(8,128)(2,1)}, u32[]{:S(2)}) copy-start(bf16[256,2048]{1,0:T(8,128)(2,1)} %get-tuple-element.172.hidden_ref) | copy-start | bytes 3145732
  30.7 13.8 %copy-start.38 = (bf16[640,768]{1,0:T(8,128)(2,1)S(1)}, bf16[640,768]{1,0:T(8,128)(2,1)}, u32[]{:S(2)}) copy-start(bf16[640,768]{1,0:T(8,128)(2,1)} %get-tuple-element.168.all_ref) | copy-start | bytes 2949124
  30.7 13.8 %copy-start.40 = (bf16[256,768]{1,0:T(8,128)(2,1)S(1)}, bf16[256,768]{1,0:T(8,128)(2,1)}, u32[]{:S(2)}) copy-start(bf16[256,768]{1,0:T(8,128)(2,1)} %get-tuple-element.170.mixed_ref) | copy-start | bytes 1179652
  30.8 13.8 %copy-start.41 = (bf16[256,768]{1,0:T(8,128)(2,1)S(1)}, bf16[256,768]{1,0:T(8,128)(2,1)}, u32[]{:S(2)}) copy-start(bf16[256,768]{1,0:T(8,128)(2,1)} %get-tuple-element.169.normed_feed_ref) | copy-start | bytes 1179652
  30.8 13.8 %copy-start.42 = (bf16[256,768]{1,0:T(8,128)(2,1)S(1)}, bf16[256,768]{1,0:T(8,128)(2,1)}, u32[]{:S(2)}) copy-start(bf16[256,768]{1,0:T(8,128)(2,1)} %get-tuple-element.171.normed_final_ref) | copy-start | bytes 1179652
  30.8 9.3 %collective-permute-start.3 = (bf16[1,128,128]{2,1,0:T(8,128)(2,1)}, bf16[1,128,128]{2,1,0:T(8,128)(2,1)S(1)}, u32[]{:S(2)}, u32[]{:S(2)}) collective-permute-start(bf16[1,128,128]{2,1,0:T(8,128)(2,1)} %bitcast.12), channel_id=1, source_target_pairs={{0,8},{1,9},{2,10},{3,11},{4,12},{5,13},{6,14},{7,15},{8,0},{9,1},... | collective-permute-start | bytes 98312 | tf_op jit(solution)/shard_map/ppermute | solution.py:55
  32.4 7.7 %collective-permute-start.4 = (bf16[1,128,128]{2,1,0:T(8,128)(2,1)}, bf16[1,128,128]{2,1,0:T(8,128)(2,1)S(1)}, u32[]{:S(2)}, u32[]{:S(2)}) collective-permute-start(bf16[1,128,128]{2,1,0:T(8,128)(2,1)} %bitcast.13), channel_id=1, source_target_pairs={{0,16},{1,17},{2,18},{3,19},{4,20},{5,21},{6,22},{7,23},{8,24},{9,... | collective-permute-start | bytes 98312 | tf_op jit(solution)/shard_map/ppermute | solution.py:55
  35.0 5.9 %collective-permute-start.5 = (bf16[1,128,128]{2,1,0:T(8,128)(2,1)}, bf16[1,128,128]{2,1,0:T(8,128)(2,1)S(1)}, u32[]{:S(2)}, u32[]{:S(2)}) collective-permute-start(bf16[1,128,128]{2,1,0:T(8,128)(2,1)} %bitcast.14), channel_id=1, source_target_pairs={{0,24},{1,25},{2,26},{3,27},{4,28},{5,29},{6,30},{7,31},{8,16},{9,... | collective-permute-start | bytes 98312 | tf_op jit(solution)/shard_map/ppermute | solution.py:55
  40.9 8.6 %collective-permute-start.6 = (bf16[4,128,128]{2,1,0:T(8,128)(2,1)S(1)}, bf16[4,128,128]{2,1,0:T(8,128)(2,1)S(1)}, u32[]{:S(2)}, u32[]{:S(2)}) collective-permute-start(bf16[4,128,128]{2,1,0:T(8,128)(2,1)S(1)} %pad_maximum_fusion.1), channel_id=1, source_target_pairs={{0,2},{1,3},{2,0},{3,1},{4,6},{5,7},{6,4},{7,5},{8,10},{9,11},{10,... | collective-permute-start | bytes 393224 | tf_op jit(solution)/shard_map/ppermute | solution.py:55
  42.4 7.1 %collective-permute-start.7 = (bf16[4,128,128]{2,1,0:T(8,128)(2,1)S(1)}, bf16[4,128,128]{2,1,0:T(8,128)(2,1)S(1)}, u32[]{:S(2)}, u32[]{:S(2)}) collective-permute-start(bf16[4,128,128]{2,1,0:T(8,128)(2,1)S(1)} %pad_maximum_fusion.1), channel_id=1, source_target_pairs={{0,4},{1,5},{2,6},{3,7},{4,0},{5,1},{6,2},{7,3},{8,12},{9,13},{10,... | collective-permute-start | bytes 393224 | tf_op jit(solution)/shard_map/ppermute | solution.py:55
  43.9 5.9 %collective-permute-start.8 = (bf16[4,128,128]{2,1,0:T(8,128)(2,1)S(1)}, bf16[4,128,128]{2,1,0:T(8,128)(2,1)S(1)}, u32[]{:S(2)}, u32[]{:S(2)}) collective-permute-start(bf16[4,128,128]{2,1,0:T(8,128)(2,1)S(1)} %pad_maximum_fusion.1), channel_id=1, source_target_pairs={{0,6},{1,7},{2,4},{3,5},{4,2},{5,3},{6,0},{7,1},{8,14},{9,15},{10,... | collective-permute-start | bytes 393224 | tf_op jit(solution)/shard_map/ppermute | solution.py:55
  44.6 18.5 %copy-start.36 = (f32[256,768]{1,0:T(8,128)S(1)}, f32[256,768]{1,0:T(8,128)}, u32[]{:S(2)}) copy-start(f32[256,768]{1,0:T(8,128)} %get-tuple-element.186.after_feed_ref.refs_5_) | copy-start | bytes 2359300
  49.8 13.2 %copy-start.43 = (f32[256,128]{1,0:T(8,128)S(1)}, f32[256,128]{1,0:T(8,128)}, u32[]{:S(2)}) copy-start(f32[256,128]{1,0:T(8,128)} %get-tuple-element.185.embed_ref.refs_4_) | copy-start | bytes 393220
  49.9 2.0 %collective-permute-start.9 = (bf16[16,128,128]{2,1,0:T(8,128)(2,1)S(1)}, bf16[16,128,128]{2,1,0:T(8,128)(2,1)S(1)}, u32[]{:S(2)}, u32[]{:S(2)}) collective-permute-start(bf16[16,128,128]{2,1,0:T(8,128)(2,1)S(1)} %constant_dynamic-update-slice_fusion.near_ref), channel_id=1, source_target_pairs={{0,1},{1,0},{2,3},{3,2},{4,5},{5,4},{6,7},{7,6},{8,9},{9,8},{10,11... | collective-permute-start | bytes 1572872 | tf_op jit(solution)/shard_map/ppermute | solution.py:55
  51.8 11.2 %copy-start = (bf16[768,2048]{1,0:T(8,128)(2,1)S(1)}, bf16[768,2048]{1,0:T(8,128)(2,1)}, u32[]{:S(2)}) copy-start(bf16[768,2048]{1,0:T(8,128)(2,1)} %refs_13_.1) | copy-start | bytes 9437188
  51.9 11.2 %copy-start.1 = (bf16[768,2048]{1,0:T(8,128)(2,1)S(1)}, bf16[768,2048]{1,0:T(8,128)(2,1)}, u32[]{:S(2)}) copy-start(bf16[768,2048]{1,0:T(8,128)(2,1)} %refs_14_.1) | copy-start | bytes 9437188
  51.9 11.2 %copy-start.9 = (bf16[2048,768]{1,0:T(8,128)(2,1)S(1)}, bf16[2048,768]{1,0:T(8,128)(2,1)}, u32[]{:S(2)}) copy-start(bf16[2048,768]{1,0:T(8,128)(2,1)} %refs_12_.1) | copy-start | bytes 9437188
  51.9 11.2 %copy-start.32 = (bf16[256,2048]{1,0:T(8,128)(2,1)S(1)}, bf16[256,2048]{1,0:T(8,128)(2,1)}, u32[]{:S(2)}) copy-start(bf16[256,2048]{1,0:T(8,128)(2,1)} %get-tuple-element.188.gate_slope_ref.refs_7_) | copy-start | bytes 3145732
  51.9 11.2 %copy-start.33 = (bf16[256,2048]{1,0:T(8,128)(2,1)S(1)}, bf16[256,2048]{1,0:T(8,128)(2,1)}, u32[]{:S(2)}) copy-start(bf16[256,2048]{1,0:T(8,128)(2,1)} %get-tuple-element.189.up_slope_ref.refs_8_) | copy-start | bytes 3145732
  51.9 11.2 %copy-start.35 = (f32[256,768]{1,0:T(8,128)S(1)}, f32[256,768]{1,0:T(8,128)}, u32[]{:S(2)}) copy-start(f32[256,768]{1,0:T(8,128)} %get-tuple-element.187.after_attend_ref.refs_6_) | copy-start | bytes 2359300
  55.2 7.8 %collective-permute-start.14 = (bf16[256,2944]{1,0:T(8,128)(2,1)S(1)}, bf16[256,2944]{1,0:T(8,128)(2,1)S(1)}, u32[]{:S(2)}, u32[]{:S(2)}) collective-permute-start(bf16[256,2944]{1,0:T(8,128)(2,1)S(1)} %get-tuple-element.183), channel_id=1, source_target_pairs={{0,1},{1,0},{2,3},{3,2},{4,5},{5,4},{6,7},{7,6},{8,9},{9,8},{10,11... | collective-permute-start | bytes 4521992 | tf_op jit(solution)/shard_map/ppermute | solution.py:55
  55.4 3.9 %collective-permute-start.10 = (bf16[16,128,128]{2,1,0:T(8,128)(2,1)S(1)}, bf16[16,128,128]{2,1,0:T(8,128)(2,1)S(1)}, u32[]{:S(2)}, u32[]{:S(2)}) collective-permute-start(bf16[16,128,128]{2,1,0:T(8,128)(2,1)S(1)} %get-tuple-element.180), channel_id=1, source_target_pairs={{0,1},{1,0},{2,3},{3,2},{4,5},{5,4},{6,7},{7,6},{8,9},{9,8},{10,11... | collective-permute-start | bytes 1572872 | tf_op jit(solution)/shard_map/ppermute | solution.py:55
  59.5 10.5 %collective-permute-start.11 = (bf16[4,128,128]{2,1,0:T(8,128)(2,1)S(1)}, bf16[4,128,128]{2,1,0:T(8,128)(2,1)S(1)}, u32[]{:S(2)}, u32[]{:S(2)}) collective-permute-start(bf16[4,128,128]{2,1,0:T(8,128)(2,1)S(1)} %get-tuple-element.301), channel_id=1, source_target_pairs={{0,4},{1,5},{2,6},{3,7},{4,0},{5,1},{6,2},{7,3},{8,12},{9,13},{10,... | collective-permute-start | bytes 393224 | tf_op jit(solution)/shard_map/ppermute | solution.py:55
  60.8 9.2 %collective-permute-start.12 = (bf16[4,128,128]{2,1,0:T(8,128)(2,1)S(1)}, bf16[4,128,128]{2,1,0:T(8,128)(2,1)S(1)}, u32[]{:S(2)}, u32[]{:S(2)}) collective-permute-start(bf16[4,128,128]{2,1,0:T(8,128)(2,1)S(1)} %get-tuple-element.300), channel_id=1, source_target_pairs={{0,2},{1,3},{2,0},{3,1},{4,6},{5,7},{6,4},{7,5},{8,10},{9,11},{10,... | collective-permute-start | bytes 393224 | tf_op jit(solution)/shard_map/ppermute | solution.py:55
  62.2 7.8 %collective-permute-start.13 = (bf16[4,128,128]{2,1,0:T(8,128)(2,1)S(1)}, bf16[4,128,128]{2,1,0:T(8,128)(2,1)S(1)}, u32[]{:S(2)}, u32[]{:S(2)}) collective-permute-start(bf16[4,128,128]{2,1,0:T(8,128)(2,1)S(1)} %get-tuple-element.299), channel_id=1, source_target_pairs={{0,6},{1,7},{2,4},{3,5},{4,2},{5,3},{6,0},{7,1},{8,14},{9,15},{10,... | collective-permute-start | bytes 393224 | tf_op jit(solution)/shard_map/ppermute | solution.py:55
  63.2 11.5 %copy-start.25 = (bf16[640,768]{1,0:T(8,128)(2,1)S(1)}, bf16[640,768]{1,0:T(8,128)(2,1)}, u32[]{:S(2)}) copy-start(bf16[640,768]{1,0:T(8,128)(2,1)} %get-tuple-element.195.key_ref) | copy-start | bytes 2949124
  63.2 11.5 %copy-start.26 = (bf16[640,768]{1,0:T(8,128)(2,1)S(1)}, bf16[640,768]{1,0:T(8,128)(2,1)}, u32[]{:S(2)}) copy-start(bf16[640,768]{1,0:T(8,128)(2,1)} %get-tuple-element.196.value_ref) | copy-start | bytes 2949124
  63.2 11.5 %copy-start.31 = (bf16[256,768]{1,0:T(8,128)(2,1)S(1)}, bf16[256,768]{1,0:T(8,128)(2,1)}, u32[]{:S(2)}) copy-start(bf16[256,768]{1,0:T(8,128)(2,1)} %get-tuple-element.194.query_ref) | copy-start | bytes 1179652
  63.2 11.5 %copy-start.39 = (bf16[6,256,128]{2,1,0:T(8,128)(2,1)S(1)}, bf16[6,256,128]{2,1,0:T(8,128)(2,1)}, u32[]{:S(2)}) copy-start(bf16[6,256,128]{2,1,0:T(8,128)(2,1)} %get-tuple-element.197.probs_ref) | copy-start | bytes 1179652
  70.1 9.7 %collective-permute-start.18 = (bf16[128,5760]{1,0:T(8,128)(2,1)S(1)}, bf16[128,5760]{1,0:T(8,128)(2,1)S(1)}, u32[]{:S(2)}, u32[]{:S(2)}) collective-permute-start(bf16[128,5760]{1,0:T(8,128)(2,1)S(1)} %get-tuple-element.238.slot_any), channel_id=1, source_target_pairs={{0,1},{1,0},{2,3},{3,2},{4,5},{5,4},{6,7},{7,6},{8,9},{9,8},{10,11... | collective-permute-start | bytes 4423688 | tf_op jit(solution)/shard_map/ppermute | solution.py:55
  70.2 8.2 %collective-permute-start.15 = (bf16[1,128,128]{2,1,0:T(8,128)(2,1)S(1)}, bf16[1,128,128]{2,1,0:T(8,128)(2,1)S(1)}, u32[]{:S(2)}, u32[]{:S(2)}) collective-permute-start(bf16[1,128,128]{2,1,0:T(8,128)(2,1)S(1)} %get-tuple-element.307), channel_id=1, source_target_pairs={{0,16},{1,17},{2,18},{3,19},{4,20},{5,21},{6,22},{7,23},{8,24},{9,... | collective-permute-start | bytes 98312 | tf_op jit(solution)/shard_map/ppermute | solution.py:55
  71.6 6.8 %collective-permute-start.16 = (bf16[1,128,128]{2,1,0:T(8,128)(2,1)S(1)}, bf16[1,128,128]{2,1,0:T(8,128)(2,1)S(1)}, u32[]{:S(2)}, u32[]{:S(2)}) collective-permute-start(bf16[1,128,128]{2,1,0:T(8,128)(2,1)S(1)} %get-tuple-element.306), channel_id=1, source_target_pairs={{0,8},{1,9},{2,10},{3,11},{4,12},{5,13},{6,14},{7,15},{8,0},{9,1},... | collective-permute-start | bytes 98312 | tf_op jit(solution)/shard_map/ppermute | solution.py:55
  74.1 5.7 %collective-permute-start.17 = (bf16[1,128,128]{2,1,0:T(8,128)(2,1)S(1)}, bf16[1,128,128]{2,1,0:T(8,128)(2,1)S(1)}, u32[]{:S(2)}, u32[]{:S(2)}) collective-permute-start(bf16[1,128,128]{2,1,0:T(8,128)(2,1)S(1)} %get-tuple-element.305), channel_id=1, source_target_pairs={{0,24},{1,25},{2,26},{3,27},{4,28},{5,29},{6,30},{7,31},{8,16},{9,... | collective-permute-start | bytes 98312 | tf_op jit(solution)/shard_map/ppermute | solution.py:55
  78.4 19.8 %copy-start.14 = (bf16[128,2304]{1,0:T(8,128)(2,1)}, bf16[128,2304]{1,0:T(8,128)(2,1)S(1)}, u32[]{:S(2)}) copy-start(bf16[128,2304]{1,0:T(8,128)(2,1)S(1)} %get-tuple-element.215.slot_any.slot_grads_ref) | copy-start | bytes 1769476
  86.6 6.8 %collective-permute-start.21 = (bf16[128,5760]{1,0:T(8,128)(2,1)S(1)}, bf16[128,5760]{1,0:T(8,128)(2,1)S(1)}, u32[]{:S(2)}, u32[]{:S(2)}) collective-permute-start(bf16[128,5760]{1,0:T(8,128)(2,1)S(1)} %get-tuple-element.240.doc_any), channel_id=1, source_target_pairs={{0,1},{1,0},{2,3},{3,2},{4,5},{5,4},{6,7},{7,6},{8,9},{9,8},{10,11... | collective-permute-start | bytes 4423688 | tf_op jit(solution)/shard_map/ppermute | solution.py:55
  92.3 5.9 %collective-permute-start.20 = (bf16[576,1536]{1,0:T(8,128)(2,1)S(1)}, bf16[576,1536]{1,0:T(8,128)(2,1)S(1)}, u32[]{:S(2)}, u32[]{:S(2)}) collective-permute-start(bf16[576,1536]{1,0:T(8,128)(2,1)S(1)} %get-tuple-element.212.grads_ref), channel_id=1, source_target_pairs={{0,1},{1,0},{2,3},{3,2},{4,5},{5,4},{6,7},{7,6},{8,9},{9,8},{10,11... | collective-permute-start | bytes 5308424 | tf_op jit(solution)/shard_map/ppermute | solution.py:55
  92.8 5.4 %collective-permute-start.19 = (bf16[128,2304]{1,0:T(8,128)(2,1)S(1)}, bf16[128,2304]{1,0:T(8,128)(2,1)S(1)}, u32[]{:S(2)}, u32[]{:S(2)}) collective-permute-start(bf16[128,2304]{1,0:T(8,128)(2,1)S(1)} %get-tuple-element.215.slot_any.slot_grads_ref), channel_id=1, source_target_pairs={{0,1},{1,0},{2,3},{3,2},{4,5},{5,4},{6,7},{7,6},{8,9},{9,8},{10,11... | collective-permute-start | bytes 1769480 | tf_op jit(solution)/shard_map/ppermute | solution.py:55
  92.9 5.3 %collective-permute-start.22 = (bf16[16,128]{1,0:T(8,128)(2,1)S(1)}, bf16[16,128]{1,0:T(8,128)(2,1)S(1)}, u32[]{:S(2)}, u32[]{:S(2)}) collective-permute-start(bf16[16,128]{1,0:T(8,128)(2,1)S(1)} %get-tuple-element.225.table_ref), channel_id=1, source_target_pairs={{0,1},{1,0},{2,3},{3,2},{4,5},{5,4},{6,7},{7,6},{8,9},{9,8},{10,11... | collective-permute-start | bytes 12296 | tf_op jit(solution)/shard_map/ppermute | solution.py:55
  97.3 26.8 %collective-permute-start.26 = (bf16[192,2816]{1,0:T(8,128)(2,1)S(1)}, bf16[192,2816]{1,0:T(8,128)(2,1)S(1)}, u32[]{:S(2)}, u32[]{:S(2)}) collective-permute-start(bf16[192,2816]{1,0:T(8,128)(2,1)S(1)} %get-tuple-element.246), channel_id=1, source_target_pairs={{0,2},{1,3},{2,0},{3,1},{4,6},{5,7},{6,4},{7,5},{8,10},{9,11},{10,... | collective-permute-start | bytes 3244040 | tf_op jit(solution)/shard_map/ppermute | solution.py:55
  106.7 27.2 %collective-permute-start.24 = (bf16[192,2176]{1,0:T(8,128)(2,1)S(1)}, bf16[192,2176]{1,0:T(8,128)(2,1)S(1)}, u32[]{:S(2)}, u32[]{:S(2)}) collective-permute-start(bf16[192,2176]{1,0:T(8,128)(2,1)S(1)} %get-tuple-element.244), channel_id=1, source_target_pairs={{0,8},{1,9},{2,10},{3,11},{4,12},{5,13},{6,14},{7,15},{8,0},{9,1},... | collective-permute-start | bytes 2506760 | tf_op jit(solution)/shard_map/ppermute | solution.py:55
  106.8 24.2 %collective-permute-start.25 = (bf16[208,2304]{1,0:T(8,128)(2,1)S(1)}, bf16[208,2304]{1,0:T(8,128)(2,1)S(1)}, u32[]{:S(2)}, u32[]{:S(2)}) collective-permute-start(bf16[208,2304]{1,0:T(8,128)(2,1)S(1)} %get-tuple-element.245), channel_id=1, source_target_pairs={{0,4},{1,5},{2,6},{3,7},{4,0},{5,1},{6,2},{7,3},{8,12},{9,13},{10,... | collective-permute-start | bytes 2875400 | tf_op jit(solution)/shard_map/ppermute | solution.py:55
  110.2 30.8 %collective-permute-start.23 = (bf16[512,768]{1,0:T(8,128)(2,1)S(1)}, bf16[512,768]{1,0:T(8,128)(2,1)S(1)}, u32[]{:S(2)}, u32[]{:S(2)}) collective-permute-start(bf16[512,768]{1,0:T(8,128)(2,1)S(1)} %get-tuple-element.243), channel_id=1, source_target_pairs={{0,2},{1,3},{2,0},{3,1},{4,6},{5,7},{6,4},{7,5},{8,10},{9,11},{10,... | collective-permute-start | bytes 2359304 | tf_op jit(solution)/shard_map/ppermute | solution.py:55
  124.3 17.5 %collective-permute-start.31 = (bf16[96,2816]{1,0:T(8,128)(2,1)S(1)}, bf16[96,2816]{1,0:T(8,128)(2,1)S(1)}, u32[]{:S(2)}, u32[]{:S(2)}) collective-permute-start(bf16[96,2816]{1,0:T(8,128)(2,1)S(1)} %get-tuple-element.259), channel_id=1, source_target_pairs={{0,4},{1,5},{2,6},{3,7},{4,0},{5,1},{6,2},{7,3},{8,12},{9,13},{10,... | collective-permute-start | bytes 1622024 | tf_op jit(solution)/shard_map/ppermute | solution.py:55
  131.9 14.2 %collective-permute-start.30 = (bf16[112,2304]{1,0:T(8,128)(2,1)}, bf16[112,2304]{1,0:T(8,128)(2,1)S(1)}, u32[]{:S(2)}, u32[]{:S(2)}) collective-permute-start(bf16[112,2304]{1,0:T(8,128)(2,1)} %get-tuple-element.258), channel_id=1, source_target_pairs={{0,8},{1,9},{2,10},{3,11},{4,12},{5,13},{6,14},{7,15},{8,0},{9,1},... | collective-permute-start | bytes 1548296 | tf_op jit(solution)/shard_map/ppermute | solution.py:55
  134.1 15.8 %collective-permute-start.29 = (bf16[96,2176]{1,0:T(8,128)(2,1)S(1)}, bf16[96,2176]{1,0:T(8,128)(2,1)S(1)}, u32[]{:S(2)}, u32[]{:S(2)}) collective-permute-start(bf16[96,2176]{1,0:T(8,128)(2,1)S(1)} %get-tuple-element.257), channel_id=1, source_target_pairs={{0,2},{1,3},{2,0},{3,1},{4,6},{5,7},{6,4},{7,5},{8,10},{9,11},{10,... | collective-permute-start | bytes 1253384 | tf_op jit(solution)/shard_map/ppermute | solution.py:55
  141.8 12.3 %collective-permute-start.28 = (bf16[256,768]{1,0:T(8,128)(2,1)}, bf16[256,768]{1,0:T(8,128)(2,1)S(1)}, u32[]{:S(2)}, u32[]{:S(2)}) collective-permute-start(bf16[256,768]{1,0:T(8,128)(2,1)} %get-tuple-element.256), channel_id=1, source_target_pairs={{0,8},{1,9},{2,10},{3,11},{4,12},{5,13},{6,14},{7,15},{8,0},{9,1},... | collective-permute-start | bytes 1179656 | tf_op jit(solution)/shard_map/ppermute | solution.py:55
  142.6 15.3 %collective-permute-start.35 = (bf16[48,2816]{1,0:T(8,128)(2,1)}, bf16[48,2816]{1,0:T(8,128)(2,1)}, u32[]{:S(2)}, u32[]{:S(2)}) collective-permute-start(bf16[48,2816]{1,0:T(8,128)(2,1)} %get-tuple-element.272), channel_id=1, source_target_pairs={{0,8},{1,9},{2,10},{3,11},{4,12},{5,13},{6,14},{7,15},{8,0},{9,1},... | collective-permute-start | bytes 811016 | tf_op jit(solution)/shard_map/ppermute | solution.py:55
  145.3 18.7 %collective-permute-start.27 = (bf16[128,1536]{1,0:T(8,128)(2,1)}, bf16[128,1536]{1,0:T(8,128)(2,1)S(1)}, u32[]{:S(2)}, u32[]{:S(2)}) collective-permute-start(bf16[128,1536]{1,0:T(8,128)(2,1)} %copy-done.16), channel_id=1, source_target_pairs={{0,2},{1,3},{2,0},{3,1},{4,6},{5,7},{6,4},{7,5},{8,10},{9,11},{10,... | collective-permute-start | bytes 1179656 | tf_op jit(solution)/shard_map/ppermute | solution.py:55
  146.1 21.0 %copy-start.11 = (bf16[576,1536]{1,0:T(8,128)(2,1)S(1)}, bf16[576,1536]{1,0:T(8,128)(2,1)}, u32[]{:S(2)}) copy-start(bf16[576,1536]{1,0:T(8,128)(2,1)} %copy-done.10) | copy-start | bytes 5308420
  154.1 13.0 %copy-start.4 = (bf16[768,768]{1,0:T(8,128)(2,1)S(1)}, bf16[768,768]{1,0:T(8,128)(2,1)}, u32[]{:S(2)}) copy-start(bf16[768,768]{1,0:T(8,128)(2,1)} %wv_ref.1) | copy-start | bytes 3538948
  154.2 9.7 %collective-permute-start.32 = (bf16[128,768]{1,0:T(8,128)(2,1)S(1)}, bf16[128,768]{1,0:T(8,128)(2,1)S(1)}, u32[]{:S(2)}, u32[]{:S(2)}) collective-permute-start(bf16[128,768]{1,0:T(8,128)(2,1)S(1)} %get-tuple-element.269), channel_id=1, source_target_pairs={{0,4},{1,5},{2,6},{3,7},{4,0},{5,1},{6,2},{7,3},{8,12},{9,13},{10,... | collective-permute-start | bytes 589832 | tf_op jit(solution)/shard_map/ppermute | solution.py:55
  155.2 8.6 %collective-permute-start.33 = (bf16[48,2176]{1,0:T(8,128)(2,1)S(1)}, bf16[48,2176]{1,0:T(8,128)(2,1)S(1)}, u32[]{:S(2)}, u32[]{:S(2)}) collective-permute-start(bf16[48,2176]{1,0:T(8,128)(2,1)S(1)} %get-tuple-element.270), channel_id=1, source_target_pairs={{0,4},{1,5},{2,6},{3,7},{4,0},{5,1},{6,2},{7,3},{8,12},{9,13},{10,... | collective-permute-start | bytes 626696 | tf_op jit(solution)/shard_map/ppermute | solution.py:55
  156.3 7.5 %collective-permute-start.34 = (bf16[64,2304]{1,0:T(8,128)(2,1)S(1)}, bf16[64,2304]{1,0:T(8,128)(2,1)S(1)}, u32[]{:S(2)}, u32[]{:S(2)}) collective-permute-start(bf16[64,2304]{1,0:T(8,128)(2,1)S(1)} %get-tuple-element.271), channel_id=1, source_target_pairs={{0,2},{1,3},{2,0},{3,1},{4,6},{5,7},{6,4},{7,5},{8,10},{9,11},{10,... | collective-permute-start | bytes 884744 | tf_op jit(solution)/shard_map/ppermute | solution.py:55
  157.9 9.2 %copy-start.7 = (f32[768]{0:T(1024)S(1)}, f32[768]{0:T(1024)}, u32[]{:S(2)}) copy-start(f32[768]{0:T(1024)} %gain_ref.1) | copy-start | bytes 9220
  157.9 9.3 %copy-start.18 = (bf16[1,128,768]{2,1,0:T(8,128)(2,1)S(1)}, bf16[1,128,768]{2,1,0:T(8,128)(2,1)}, u32[]{:S(2)}) copy-start(bf16[1,128,768]{2,1,0:T(8,128)(2,1)} %param.17) | copy-start | bytes 589828
  159.1 18.5 %collective-permute-start.37 = (bf16[24,2816]{1,0:T(8,128)(2,1)S(1)}, bf16[24,2816]{1,0:T(8,128)(2,1)S(1)}, u32[]{:S(2)}, u32[]{:S(2)}) collective-permute-start(bf16[24,2816]{1,0:T(8,128)(2,1)S(1)} %get-tuple-element.303), channel_id=1, source_target_pairs={{0,16},{1,17},{2,18},{3,19},{4,20},{5,21},{6,22},{7,23},{8,24},{9,... | collective-permute-start | bytes 405512 | tf_op jit(solution)/shard_map/ppermute | solution.py:55
  164.0 16.5 %collective-permute-start.38 = (bf16[24,2176]{1,0:T(8,128)(2,1)S(1)}, bf16[24,2176]{1,0:T(8,128)(2,1)S(1)}, u32[]{:S(2)}, u32[]{:S(2)}) collective-permute-start(bf16[24,2176]{1,0:T(8,128)(2,1)S(1)} %get-tuple-element.311), channel_id=1, source_target_pairs={{0,16},{1,17},{2,18},{3,19},{4,20},{5,21},{6,22},{7,23},{8,24},{9,... | collective-permute-start | bytes 313352 | tf_op jit(solution)/shard_map/ppermute | solution.py:55
  164.6 15.8 %collective-permute-start.36 = (bf16[40,2304]{1,0:T(8,128)(2,1)S(1)}, bf16[40,2304]{1,0:T(8,128)(2,1)S(1)}, u32[]{:S(2)}, u32[]{:S(2)}) collective-permute-start(bf16[40,2304]{1,0:T(8,128)(2,1)S(1)} %pad_maximum_fusion), channel_id=1, source_target_pairs={{0,16},{1,17},{2,18},{3,19},{4,20},{5,21},{6,22},{7,23},{8,24},{9,... | collective-permute-start | bytes 552968 | tf_op jit(solution)/shard_map/ppermute | solution.py:55
  178.3 6.2 %collective-permute-start.39 = (bf16[64,768]{1,0:T(8,128)(2,1)S(1)}, bf16[64,768]{1,0:T(8,128)(2,1)S(1)}, u32[]{:S(2)}, u32[]{:S(2)}) collective-permute-start(bf16[64,768]{1,0:T(8,128)(2,1)S(1)} %get-tuple-element.285), channel_id=1, source_target_pairs={{0,16},{1,17},{2,18},{3,19},{4,20},{5,21},{6,22},{7,23},{8,24},{9,... | collective-permute-start | bytes 294920 | tf_op jit(solution)/shard_map/ppermute | solution.py:55
  (25 other events, 114.2 us)

commit v5 on v4

--- a/solution.py
+++ b/solution.py
@@ -10,7 +10,7 @@
 BUCKETS = 32
 LANES = 128
 CHUNK = 512
-VM = (60, 34, 24, 16, 8)
+VM = (12, 12, 12, 16, 8)
 COST = 1.1e9
 
 epsilon = 1e-06
@@ -233,14 +233,11 @@
 def forward_kernel(
     slots, slot_length, rank_ref, lengths_ref, queries_ref, own_ref, near_ref, far_ref, last_ref, doc_bias_ref,
     slot_bias_ref, attend_gain_ref, feed_gain_ref, final_gain_ref,
-    wq_any, wk_any, wv_any, wo_any, wg_any, wu_any, wd_any, wp_any,
-    all_any, query_any, key_any, value_any, doc_probs_any, slot_probs_any, mixed_any, after_attend_any,
-    normed_feed_any, hidden_any, gate_slope_any, up_slope_any, after_feed_any, normed_final_any, embed_any,
-    slot_unit_any, doc_unit_any,
+    wq_ref, wk_ref, wv_ref, wo_ref, wg_ref, wu_ref, wd_ref, wp_ref,
     all_ref, query_ref, key_ref, value_ref, doc_probs_ref, slot_probs_ref, mixed_ref, after_attend_ref,
     normed_feed_ref, hidden_ref, gate_slope_ref, up_slope_ref, after_feed_ref, normed_final_ref, embed_ref,
     slot_unit_ref, doc_unit_ref,
-    wq_ref, wk_ref, wv_ref, wo_ref, wg_ref, wu_ref, wd_ref, wp_ref, slot_ref, load_sems, store_sems, slot_sem,
+    slot_ref, slot_sem,
 ):
     slot_rows = slots * slot_length
     rows, width = query_ref.shape
@@ -250,22 +247,6 @@
     first = (rank_ref[0] & (narrow_size - 1)) * slots
     load_slots = pltpu.make_async_copy(queries_ref.at[pl.ds(first, slots)], slot_ref, slot_sem)
     load_slots.start()
-    weights = loads(
-        (wq_any, wk_any, wv_any, wo_any, wg_any, wu_any, wd_any, wp_any),
-        (wq_ref, wk_ref, wv_ref, wo_ref, wg_ref, wu_ref, wd_ref, wp_ref),
-        load_sems,
-    )
-    stores = loads(
-        (all_ref, query_ref, key_ref, value_ref, doc_probs_ref, slot_probs_ref, mixed_ref, after_attend_ref,
-         normed_feed_ref, hidden_ref, gate_slope_ref, up_slope_ref, after_feed_ref, normed_final_ref, embed_ref,
-         slot_unit_ref, doc_unit_ref),
-        (all_any, query_any, key_any, value_any, doc_probs_any, slot_probs_any, mixed_any, after_attend_any,
-         normed_feed_any, hidden_any, gate_slope_any, up_slope_any, after_feed_any, normed_final_any, embed_any,
-         slot_unit_any, doc_unit_any),
-        store_sems,
-    )
-    for weight in weights[:3]:
-        weight.start()
     gain = attend_gain_ref[...].reshape(1, width)
     place = slot_rows
     for ref in (own_ref, near_ref, far_ref, last_ref):
@@ -276,18 +257,9 @@
     slot_tokens = slot_ref[...].reshape(slot_rows, width).astype(f32)
     all_ref[:slot_rows, :] = (slot_tokens * rms_scale(slot_tokens) * gain).astype(bf16)
     normed = all_ref[:rows, :]
-    stores[0].start()
-    weights[0].wait()
-    for weight in weights[3:]:
-        weight.start()
     query_ref[...] = product(normed, wq_ref[...]).astype(bf16)
-    stores[1].start()
-    weights[1].wait()
     key_ref[...] = product(all_ref[...], wk_ref[...]).astype(bf16)
-    stores[2].start()
-    weights[2].wait()
     value_ref[...] = product(all_ref[...], wv_ref[...]).astype(bf16)
-    stores[3].start()
 
     lane = lax.broadcasted_iota(jnp.int32, (slot_rows, LANES), 1)
     row = lax.broadcasted_iota(jnp.int32, (slot_rows, slot_rows), 0)
@@ -321,21 +293,14 @@
         mixed_ref[slot_rows:, lanes] = joined(doc_mixed, first_lanes).astype(bf16)
         return carry
 
-    lax.fori_loop(0, pairs, one_pair, 0)
-    for store in stores[4:7]:
-        store.start()
-
-    weights[3].wait()
+    lax.fori_loop(0, pairs, one_pair, 0, unroll=2)
+
     attended = product(mixed_ref[...], wo_ref[...])
     after_attend_ref[:slot_rows, :] = slot_ref[...].reshape(slot_rows, width).astype(f32) + attended[:slot_rows]
     after_attend_ref[slot_rows:, :] = own_ref[...].astype(f32) + attended[slot_rows:]
-    stores[7].start()
     after_attend = after_attend_ref[...]
     feed_gain = feed_gain_ref[...].reshape(1, width)
     normed_feed_ref[...] = (after_attend * rms_scale(after_attend) * feed_gain).astype(bf16)
-    stores[8].start()
-    weights[4].wait()
-    weights[5].wait()
 
     def one_part(step, carry):
         part = tile(step, CHUNK)
@@ -351,27 +316,17 @@
         up_slope_ref[:, part] = curve.astype(bf16)
         return carry
 
-    lax.fori_loop(0, hidden_ref.shape[1] // CHUNK, one_part, 0)
-    for store in stores[9:12]:
-        store.start()
-    weights[6].wait()
+    lax.fori_loop(0, hidden_ref.shape[1] // CHUNK, one_part, 0, unroll=2)
     after_feed = after_attend_ref[...] + product(hidden_ref[...], wd_ref[...])
     after_feed_ref[...] = after_feed
-    stores[12].start()
     final_gain = final_gain_ref[...].reshape(1, width)
     normed_final = (after_feed * rms_scale(after_feed) * final_gain).astype(bf16)
     normed_final_ref[...] = normed_final
-    stores[13].start()
-    weights[7].wait()
     embed = product(normed_final, wp_ref[...])
     embed_ref[...] = embed
     unit = (embed * lax.rsqrt(jnp.sum(embed * embed, -1, keepdims=True) + epsilon)).astype(bf16)
     slot_unit_ref[...] = unit[:slot_rows]
     doc_unit_ref[...] = unit[slot_rows:]
-    for store in stores[14:]:
-        store.start()
-    for store in stores:
-        store.wait()
 
 
 def loss_kernel(
@@ -449,7 +404,7 @@
 
 
 def feed_back(
-    part, waits, grad_unit, embed_ref, after_feed_ref, after_attend_ref, gate_slope_ref, up_slope_ref, feed_gain_ref,
+    part, grad_unit, embed_ref, after_feed_ref, after_attend_ref, gate_slope_ref, up_slope_ref, feed_gain_ref,
     final_gain_ref, wo_ref, wg_ref, wu_ref, wd_ref, wp_ref, grads_out, after_out, mixed_out, more_ref,
 ):
     units, width = wd_ref.shape
@@ -460,16 +415,12 @@
     inner = jnp.sum(grad_unit * embed, -1, keepdims=True)
     grad_embed = (scale * grad_unit - embed * (scale * scale * scale * inner)).astype(bf16)
     grads_out[:, embed_start : embed_start + embed.shape[1]] = grad_embed
-    waits[0].wait()
     grad_after_feed = rms_back(
         after_feed_ref[part, :], final_gain_ref[...].reshape(1, -1), right_product(grad_embed, wp_ref[...])
     )
     after_out[...] = grad_after_feed
     grad_feed = grad_after_feed.astype(bf16)
     grads_out[:, feed_start:attend_start] = grad_feed
-    for wait in waits[1:4]:
-        wait.wait()
-
     def one_part(step, total):
         cols = tile(step, CHUNK)
         grad_hidden = right_product(grads_out[:, feed_start:attend_start], wd_ref[cols, :])
@@ -481,14 +432,13 @@
         return total
 
     more_ref[...] = jnp.zeros_like(more_ref)
-    lax.fori_loop(0, units // CHUNK, one_part, 0)
+    lax.fori_loop(0, units // CHUNK, one_part, 0, unroll=2)
     total = more_ref[...]
     more = rms_back(after_attend_ref[part, :], feed_gain_ref[...].reshape(1, -1), total)
     grad_after_attend = after_out[...] + more
     after_out[...] = grad_after_attend
     grad_attend = grad_after_attend.astype(bf16)
     grads_out[:, attend_start:embed_start] = grad_attend
-    waits[4].wait()
     mixed_out[...] = right_product(grad_attend, wo_ref[...]).astype(bf16)
 
 
@@ -533,7 +483,7 @@
                 )
         return carry
 
-    lax.fori_loop(0, probs_ref.shape[0], one_pair, 0)
+    lax.fori_loop(0, probs_ref.shape[0], one_pair, 0, unroll=2)
 
 
 def input_back(tokens, gain_ref, after_ref, query, key, value, wq_ref, wk_ref, wv_ref):
@@ -559,17 +509,11 @@
 
 def slot_feed_kernel(
     grad_unit_ref, embed_ref, after_feed_ref, after_attend_ref, gate_slope_ref, up_slope_ref, feed_gain_ref,
-    final_gain_ref, wp_any, wd_any, wg_any, wu_any, wo_any,
-    grads_out, after_out, mixed_out,
-    wp_ref, wd_ref, wg_ref, wu_ref, wo_ref, more_ref, load_sems,
-):
-    weights = loads(
-        (wp_any, wd_any, wg_any, wu_any, wo_any), (wp_ref, wd_ref, wg_ref, wu_ref, wo_ref), load_sems
-    )
-    for weight in weights:
-        weight.start()
+    final_gain_ref, wp_ref, wd_ref, wg_ref, wu_ref, wo_ref,
+    grads_out, after_out, mixed_out, more_ref,
+):
     feed_back(
-        slice(0, after_out.shape[0]), weights, grad_unit_ref[...], embed_ref, after_feed_ref, after_attend_ref,
+        slice(0, after_out.shape[0]), grad_unit_ref[...], embed_ref, after_feed_ref, after_attend_ref,
         gate_slope_ref, up_slope_ref, feed_gain_ref, final_gain_ref, wo_ref, wg_ref, wu_ref, wd_ref, wp_ref, grads_out,
         after_out, mixed_out, more_ref,
     )
@@ -597,19 +541,13 @@
     parts, refs = refs[:came], refs[came:]
     (
         embed_ref, after_feed_ref, after_attend_ref, gate_slope_ref, up_slope_ref, feed_gain_ref, final_gain_ref,
-        wp_any, wd_any, wg_any, wu_any, wo_any,
-        grads_out, after_out, mixed_out,
-        wp_ref, wd_ref, wg_ref, wu_ref, wo_ref, more_ref, load_sems,
+        wp_ref, wd_ref, wg_ref, wu_ref, wo_ref,
+        grads_out, after_out, mixed_out, more_ref,
     ) = refs
-    weights = loads(
-        (wp_any, wd_any, wg_any, wu_any, wo_any), (wp_ref, wd_ref, wg_ref, wu_ref, wo_ref), load_sems
-    )
-    for weight in weights:
-        weight.start()
     rows = after_out.shape[0]
     grad_unit = add(*(part[0] for part in parts)).T
     feed_back(
-        slice(embed_ref.shape[0] - rows, embed_ref.shape[0]), weights, grad_unit, embed_ref, after_feed_ref,
+        slice(embed_ref.shape[0] - rows, embed_ref.shape[0]), grad_unit, embed_ref, after_feed_ref,
         after_attend_ref, gate_slope_ref, up_slope_ref, feed_gain_ref, final_gain_ref, wo_ref, wg_ref, wu_ref, wd_ref,
         wp_ref, grads_out, after_out, mixed_out, more_ref,
     )
@@ -721,7 +659,7 @@
         one_part(place * size, size)
         return carry
 
-    lax.fori_loop(0, columns // size, step, 0)
+    lax.fori_loop(0, columns // size, step, 0, unroll=2)
     if columns % size:
         one_part(columns // size * size, columns % size)
 
@@ -805,14 +743,9 @@
     sent_out[tail:, :LANES] = add(table_ref[...], other_table_ref[...]).astype(bf16)
 
 
-def input_kernel(
-    slots, rank_ref, tokens_ref, gain_ref, after_ref, grads_ref, kept_ref, came_ref, queries_any, slot_after_ref,
-    slot_grads_ref, wq_ref, wk_ref, wv_ref, tokens_out, queries_out, slot_room, sem,
-):
-    narrow_size = queries_any.shape[0] // slots
-    first = (rank_ref[0] & (narrow_size - 1)) * slots
-    load = pltpu.make_async_copy(queries_any.at[pl.ds(first, slots)], slot_room, sem)
-    load.start()
+def doc_input_kernel(
+    tokens_ref, gain_ref, after_ref, grads_ref, kept_ref, came_ref, wq_ref, wk_ref, wv_ref, tokens_out
+):
     rows, width = tokens_ref.shape
     rest = grads_ref.shape[0] - rows // 2
     query = jnp.concatenate([grads_ref[rest:, :width], grads_ref[rest:, width:]], 0)
@@ -820,11 +753,21 @@
     tokens_out[...] = input_back(
         tokens_ref[...].astype(f32), gain_ref, after_ref, query, pair[:, :width], pair[:, width:], wq_ref, wk_ref, wv_ref
     )
+
+
+def slot_input_kernel(
+    slots, rank_ref, tokens_any, gain_ref, after_ref, grads_ref, wq_ref, wk_ref, wv_ref, tokens_out, slot_room, sem
+):
+    narrow_size = tokens_any.shape[0] // slots
+    first = (rank_ref[0] & (narrow_size - 1)) * slots
+    load = pltpu.make_async_copy(tokens_any.at[pl.ds(first, slots)], slot_room, sem)
+    load.start()
     load.wait()
-    query, key, value = (slot_grads_ref[:, place * width : (place + 1) * width] for place in range(3))
-    queries_out[...] = input_back(
-        slot_room[...].reshape(queries_out.shape).astype(f32), gain_ref, slot_after_ref, query, key, value, wq_ref,
-        wk_ref, wv_ref,
+    width = tokens_out.shape[1]
+    query, key, value = (grads_ref[:, place * width : (place + 1) * width] for place in range(3))
+    tokens_out[...] = input_back(
+        slot_room[...].reshape(tokens_out.shape).astype(f32), gain_ref, after_ref, query, key, value, wq_ref, wk_ref,
+        wv_ref,
     )
 
 
@@ -853,7 +796,12 @@
     dma = pltpu.SemaphoreType.DMA
     waxes = list(range(3, bits))
 
-    orders = ([1, 2] + waxes, waxes[:1] + [1, 2] + waxes[1:], [1] + waxes[:1] + [2] + waxes[1:], [2] + waxes[:1] + [1] + waxes[1:])
+    orders = (
+        waxes[:1] + [2] + [1] + waxes[1:],
+        [1] + [2] + waxes[:1] + waxes[1:],
+        waxes[:1] + [2] + [1] + waxes[1:],
+        [2] + [1] + waxes[:1] + waxes[1:],
+    )
     own_tokens = doc_tokens[0]
     y_tokens = swap(own_tokens, 2)
     core_tokens = swap(own_tokens, 1)
@@ -902,10 +850,8 @@
             rank_word, query_lengths, query_tokens, own_tokens, core_tokens, y_tokens, both_tokens, doc_bias, slot_bias,
             *gains, *weights,
         ],
-        "ssa" + "v" * 9 + "h" * 8 + "a" * len(forward_shapes),
-        [room(value) for value in forward_shapes]
-        + [room(weight) for weight in weights]
-        + [slot_room, dma((8,)), dma((len(forward_shapes),)), dma],
+        "ssa" + "v" * 9 + "v" * 8 + "v" * len(forward_shapes),
+        [slot_room, dma],
         vmem=VM[0],
         us=18,
     )
@@ -994,8 +940,8 @@
                 [after(grad_slot_unit, pieces[1], turned_came)]
                 + [embed, after_feed, after_attend, gate_slope, up_slope, gains[1], gains[2]]
                 + back_weights,
-                "v" * 8 + "a" * 5,
-                [room(weight) for weight in back_weights] + [pltpu.VMEM((slot_rows, width), f32), dma((5,))],
+                "",
+                [pltpu.VMEM((slot_rows, width), f32)],
                 vmem=VM[1],
                 us=7,
             )
@@ -1018,8 +964,8 @@
         parts + after(came, slot_came)
         + [embed, after_feed, after_attend, gate_slope, up_slope, gains[1], gains[2]]
         + back_weights,
-        "v" * (8 + len(came)) + "a" * 5,
-        [room(weight) for weight in back_weights] + [pltpu.VMEM((doc_rows, width), f32), dma((5,))],
+        "",
+        [pltpu.VMEM((doc_rows, width), f32)],
         vmem=VM[2],
         us=7,
     )
@@ -1101,48 +1047,64 @@
         fourth_kept,
     )
     third = weight_product([(4 * small_half, units // 2, 2 * units, width)], orders[2], second.kept)
-    done = third.kept
-    for step in range(bits - 1):
-        for stream in (first, fourth, second, third):
-            done = stream.advance(done)
-        if step == 0:
-            pair_came = swap(after(pair_sent, done), 2)
-        if step == 2:
-            doc_grad, query_grad = call(
-                functools.partial(input_kernel, slots),
-                [shape((doc_rows, width)), shape((slot_rows, width))],
-                [rank_word, own_tokens, gains[0], doc_after, att_grads, pair_kept, after(pair_came, done)]
-                + [query_tokens, slot_after, slot_thirds, query_weight, key_weight, value_weight],
-                "s" + "v" * 6 + "a",
-                [slot_room, dma],
-                us=4,
-            )
-            done = doc_grad
-
     def own_rows(values):
         return lax.dynamic_slice_in_dim(values, rank * (width >> bits), width >> bits, 0).astype(f32)
 
     def gain_grad(gain, *pairs):
         return sum(jnp.sum(own_rows(weight) * grad, 1) for weight, grad in pairs) / own_rows(gain)
 
+    streams = {"A": first, "B": second, "C": third, "D": fourth}
+    plan = "JADBACDpBADCBCIABDC"
+    if bits != 5:
+        plan = "J" + "ADBC" + "p" + "ADBC" * (bits - 3) + "I" + "ABDC"
+    done = third.kept
+    for event in plan[:-1]:
+        if event in streams:
+            done = streams[event].advance(done)
+        elif event == "p":
+            pair_came = swap(after(pair_sent, done), 2)
+        elif event == "I":
+            (done,) = call(
+                doc_input_kernel,
+                [shape((doc_rows, width))],
+                [own_tokens, gains[0], doc_after, att_grads, pair_kept, after(pair_came, done)]
+                + [query_weight, key_weight, value_weight],
+                us=3,
+            )
+            doc_grad = done
+        else:
+            (done,) = call(
+                functools.partial(slot_input_kernel, slots),
+                [shape((slot_rows, width))],
+                [rank_word, query_tokens, gains[0], slot_after, after(slot_thirds, done)]
+                + [query_weight, key_weight, value_weight],
+                "sa",
+                [slot_room, dma],
+                us=3,
+            )
+            query_grad = done
     gate_grad, output_grad = first.result[:, :units], first.result[:, units:]
     up_grad, proj_grad = second.result[:, :units], second.result[:, units:]
     query_g, key_g, value_g = (fourth.result[:, place * width : (place + 1) * width] for place in range(3))
+    attend_gain_grad = gain_grad(attend_gain, (query_weight, query_g), (key_weight, key_g), (value_weight, value_g))
+    feed_gain_grad = gain_grad(feed_gain, (gate_weight, gate_grad), (up_weight, up_grad))
+    final_gain_grad = gain_grad(final_gain, (proj_weight, proj_grad))
+    third.advance(done, attend_gain_grad, feed_gain_grad, final_gain_grad)
     return (
         losses[:, 0],
         doc_grad[None],
         query_grad.reshape(slots, slot_length, width),
-        gain_grad(attend_gain, (query_weight, query_g), (key_weight, key_g), (value_weight, value_g)),
+        attend_gain_grad,
         query_g,
         key_g,
         value_g,
         output_grad,
         fourth.small[:heads, :BUCKETS].astype(f32).T,
-        gain_grad(feed_gain, (gate_weight, gate_grad), (up_weight, up_grad)),
+        feed_gain_grad,
         gate_grad,
         up_grad,
         third.result,
-        gain_grad(final_gain, (proj_weight, proj_grad)),
+        final_gain_grad,
         proj_grad,
     )
 

time: 187 us -> 172 us (0.920)
  Pallas kernels: 79.4 us -> 64.8 us
  waiting for transfers between devices: 46.5 us -> 54.4 us
  local copies, waits for them, and re-layouts: 11.5 us -> 4.87 us
    pallas_call x23 -> x24, Pallas kernels: 79.4 us -> 64.8 us  [call(): pl.pallas_call(kernel, out_shape=tuple(outs), in_specs=specs[:len(args)],...]
    ppermute x40, waiting for transfers between devices: 46.5 us -> 54.4 us  [swap(): return lax.ppermute(values, ('wide', 'narrow'), pairs)]
    unnamed x105 -> x71, local copies, waits for them, and re-layouts: 10.2 us -> 3.57 us
  transfers between devices with their start and end apart: 40 -> 40, of which waited for: 14 -> 20; matrix products, arithmetic and copies ran while one was open for 4% -> 5% of each run, Pallas kernels for 27% -> 26%
where the time goes in v5:
time: 172 us
  Pallas kernels  64.8 us (38%)
  waiting for transfers between devices  54.4 us (32%)
  starting transfers between devices  38.4 us (22%)
  other arithmetic  8.17 us (5%)
  local copies, waits for them, and re-layouts  4.87 us (3%)
    pallas_call x24, Pallas kernels, call(): pl.pallas_call(kernel, out_shape=tuple(outs), in_specs=specs[:len(args)],...  64.8 us
    ppermute x40, waiting for transfers between devices, swap(): return lax.ppermute(values, ('wide', 'narrow'), pairs)  54.4 us
    ppermute x40, starting transfers between devices, swap(): return lax.ppermute(values, ('wide', 'narrow'), pairs)  38.4 us
    reduce_sum x3, other arithmetic, gain_grad(): jnp.sum(own_rows(weight) * grad, 1)  4.08 us
    unnamed x71, local copies, waits for them, and re-layouts  3.57 us
  transfers between devices with their start and end apart: 40, of which 20 were waited for; matrix products, arithmetic and copies ran while one was open for 5% of the time, Pallas kernels for 26%

profile of v5, /device:TPU:0, one launch (start us, length us, event | category | flops | bytes accessed | tf_op | source)
XLA Modules:
  0.0 171.9 jit_solution(16873571223195797546)
XLA Ops:
  0.6 3.0 %collective-permute-start.1 = (bf16[128,768]{1,0:T(8,128)(2,1)}, bf16[128,768]{1,0:T(8,128)(2,1)S(1)}, u32[]{:S(2)}, u32[]{:S(2)}) collective-permute-start(bf16[128,768]{1,0:T(8,128)(2,1)} %bitcast.12), channel_id=1, source_target_pairs={{0,2},{1,3},{2,0},{3,1},{4,6},{5,7},{6,4},{7,5},{8,10},{9,11},{10,... | collective-permute-start | bytes 589832 | tf_op jit(solution)/shard_map/ppermute | solution.py:55
  3.7 0.8 copy.33.table_ref
  4.6 2.7 %shard_map.280 = (f32[6,256,512]{2,1,0:T(8,128)S(1)}, f32[6,256,128]{2,1,0:T(8,128)S(1)}) custom-call(s32[1]{0:T(128)} %bitcast.rank_ref, f32[32,12]{1,0:T(8,128)S(1)} %copy.33.table_ref), custom_call_target="tpu_custom_call" | custom-call | flops 3300000000 | tf_op jit(solution)/shard_map/pallas_call | solution.py:115
  7.3 1.5 collective-permute-done.1.far_ref
  8.8 1.4 collective-permute-done.2.last_ref
  10.4 1.9 %copy-done.14 = bf16[2048,768]{1,0:T(8,128)(2,1)S(1)} copy-done((bf16[2048,768]{1,0:T(8,128)(2,1)S(1)}, bf16[2048,768]{1,0:T(8,128)(2,1)}, u32[]{:S(2)}) %copy-start.14) | copy-done | bytes 3145752
  12.2 13.1 %shard_map.281 = (bf16[640,768]{1,0:T(8,128)(2,1)S(1)}, bf16[256,768]{1,0:T(8,128)(2,1)S(1)}, bf16[640,768]{1,0:T(8,128)(2,1)S(1)}, bf16[640,768]{1,0:T(8,128)(2...) custom-call(s32[1]{0:T(128)} %bitcast.rank_ref, ...), custom_call_target="tpu_custom_call" | custom-call | flops 19800000512 | tf_op jit(solution)/shard_map/pallas_call | solution.py:115
  25.3 1.9 %collective-permute-start.3 = (bf16[1,128,128]{2,1,0:T(8,128)(2,1)S(1)}, bf16[1,128,128]{2,1,0:T(8,128)(2,1)S(1)}, u32[]{:S(2)}, u32[]{:S(2)}) collective-permute-start(bf16[1,128,128]{2,1,0:T(8,128)(2,1)S(1)} %bitcast.8), channel_id=1, source_target_pairs={{0,8},{1,9},{2,10},{3,11},{4,12},{5,13},{6,14},{7,15},{8,0},{9,1},... | collective-permute-start | bytes 98312 | tf_op jit(solution)/shard_map/ppermute | solution.py:55
  27.2 2.6 %collective-permute-start.4 = (bf16[1,128,128]{2,1,0:T(8,128)(2,1)S(1)}, bf16[1,128,128]{2,1,0:T(8,128)(2,1)S(1)}, u32[]{:S(2)}, u32[]{:S(2)}) collective-permute-start(bf16[1,128,128]{2,1,0:T(8,128)(2,1)S(1)} %bitcast.9), channel_id=1, source_target_pairs={{0,16},{1,17},{2,18},{3,19},{4,20},{5,21},{6,22},{7,23},{8,24},{9,... | collective-permute-start | bytes 98312 | tf_op jit(solution)/shard_map/ppermute | solution.py:55
  29.8 4.9 %shard_map.282 = (bf16[32,128,128]{2,1,0:T(8,128)(2,1)S(1)}, f32[128,128]{1,0:T(8,128)S(1)}) custom-call(s32[1]{0:T(128)} %bitcast.rank_ref, s32[16,32,128]{2,1,0:T(8,128)S(1)} %copy-done.23), custom_call_target="tpu_custom_call" | custom-call | flops 5500000256 | tf_op jit(solution)/shard_map/pallas_call | solution.py:115
  34.7 0.8 collective-permute-done.5
  35.5 1.6 collective-permute-start.6
  37.1 1.5 collective-permute-start.7
  39.1 4.8 %shard_map.283 = (bf16[256,2944]{1,0:T(8,128)(2,1)S(1)}, bf16[256,2944]{1,0:T(8,128)(2,1)S(1)}, bf16[512,384]{1,0:T(8,128)(2,1)S(1)}) custom-call(s32[1]{0:T(128)} %bitcast.rank_ref, bf16[640,768]{1,0:T(8,128)(2,1)S(1)} %get-tuple-element.167.all_ref, bf16[256,768]{1,0:T(8,128)(2,1)S(1)} %get-tuple-element.168.normed_feed_ref, ...), custom_call_target="tpu_custom_call" | custom-call | flops 5500000256 | tf_op jit(solution)/shard_map/pallas_call | solution.py:115
  44.7 1.9 %collective-permute-done.9.far_ref = bf16[16,128,128]{2,1,0:T(8,128)(2,1)S(1)} collective-permute-done((bf16[16,128,128]{2,1,0:T(8,128)(2,1)S(1)}, bf16[16,128,128]{2,1,0:T(8,128)(2,1)S(1)}, u32[]{:S(2)}, u32[]{:S(2)}) %collective-permute-start.9) | collective-permute-done | bytes 524320 | tf_op jit(solution)/shard_map/ppermute | solution.py:55
  46.6 3.2 %shard_map.284 = (f32[4,128]{1,0:T(4,128)S(1)}, f32[128,128]{1,0:T(8,128)S(1)}, bf16[16,128,128]{2,1,0:T(8,128)(2,1)S(1)}, bf16[16,128,128]{2,1,0:T(8,128)(2,1)S(1)}) custom-call(s32[1]{0:T(128)} %bitcast.rank_ref, s32[16]{0:T(128)S(1)} %copy-done.26, s32[16]{0:T(128)S(1)} %copy-done.27, bf16[32,128,128]{2,1,0:T(8,128)(2,1)S(1)} %get-tuple-element.156.counts_ref, ...), custom_call_target="tpu_custom_call" | custom-call | flops 3300000000 | tf_op jit(solution)/shard_map/pallas_call | solution.py:115
  50.4 3.6 %collective-permute-done.10 = bf16[16,128,128]{2,1,0:T(8,128)(2,1)S(1)} collective-permute-done((bf16[16,128,128]{2,1,0:T(8,128)(2,1)S(1)}, bf16[16,128,128]{2,1,0:T(8,128)(2,1)S(1)}, u32[]{:S(2)}, u32[]{:S(2)}) %collective-permute-start.10) | collective-permute-done | bytes 524320 | tf_op jit(solution)/shard_map/ppermute | solution.py:55
  54.1 1.0 collective-permute-start.11
  55.1 1.5 collective-permute-start.12
  56.6 1.0 collective-permute-start.13
  57.7 4.6 %shard_map.285 = (bf16[128,5760]{1,0:T(8,128)(2,1)S(1)}, f32[128,768]{1,0:T(8,128)S(1)}, bf16[128,768]{1,0:T(8,128)(2,1)S(1)}) custom-call(f32[128,128]{1,0:T(8,128)S(1)} %get-tuple-element.183.grad_unit_ref, f32[256,128]{1,0:T(8,128)S(1)} %get-tuple-element.184.embed_ref.refs_4_, f32[256,768]{1,0:T(8,128)S(1)} %get-tuple-element.185.after_feed_ref.refs_5_, ...), custom_call_target="tpu_custom_call" | custom-call | flops 7699999744 | tf_op jit(solution)/shard_map/pallas_call | solution.py:115
  62.3 0.9 collective-permute-done.12
  63.3 1.5 collective-permute-start.15
  64.8 2.5 %collective-permute-start.16 = (bf16[1,128,128]{2,1,0:T(8,128)(2,1)S(1)}, bf16[1,128,128]{2,1,0:T(8,128)(2,1)S(1)}, u32[]{:S(2)}, u32[]{:S(2)}) collective-permute-start(bf16[1,128,128]{2,1,0:T(8,128)(2,1)S(1)} %get-tuple-element.304), channel_id=1, source_target_pairs={{0,8},{1,9},{2,10},{3,11},{4,12},{5,13},{6,14},{7,15},{8,0},{9,1},... | collective-permute-start | bytes 98312 | tf_op jit(solution)/shard_map/ppermute | solution.py:55
  67.8 3.0 %shard_map.286 = (bf16[128,2304]{1,0:T(8,128)(2,1)S(1)}, f32[12,128]{1,0:T(8,128)S(1)}) custom-call(bf16[256,768]{1,0:T(8,128)(2,1)S(1)} %get-tuple-element.193.query_ref, bf16[640,768]{1,0:T(8,128)(2,1)S(1)} %get-tuple-element.194.key_ref, bf16[640,768]{1,0:T(8,128)(2,1)S(1)} %get-tuple-element.195.value_ref, ...), custom_call_target="tpu_custom_call" | custom-call | flops 4400000000 | tf_op jit(solution)/shard_map/pallas_call | solution.py:115
  70.8 2.1 %collective-permute-done.17.refs_3_ = bf16[1,128,128]{2,1,0:T(8,128)(2,1)S(1)} collective-permute-done((bf16[1,128,128]{2,1,0:T(8,128)(2,1)S(1)}, bf16[1,128,128]{2,1,0:T(8,128)(2,1)S(1)}, u32[]{:S(2)}, u32[]{:S(2)}) %collective-permute-start.17) | collective-permute-done | bytes 32800 | tf_op jit(solution)/shard_map/ppermute | solution.py:55
  73.0 4.5 %shard_map.287 = (bf16[128,5760]{1,0:T(8,128)(2,1)S(1)}, f32[128,768]{1,0:T(8,128)S(1)}, bf16[128,768]{1,0:T(8,128)(2,1)S(1)}) custom-call(bf16[1,128,128]{2,1,0:T(8,128)(2,1)S(1)} %get-tuple-element.306.refs_0_, bf16[1,128,128]{2,1,0:T(8,128)(2,1)S(1)} %collective-permute-done.15.refs_1_, bf16[1,128,128]{2,1,0:T(8,128)(2,1)S(1)} %collective-permute-done.16.refs_2_, ...), custom_call_target="tpu_custom_call" | custom-call | flops 7699999744 | tf_op jit(solution)/shard_map/pallas_call | solution.py:115
  77.6 5.1 %shard_map.288 = (bf16[576,1536]{1,0:T(8,128)(2,1)S(1)}, bf16[16,128]{1,0:T(8,128)(2,1)S(1)}) custom-call(s32[1]{0:T(128)} %bitcast.rank_ref, bf16[256,768]{1,0:T(8,128)(2,1)S(1)} %get-tuple-element.193.query_ref, bf16[640,768]{1,0:T(8,128)(2,1)S(1)} %get-tuple-element.194.key_ref, bf16[640,768]{1,0:T(8,128)(2,1)S(1)} %get-tuple-element.195.value_ref, ...), custom_call_target="tpu_custom_call" | custom-call | flops 3300000000 | tf_op jit(solution)/shard_map/pallas_call | solution.py:115
  83.8 2.7 %shard_map.289 = (bf16[192,2816]{1,0:T(8,128)(2,1)S(1)}, bf16[192,2816]{1,0:T(8,128)(2,1)S(1)}) custom-call(bf16[256,2944]{1,0:T(8,128)(2,1)S(1)} %get-tuple-element.237.kept_any, bf16[256,2944]{1,0:T(8,128)(2,1)S(1)} %collective-permute-done.14.came_any, bf16[128,5760]{1,0:T(8,128)(2,1)S(1)} %get-tuple-element.239.slot_any, ...), custom_call_target="tpu_custom_call" | custom-call | flops 3300000000 | tf_op jit(solution)/shard_map/pallas_call | solution.py:115
  86.5 0.9 collective-permute-done.22.other_table_ref
  87.5 3.4 %shard_map.290 = (bf16[192,2304]{1,0:T(8,128)(2,1)S(1)}, bf16[208,2304]{1,0:T(8,128)(2,1)S(1)}, bf16[128,1536]{1,0:T(8,128)(2,1)S(1)}, bf16[128,1536]{1,0:T(8,128)(2,1)S(1)}) custom-call(bf16[512,384]{1,0:T(8,128)(2,1)S(1)} %get-tuple-element.212.doc_ref, bf16[256,2944]{1,0:T(8,128)(2,1)S(1)} %get-tuple-element.237.kept_any, ...), custom_call_target="tpu_custom_call" | custom-call | flops 3300000000 | tf_op jit(solution)/shard_map/pallas_call | solution.py:115
  90.8 1.3 collective-permute-start.23
  92.2 2.4 %shard_map.291 = (bf16[192,2176]{1,0:T(8,128)(2,1)S(1)}, bf16[192,2176]{1,0:T(8,128)(2,1)S(1)}) custom-call(bf16[256,2944]{1,0:T(8,128)(2,1)S(1)} %get-tuple-element.237.kept_any, bf16[256,2944]{1,0:T(8,128)(2,1)S(1)} %collective-permute-done.14.came_any, bf16[128,5760]{1,0:T(8,128)(2,1)S(1)} %get-tuple-element.239.slot_any, ...), custom_call_target="tpu_custom_call" | custom-call | flops 3300000000 | tf_op jit(solution)/shard_map/pallas_call | solution.py:115
  94.6 0.9 collective-permute-start.28
  95.5 2.1 %shard_map.292 = (bf16[512,768]{1,0:T(8,128)(2,1)S(1)}, bf16[512,768]{1,0:T(8,128)(2,1)}) custom-call(bf16[256,2944]{1,0:T(8,128)(2,1)S(1)} %get-tuple-element.237.kept_any, bf16[256,2944]{1,0:T(8,128)(2,1)S(1)} %collective-permute-done.14.came_any, bf16[128,5760]{1,0:T(8,128)(2,1)S(1)} %get-tuple-element.239.slot_any, ...), custom_call_target="tpu_custom_call" | custom-call | flops 3300000000 | tf_op jit(solution)/shard_map/pallas_call | solution.py:115
  97.7 2.6 %shard_map.293 = f32[128,768]{1,0:T(8,128)} custom-call(s32[1]{0:T(128)} %bitcast.rank_ref, bf16[16,32,768]{2,1,0:T(8,128)(2,1)S(1)} %copy-done.20, f32[768]{0:T(1024)S(1)} %copy-done.11, f32[128,768]{1,0:T(8,128)S(1)} %get-tuple-element.189.after_ref, bf16[128,2304]{1,0:T(8,128)(2,1)S(1)} %get-tuple-element.244.slot_any.grads_ref, ...), custom_call_target="tpu_custom_call" | custom-call | flops 3300000000 | tf_op jit(solution)/shard_map/pallas_call | solution.py:115
  100.3 12.0 %collective-permute-done.24.came_ref = bf16[192,2816]{1,0:T(8,128)(2,1)S(1)} collective-permute-done((bf16[192,2816]{1,0:T(8,128)(2,1)S(1)}, bf16[192,2816]{1,0:T(8,128)(2,1)S(1)}, u32[]{:S(2)}, u32[]{:S(2)}) %collective-permute-start.24) | collective-permute-done | bytes 1081376 | tf_op jit(solution)/shard_map/ppermute | solution.py:55
  112.6 1.3 collective-permute-start.27
  114.4 0.9 shard_map.295
  115.4 1.5 collective-permute-start.25
  116.9 0.9 shard_map.296
  118.4 9.5 %collective-permute-done.27.came_ref = bf16[96,2816]{1,0:T(8,128)(2,1)S(1)} collective-permute-done((bf16[96,2816]{1,0:T(8,128)(2,1)S(1)}, bf16[96,2816]{1,0:T(8,128)(2,1)S(1)}, u32[]{:S(2)}, u32[]{:S(2)}) %collective-permute-start.27) | collective-permute-done | bytes 540704 | tf_op jit(solution)/shard_map/ppermute | solution.py:55
  127.9 0.8 shard_map.297
  128.7 0.7 copy-done
  129.4 1.5 collective-permute-start.32
  130.9 0.6 slice_reduce_fusion
  131.5 1.0 collective-permute-done.26.came_ref
  132.8 0.8 collective-permute-start.30
  133.7 2.9 %collective-permute-done.33.came_ref = bf16[96,2176]{1,0:T(8,128)(2,1)S(1)} collective-permute-done((bf16[96,2176]{1,0:T(8,128)(2,1)}, bf16[96,2176]{1,0:T(8,128)(2,1)S(1)}, u32[]{:S(2)}, u32[]{:S(2)}) %collective-permute-start.33) | collective-permute-done | bytes 417824 | tf_op jit(solution)/shard_map/ppermute | solution.py:55
  137.0 1.8 %collective-permute-start.35 = (bf16[48,2176]{1,0:T(8,128)(2,1)S(1)}, bf16[48,2176]{1,0:T(8,128)(2,1)S(1)}, u32[]{:S(2)}, u32[]{:S(2)}) collective-permute-start(bf16[48,2176]{1,0:T(8,128)(2,1)S(1)} %get-tuple-element.274), channel_id=1, source_target_pairs={{0,8},{1,9},{2,10},{3,11},{4,12},{5,13},{6,14},{7,15},{8,0},{9,1},... | collective-permute-start | bytes 626696 | tf_op jit(solution)/shard_map/ppermute | solution.py:55
  138.8 1.8 %collective-permute-start.29 = (bf16[128,1536]{1,0:T(8,128)(2,1)S(1)}, bf16[128,1536]{1,0:T(8,128)(2,1)S(1)}, u32[]{:S(2)}, u32[]{:S(2)}) collective-permute-start(bf16[128,1536]{1,0:T(8,128)(2,1)S(1)} %copy-done.22), channel_id=1, source_target_pairs={{0,2},{1,3},{2,0},{3,1},{4,6},{5,7},{6,4},{7,5},{8,10},{9,11},{10,... | collective-permute-start | bytes 1179656 | tf_op jit(solution)/shard_map/ppermute | solution.py:55
  140.6 1.1 add_convert_fusion
  141.8 4.4 %collective-permute-done.31 = bf16[64,2304]{1,0:T(8,128)(2,1)S(1)} collective-permute-done((bf16[64,2304]{1,0:T(8,128)(2,1)S(1)}, bf16[64,2304]{1,0:T(8,128)(2,1)S(1)}, u32[]{:S(2)}, u32[]{:S(2)}) %collective-permute-start.31) | collective-permute-done | bytes 294944 | tf_op jit(solution)/shard_map/ppermute | solution.py:55
  146.4 3.6 %collective-permute-done.35 = bf16[48,2176]{1,0:T(8,128)(2,1)S(1)} collective-permute-done((bf16[48,2176]{1,0:T(8,128)(2,1)S(1)}, bf16[48,2176]{1,0:T(8,128)(2,1)S(1)}, u32[]{:S(2)}, u32[]{:S(2)}) %collective-permute-start.35) | collective-permute-done | bytes 208928 | tf_op jit(solution)/shard_map/ppermute | solution.py:55
  150.0 2.1 %collective-permute-start.34 = (bf16[128,768]{1,0:T(8,128)(2,1)S(1)}, bf16[128,768]{1,0:T(8,128)(2,1)S(1)}, u32[]{:S(2)}, u32[]{:S(2)}) collective-permute-start(bf16[128,768]{1,0:T(8,128)(2,1)S(1)} %get-tuple-element.273), channel_id=1, source_target_pairs={{0,2},{1,3},{2,0},{3,1},{4,6},{5,7},{6,4},{7,5},{8,10},{9,11},{10,... | collective-permute-start | bytes 589832 | tf_op jit(solution)/shard_map/ppermute | solution.py:55
  152.8 2.5 %collective-permute-start.36 = (bf16[40,2304]{1,0:T(8,128)(2,1)S(1)}, bf16[40,2304]{1,0:T(8,128)(2,1)S(1)}, u32[]{:S(2)}, u32[]{:S(2)}) collective-permute-start(bf16[40,2304]{1,0:T(8,128)(2,1)S(1)} %pad_maximum_fusion), channel_id=1, source_target_pairs={{0,16},{1,17},{2,18},{3,19},{4,20},{5,21},{6,22},{7,23},{8,24},{9,... | collective-permute-start | bytes 552968 | tf_op jit(solution)/shard_map/ppermute | solution.py:55
  156.0 2.2 %shard_map.303 = f32[128,768]{1,0:T(8,128)} custom-call(bf16[128,768]{1,0:T(8,128)(2,1)S(1)} %bitcast.15, f32[768]{0:T(1024)S(1)} %copy-done.11, f32[128,768]{1,0:T(8,128)S(1)} %copy-done.31, bf16[576,1536]{1,0:T(8,128)(2,1)S(1)} %copy-done.17, bf16[128,1536]{1,0:T(8,128)(2,1)S(1)} %copy-done.29, bf16[128,1536]{1,0:T(8,128)(2,1)S(1)} %collective-permute-done.29.came_ref, ...), custom_call_target="tpu_custom_call" | custom-call | flops 3300000000 | tf_op jit(solution)/shard_map/pallas_call | solution.py:115
  158.7 1.8 %multiply_reduce_fusion = (f32[24]{0:T(128)S(1)}, f32[24,2048]{1,0:T(8,128)}, f32[24]{0:T(128)S(1)}, f32[24,2048]{1,0:T(8,128)}) fusion(bf16[768,2048]{1,0:T(8,128)(2,1)} %refs_14_.1, s32[]{:T(128)S(6)} %select_n.2, f32[24,2176]{1,0:T(8,128)S(1)} %convert_add_fusion.2, f32[24,2816]{1,0:T(8,128)S(1)} %convert_add_fusion, bf16[768,2048]{1,0:T(8,128)(2,1)} %refs_13_.1), kind=kLoop, calls=%fused_computation.14 | loop fusion | flops 294864 | bytes 983236 | tf_op jit(solution)/shard_map/reduce_sum | solution.py:1054
  160.5 1.4 multiply_reduce_fusion.5
  161.9 2.8 %collective-permute-done.36 = bf16[40,2304]{1,0:T(8,128)(2,1)S(1)} collective-permute-done((bf16[40,2304]{1,0:T(8,128)(2,1)S(1)}, bf16[40,2304]{1,0:T(8,128)(2,1)S(1)}, u32[]{:S(2)}, u32[]{:S(2)}) %collective-permute-start.36) | collective-permute-done | bytes 184352 | tf_op jit(solution)/shard_map/ppermute | solution.py:55
  164.7 0.8 multiply_reduce_fusion.3
  167.4 0.6 slice.210
  168.1 3.2 %collective-permute-done.39 = bf16[64,768]{1,0:T(8,128)(2,1)S(1)} collective-permute-done((bf16[64,768]{1,0:T(8,128)(2,1)S(1)}, bf16[64,768]{1,0:T(8,128)(2,1)S(1)}, u32[]{:S(2)}, u32[]{:S(2)}) %collective-permute-start.39) | collective-permute-done | bytes 98336 | tf_op jit(solution)/shard_map/ppermute | solution.py:55
  171.2 0.7 convert_add_fusion.3
  (134 shorter events, 10.0 us)
Async XLA Ops:
  0.6 8.1 %collective-permute-start.1 = (bf16[128,768]{1,0:T(8,128)(2,1)}, bf16[128,768]{1,0:T(8,128)(2,1)S(1)}, u32[]{:S(2)}, u32[]{:S(2)}) collective-permute-start(bf16[128,768]{1,0:T(8,128)(2,1)} %bitcast.12), channel_id=1, source_target_pairs={{0,2},{1,3},{2,0},{3,1},{4,6},{5,7},{6,4},{7,5},{8,10},{9,11},{10,... | collective-permute-start | bytes 589832 | tf_op jit(solution)/shard_map/ppermute | solution.py:55
  3.7 5.1 %collective-permute-start = (bf16[128,768]{1,0:T(8,128)(2,1)}, bf16[128,768]{1,0:T(8,128)(2,1)S(1)}, u32[]{:S(2)}, u32[]{:S(2)}) collective-permute-start(bf16[128,768]{1,0:T(8,128)(2,1)} %bitcast.13), channel_id=1, source_target_pairs={{0,1},{1,0},{2,3},{3,2},{4,5},{5,4},{6,7},{7,6},{8,9},{9,8},{10,11... | collective-permute-start | bytes 589832 | tf_op jit(solution)/shard_map/ppermute | solution.py:55
  4.5 5.8 %copy-start.2 = (bf16[768,2048]{1,0:T(8,128)(2,1)S(1)}, bf16[768,2048]{1,0:T(8,128)(2,1)}, u32[]{:S(2)}) copy-start(bf16[768,2048]{1,0:T(8,128)(2,1)} %refs_13_.1) | copy-start | bytes 9437188
  4.5 5.8 %copy-start.3 = (bf16[768,2048]{1,0:T(8,128)(2,1)S(1)}, bf16[768,2048]{1,0:T(8,128)(2,1)}, u32[]{:S(2)}) copy-start(bf16[768,2048]{1,0:T(8,128)(2,1)} %refs_14_.1) | copy-start | bytes 9437188
  4.5 5.8 %copy-start.4 = (bf16[768,768]{1,0:T(8,128)(2,1)S(1)}, bf16[768,768]{1,0:T(8,128)(2,1)}, u32[]{:S(2)}) copy-start(bf16[768,768]{1,0:T(8,128)(2,1)} %wq_ref.5) | copy-start | bytes 3538948
  4.5 5.8 %copy-start.6 = (bf16[768,768]{1,0:T(8,128)(2,1)S(1)}, bf16[768,768]{1,0:T(8,128)(2,1)}, u32[]{:S(2)}) copy-start(bf16[768,768]{1,0:T(8,128)(2,1)} %wk_ref.5) | copy-start | bytes 3538948
  4.5 5.8 %copy-start.8 = (bf16[768,768]{1,0:T(8,128)(2,1)S(1)}, bf16[768,768]{1,0:T(8,128)(2,1)}, u32[]{:S(2)}) copy-start(bf16[768,768]{1,0:T(8,128)(2,1)} %wv_ref.5) | copy-start | bytes 3538948
  4.5 5.8 %copy-start.10 = (bf16[768,128]{1,0:T(8,128)(2,1)S(1)}, bf16[768,128]{1,0:T(8,128)(2,1)}, u32[]{:S(2)}) copy-start(bf16[768,128]{1,0:T(8,128)(2,1)} %refs_11_.1) | copy-start | bytes 589828
  4.5 5.8 %copy-start.11 = (f32[768]{0:T(1024)S(1)}, f32[768]{0:T(1024)}, u32[]{:S(2)}) copy-start(f32[768]{0:T(1024)} %gain_ref.3) | copy-start | bytes 9220
  4.5 5.8 %copy-start.12 = (f32[768]{0:T(1024)S(1)}, f32[768]{0:T(1024)}, u32[]{:S(2)}) copy-start(f32[768]{0:T(1024)} %refs_10_.1) | copy-start | bytes 9220
  4.5 5.8 %copy-start.13 = (f32[768]{0:T(1024)S(1)}, f32[768]{0:T(1024)}, u32[]{:S(2)}) copy-start(f32[768]{0:T(1024)} %refs_9_.1) | copy-start | bytes 9220
  4.5 5.8 %copy-start.18 = (bf16[768,768]{1,0:T(8,128)(2,1)S(1)}, bf16[768,768]{1,0:T(8,128)(2,1)}, u32[]{:S(2)}) copy-start(bf16[768,768]{1,0:T(8,128)(2,1)} %refs_15_.1) | copy-start | bytes 3538948
  4.5 5.8 %copy-start.19 = (bf16[16,32,768]{2,1,0:T(8,128)(2,1)S(1)}, bf16[16,32,768]{2,1,0:T(8,128)(2,1)}, u32[]{:S(2)}) copy-start(bf16[16,32,768]{2,1,0:T(8,128)(2,1)} %tokens_any.1) | copy-start | bytes 2359300
  4.6 5.8 %copy-start.24 = (bf16[1,128,768]{2,1,0:T(8,128)(2,1)S(1)}, bf16[1,128,768]{2,1,0:T(8,128)(2,1)}, u32[]{:S(2)}) copy-start(bf16[1,128,768]{2,1,0:T(8,128)(2,1)} %param.17) | copy-start | bytes 589828
  8.8 1.4 collective-permute-start.2
  12.2 17.6 %copy-start.23 = (s32[16,32,128]{2,1,0:T(8,128)S(1)}, s32[16,32,128]{2,1,0:T(8,128)}, u32[]{:S(2)}) copy-start(s32[16,32,128]{2,1,0:T(8,128)} %picked_ref) | copy-start | bytes 786436
  25.3 9.3 %collective-permute-start.3 = (bf16[1,128,128]{2,1,0:T(8,128)(2,1)S(1)}, bf16[1,128,128]{2,1,0:T(8,128)(2,1)S(1)}, u32[]{:S(2)}, u32[]{:S(2)}) collective-permute-start(bf16[1,128,128]{2,1,0:T(8,128)(2,1)S(1)} %bitcast.8), channel_id=1, source_target_pairs={{0,8},{1,9},{2,10},{3,11},{4,12},{5,13},{6,14},{7,15},{8,0},{9,1},... | collective-permute-start | bytes 98312 | tf_op jit(solution)/shard_map/ppermute | solution.py:55
  27.2 7.5 %collective-permute-start.4 = (bf16[1,128,128]{2,1,0:T(8,128)(2,1)S(1)}, bf16[1,128,128]{2,1,0:T(8,128)(2,1)S(1)}, u32[]{:S(2)}, u32[]{:S(2)}) collective-permute-start(bf16[1,128,128]{2,1,0:T(8,128)(2,1)S(1)} %bitcast.9), channel_id=1, source_target_pairs={{0,16},{1,17},{2,18},{3,19},{4,20},{5,21},{6,22},{7,23},{8,24},{9,... | collective-permute-start | bytes 98312 | tf_op jit(solution)/shard_map/ppermute | solution.py:55
  29.8 5.7 %collective-permute-start.5 = (bf16[1,128,128]{2,1,0:T(8,128)(2,1)S(1)}, bf16[1,128,128]{2,1,0:T(8,128)(2,1)S(1)}, u32[]{:S(2)}, u32[]{:S(2)}) collective-permute-start(bf16[1,128,128]{2,1,0:T(8,128)(2,1)S(1)} %bitcast.10), channel_id=1, source_target_pairs={{0,24},{1,25},{2,26},{3,27},{4,28},{5,29},{6,30},{7,31},{8,16},{9,... | collective-permute-start | bytes 98312 | tf_op jit(solution)/shard_map/ppermute | solution.py:55
  35.5 8.4 %collective-permute-start.6 = (bf16[4,128,128]{2,1,0:T(8,128)(2,1)S(1)}, bf16[4,128,128]{2,1,0:T(8,128)(2,1)S(1)}, u32[]{:S(2)}, u32[]{:S(2)}) collective-permute-start(bf16[4,128,128]{2,1,0:T(8,128)(2,1)S(1)} %pad_maximum_fusion.1), channel_id=1, source_target_pairs={{0,2},{1,3},{2,0},{3,1},{4,6},{5,7},{6,4},{7,5},{8,10},{9,11},{10,... | collective-permute-start | bytes 393224 | tf_op jit(solution)/shard_map/ppermute | solution.py:55
  37.1 6.9 %collective-permute-start.7 = (bf16[4,128,128]{2,1,0:T(8,128)(2,1)S(1)}, bf16[4,128,128]{2,1,0:T(8,128)(2,1)S(1)}, u32[]{:S(2)}, u32[]{:S(2)}) collective-permute-start(bf16[4,128,128]{2,1,0:T(8,128)(2,1)S(1)} %pad_maximum_fusion.1), channel_id=1, source_target_pairs={{0,4},{1,5},{2,6},{3,7},{4,0},{5,1},{6,2},{7,3},{8,12},{9,13},{10,... | collective-permute-start | bytes 393224 | tf_op jit(solution)/shard_map/ppermute | solution.py:55
  38.6 5.9 %collective-permute-start.8 = (bf16[4,128,128]{2,1,0:T(8,128)(2,1)S(1)}, bf16[4,128,128]{2,1,0:T(8,128)(2,1)S(1)}, u32[]{:S(2)}, u32[]{:S(2)}) collective-permute-start(bf16[4,128,128]{2,1,0:T(8,128)(2,1)S(1)} %pad_maximum_fusion.1), channel_id=1, source_target_pairs={{0,6},{1,7},{2,4},{3,5},{4,2},{5,3},{6,0},{7,1},{8,14},{9,15},{10,... | collective-permute-start | bytes 393224 | tf_op jit(solution)/shard_map/ppermute | solution.py:55
  39.1 7.5 %copy-start.27 = (s32[16]{0:T(128)S(1)}, s32[16]{0:T(128)}, u32[]{:S(2)}) copy-start(s32[16]{0:T(128)} %positives_ref.1) | copy-start | bytes 196
  44.6 2.0 %collective-permute-start.9 = (bf16[16,128,128]{2,1,0:T(8,128)(2,1)S(1)}, bf16[16,128,128]{2,1,0:T(8,128)(2,1)S(1)}, u32[]{:S(2)}, u32[]{:S(2)}) collective-permute-start(bf16[16,128,128]{2,1,0:T(8,128)(2,1)S(1)} %constant_dynamic-update-slice_fusion.near_ref), channel_id=1, source_target_pairs={{0,1},{1,0},{2,3},{3,2},{4,5},{5,4},{6,7},{7,6},{8,9},{9,8},{10,11... | collective-permute-start | bytes 1572872 | tf_op jit(solution)/shard_map/ppermute | solution.py:55
  46.6 11.1 %copy-start.15 = (bf16[2048,768]{1,0:T(8,128)(2,1)S(1)}, bf16[2048,768]{1,0:T(8,128)(2,1)}, u32[]{:S(2)}) copy-start(bf16[2048,768]{1,0:T(8,128)(2,1)} %refs_12_.1) | copy-start | bytes 9437188
  49.8 7.8 %collective-permute-start.14 = (bf16[256,2944]{1,0:T(8,128)(2,1)S(1)}, bf16[256,2944]{1,0:T(8,128)(2,1)S(1)}, u32[]{:S(2)}, u32[]{:S(2)}) collective-permute-start(bf16[256,2944]{1,0:T(8,128)(2,1)S(1)} %get-tuple-element.182), channel_id=1, source_target_pairs={{0,1},{1,0},{2,3},{3,2},{4,5},{5,4},{6,7},{7,6},{8,9},{9,8},{10,11... | collective-permute-start | bytes 4521992 | tf_op jit(solution)/shard_map/ppermute | solution.py:55
  50.0 3.9 %collective-permute-start.10 = (bf16[16,128,128]{2,1,0:T(8,128)(2,1)S(1)}, bf16[16,128,128]{2,1,0:T(8,128)(2,1)S(1)}, u32[]{:S(2)}, u32[]{:S(2)}) collective-permute-start(bf16[16,128,128]{2,1,0:T(8,128)(2,1)S(1)} %get-tuple-element.179), channel_id=1, source_target_pairs={{0,1},{1,0},{2,3},{3,2},{4,5},{5,4},{6,7},{7,6},{8,9},{9,8},{10,11... | collective-permute-start | bytes 1572872 | tf_op jit(solution)/shard_map/ppermute | solution.py:55
  54.1 8.2 %collective-permute-start.11 = (bf16[4,128,128]{2,1,0:T(8,128)(2,1)S(1)}, bf16[4,128,128]{2,1,0:T(8,128)(2,1)S(1)}, u32[]{:S(2)}, u32[]{:S(2)}) collective-permute-start(bf16[4,128,128]{2,1,0:T(8,128)(2,1)S(1)} %get-tuple-element.299), channel_id=1, source_target_pairs={{0,4},{1,5},{2,6},{3,7},{4,0},{5,1},{6,2},{7,3},{8,12},{9,13},{10,... | collective-permute-start | bytes 393224 | tf_op jit(solution)/shard_map/ppermute | solution.py:55
  55.1 8.1 %collective-permute-start.12 = (bf16[4,128,128]{2,1,0:T(8,128)(2,1)S(1)}, bf16[4,128,128]{2,1,0:T(8,128)(2,1)S(1)}, u32[]{:S(2)}, u32[]{:S(2)}) collective-permute-start(bf16[4,128,128]{2,1,0:T(8,128)(2,1)S(1)} %get-tuple-element.298), channel_id=1, source_target_pairs={{0,2},{1,3},{2,0},{3,1},{4,6},{5,7},{6,4},{7,5},{8,10},{9,11},{10,... | collective-permute-start | bytes 393224 | tf_op jit(solution)/shard_map/ppermute | solution.py:55
  56.6 6.6 %collective-permute-start.13 = (bf16[4,128,128]{2,1,0:T(8,128)(2,1)S(1)}, bf16[4,128,128]{2,1,0:T(8,128)(2,1)S(1)}, u32[]{:S(2)}, u32[]{:S(2)}) collective-permute-start(bf16[4,128,128]{2,1,0:T(8,128)(2,1)S(1)} %get-tuple-element.297), channel_id=1, source_target_pairs={{0,6},{1,7},{2,4},{3,5},{4,2},{5,3},{6,0},{7,1},{8,14},{9,15},{10,... | collective-permute-start | bytes 393224 | tf_op jit(solution)/shard_map/ppermute | solution.py:55
  63.3 9.7 %collective-permute-start.18 = (bf16[128,5760]{1,0:T(8,128)(2,1)S(1)}, bf16[128,5760]{1,0:T(8,128)(2,1)S(1)}, u32[]{:S(2)}, u32[]{:S(2)}) collective-permute-start(bf16[128,5760]{1,0:T(8,128)(2,1)S(1)} %get-tuple-element.239.slot_any), channel_id=1, source_target_pairs={{0,1},{1,0},{2,3},{3,2},{4,5},{5,4},{6,7},{7,6},{8,9},{9,8},{10,11... | collective-permute-start | bytes 4423688 | tf_op jit(solution)/shard_map/ppermute | solution.py:55
  63.3 7.5 %collective-permute-start.15 = (bf16[1,128,128]{2,1,0:T(8,128)(2,1)S(1)}, bf16[1,128,128]{2,1,0:T(8,128)(2,1)S(1)}, u32[]{:S(2)}, u32[]{:S(2)}) collective-permute-start(bf16[1,128,128]{2,1,0:T(8,128)(2,1)S(1)} %get-tuple-element.305), channel_id=1, source_target_pairs={{0,16},{1,17},{2,18},{3,19},{4,20},{5,21},{6,22},{7,23},{8,24},{9,... | collective-permute-start | bytes 98312 | tf_op jit(solution)/shard_map/ppermute | solution.py:55
  64.8 6.0 %collective-permute-start.16 = (bf16[1,128,128]{2,1,0:T(8,128)(2,1)S(1)}, bf16[1,128,128]{2,1,0:T(8,128)(2,1)S(1)}, u32[]{:S(2)}, u32[]{:S(2)}) collective-permute-start(bf16[1,128,128]{2,1,0:T(8,128)(2,1)S(1)} %get-tuple-element.304), channel_id=1, source_target_pairs={{0,8},{1,9},{2,10},{3,11},{4,12},{5,13},{6,14},{7,15},{8,0},{9,1},... | collective-permute-start | bytes 98312 | tf_op jit(solution)/shard_map/ppermute | solution.py:55
  67.3 5.7 %collective-permute-start.17 = (bf16[1,128,128]{2,1,0:T(8,128)(2,1)S(1)}, bf16[1,128,128]{2,1,0:T(8,128)(2,1)S(1)}, u32[]{:S(2)}, u32[]{:S(2)}) collective-permute-start(bf16[1,128,128]{2,1,0:T(8,128)(2,1)S(1)} %get-tuple-element.303), channel_id=1, source_target_pairs={{0,24},{1,25},{2,26},{3,27},{4,28},{5,29},{6,30},{7,31},{8,16},{9,... | collective-permute-start | bytes 98312 | tf_op jit(solution)/shard_map/ppermute | solution.py:55
  77.5 6.3 %collective-permute-start.21 = (bf16[128,5760]{1,0:T(8,128)(2,1)S(1)}, bf16[128,5760]{1,0:T(8,128)(2,1)S(1)}, u32[]{:S(2)}, u32[]{:S(2)}) collective-permute-start(bf16[128,5760]{1,0:T(8,128)(2,1)S(1)} %get-tuple-element.241.doc_any), channel_id=1, source_target_pairs={{0,1},{1,0},{2,3},{3,2},{4,5},{5,4},{6,7},{7,6},{8,9},{9,8},{10,11... | collective-permute-start | bytes 4423688 | tf_op jit(solution)/shard_map/ppermute | solution.py:55
  82.7 4.7 %collective-permute-start.20 = (bf16[576,1536]{1,0:T(8,128)(2,1)S(1)}, bf16[576,1536]{1,0:T(8,128)(2,1)S(1)}, u32[]{:S(2)}, u32[]{:S(2)}) collective-permute-start(bf16[576,1536]{1,0:T(8,128)(2,1)S(1)} %get-tuple-element.211.grads_ref), channel_id=1, source_target_pairs={{0,1},{1,0},{2,3},{3,2},{4,5},{5,4},{6,7},{7,6},{8,9},{9,8},{10,11... | collective-permute-start | bytes 5308424 | tf_op jit(solution)/shard_map/ppermute | solution.py:55
  83.3 4.2 %collective-permute-start.19 = (bf16[128,2304]{1,0:T(8,128)(2,1)S(1)}, bf16[128,2304]{1,0:T(8,128)(2,1)S(1)}, u32[]{:S(2)}, u32[]{:S(2)}) collective-permute-start(bf16[128,2304]{1,0:T(8,128)(2,1)S(1)} %get-tuple-element.244.slot_any.grads_ref), channel_id=1, source_target_pairs={{0,1},{1,0},{2,3},{3,2},{4,5},{5,4},{6,7},{7,6},{8,9},{9,8},{10,11... | collective-permute-start | bytes 1769480 | tf_op jit(solution)/shard_map/ppermute | solution.py:55
  83.4 4.1 %collective-permute-start.22 = (bf16[16,128]{1,0:T(8,128)(2,1)S(1)}, bf16[16,128]{1,0:T(8,128)(2,1)S(1)}, u32[]{:S(2)}, u32[]{:S(2)}) collective-permute-start(bf16[16,128]{1,0:T(8,128)(2,1)S(1)} %get-tuple-element.224.table_ref), channel_id=1, source_target_pairs={{0,1},{1,0},{2,3},{3,2},{4,5},{5,4},{6,7},{7,6},{8,9},{9,8},{10,11... | collective-permute-start | bytes 12296 | tf_op jit(solution)/shard_map/ppermute | solution.py:55
  86.5 25.9 %collective-permute-start.24 = (bf16[192,2816]{1,0:T(8,128)(2,1)S(1)}, bf16[192,2816]{1,0:T(8,128)(2,1)S(1)}, u32[]{:S(2)}, u32[]{:S(2)}) collective-permute-start(bf16[192,2816]{1,0:T(8,128)(2,1)S(1)} %get-tuple-element.229), channel_id=1, source_target_pairs={{0,8},{1,9},{2,10},{3,11},{4,12},{5,13},{6,14},{7,15},{8,0},{9,1},... | collective-permute-start | bytes 3244040 | tf_op jit(solution)/shard_map/ppermute | solution.py:55
  90.8 23.6 %collective-permute-start.23 = (bf16[208,2304]{1,0:T(8,128)(2,1)S(1)}, bf16[208,2304]{1,0:T(8,128)(2,1)S(1)}, u32[]{:S(2)}, u32[]{:S(2)}) collective-permute-start(bf16[208,2304]{1,0:T(8,128)(2,1)S(1)} %get-tuple-element.228), channel_id=1, source_target_pairs={{0,4},{1,5},{2,6},{3,7},{4,0},{5,1},{6,2},{7,3},{8,12},{9,13},{10,... | collective-permute-start | bytes 2875400 | tf_op jit(solution)/shard_map/ppermute | solution.py:55
  94.6 22.2 %collective-permute-start.28 = (bf16[192,2176]{1,0:T(8,128)(2,1)S(1)}, bf16[192,2176]{1,0:T(8,128)(2,1)S(1)}, u32[]{:S(2)}, u32[]{:S(2)}) collective-permute-start(bf16[192,2176]{1,0:T(8,128)(2,1)S(1)} %get-tuple-element.252), channel_id=1, source_target_pairs={{0,2},{1,3},{2,0},{3,1},{4,6},{5,7},{6,4},{7,5},{8,10},{9,11},{10,... | collective-permute-start | bytes 2506760 | tf_op jit(solution)/shard_map/ppermute | solution.py:55
  112.6 15.3 %collective-permute-start.27 = (bf16[96,2816]{1,0:T(8,128)(2,1)S(1)}, bf16[96,2816]{1,0:T(8,128)(2,1)S(1)}, u32[]{:S(2)}, u32[]{:S(2)}) collective-permute-start(bf16[96,2816]{1,0:T(8,128)(2,1)S(1)} %get-tuple-element.251), channel_id=1, source_target_pairs={{0,4},{1,5},{2,6},{3,7},{4,0},{5,1},{6,2},{7,3},{8,12},{9,13},{10,... | collective-permute-start | bytes 1622024 | tf_op jit(solution)/shard_map/ppermute | solution.py:55
  113.9 18.6 %collective-permute-start.26 = (bf16[512,768]{1,0:T(8,128)(2,1)}, bf16[512,768]{1,0:T(8,128)(2,1)S(1)}, u32[]{:S(2)}, u32[]{:S(2)}) collective-permute-start(bf16[512,768]{1,0:T(8,128)(2,1)} %get-tuple-element.250), channel_id=1, source_target_pairs={{0,8},{1,9},{2,10},{3,11},{4,12},{5,13},{6,14},{7,15},{8,0},{9,1},... | collective-permute-start | bytes 2359304 | tf_op jit(solution)/shard_map/ppermute | solution.py:55
  115.4 18.2 %collective-permute-start.25 = (bf16[112,2304]{1,0:T(8,128)(2,1)}, bf16[112,2304]{1,0:T(8,128)(2,1)S(1)}, u32[]{:S(2)}, u32[]{:S(2)}) collective-permute-start(bf16[112,2304]{1,0:T(8,128)(2,1)} %get-tuple-element.249), channel_id=1, source_target_pairs={{0,2},{1,3},{2,0},{3,1},{4,6},{5,7},{6,4},{7,5},{8,10},{9,11},{10,... | collective-permute-start | bytes 1548296 | tf_op jit(solution)/shard_map/ppermute | solution.py:55
  117.8 18.8 %collective-permute-start.33 = (bf16[96,2176]{1,0:T(8,128)(2,1)}, bf16[96,2176]{1,0:T(8,128)(2,1)S(1)}, u32[]{:S(2)}, u32[]{:S(2)}) collective-permute-start(bf16[96,2176]{1,0:T(8,128)(2,1)} %get-tuple-element.266), channel_id=1, source_target_pairs={{0,4},{1,5},{2,6},{3,7},{4,0},{5,1},{6,2},{7,3},{8,12},{9,13},{10,... | collective-permute-start | bytes 1253384 | tf_op jit(solution)/shard_map/ppermute | solution.py:55
  129.4 11.2 %collective-permute-start.32 = (bf16[48,2816]{1,0:T(8,128)(2,1)}, bf16[48,2816]{1,0:T(8,128)(2,1)}, u32[]{:S(2)}, u32[]{:S(2)}) collective-permute-start(bf16[48,2816]{1,0:T(8,128)(2,1)} %get-tuple-element.265), channel_id=1, source_target_pairs={{0,2},{1,3},{2,0},{3,1},{4,6},{5,7},{6,4},{7,5},{8,10},{9,11},{10,... | collective-permute-start | bytes 811016 | tf_op jit(solution)/shard_map/ppermute | solution.py:55
  132.6 6.2 %copy-start.22 = (bf16[128,1536]{1,0:T(8,128)(2,1)S(1)}, bf16[128,1536]{1,0:T(8,128)(2,1)}, u32[]{:S(2)}) copy-start(bf16[128,1536]{1,0:T(8,128)(2,1)} %copy-done.21) | copy-start | bytes 1179652
  132.6 8.0 %copy-start.1 = (bf16[48,2816]{1,0:T(8,128)(2,1)S(1)}, bf16[48,2816]{1,0:T(8,128)(2,1)}, u32[]{:S(2)}) copy-start(bf16[48,2816]{1,0:T(8,128)(2,1)} %copy-done) | copy-start | bytes 811012
  132.6 23.3 %copy-start.29 = (bf16[128,1536]{1,0:T(8,128)(2,1)S(1)}, bf16[128,1536]{1,0:T(8,128)(2,1)}, u32[]{:S(2)}) copy-start(bf16[128,1536]{1,0:T(8,128)(2,1)} %copy-done.28) | copy-start | bytes 1179652
  132.6 23.3 %copy-start.31 = (f32[128,768]{1,0:T(8,128)S(1)}, f32[128,768]{1,0:T(8,128)}, u32[]{:S(2)}) copy-start(f32[128,768]{1,0:T(8,128)} %copy-done.30) | copy-start | bytes 1179652
  132.8 13.6 %collective-permute-start.30 = (bf16[256,768]{1,0:T(8,128)(2,1)S(1)}, bf16[256,768]{1,0:T(8,128)(2,1)S(1)}, u32[]{:S(2)}, u32[]{:S(2)}) collective-permute-start(bf16[256,768]{1,0:T(8,128)(2,1)S(1)} %get-tuple-element.263), channel_id=1, source_target_pairs={{0,4},{1,5},{2,6},{3,7},{4,0},{5,1},{6,2},{7,3},{8,12},{9,13},{10,... | collective-permute-start | bytes 1179656 | tf_op jit(solution)/shard_map/ppermute | solution.py:55
  133.6 22.3 %copy-start.17 = (bf16[576,1536]{1,0:T(8,128)(2,1)S(1)}, bf16[576,1536]{1,0:T(8,128)(2,1)}, u32[]{:S(2)}) copy-start(bf16[576,1536]{1,0:T(8,128)(2,1)} %copy-done.16) | copy-start | bytes 5308420
  136.7 9.6 %collective-permute-start.31 = (bf16[64,2304]{1,0:T(8,128)(2,1)S(1)}, bf16[64,2304]{1,0:T(8,128)(2,1)S(1)}, u32[]{:S(2)}, u32[]{:S(2)}) collective-permute-start(bf16[64,2304]{1,0:T(8,128)(2,1)S(1)} %get-tuple-element.264), channel_id=1, source_target_pairs={{0,8},{1,9},{2,10},{3,11},{4,12},{5,13},{6,14},{7,15},{8,0},{9,1},... | collective-permute-start | bytes 884744 | tf_op jit(solution)/shard_map/ppermute | solution.py:55
  137.0 13.0 %collective-permute-start.35 = (bf16[48,2176]{1,0:T(8,128)(2,1)S(1)}, bf16[48,2176]{1,0:T(8,128)(2,1)S(1)}, u32[]{:S(2)}, u32[]{:S(2)}) collective-permute-start(bf16[48,2176]{1,0:T(8,128)(2,1)S(1)} %get-tuple-element.274), channel_id=1, source_target_pairs={{0,8},{1,9},{2,10},{3,11},{4,12},{5,13},{6,14},{7,15},{8,0},{9,1},... | collective-permute-start | bytes 626696 | tf_op jit(solution)/shard_map/ppermute | solution.py:55
  138.8 17.1 %collective-permute-start.29 = (bf16[128,1536]{1,0:T(8,128)(2,1)S(1)}, bf16[128,1536]{1,0:T(8,128)(2,1)S(1)}, u32[]{:S(2)}, u32[]{:S(2)}) collective-permute-start(bf16[128,1536]{1,0:T(8,128)(2,1)S(1)} %copy-done.22), channel_id=1, source_target_pairs={{0,2},{1,3},{2,0},{3,1},{4,6},{5,7},{6,4},{7,5},{8,10},{9,11},{10,... | collective-permute-start | bytes 1179656 | tf_op jit(solution)/shard_map/ppermute | solution.py:55
  140.6 15.3 %copy-start.9 = (bf16[768,768]{1,0:T(8,128)(2,1)S(1)}, bf16[768,768]{1,0:T(8,128)(2,1)}, u32[]{:S(2)}) copy-start(bf16[768,768]{1,0:T(8,128)(2,1)} %wv_ref.5) | copy-start | bytes 3538948
  141.7 16.4 %collective-permute-start.38 = (bf16[24,2816]{1,0:T(8,128)(2,1)S(1)}, bf16[24,2816]{1,0:T(8,128)(2,1)S(1)}, u32[]{:S(2)}, u32[]{:S(2)}) collective-permute-start(bf16[24,2816]{1,0:T(8,128)(2,1)S(1)} %get-tuple-element.301), channel_id=1, source_target_pairs={{0,16},{1,17},{2,18},{3,19},{4,20},{5,21},{6,22},{7,23},{8,24},{9,... | collective-permute-start | bytes 405512 | tf_op jit(solution)/shard_map/ppermute | solution.py:55
  146.3 9.7 %copy-start.5 = (bf16[768,768]{1,0:T(8,128)(2,1)S(1)}, bf16[768,768]{1,0:T(8,128)(2,1)}, u32[]{:S(2)}) copy-start(bf16[768,768]{1,0:T(8,128)(2,1)} %wq_ref.5) | copy-start | bytes 3538948
  146.3 9.7 %copy-start.7 = (bf16[768,768]{1,0:T(8,128)(2,1)S(1)}, bf16[768,768]{1,0:T(8,128)(2,1)}, u32[]{:S(2)}) copy-start(bf16[768,768]{1,0:T(8,128)(2,1)} %wk_ref.5) | copy-start | bytes 3538948
  146.3 9.7 %copy-start.25 = (bf16[1,128,768]{2,1,0:T(8,128)(2,1)S(1)}, bf16[1,128,768]{2,1,0:T(8,128)(2,1)}, u32[]{:S(2)}) copy-start(bf16[1,128,768]{2,1,0:T(8,128)(2,1)} %param.17) | copy-start | bytes 589828
  150.0 5.8 %collective-permute-start.34 = (bf16[128,768]{1,0:T(8,128)(2,1)S(1)}, bf16[128,768]{1,0:T(8,128)(2,1)S(1)}, u32[]{:S(2)}, u32[]{:S(2)}) collective-permute-start(bf16[128,768]{1,0:T(8,128)(2,1)S(1)} %get-tuple-element.273), channel_id=1, source_target_pairs={{0,2},{1,3},{2,0},{3,1},{4,6},{5,7},{6,4},{7,5},{8,10},{9,11},{10,... | collective-permute-start | bytes 589832 | tf_op jit(solution)/shard_map/ppermute | solution.py:55
  152.2 6.5 %collective-permute-start.37 = (bf16[24,2176]{1,0:T(8,128)(2,1)S(1)}, bf16[24,2176]{1,0:T(8,128)(2,1)S(1)}, u32[]{:S(2)}, u32[]{:S(2)}) collective-permute-start(bf16[24,2176]{1,0:T(8,128)(2,1)S(1)} %get-tuple-element.309), channel_id=1, source_target_pairs={{0,16},{1,17},{2,18},{3,19},{4,20},{5,21},{6,22},{7,23},{8,24},{9,... | collective-permute-start | bytes 313352 | tf_op jit(solution)/shard_map/ppermute | solution.py:55
  152.8 11.9 %collective-permute-start.36 = (bf16[40,2304]{1,0:T(8,128)(2,1)S(1)}, bf16[40,2304]{1,0:T(8,128)(2,1)S(1)}, u32[]{:S(2)}, u32[]{:S(2)}) collective-permute-start(bf16[40,2304]{1,0:T(8,128)(2,1)S(1)} %pad_maximum_fusion), channel_id=1, source_target_pairs={{0,16},{1,17},{2,18},{3,19},{4,20},{5,21},{6,22},{7,23},{8,24},{9,... | collective-permute-start | bytes 552968 | tf_op jit(solution)/shard_map/ppermute | solution.py:55
  165.6 5.7 %collective-permute-start.39 = (bf16[64,768]{1,0:T(8,128)(2,1)S(1)}, bf16[64,768]{1,0:T(8,128)(2,1)S(1)}, u32[]{:S(2)}, u32[]{:S(2)}) collective-permute-start(bf16[64,768]{1,0:T(8,128)(2,1)S(1)} %get-tuple-element.283), channel_id=1, source_target_pairs={{0,16},{1,17},{2,18},{3,19},{4,20},{5,21},{6,22},{7,23},{8,24},{9,... | collective-permute-start | bytes 294920 | tf_op jit(solution)/shard_map/ppermute | solution.py:55
  (8 other events, 28.9 us)

commit v6 on v5

--- a/solution.py
+++ b/solution.py
@@ -813,7 +813,21 @@
         "s",
         [pltpu.VMEM((heads, 2 * doc_length + LANES), f32)],
     )
-    y_tokens = after(y_tokens, doc_bias)
+    counts, tally = call(
+        functools.partial(count_kernel, doc_length, doc_total),
+        [shape((blocks, slot_rows, LANES), bf16), shape((slot_rows, LANES))],
+        [rank_word, after(retrieved, slot_bias)],
+        "sa",
+        [
+            pltpu.VMEM((slots, slot_length, retrieved.shape[2]), jnp.int32),
+            pltpu.VMEM((slot_rows, retrieved.shape[2]), jnp.int32),
+            pltpu.VMEM((blocks * slot_rows, LANES), f32),
+            dma,
+        ],
+        us=5,
+        wide=bits > 5,
+    )
+    y_tokens = after(y_tokens, doc_bias, tally)
     both_tokens = swap(y_tokens, 1)
 
     all_rows = slot_rows + doc_length
@@ -864,21 +878,7 @@
         masks = [gather_order(place, group) for place in range(1, 1 << len(group))]
         came = [swap(near_units, mask) for mask in masks]
         if phase == 0:
-            counts, tally = call(
-                functools.partial(count_kernel, doc_length, doc_total),
-                [shape((blocks, slot_rows, LANES), bf16), shape((slot_rows, LANES))],
-                after([rank_word, retrieved], doc_unit),
-                "sa",
-                [
-                    pltpu.VMEM((slots, slot_length, retrieved.shape[2]), jnp.int32),
-                    pltpu.VMEM((slot_rows, retrieved.shape[2]), jnp.int32),
-                    pltpu.VMEM((blocks * slot_rows, LANES), f32),
-                    dma,
-                ],
-                us=5,
-                wide=bits > 5,
-            )
-            came = after(came, tally)
+            pass
         if phase == 1:
             turned_cols = 5 * width // 2 + units // 2
             turned, turned_sent, turned_docs = call(
@@ -913,7 +913,6 @@
         ],
         wide=bits > 5,
     )
-    turned_came = swap(after(turned_sent, losses), 1)
     back_weights = [proj_weight, down_weight, gate_weight, up_weight, output_weight]
     doc_cols = 2 * units + 2 * width + columns
 
@@ -937,7 +936,7 @@
             slot_grads, slot_after, slot_mixed = call(
                 slot_feed_kernel,
                 feed_shapes,
-                [after(grad_slot_unit, pieces[1], turned_came)]
+                [after(grad_slot_unit, pieces[1])]
                 + [embed, after_feed, after_attend, gate_slope, up_slope, gains[1], gains[2]]
                 + back_weights,
                 "",
@@ -948,6 +947,7 @@
             came = after(came, slot_after)
         if phase == 1:
             slot_came = swap(after(slot_grads, *pieces[1:]), 1)
+            turned_came = swap(after(turned_sent, *pieces[1:]), 1)
             slot_thirds, slot_table = call(
                 slot_attend_kernel,
                 [shape((slot_rows, 3 * width), bf16), shape((heads, LANES))],
@@ -961,7 +961,7 @@
     doc_grads, doc_after, doc_mixed = call(
         functools.partial(doc_feed_kernel, 1 + len(came)),
         feed_shapes,
-        parts + after(came, slot_came)
+        parts + after(came, slot_came, turned_came)
         + [embed, after_feed, after_attend, gate_slope, up_slope, gains[1], gains[2]]
         + back_weights,
         "",
@@ -1054,15 +1054,26 @@
         return sum(jnp.sum(own_rows(weight) * grad, 1) for weight, grad in pairs) / own_rows(gain)
 
     streams = {"A": first, "B": second, "C": third, "D": fourth}
-    plan = "JADBACDpBADCBCIABDC"
+    plan = "JADBACDpBADCBCIABDCfa"
     if bits != 5:
-        plan = "J" + "ADBC" + "p" + "ADBC" * (bits - 3) + "I" + "ABDC"
+        plan = "J" + "ADBC" + "p" + "ADBC" * (bits - 3) + "I" + "ABfDaC"
     done = third.kept
-    for event in plan[:-1]:
+    for event in plan:
         if event in streams:
             done = streams[event].advance(done)
         elif event == "p":
             pair_came = swap(after(pair_sent, done), 2)
+        elif event == "f":
+            gate_grad, output_grad = first.result[:, :units], first.result[:, units:]
+            up_grad, proj_grad = second.result[:, :units], second.result[:, units:]
+            feed_gain_grad = gain_grad(feed_gain, (gate_weight, gate_grad), (up_weight, up_grad))
+            final_gain_grad = gain_grad(final_gain, (proj_weight, proj_grad))
+            done = jnp.concatenate([feed_gain_grad, final_gain_grad])
+            feed_gain_grad, final_gain_grad = done[: width >> bits], done[width >> bits :]
+        elif event == "a":
+            query_g, key_g, value_g = (fourth.result[:, place * width : (place + 1) * width] for place in range(3))
+            done = gain_grad(attend_gain, (query_weight, query_g), (key_weight, key_g), (value_weight, value_g))
+            attend_gain_grad = done
         elif event == "I":
             (done,) = call(
                 doc_input_kernel,
@@ -1083,13 +1094,6 @@
                 us=3,
             )
             query_grad = done
-    gate_grad, output_grad = first.result[:, :units], first.result[:, units:]
-    up_grad, proj_grad = second.result[:, :units], second.result[:, units:]
-    query_g, key_g, value_g = (fourth.result[:, place * width : (place + 1) * width] for place in range(3))
-    attend_gain_grad = gain_grad(attend_gain, (query_weight, query_g), (key_weight, key_g), (value_weight, value_g))
-    feed_gain_grad = gain_grad(feed_gain, (gate_weight, gate_grad), (up_weight, up_grad))
-    final_gain_grad = gain_grad(final_gain, (proj_weight, proj_grad))
-    third.advance(done, attend_gain_grad, feed_gain_grad, final_gain_grad)
     return (
         losses[:, 0],
         doc_grad[None],

time: 172 us -> 169 us (0.983)
  starting transfers between devices: 38.4 us -> 33.5 us
  waiting for transfers between devices: 54.4 us -> 58.1 us
  local copies, waits for them, and re-layouts: 4.87 us -> 3 us
    ppermute x40, starting transfers between devices: 38.4 us -> 33.5 us  [swap(): return lax.ppermute(values, ('wide', 'narrow'), pairs)]
    ppermute x40, waiting for transfers between devices: 54.4 us -> 58.1 us  [swap(): return lax.ppermute(values, ('wide', 'narrow'), pairs)]
    unnamed x71 -> x69, local copies, waits for them, and re-layouts: 3.57 us -> 1.71 us
  transfers between devices with their start and end apart: 40 -> 40, of which waited for: 20 -> 17; matrix products, arithmetic and copies ran while one was open for 5% -> 4% of each run, Pallas kernels for 26% -> 26%
where the time goes in v6:
time: 169 us
  Pallas kernels  64.9 us (38%)
  waiting for transfers between devices  58.1 us (34%)
  starting transfers between devices  33.5 us (20%)
  other arithmetic  8.18 us (5%)
  local copies, waits for them, and re-layouts  3 us (2%)
    pallas_call x24, Pallas kernels, call(): pl.pallas_call(kernel, out_shape=tuple(outs), in_specs=specs[:len(args)],...  64.9 us
    ppermute x40, waiting for transfers between devices, swap(): return lax.ppermute(values, ('wide', 'narrow'), pairs)  58.1 us
    ppermute x40, starting transfers between devices, swap(): return lax.ppermute(values, ('wide', 'narrow'), pairs)  33.5 us
    reduce_sum x3, other arithmetic, gain_grad(): jnp.sum(own_rows(weight) * grad, 1)  4.08 us
  transfers between devices with their start and end apart: 40, of which 17 were waited for; matrix products, arithmetic and copies ran while one was open for 4% of the time, Pallas kernels for 26%

profile of v6, /device:TPU:0, one launch (start us, length us, event | category | flops | bytes accessed | tf_op | source)
XLA Modules:
  0.0 169.0 jit_solution(12675500802199718776)
XLA Ops:
  0.6 3.0 %collective-permute-start.1 = (bf16[128,768]{1,0:T(8,128)(2,1)}, bf16[128,768]{1,0:T(8,128)(2,1)S(1)}, u32[]{:S(2)}, u32[]{:S(2)}) collective-permute-start(bf16[128,768]{1,0:T(8,128)(2,1)} %bitcast.12), channel_id=1, source_target_pairs={{0,2},{1,3},{2,0},{3,1},{4,6},{5,7},{6,4},{7,5},{8,10},{9,11},{10,... | collective-permute-start | bytes 589832 | tf_op jit(solution)/shard_map/ppermute | solution.py:55
  3.7 0.8 copy.33.table_ref
  4.5 2.7 %shard_map.280 = (f32[6,256,512]{2,1,0:T(8,128)S(1)}, f32[6,256,128]{2,1,0:T(8,128)S(1)}) custom-call(s32[1]{0:T(128)} %bitcast.rank_ref, f32[32,12]{1,0:T(8,128)S(1)} %copy.33.table_ref), custom_call_target="tpu_custom_call" | custom-call | flops 3300000000 | tf_op jit(solution)/shard_map/pallas_call | solution.py:115
  7.4 4.9 %shard_map.281 = (bf16[32,128,128]{2,1,0:T(8,128)(2,1)S(1)}, f32[128,128]{1,0:T(8,128)S(1)}) custom-call(s32[1]{0:T(128)} %bitcast.rank_ref, s32[16,32,128]{2,1,0:T(8,128)S(1)} %copy-done.22), custom_call_target="tpu_custom_call" | custom-call | flops 5500000256 | tf_op jit(solution)/shard_map/pallas_call | solution.py:115
  12.8 1.1 collective-permute-done.2.last_ref
  14.0 13.1 %shard_map.282 = (bf16[640,768]{1,0:T(8,128)(2,1)S(1)}, bf16[256,768]{1,0:T(8,128)(2,1)S(1)}, bf16[640,768]{1,0:T(8,128)(2,1)S(1)}, bf16[640,768]{1,0:T(8,128)(2...) custom-call(s32[1]{0:T(128)} %bitcast.rank_ref, ...), custom_call_target="tpu_custom_call" | custom-call | flops 19800000512 | tf_op jit(solution)/shard_map/pallas_call | solution.py:115
  27.1 1.7 collective-permute-start.3
  28.8 2.6 %collective-permute-start.4 = (bf16[1,128,128]{2,1,0:T(8,128)(2,1)S(1)}, bf16[1,128,128]{2,1,0:T(8,128)(2,1)S(1)}, u32[]{:S(2)}, u32[]{:S(2)}) collective-permute-start(bf16[1,128,128]{2,1,0:T(8,128)(2,1)S(1)} %bitcast.9), channel_id=1, source_target_pairs={{0,16},{1,17},{2,18},{3,19},{4,20},{5,21},{6,22},{7,23},{8,24},{9,... | collective-permute-start | bytes 98312 | tf_op jit(solution)/shard_map/ppermute | solution.py:55
  31.6 2.6 %collective-permute-done.4 = bf16[1,128,128]{2,1,0:T(8,128)(2,1)S(1)} collective-permute-done((bf16[1,128,128]{2,1,0:T(8,128)(2,1)S(1)}, bf16[1,128,128]{2,1,0:T(8,128)(2,1)S(1)}, u32[]{:S(2)}, u32[]{:S(2)}) %collective-permute-start.4) | collective-permute-done | bytes 32800 | tf_op jit(solution)/shard_map/ppermute | solution.py:55
  34.2 2.9 %collective-permute-done.5 = bf16[1,128,128]{2,1,0:T(8,128)(2,1)S(1)} collective-permute-done((bf16[1,128,128]{2,1,0:T(8,128)(2,1)S(1)}, bf16[1,128,128]{2,1,0:T(8,128)(2,1)S(1)}, u32[]{:S(2)}, u32[]{:S(2)}) %collective-permute-start.5) | collective-permute-done | bytes 32800 | tf_op jit(solution)/shard_map/ppermute | solution.py:55
  37.7 1.5 collective-permute-start.7
  39.2 1.5 collective-permute-start.8
  40.7 4.8 %shard_map.283 = (bf16[256,2944]{1,0:T(8,128)(2,1)S(1)}, bf16[256,2944]{1,0:T(8,128)(2,1)S(1)}, bf16[512,384]{1,0:T(8,128)(2,1)S(1)}) custom-call(s32[1]{0:T(128)} %bitcast.rank_ref, bf16[640,768]{1,0:T(8,128)(2,1)S(1)} %get-tuple-element.159.all_ref, bf16[256,768]{1,0:T(8,128)(2,1)S(1)} %get-tuple-element.160.normed_feed_ref, ...), custom_call_target="tpu_custom_call" | custom-call | flops 5500000256 | tf_op jit(solution)/shard_map/pallas_call | solution.py:115
  45.7 1.9 %collective-permute-done.9.far_ref = bf16[16,128,128]{2,1,0:T(8,128)(2,1)S(1)} collective-permute-done((bf16[16,128,128]{2,1,0:T(8,128)(2,1)S(1)}, bf16[16,128,128]{2,1,0:T(8,128)(2,1)S(1)}, u32[]{:S(2)}, u32[]{:S(2)}) %collective-permute-start.9) | collective-permute-done | bytes 524320 | tf_op jit(solution)/shard_map/ppermute | solution.py:55
  47.6 3.2 %shard_map.284 = (f32[4,128]{1,0:T(4,128)S(1)}, f32[128,128]{1,0:T(8,128)S(1)}, bf16[16,128,128]{2,1,0:T(8,128)(2,1)S(1)}, bf16[16,128,128]{2,1,0:T(8,128)(2,1)S(1)}) custom-call(s32[1]{0:T(128)} %bitcast.rank_ref, s32[16]{0:T(128)S(1)} %copy-done.25, s32[16]{0:T(128)S(1)} %copy-done.26, bf16[32,128,128]{2,1,0:T(8,128)(2,1)S(1)} %get-tuple-element.148.counts_ref, ...), custom_call_target="tpu_custom_call" | custom-call | flops 3300000000 | tf_op jit(solution)/shard_map/pallas_call | solution.py:115
  51.1 1.8 %collective-permute-done.10 = bf16[16,128,128]{2,1,0:T(8,128)(2,1)S(1)} collective-permute-done((bf16[16,128,128]{2,1,0:T(8,128)(2,1)S(1)}, bf16[16,128,128]{2,1,0:T(8,128)(2,1)S(1)}, u32[]{:S(2)}, u32[]{:S(2)}) %collective-permute-start.10) | collective-permute-done | bytes 524320 | tf_op jit(solution)/shard_map/ppermute | solution.py:55
  53.0 1.6 collective-permute-start.11
  55.1 1.5 collective-permute-start.13
  56.6 4.6 %shard_map.285 = (bf16[128,5760]{1,0:T(8,128)(2,1)S(1)}, f32[128,768]{1,0:T(8,128)S(1)}, bf16[128,768]{1,0:T(8,128)(2,1)S(1)}) custom-call(f32[128,128]{1,0:T(8,128)S(1)} %get-tuple-element.173.grad_unit_ref, f32[256,128]{1,0:T(8,128)S(1)} %get-tuple-element.174.embed_ref.refs_4_, f32[256,768]{1,0:T(8,128)S(1)} %get-tuple-element.175.after_feed_ref.refs_5_, ...), custom_call_target="tpu_custom_call" | custom-call | flops 7699999744 | tf_op jit(solution)/shard_map/pallas_call | solution.py:115
  61.2 1.5 collective-permute-done.12
  63.3 0.9 collective-permute-start.15
  64.2 3.5 %collective-permute-start.16 = (bf16[1,128,128]{2,1,0:T(8,128)(2,1)S(1)}, bf16[1,128,128]{2,1,0:T(8,128)(2,1)S(1)}, u32[]{:S(2)}, u32[]{:S(2)}) collective-permute-start(bf16[1,128,128]{2,1,0:T(8,128)(2,1)S(1)} %get-tuple-element.295), channel_id=1, source_target_pairs={{0,24},{1,25},{2,26},{3,27},{4,28},{5,29},{6,30},{7,31},{8,16},{9,... | collective-permute-start | bytes 98312 | tf_op jit(solution)/shard_map/ppermute | solution.py:55
  67.7 3.0 %shard_map.286 = (bf16[128,2304]{1,0:T(8,128)(2,1)S(1)}, f32[12,128]{1,0:T(8,128)S(1)}) custom-call(bf16[256,768]{1,0:T(8,128)(2,1)S(1)} %get-tuple-element.183.query_ref, bf16[640,768]{1,0:T(8,128)(2,1)S(1)} %get-tuple-element.184.key_ref, bf16[640,768]{1,0:T(8,128)(2,1)S(1)} %get-tuple-element.185.value_ref, ...), custom_call_target="tpu_custom_call" | custom-call | flops 4400000000 | tf_op jit(solution)/shard_map/pallas_call | solution.py:115
  70.8 4.5 %shard_map.287 = (bf16[128,5760]{1,0:T(8,128)(2,1)S(1)}, f32[128,768]{1,0:T(8,128)S(1)}, bf16[128,768]{1,0:T(8,128)(2,1)S(1)}) custom-call(bf16[1,128,128]{2,1,0:T(8,128)(2,1)S(1)} %get-tuple-element.298.refs_0_, bf16[1,128,128]{2,1,0:T(8,128)(2,1)S(1)} %collective-permute-done.14.refs_1_, bf16[1,128,128]{2,1,0:T(8,128)(2,1)S(1)} %collective-permute-done.15.refs_2_, ...), custom_call_target="tpu_custom_call" | custom-call | flops 7699999744 | tf_op jit(solution)/shard_map/pallas_call | solution.py:115
  75.4 5.1 %shard_map.288 = (bf16[576,1536]{1,0:T(8,128)(2,1)S(1)}, bf16[16,128]{1,0:T(8,128)(2,1)S(1)}) custom-call(s32[1]{0:T(128)} %bitcast.rank_ref, bf16[256,768]{1,0:T(8,128)(2,1)S(1)} %get-tuple-element.183.query_ref, bf16[640,768]{1,0:T(8,128)(2,1)S(1)} %get-tuple-element.184.key_ref, bf16[640,768]{1,0:T(8,128)(2,1)S(1)} %get-tuple-element.185.value_ref, ...), custom_call_target="tpu_custom_call" | custom-call | flops 3300000000 | tf_op jit(solution)/shard_map/pallas_call | solution.py:115
  81.6 2.7 %shard_map.289 = (bf16[192,2816]{1,0:T(8,128)(2,1)S(1)}, bf16[192,2816]{1,0:T(8,128)(2,1)S(1)}) custom-call(bf16[256,2944]{1,0:T(8,128)(2,1)S(1)} %get-tuple-element.229.kept_any, bf16[256,2944]{1,0:T(8,128)(2,1)S(1)} %collective-permute-done.18.came_any, bf16[128,5760]{1,0:T(8,128)(2,1)S(1)} %get-tuple-element.231.slot_any, ...), custom_call_target="tpu_custom_call" | custom-call | flops 3300000000 | tf_op jit(solution)/shard_map/pallas_call | solution.py:115
  84.3 0.9 collective-permute-done.22.other_table_ref
  85.3 3.4 %shard_map.290 = (bf16[192,2304]{1,0:T(8,128)(2,1)S(1)}, bf16[208,2304]{1,0:T(8,128)(2,1)S(1)}, bf16[128,1536]{1,0:T(8,128)(2,1)S(1)}, bf16[128,1536]{1,0:T(8,128)(2,1)S(1)}) custom-call(bf16[512,384]{1,0:T(8,128)(2,1)S(1)} %get-tuple-element.204.doc_ref, bf16[256,2944]{1,0:T(8,128)(2,1)S(1)} %get-tuple-element.229.kept_any, ...), custom_call_target="tpu_custom_call" | custom-call | flops 3300000000 | tf_op jit(solution)/shard_map/pallas_call | solution.py:115
  88.6 0.6 collective-permute-start.23
  89.2 2.4 %shard_map.291 = (bf16[192,2176]{1,0:T(8,128)(2,1)S(1)}, bf16[192,2176]{1,0:T(8,128)(2,1)S(1)}) custom-call(bf16[256,2944]{1,0:T(8,128)(2,1)S(1)} %get-tuple-element.229.kept_any, bf16[256,2944]{1,0:T(8,128)(2,1)S(1)} %collective-permute-done.18.came_any, bf16[128,5760]{1,0:T(8,128)(2,1)S(1)} %get-tuple-element.231.slot_any, ...), custom_call_target="tpu_custom_call" | custom-call | flops 3300000000 | tf_op jit(solution)/shard_map/pallas_call | solution.py:115
  91.7 1.3 collective-permute-start.28
  93.0 2.1 %shard_map.292 = (bf16[512,768]{1,0:T(8,128)(2,1)S(1)}, bf16[512,768]{1,0:T(8,128)(2,1)}) custom-call(bf16[256,2944]{1,0:T(8,128)(2,1)S(1)} %get-tuple-element.229.kept_any, bf16[256,2944]{1,0:T(8,128)(2,1)S(1)} %collective-permute-done.18.came_any, bf16[128,5760]{1,0:T(8,128)(2,1)S(1)} %get-tuple-element.231.slot_any, ...), custom_call_target="tpu_custom_call" | custom-call | flops 3300000000 | tf_op jit(solution)/shard_map/pallas_call | solution.py:115
  95.1 2.6 %shard_map.293 = f32[128,768]{1,0:T(8,128)} custom-call(s32[1]{0:T(128)} %bitcast.rank_ref, bf16[16,32,768]{2,1,0:T(8,128)(2,1)S(1)} %copy-done.19, f32[768]{0:T(1024)S(1)} %copy-done.11, f32[128,768]{1,0:T(8,128)S(1)} %get-tuple-element.179.after_ref, bf16[128,2304]{1,0:T(8,128)(2,1)S(1)} %get-tuple-element.236.slot_any.grads_ref, ...), custom_call_target="tpu_custom_call" | custom-call | flops 3300000000 | tf_op jit(solution)/shard_map/pallas_call | solution.py:115
  97.8 12.4 %collective-permute-done.24.came_ref = bf16[192,2816]{1,0:T(8,128)(2,1)S(1)} collective-permute-done((bf16[192,2816]{1,0:T(8,128)(2,1)S(1)}, bf16[192,2816]{1,0:T(8,128)(2,1)S(1)}, u32[]{:S(2)}, u32[]{:S(2)}) %collective-permute-start.24) | collective-permute-done | bytes 1081376 | tf_op jit(solution)/shard_map/ppermute | solution.py:55
  110.4 0.6 collective-permute-start.27
  111.3 0.9 collective-permute-done.23.came_ref
  112.2 0.9 shard_map.295
  113.7 0.9 shard_map.296
  114.5 1.2 collective-permute-start.33
  115.8 9.9 %collective-permute-done.27.came_ref = bf16[96,2816]{1,0:T(8,128)(2,1)S(1)} collective-permute-done((bf16[96,2816]{1,0:T(8,128)(2,1)S(1)}, bf16[96,2816]{1,0:T(8,128)(2,1)S(1)}, u32[]{:S(2)}, u32[]{:S(2)}) %collective-permute-start.27) | collective-permute-done | bytes 540704 | tf_op jit(solution)/shard_map/ppermute | solution.py:55
  125.7 0.8 shard_map.297
  126.5 0.7 copy-done
  127.7 0.6 slice_reduce_fusion
  128.3 1.3 collective-permute-done.26.came_ref
  129.8 1.6 collective-permute-start.30
  131.5 3.1 %collective-permute-done.33.came_ref = bf16[96,2176]{1,0:T(8,128)(2,1)S(1)} collective-permute-done((bf16[96,2176]{1,0:T(8,128)(2,1)}, bf16[96,2176]{1,0:T(8,128)(2,1)S(1)}, u32[]{:S(2)}, u32[]{:S(2)}) %collective-permute-start.33) | collective-permute-done | bytes 417824 | tf_op jit(solution)/shard_map/ppermute | solution.py:55
  135.1 1.8 %collective-permute-start.35 = (bf16[48,2176]{1,0:T(8,128)(2,1)S(1)}, bf16[48,2176]{1,0:T(8,128)(2,1)S(1)}, u32[]{:S(2)}, u32[]{:S(2)}) collective-permute-start(bf16[48,2176]{1,0:T(8,128)(2,1)S(1)} %get-tuple-element.266), channel_id=1, source_target_pairs={{0,8},{1,9},{2,10},{3,11},{4,12},{5,13},{6,14},{7,15},{8,0},{9,1},... | collective-permute-start | bytes 626696 | tf_op jit(solution)/shard_map/ppermute | solution.py:55
  137.1 1.1 add_convert_fusion
  138.3 1.5 collective-permute-start.38
  139.8 7.7 %collective-permute-done.31 = bf16[64,2304]{1,0:T(8,128)(2,1)S(1)} collective-permute-done((bf16[64,2304]{1,0:T(8,128)(2,1)S(1)}, bf16[64,2304]{1,0:T(8,128)(2,1)S(1)}, u32[]{:S(2)}, u32[]{:S(2)}) %collective-permute-start.31) | collective-permute-done | bytes 294944 | tf_op jit(solution)/shard_map/ppermute | solution.py:55
  148.2 2.3 %collective-permute-done.35 = bf16[48,2176]{1,0:T(8,128)(2,1)S(1)} collective-permute-done((bf16[48,2176]{1,0:T(8,128)(2,1)S(1)}, bf16[48,2176]{1,0:T(8,128)(2,1)S(1)}, u32[]{:S(2)}, u32[]{:S(2)}) %collective-permute-start.35) | collective-permute-done | bytes 208928 | tf_op jit(solution)/shard_map/ppermute | solution.py:55
  150.5 0.9 collective-permute-start.37
  151.4 4.7 %collective-permute-done.34.came_ref = bf16[128,768]{1,0:T(8,128)(2,1)S(1)} collective-permute-done((bf16[128,768]{1,0:T(8,128)(2,1)S(1)}, bf16[128,768]{1,0:T(8,128)(2,1)S(1)}, u32[]{:S(2)}, u32[]{:S(2)}) %collective-permute-start.34) | collective-permute-done | bytes 196640 | tf_op jit(solution)/shard_map/ppermute | solution.py:55
  156.2 2.2 %shard_map.303 = f32[128,768]{1,0:T(8,128)} custom-call(bf16[128,768]{1,0:T(8,128)(2,1)S(1)} %bitcast.15, f32[768]{0:T(1024)S(1)} %copy-done.11, f32[128,768]{1,0:T(8,128)S(1)} %copy-done.30, bf16[576,1536]{1,0:T(8,128)(2,1)S(1)} %copy-done.16, bf16[128,1536]{1,0:T(8,128)(2,1)S(1)} %copy-done.28, bf16[128,1536]{1,0:T(8,128)(2,1)S(1)} %collective-permute-done.29.came_ref, ...), custom_call_target="tpu_custom_call" | custom-call | flops 3300000000 | tf_op jit(solution)/shard_map/pallas_call | solution.py:115
  158.5 0.6 collective-permute-done.37
  159.2 1.8 %multiply_reduce_fusion = (f32[24]{0:T(128)S(1)}, f32[24,2048]{1,0:T(8,128)}, f32[24]{0:T(128)S(1)}, f32[24,2048]{1,0:T(8,128)}) fusion(bf16[768,2048]{1,0:T(8,128)(2,1)} %refs_14_.1, s32[]{:T(128)S(6)} %select_n.2, f32[24,2176]{1,0:T(8,128)S(1)} %convert_add_fusion.2, f32[24,2816]{1,0:T(8,128)S(1)} %convert_add_fusion, bf16[768,2048]{1,0:T(8,128)(2,1)} %refs_13_.1), kind=kLoop, calls=%fused_computation.14 | loop fusion | flops 294864 | bytes 983236 | tf_op jit(solution)/shard_map/reduce_sum | solution.py:1054
  161.0 1.4 multiply_reduce_fusion.5
  162.5 0.6 convert_bitcast_fusion
  163.1 0.8 multiply_reduce_fusion.3
  163.9 0.6 dynamic-slice_divide_fusion
  164.5 0.6 dynamic-slice_divide_fusion.1
  165.1 0.6 slice.210
  165.8 2.6 %collective-permute-done.39 = bf16[64,768]{1,0:T(8,128)(2,1)S(1)} collective-permute-done((bf16[64,768]{1,0:T(8,128)(2,1)S(1)}, bf16[64,768]{1,0:T(8,128)(2,1)S(1)}, u32[]{:S(2)}, u32[]{:S(2)}) %collective-permute-start.39) | collective-permute-done | bytes 98336 | tf_op jit(solution)/shard_map/ppermute | solution.py:55
  168.3 0.7 convert_add_fusion.3
  (132 shorter events, 8.0 us)
Async XLA Ops:
  0.6 11.6 %collective-permute-start.1 = (bf16[128,768]{1,0:T(8,128)(2,1)}, bf16[128,768]{1,0:T(8,128)(2,1)S(1)}, u32[]{:S(2)}, u32[]{:S(2)}) collective-permute-start(bf16[128,768]{1,0:T(8,128)(2,1)} %bitcast.12), channel_id=1, source_target_pairs={{0,2},{1,3},{2,0},{3,1},{4,6},{5,7},{6,4},{7,5},{8,10},{9,11},{10,... | collective-permute-start | bytes 589832 | tf_op jit(solution)/shard_map/ppermute | solution.py:55
  3.7 9.2 %collective-permute-start = (bf16[128,768]{1,0:T(8,128)(2,1)}, bf16[128,768]{1,0:T(8,128)(2,1)S(1)}, u32[]{:S(2)}, u32[]{:S(2)}) collective-permute-start(bf16[128,768]{1,0:T(8,128)(2,1)} %bitcast.13), channel_id=1, source_target_pairs={{0,1},{1,0},{2,3},{3,2},{4,5},{5,4},{6,7},{7,6},{8,9},{9,8},{10,11... | collective-permute-start | bytes 589832 | tf_op jit(solution)/shard_map/ppermute | solution.py:55
  7.2 6.7 %copy-start.2 = (bf16[768,2048]{1,0:T(8,128)(2,1)S(1)}, bf16[768,2048]{1,0:T(8,128)(2,1)}, u32[]{:S(2)}) copy-start(bf16[768,2048]{1,0:T(8,128)(2,1)} %refs_13_.1) | copy-start | bytes 9437188
  7.2 6.7 %copy-start.3 = (bf16[768,2048]{1,0:T(8,128)(2,1)S(1)}, bf16[768,2048]{1,0:T(8,128)(2,1)}, u32[]{:S(2)}) copy-start(bf16[768,2048]{1,0:T(8,128)(2,1)} %refs_14_.1) | copy-start | bytes 9437188
  7.2 6.7 %copy-start.4 = (bf16[768,768]{1,0:T(8,128)(2,1)S(1)}, bf16[768,768]{1,0:T(8,128)(2,1)}, u32[]{:S(2)}) copy-start(bf16[768,768]{1,0:T(8,128)(2,1)} %wq_ref.5) | copy-start | bytes 3538948
  7.2 6.7 %copy-start.6 = (bf16[768,768]{1,0:T(8,128)(2,1)S(1)}, bf16[768,768]{1,0:T(8,128)(2,1)}, u32[]{:S(2)}) copy-start(bf16[768,768]{1,0:T(8,128)(2,1)} %wk_ref.5) | copy-start | bytes 3538948
  7.2 6.7 %copy-start.8 = (bf16[768,768]{1,0:T(8,128)(2,1)S(1)}, bf16[768,768]{1,0:T(8,128)(2,1)}, u32[]{:S(2)}) copy-start(bf16[768,768]{1,0:T(8,128)(2,1)} %wv_ref.5) | copy-start | bytes 3538948
  7.3 6.7 %copy-start.10 = (bf16[768,128]{1,0:T(8,128)(2,1)S(1)}, bf16[768,128]{1,0:T(8,128)(2,1)}, u32[]{:S(2)}) copy-start(bf16[768,128]{1,0:T(8,128)(2,1)} %refs_11_.1) | copy-start | bytes 589828
  7.3 6.7 %copy-start.11 = (f32[768]{0:T(1024)S(1)}, f32[768]{0:T(1024)}, u32[]{:S(2)}) copy-start(f32[768]{0:T(1024)} %gain_ref.3) | copy-start | bytes 9220
  7.3 6.7 %copy-start.12 = (f32[768]{0:T(1024)S(1)}, f32[768]{0:T(1024)}, u32[]{:S(2)}) copy-start(f32[768]{0:T(1024)} %refs_10_.1) | copy-start | bytes 9220
  7.3 6.7 %copy-start.13 = (f32[768]{0:T(1024)S(1)}, f32[768]{0:T(1024)}, u32[]{:S(2)}) copy-start(f32[768]{0:T(1024)} %refs_9_.1) | copy-start | bytes 9220
  7.3 6.7 %copy-start.14 = (bf16[2048,768]{1,0:T(8,128)(2,1)S(1)}, bf16[2048,768]{1,0:T(8,128)(2,1)}, u32[]{:S(2)}) copy-start(bf16[2048,768]{1,0:T(8,128)(2,1)} %refs_12_.1) | copy-start | bytes 9437188
  7.3 6.7 %copy-start.17 = (bf16[768,768]{1,0:T(8,128)(2,1)S(1)}, bf16[768,768]{1,0:T(8,128)(2,1)}, u32[]{:S(2)}) copy-start(bf16[768,768]{1,0:T(8,128)(2,1)} %refs_15_.1) | copy-start | bytes 3538948
  7.3 6.7 %copy-start.18 = (bf16[16,32,768]{2,1,0:T(8,128)(2,1)S(1)}, bf16[16,32,768]{2,1,0:T(8,128)(2,1)}, u32[]{:S(2)}) copy-start(bf16[16,32,768]{2,1,0:T(8,128)(2,1)} %tokens_any.1) | copy-start | bytes 2359300
  7.3 6.7 %copy-start.23 = (bf16[1,128,768]{2,1,0:T(8,128)(2,1)S(1)}, bf16[1,128,768]{2,1,0:T(8,128)(2,1)}, u32[]{:S(2)}) copy-start(bf16[1,128,768]{2,1,0:T(8,128)(2,1)} %param.17) | copy-start | bytes 589828
  7.4 6.7 %copy-start.25 = (s32[16]{0:T(128)S(1)}, s32[16]{0:T(128)}, u32[]{:S(2)}) copy-start(s32[16]{0:T(128)} %lengths_ref.3) | copy-start | bytes 196
  12.3 1.6 collective-permute-start.2
  27.1 4.5 %collective-permute-start.3 = (bf16[1,128,128]{2,1,0:T(8,128)(2,1)S(1)}, bf16[1,128,128]{2,1,0:T(8,128)(2,1)S(1)}, u32[]{:S(2)}, u32[]{:S(2)}) collective-permute-start(bf16[1,128,128]{2,1,0:T(8,128)(2,1)S(1)} %bitcast.8), channel_id=1, source_target_pairs={{0,8},{1,9},{2,10},{3,11},{4,12},{5,13},{6,14},{7,15},{8,0},{9,1},... | collective-permute-start | bytes 98312 | tf_op jit(solution)/shard_map/ppermute | solution.py:55
  28.8 5.4 %collective-permute-start.4 = (bf16[1,128,128]{2,1,0:T(8,128)(2,1)S(1)}, bf16[1,128,128]{2,1,0:T(8,128)(2,1)S(1)}, u32[]{:S(2)}, u32[]{:S(2)}) collective-permute-start(bf16[1,128,128]{2,1,0:T(8,128)(2,1)S(1)} %bitcast.9), channel_id=1, source_target_pairs={{0,16},{1,17},{2,18},{3,19},{4,20},{5,21},{6,22},{7,23},{8,24},{9,... | collective-permute-start | bytes 98312 | tf_op jit(solution)/shard_map/ppermute | solution.py:55
  31.4 5.7 %collective-permute-start.5 = (bf16[1,128,128]{2,1,0:T(8,128)(2,1)S(1)}, bf16[1,128,128]{2,1,0:T(8,128)(2,1)S(1)}, u32[]{:S(2)}, u32[]{:S(2)}) collective-permute-start(bf16[1,128,128]{2,1,0:T(8,128)(2,1)S(1)} %bitcast.10), channel_id=1, source_target_pairs={{0,24},{1,25},{2,26},{3,27},{4,28},{5,29},{6,30},{7,31},{8,16},{9,... | collective-permute-start | bytes 98312 | tf_op jit(solution)/shard_map/ppermute | solution.py:55
  37.1 8.4 %collective-permute-start.6 = (bf16[4,128,128]{2,1,0:T(8,128)(2,1)S(1)}, bf16[4,128,128]{2,1,0:T(8,128)(2,1)S(1)}, u32[]{:S(2)}, u32[]{:S(2)}) collective-permute-start(bf16[4,128,128]{2,1,0:T(8,128)(2,1)S(1)} %pad_maximum_fusion.1), channel_id=1, source_target_pairs={{0,2},{1,3},{2,0},{3,1},{4,6},{5,7},{6,4},{7,5},{8,10},{9,11},{10,... | collective-permute-start | bytes 393224 | tf_op jit(solution)/shard_map/ppermute | solution.py:55
  37.7 7.9 %collective-permute-start.7 = (bf16[4,128,128]{2,1,0:T(8,128)(2,1)S(1)}, bf16[4,128,128]{2,1,0:T(8,128)(2,1)S(1)}, u32[]{:S(2)}, u32[]{:S(2)}) collective-permute-start(bf16[4,128,128]{2,1,0:T(8,128)(2,1)S(1)} %pad_maximum_fusion.1), channel_id=1, source_target_pairs={{0,4},{1,5},{2,6},{3,7},{4,0},{5,1},{6,2},{7,3},{8,12},{9,13},{10,... | collective-permute-start | bytes 393224 | tf_op jit(solution)/shard_map/ppermute | solution.py:55
  39.2 6.4 %collective-permute-start.8 = (bf16[4,128,128]{2,1,0:T(8,128)(2,1)S(1)}, bf16[4,128,128]{2,1,0:T(8,128)(2,1)S(1)}, u32[]{:S(2)}, u32[]{:S(2)}) collective-permute-start(bf16[4,128,128]{2,1,0:T(8,128)(2,1)S(1)} %pad_maximum_fusion.1), channel_id=1, source_target_pairs={{0,6},{1,7},{2,4},{3,5},{4,2},{5,3},{6,0},{7,1},{8,14},{9,15},{10,... | collective-permute-start | bytes 393224 | tf_op jit(solution)/shard_map/ppermute | solution.py:55
  40.7 7.0 %copy-start.26 = (s32[16]{0:T(128)S(1)}, s32[16]{0:T(128)}, u32[]{:S(2)}) copy-start(s32[16]{0:T(128)} %positives_ref.1) | copy-start | bytes 196
  45.7 2.0 %collective-permute-start.9 = (bf16[16,128,128]{2,1,0:T(8,128)(2,1)S(1)}, bf16[16,128,128]{2,1,0:T(8,128)(2,1)S(1)}, u32[]{:S(2)}, u32[]{:S(2)}) collective-permute-start(bf16[16,128,128]{2,1,0:T(8,128)(2,1)S(1)} %constant_dynamic-update-slice_fusion.near_ref), channel_id=1, source_target_pairs={{0,1},{1,0},{2,3},{3,2},{4,5},{5,4},{6,7},{7,6},{8,9},{9,8},{10,11... | collective-permute-start | bytes 1572872 | tf_op jit(solution)/shard_map/ppermute | solution.py:55
  50.9 2.0 %collective-permute-start.10 = (bf16[16,128,128]{2,1,0:T(8,128)(2,1)S(1)}, bf16[16,128,128]{2,1,0:T(8,128)(2,1)S(1)}, u32[]{:S(2)}, u32[]{:S(2)}) collective-permute-start(bf16[16,128,128]{2,1,0:T(8,128)(2,1)S(1)} %get-tuple-element.171), channel_id=1, source_target_pairs={{0,1},{1,0},{2,3},{3,2},{4,5},{5,4},{6,7},{7,6},{8,9},{9,8},{10,11... | collective-permute-start | bytes 1572872 | tf_op jit(solution)/shard_map/ppermute | solution.py:55
  53.0 8.2 %collective-permute-start.11 = (bf16[4,128,128]{2,1,0:T(8,128)(2,1)S(1)}, bf16[4,128,128]{2,1,0:T(8,128)(2,1)S(1)}, u32[]{:S(2)}, u32[]{:S(2)}) collective-permute-start(bf16[4,128,128]{2,1,0:T(8,128)(2,1)S(1)} %get-tuple-element.291), channel_id=1, source_target_pairs={{0,4},{1,5},{2,6},{3,7},{4,0},{5,1},{6,2},{7,3},{8,12},{9,13},{10,... | collective-permute-start | bytes 393224 | tf_op jit(solution)/shard_map/ppermute | solution.py:55
  54.6 8.1 %collective-permute-start.12 = (bf16[4,128,128]{2,1,0:T(8,128)(2,1)S(1)}, bf16[4,128,128]{2,1,0:T(8,128)(2,1)S(1)}, u32[]{:S(2)}, u32[]{:S(2)}) collective-permute-start(bf16[4,128,128]{2,1,0:T(8,128)(2,1)S(1)} %get-tuple-element.290), channel_id=1, source_target_pairs={{0,2},{1,3},{2,0},{3,1},{4,6},{5,7},{6,4},{7,5},{8,10},{9,11},{10,... | collective-permute-start | bytes 393224 | tf_op jit(solution)/shard_map/ppermute | solution.py:55
  55.1 7.6 %collective-permute-start.13 = (bf16[4,128,128]{2,1,0:T(8,128)(2,1)S(1)}, bf16[4,128,128]{2,1,0:T(8,128)(2,1)S(1)}, u32[]{:S(2)}, u32[]{:S(2)}) collective-permute-start(bf16[4,128,128]{2,1,0:T(8,128)(2,1)S(1)} %get-tuple-element.289), channel_id=1, source_target_pairs={{0,6},{1,7},{2,4},{3,5},{4,2},{5,3},{6,0},{7,1},{8,14},{9,15},{10,... | collective-permute-start | bytes 393224 | tf_op jit(solution)/shard_map/ppermute | solution.py:55
  62.7 8.0 %collective-permute-start.18 = (bf16[256,2944]{1,0:T(8,128)(2,1)S(1)}, bf16[256,2944]{1,0:T(8,128)(2,1)S(1)}, u32[]{:S(2)}, u32[]{:S(2)}) collective-permute-start(bf16[256,2944]{1,0:T(8,128)(2,1)S(1)} %get-tuple-element.196), channel_id=1, source_target_pairs={{0,1},{1,0},{2,3},{3,2},{4,5},{5,4},{6,7},{7,6},{8,9},{9,8},{10,11... | collective-permute-start | bytes 4521992 | tf_op jit(solution)/shard_map/ppermute | solution.py:55
  62.8 7.9 %collective-permute-start.17 = (bf16[128,5760]{1,0:T(8,128)(2,1)S(1)}, bf16[128,5760]{1,0:T(8,128)(2,1)S(1)}, u32[]{:S(2)}, u32[]{:S(2)}) collective-permute-start(bf16[128,5760]{1,0:T(8,128)(2,1)S(1)} %get-tuple-element.231.slot_any), channel_id=1, source_target_pairs={{0,1},{1,0},{2,3},{3,2},{4,5},{5,4},{6,7},{7,6},{8,9},{9,8},{10,11... | collective-permute-start | bytes 4423688 | tf_op jit(solution)/shard_map/ppermute | solution.py:55
  63.3 7.4 %collective-permute-start.14 = (bf16[1,128,128]{2,1,0:T(8,128)(2,1)S(1)}, bf16[1,128,128]{2,1,0:T(8,128)(2,1)S(1)}, u32[]{:S(2)}, u32[]{:S(2)}) collective-permute-start(bf16[1,128,128]{2,1,0:T(8,128)(2,1)S(1)} %get-tuple-element.297), channel_id=1, source_target_pairs={{0,16},{1,17},{2,18},{3,19},{4,20},{5,21},{6,22},{7,23},{8,24},{9,... | collective-permute-start | bytes 98312 | tf_op jit(solution)/shard_map/ppermute | solution.py:55
  63.3 7.4 %collective-permute-start.15 = (bf16[1,128,128]{2,1,0:T(8,128)(2,1)S(1)}, bf16[1,128,128]{2,1,0:T(8,128)(2,1)S(1)}, u32[]{:S(2)}, u32[]{:S(2)}) collective-permute-start(bf16[1,128,128]{2,1,0:T(8,128)(2,1)S(1)} %get-tuple-element.296), channel_id=1, source_target_pairs={{0,8},{1,9},{2,10},{3,11},{4,12},{5,13},{6,14},{7,15},{8,0},{9,1},... | collective-permute-start | bytes 98312 | tf_op jit(solution)/shard_map/ppermute | solution.py:55
  64.2 6.5 %collective-permute-start.16 = (bf16[1,128,128]{2,1,0:T(8,128)(2,1)S(1)}, bf16[1,128,128]{2,1,0:T(8,128)(2,1)S(1)}, u32[]{:S(2)}, u32[]{:S(2)}) collective-permute-start(bf16[1,128,128]{2,1,0:T(8,128)(2,1)S(1)} %get-tuple-element.295), channel_id=1, source_target_pairs={{0,24},{1,25},{2,26},{3,27},{4,28},{5,29},{6,30},{7,31},{8,16},{9,... | collective-permute-start | bytes 98312 | tf_op jit(solution)/shard_map/ppermute | solution.py:55
  75.3 6.3 %collective-permute-start.21 = (bf16[128,5760]{1,0:T(8,128)(2,1)S(1)}, bf16[128,5760]{1,0:T(8,128)(2,1)S(1)}, u32[]{:S(2)}, u32[]{:S(2)}) collective-permute-start(bf16[128,5760]{1,0:T(8,128)(2,1)S(1)} %get-tuple-element.233.doc_any), channel_id=1, source_target_pairs={{0,1},{1,0},{2,3},{3,2},{4,5},{5,4},{6,7},{7,6},{8,9},{9,8},{10,11... | collective-permute-start | bytes 4423688 | tf_op jit(solution)/shard_map/ppermute | solution.py:55
  80.5 4.7 %collective-permute-start.20 = (bf16[576,1536]{1,0:T(8,128)(2,1)S(1)}, bf16[576,1536]{1,0:T(8,128)(2,1)S(1)}, u32[]{:S(2)}, u32[]{:S(2)}) collective-permute-start(bf16[576,1536]{1,0:T(8,128)(2,1)S(1)} %get-tuple-element.203.grads_ref), channel_id=1, source_target_pairs={{0,1},{1,0},{2,3},{3,2},{4,5},{5,4},{6,7},{7,6},{8,9},{9,8},{10,11... | collective-permute-start | bytes 5308424 | tf_op jit(solution)/shard_map/ppermute | solution.py:55
  81.1 4.2 %collective-permute-start.19 = (bf16[128,2304]{1,0:T(8,128)(2,1)S(1)}, bf16[128,2304]{1,0:T(8,128)(2,1)S(1)}, u32[]{:S(2)}, u32[]{:S(2)}) collective-permute-start(bf16[128,2304]{1,0:T(8,128)(2,1)S(1)} %get-tuple-element.236.slot_any.grads_ref), channel_id=1, source_target_pairs={{0,1},{1,0},{2,3},{3,2},{4,5},{5,4},{6,7},{7,6},{8,9},{9,8},{10,11... | collective-permute-start | bytes 1769480 | tf_op jit(solution)/shard_map/ppermute | solution.py:55
  81.2 4.1 %collective-permute-start.22 = (bf16[16,128]{1,0:T(8,128)(2,1)S(1)}, bf16[16,128]{1,0:T(8,128)(2,1)S(1)}, u32[]{:S(2)}, u32[]{:S(2)}) collective-permute-start(bf16[16,128]{1,0:T(8,128)(2,1)S(1)} %get-tuple-element.216.table_ref), channel_id=1, source_target_pairs={{0,1},{1,0},{2,3},{3,2},{4,5},{5,4},{6,7},{7,6},{8,9},{9,8},{10,11... | collective-permute-start | bytes 12296 | tf_op jit(solution)/shard_map/ppermute | solution.py:55
  84.3 25.9 %collective-permute-start.24 = (bf16[192,2816]{1,0:T(8,128)(2,1)S(1)}, bf16[192,2816]{1,0:T(8,128)(2,1)S(1)}, u32[]{:S(2)}, u32[]{:S(2)}) collective-permute-start(bf16[192,2816]{1,0:T(8,128)(2,1)S(1)} %get-tuple-element.221), channel_id=1, source_target_pairs={{0,8},{1,9},{2,10},{3,11},{4,12},{5,13},{6,14},{7,15},{8,0},{9,1},... | collective-permute-start | bytes 3244040 | tf_op jit(solution)/shard_map/ppermute | solution.py:55
  88.6 23.6 %collective-permute-start.23 = (bf16[208,2304]{1,0:T(8,128)(2,1)S(1)}, bf16[208,2304]{1,0:T(8,128)(2,1)S(1)}, u32[]{:S(2)}, u32[]{:S(2)}) collective-permute-start(bf16[208,2304]{1,0:T(8,128)(2,1)S(1)} %get-tuple-element.220), channel_id=1, source_target_pairs={{0,4},{1,5},{2,6},{3,7},{4,0},{5,1},{6,2},{7,3},{8,12},{9,13},{10,... | collective-permute-start | bytes 2875400 | tf_op jit(solution)/shard_map/ppermute | solution.py:55
  91.7 22.0 %collective-permute-start.28 = (bf16[192,2176]{1,0:T(8,128)(2,1)S(1)}, bf16[192,2176]{1,0:T(8,128)(2,1)S(1)}, u32[]{:S(2)}, u32[]{:S(2)}) collective-permute-start(bf16[192,2176]{1,0:T(8,128)(2,1)S(1)} %get-tuple-element.244), channel_id=1, source_target_pairs={{0,2},{1,3},{2,0},{3,1},{4,6},{5,7},{6,4},{7,5},{8,10},{9,11},{10,... | collective-permute-start | bytes 2506760 | tf_op jit(solution)/shard_map/ppermute | solution.py:55
  110.4 15.3 %collective-permute-start.27 = (bf16[96,2816]{1,0:T(8,128)(2,1)S(1)}, bf16[96,2816]{1,0:T(8,128)(2,1)S(1)}, u32[]{:S(2)}, u32[]{:S(2)}) collective-permute-start(bf16[96,2816]{1,0:T(8,128)(2,1)S(1)} %get-tuple-element.243), channel_id=1, source_target_pairs={{0,4},{1,5},{2,6},{3,7},{4,0},{5,1},{6,2},{7,3},{8,12},{9,13},{10,... | collective-permute-start | bytes 1622024 | tf_op jit(solution)/shard_map/ppermute | solution.py:55
  111.0 18.6 %collective-permute-start.26 = (bf16[512,768]{1,0:T(8,128)(2,1)}, bf16[512,768]{1,0:T(8,128)(2,1)S(1)}, u32[]{:S(2)}, u32[]{:S(2)}) collective-permute-start(bf16[512,768]{1,0:T(8,128)(2,1)} %get-tuple-element.242), channel_id=1, source_target_pairs={{0,8},{1,9},{2,10},{3,11},{4,12},{5,13},{6,14},{7,15},{8,0},{9,1},... | collective-permute-start | bytes 2359304 | tf_op jit(solution)/shard_map/ppermute | solution.py:55
  113.1 18.3 %collective-permute-start.25 = (bf16[112,2304]{1,0:T(8,128)(2,1)}, bf16[112,2304]{1,0:T(8,128)(2,1)S(1)}, u32[]{:S(2)}, u32[]{:S(2)}) collective-permute-start(bf16[112,2304]{1,0:T(8,128)(2,1)} %get-tuple-element.241), channel_id=1, source_target_pairs={{0,2},{1,3},{2,0},{3,1},{4,6},{5,7},{6,4},{7,5},{8,10},{9,11},{10,... | collective-permute-start | bytes 1548296 | tf_op jit(solution)/shard_map/ppermute | solution.py:55
  114.5 20.1 %collective-permute-start.33 = (bf16[96,2176]{1,0:T(8,128)(2,1)}, bf16[96,2176]{1,0:T(8,128)(2,1)S(1)}, u32[]{:S(2)}, u32[]{:S(2)}) collective-permute-start(bf16[96,2176]{1,0:T(8,128)(2,1)} %get-tuple-element.258), channel_id=1, source_target_pairs={{0,4},{1,5},{2,6},{3,7},{4,0},{5,1},{6,2},{7,3},{8,12},{9,13},{10,... | collective-permute-start | bytes 1253384 | tf_op jit(solution)/shard_map/ppermute | solution.py:55
  127.2 10.0 %collective-permute-start.32 = (bf16[48,2816]{1,0:T(8,128)(2,1)}, bf16[48,2816]{1,0:T(8,128)(2,1)}, u32[]{:S(2)}, u32[]{:S(2)}) collective-permute-start(bf16[48,2816]{1,0:T(8,128)(2,1)} %get-tuple-element.257), channel_id=1, source_target_pairs={{0,2},{1,3},{2,0},{3,1},{4,6},{5,7},{6,4},{7,5},{8,10},{9,11},{10,... | collective-permute-start | bytes 811016 | tf_op jit(solution)/shard_map/ppermute | solution.py:55
  129.6 7.2 %copy-start.21 = (bf16[128,1536]{1,0:T(8,128)(2,1)S(1)}, bf16[128,1536]{1,0:T(8,128)(2,1)}, u32[]{:S(2)}) copy-start(bf16[128,1536]{1,0:T(8,128)(2,1)} %copy-done.20) | copy-start | bytes 1179652
  129.6 7.5 %copy-start.1 = (bf16[48,2816]{1,0:T(8,128)(2,1)S(1)}, bf16[48,2816]{1,0:T(8,128)(2,1)}, u32[]{:S(2)}) copy-start(bf16[48,2816]{1,0:T(8,128)(2,1)} %copy-done) | copy-start | bytes 811012
  129.6 26.5 %copy-start.28 = (bf16[128,1536]{1,0:T(8,128)(2,1)S(1)}, bf16[128,1536]{1,0:T(8,128)(2,1)}, u32[]{:S(2)}) copy-start(bf16[128,1536]{1,0:T(8,128)(2,1)} %copy-done.27) | copy-start | bytes 1179652
  129.6 26.5 %copy-start.30 = (f32[128,768]{1,0:T(8,128)S(1)}, f32[128,768]{1,0:T(8,128)}, u32[]{:S(2)}) copy-start(f32[128,768]{1,0:T(8,128)} %copy-done.29) | copy-start | bytes 1179652
  129.8 18.3 %collective-permute-start.30 = (bf16[256,768]{1,0:T(8,128)(2,1)S(1)}, bf16[256,768]{1,0:T(8,128)(2,1)S(1)}, u32[]{:S(2)}, u32[]{:S(2)}) collective-permute-start(bf16[256,768]{1,0:T(8,128)(2,1)S(1)} %get-tuple-element.255), channel_id=1, source_target_pairs={{0,4},{1,5},{2,6},{3,7},{4,0},{5,1},{6,2},{7,3},{8,12},{9,13},{10,... | collective-permute-start | bytes 1179656 | tf_op jit(solution)/shard_map/ppermute | solution.py:55
  131.4 24.8 %copy-start.16 = (bf16[576,1536]{1,0:T(8,128)(2,1)S(1)}, bf16[576,1536]{1,0:T(8,128)(2,1)}, u32[]{:S(2)}) copy-start(bf16[576,1536]{1,0:T(8,128)(2,1)} %copy-done.15) | copy-start | bytes 5308420
  134.8 12.7 %collective-permute-start.31 = (bf16[64,2304]{1,0:T(8,128)(2,1)S(1)}, bf16[64,2304]{1,0:T(8,128)(2,1)S(1)}, u32[]{:S(2)}, u32[]{:S(2)}) collective-permute-start(bf16[64,2304]{1,0:T(8,128)(2,1)S(1)} %get-tuple-element.256), channel_id=1, source_target_pairs={{0,8},{1,9},{2,10},{3,11},{4,12},{5,13},{6,14},{7,15},{8,0},{9,1},... | collective-permute-start | bytes 884744 | tf_op jit(solution)/shard_map/ppermute | solution.py:55
  135.1 15.3 %collective-permute-start.35 = (bf16[48,2176]{1,0:T(8,128)(2,1)S(1)}, bf16[48,2176]{1,0:T(8,128)(2,1)S(1)}, u32[]{:S(2)}, u32[]{:S(2)}) collective-permute-start(bf16[48,2176]{1,0:T(8,128)(2,1)S(1)} %get-tuple-element.266), channel_id=1, source_target_pairs={{0,8},{1,9},{2,10},{3,11},{4,12},{5,13},{6,14},{7,15},{8,0},{9,1},... | collective-permute-start | bytes 626696 | tf_op jit(solution)/shard_map/ppermute | solution.py:55
  136.9 19.3 %collective-permute-start.29 = (bf16[128,1536]{1,0:T(8,128)(2,1)S(1)}, bf16[128,1536]{1,0:T(8,128)(2,1)S(1)}, u32[]{:S(2)}, u32[]{:S(2)}) collective-permute-start(bf16[128,1536]{1,0:T(8,128)(2,1)S(1)} %copy-done.21), channel_id=1, source_target_pairs={{0,2},{1,3},{2,0},{3,1},{4,6},{5,7},{6,4},{7,5},{8,10},{9,11},{10,... | collective-permute-start | bytes 1179656 | tf_op jit(solution)/shard_map/ppermute | solution.py:55
  137.1 19.1 %copy-start.9 = (bf16[768,768]{1,0:T(8,128)(2,1)S(1)}, bf16[768,768]{1,0:T(8,128)(2,1)}, u32[]{:S(2)}) copy-start(bf16[768,768]{1,0:T(8,128)(2,1)} %wv_ref.5) | copy-start | bytes 3538948
  138.3 20.1 %collective-permute-start.38 = (bf16[24,2816]{1,0:T(8,128)(2,1)S(1)}, bf16[24,2816]{1,0:T(8,128)(2,1)S(1)}, u32[]{:S(2)}, u32[]{:S(2)}) collective-permute-start(bf16[24,2816]{1,0:T(8,128)(2,1)S(1)} %get-tuple-element.293), channel_id=1, source_target_pairs={{0,16},{1,17},{2,18},{3,19},{4,20},{5,21},{6,22},{7,23},{8,24},{9,... | collective-permute-start | bytes 405512 | tf_op jit(solution)/shard_map/ppermute | solution.py:55
  147.5 8.7 %copy-start.5 = (bf16[768,768]{1,0:T(8,128)(2,1)S(1)}, bf16[768,768]{1,0:T(8,128)(2,1)}, u32[]{:S(2)}) copy-start(bf16[768,768]{1,0:T(8,128)(2,1)} %wq_ref.5) | copy-start | bytes 3538948
  147.5 8.7 %copy-start.7 = (bf16[768,768]{1,0:T(8,128)(2,1)S(1)}, bf16[768,768]{1,0:T(8,128)(2,1)}, u32[]{:S(2)}) copy-start(bf16[768,768]{1,0:T(8,128)(2,1)} %wk_ref.5) | copy-start | bytes 3538948
  147.5 8.7 %copy-start.24 = (bf16[1,128,768]{2,1,0:T(8,128)(2,1)S(1)}, bf16[1,128,768]{2,1,0:T(8,128)(2,1)}, u32[]{:S(2)}) copy-start(bf16[1,128,768]{2,1,0:T(8,128)(2,1)} %param.17) | copy-start | bytes 589828
  147.6 11.5 %collective-permute-start.36 = (bf16[40,2304]{1,0:T(8,128)(2,1)S(1)}, bf16[40,2304]{1,0:T(8,128)(2,1)S(1)}, u32[]{:S(2)}, u32[]{:S(2)}) collective-permute-start(bf16[40,2304]{1,0:T(8,128)(2,1)S(1)} %pad_maximum_fusion), channel_id=1, source_target_pairs={{0,16},{1,17},{2,18},{3,19},{4,20},{5,21},{6,22},{7,23},{8,24},{9,... | collective-permute-start | bytes 552968 | tf_op jit(solution)/shard_map/ppermute | solution.py:55
  150.4 5.7 %collective-permute-start.34 = (bf16[128,768]{1,0:T(8,128)(2,1)S(1)}, bf16[128,768]{1,0:T(8,128)(2,1)S(1)}, u32[]{:S(2)}, u32[]{:S(2)}) collective-permute-start(bf16[128,768]{1,0:T(8,128)(2,1)S(1)} %get-tuple-element.265), channel_id=1, source_target_pairs={{0,2},{1,3},{2,0},{3,1},{4,6},{5,7},{6,4},{7,5},{8,10},{9,11},{10,... | collective-permute-start | bytes 589832 | tf_op jit(solution)/shard_map/ppermute | solution.py:55
  150.5 8.6 %collective-permute-start.37 = (bf16[24,2176]{1,0:T(8,128)(2,1)S(1)}, bf16[24,2176]{1,0:T(8,128)(2,1)S(1)}, u32[]{:S(2)}, u32[]{:S(2)}) collective-permute-start(bf16[24,2176]{1,0:T(8,128)(2,1)S(1)} %get-tuple-element.301), channel_id=1, source_target_pairs={{0,16},{1,17},{2,18},{3,19},{4,20},{5,21},{6,22},{7,23},{8,24},{9,... | collective-permute-start | bytes 313352 | tf_op jit(solution)/shard_map/ppermute | solution.py:55
  162.4 5.9 %collective-permute-start.39 = (bf16[64,768]{1,0:T(8,128)(2,1)S(1)}, bf16[64,768]{1,0:T(8,128)(2,1)S(1)}, u32[]{:S(2)}, u32[]{:S(2)}) collective-permute-start(bf16[64,768]{1,0:T(8,128)(2,1)S(1)} %get-tuple-element.275), channel_id=1, source_target_pairs={{0,16},{1,17},{2,18},{3,19},{4,20},{5,21},{6,22},{7,23},{8,24},{9,... | collective-permute-start | bytes 294920 | tf_op jit(solution)/shard_map/ppermute | solution.py:55
  (7 other events, 22.9 us)

commit v7 on v6

--- a/solution.py
+++ b/solution.py
@@ -797,10 +797,10 @@
     waxes = list(range(3, bits))
 
     orders = (
-        waxes[:1] + [2] + [1] + waxes[1:],
-        [1] + [2] + waxes[:1] + waxes[1:],
-        waxes[:1] + [2] + [1] + waxes[1:],
         [2] + [1] + waxes[:1] + waxes[1:],
+        waxes[:1] + [1] + [2] + waxes[1:],
+        [2] + [1] + waxes[:1] + waxes[1:],
+        [1] + waxes[:1] + [2] + waxes[1:],
     )
     own_tokens = doc_tokens[0]
     y_tokens = swap(own_tokens, 2)

time: 169 us -> 166 us (0.982)
  waiting for transfers between devices: 58.1 us -> 53.4 us
  starting transfers between devices: 33.5 us -> 35.2 us
    ppermute x40, waiting for transfers between devices: 58.1 us -> 53.4 us  [swap(): return lax.ppermute(values, ('wide', 'narrow'), pairs)]
    ppermute x40, starting transfers between devices: 33.5 us -> 35.2 us  [swap(): return lax.ppermute(values, ('wide', 'narrow'), pairs)]
  transfers between devices with their start and end apart: 40 -> 40, of which waited for: 17 -> 16; matrix products, arithmetic and copies ran while one was open for 4% -> 4% of each run, Pallas kernels for 26% -> 27%
where the time goes in v7:
time: 166 us
  Pallas kernels  64.9 us (39%)
  waiting for transfers between devices  53.4 us (32%)
  starting transfers between devices  35.2 us (21%)
  other arithmetic  8.17 us (5%)
  local copies, waits for them, and re-layouts  3 us (2%)
    pallas_call x24, Pallas kernels, call(): pl.pallas_call(kernel, out_shape=tuple(outs), in_specs=specs[:len(args)],...  64.9 us
    ppermute x40, waiting for transfers between devices, swap(): return lax.ppermute(values, ('wide', 'narrow'), pairs)  53.4 us
    ppermute x40, starting transfers between devices, swap(): return lax.ppermute(values, ('wide', 'narrow'), pairs)  35.2 us
    reduce_sum x3, other arithmetic, gain_grad(): jnp.sum(own_rows(weight) * grad, 1)  4.08 us
  transfers between devices with their start and end apart: 40, of which 16 were waited for; matrix products, arithmetic and copies ran while one was open for 4% of the time, Pallas kernels for 27%

profile of v7, /device:TPU:0, one launch (start us, length us, event | category | flops | bytes accessed | tf_op | source)
XLA Modules:
  0.0 166.1 jit_solution(3131725123007649361)
XLA Ops:
  0.6 3.0 %collective-permute-start.1 = (bf16[128,768]{1,0:T(8,128)(2,1)}, bf16[128,768]{1,0:T(8,128)(2,1)S(1)}, u32[]{:S(2)}, u32[]{:S(2)}) collective-permute-start(bf16[128,768]{1,0:T(8,128)(2,1)} %bitcast.12), channel_id=1, source_target_pairs={{0,2},{1,3},{2,0},{3,1},{4,6},{5,7},{6,4},{7,5},{8,10},{9,11},{10,... | collective-permute-start | bytes 589832 | tf_op jit(solution)/shard_map/ppermute | solution.py:55
  3.7 0.8 copy.33.table_ref
  4.5 2.7 %shard_map.280 = (f32[6,256,512]{2,1,0:T(8,128)S(1)}, f32[6,256,128]{2,1,0:T(8,128)S(1)}) custom-call(s32[1]{0:T(128)} %bitcast.rank_ref, f32[32,12]{1,0:T(8,128)S(1)} %copy.33.table_ref), custom_call_target="tpu_custom_call" | custom-call | flops 3300000000 | tf_op jit(solution)/shard_map/pallas_call | solution.py:115
  7.4 4.9 %shard_map.281 = (bf16[32,128,128]{2,1,0:T(8,128)(2,1)S(1)}, f32[128,128]{1,0:T(8,128)S(1)}) custom-call(s32[1]{0:T(128)} %bitcast.rank_ref, s32[16,32,128]{2,1,0:T(8,128)S(1)} %copy-done.22), custom_call_target="tpu_custom_call" | custom-call | flops 5500000256 | tf_op jit(solution)/shard_map/pallas_call | solution.py:115
  12.3 0.6 collective-permute-start.2
  12.8 1.1 collective-permute-done.2.last_ref
  14.0 13.1 %shard_map.282 = (bf16[640,768]{1,0:T(8,128)(2,1)S(1)}, bf16[256,768]{1,0:T(8,128)(2,1)S(1)}, bf16[640,768]{1,0:T(8,128)(2,1)S(1)}, bf16[640,768]{1,0:T(8,128)(2...) custom-call(s32[1]{0:T(128)} %bitcast.rank_ref, ...), custom_call_target="tpu_custom_call" | custom-call | flops 19800000512 | tf_op jit(solution)/shard_map/pallas_call | solution.py:115
  27.1 1.7 collective-permute-start.3
  28.8 2.6 %collective-permute-start.4 = (bf16[1,128,128]{2,1,0:T(8,128)(2,1)S(1)}, bf16[1,128,128]{2,1,0:T(8,128)(2,1)S(1)}, u32[]{:S(2)}, u32[]{:S(2)}) collective-permute-start(bf16[1,128,128]{2,1,0:T(8,128)(2,1)S(1)} %bitcast.9), channel_id=1, source_target_pairs={{0,16},{1,17},{2,18},{3,19},{4,20},{5,21},{6,22},{7,23},{8,24},{9,... | collective-permute-start | bytes 98312 | tf_op jit(solution)/shard_map/ppermute | solution.py:55
  31.6 2.6 %collective-permute-done.4 = bf16[1,128,128]{2,1,0:T(8,128)(2,1)S(1)} collective-permute-done((bf16[1,128,128]{2,1,0:T(8,128)(2,1)S(1)}, bf16[1,128,128]{2,1,0:T(8,128)(2,1)S(1)}, u32[]{:S(2)}, u32[]{:S(2)}) %collective-permute-start.4) | collective-permute-done | bytes 32800 | tf_op jit(solution)/shard_map/ppermute | solution.py:55
  34.2 2.9 %collective-permute-done.5 = bf16[1,128,128]{2,1,0:T(8,128)(2,1)S(1)} collective-permute-done((bf16[1,128,128]{2,1,0:T(8,128)(2,1)S(1)}, bf16[1,128,128]{2,1,0:T(8,128)(2,1)S(1)}, u32[]{:S(2)}, u32[]{:S(2)}) %collective-permute-start.5) | collective-permute-done | bytes 32800 | tf_op jit(solution)/shard_map/ppermute | solution.py:55
  37.7 1.5 collective-permute-start.7
  39.2 1.5 collective-permute-start.8
  40.7 4.8 %shard_map.283 = (bf16[256,2944]{1,0:T(8,128)(2,1)S(1)}, bf16[256,2944]{1,0:T(8,128)(2,1)S(1)}, bf16[512,384]{1,0:T(8,128)(2,1)S(1)}) custom-call(s32[1]{0:T(128)} %bitcast.rank_ref, bf16[640,768]{1,0:T(8,128)(2,1)S(1)} %get-tuple-element.159.all_ref, bf16[256,768]{1,0:T(8,128)(2,1)S(1)} %get-tuple-element.160.normed_feed_ref, ...), custom_call_target="tpu_custom_call" | custom-call | flops 5500000256 | tf_op jit(solution)/shard_map/pallas_call | solution.py:115
  45.7 1.9 %collective-permute-done.9.far_ref = bf16[16,128,128]{2,1,0:T(8,128)(2,1)S(1)} collective-permute-done((bf16[16,128,128]{2,1,0:T(8,128)(2,1)S(1)}, bf16[16,128,128]{2,1,0:T(8,128)(2,1)S(1)}, u32[]{:S(2)}, u32[]{:S(2)}) %collective-permute-start.9) | collective-permute-done | bytes 524320 | tf_op jit(solution)/shard_map/ppermute | solution.py:55
  47.6 3.2 %shard_map.284 = (f32[4,128]{1,0:T(4,128)S(1)}, f32[128,128]{1,0:T(8,128)S(1)}, bf16[16,128,128]{2,1,0:T(8,128)(2,1)S(1)}, bf16[16,128,128]{2,1,0:T(8,128)(2,1)S(1)}) custom-call(s32[1]{0:T(128)} %bitcast.rank_ref, s32[16]{0:T(128)S(1)} %copy-done.25, s32[16]{0:T(128)S(1)} %copy-done.26, bf16[32,128,128]{2,1,0:T(8,128)(2,1)S(1)} %get-tuple-element.148.counts_ref, ...), custom_call_target="tpu_custom_call" | custom-call | flops 3300000000 | tf_op jit(solution)/shard_map/pallas_call | solution.py:115
  51.1 1.8 %collective-permute-done.10 = bf16[16,128,128]{2,1,0:T(8,128)(2,1)S(1)} collective-permute-done((bf16[16,128,128]{2,1,0:T(8,128)(2,1)S(1)}, bf16[16,128,128]{2,1,0:T(8,128)(2,1)S(1)}, u32[]{:S(2)}, u32[]{:S(2)}) %collective-permute-start.10) | collective-permute-done | bytes 524320 | tf_op jit(solution)/shard_map/ppermute | solution.py:55
  53.0 1.6 collective-permute-start.11
  55.1 1.5 collective-permute-start.13
  56.6 4.6 %shard_map.285 = (bf16[128,5760]{1,0:T(8,128)(2,1)S(1)}, f32[128,768]{1,0:T(8,128)S(1)}, bf16[128,768]{1,0:T(8,128)(2,1)S(1)}) custom-call(f32[128,128]{1,0:T(8,128)S(1)} %get-tuple-element.173.grad_unit_ref, f32[256,128]{1,0:T(8,128)S(1)} %get-tuple-element.174.embed_ref.refs_4_, f32[256,768]{1,0:T(8,128)S(1)} %get-tuple-element.175.after_feed_ref.refs_5_, ...), custom_call_target="tpu_custom_call" | custom-call | flops 7699999744 | tf_op jit(solution)/shard_map/pallas_call | solution.py:115
  61.2 1.5 collective-permute-done.12
  63.3 0.9 collective-permute-start.15
  64.2 3.5 %collective-permute-start.16 = (bf16[1,128,128]{2,1,0:T(8,128)(2,1)S(1)}, bf16[1,128,128]{2,1,0:T(8,128)(2,1)S(1)}, u32[]{:S(2)}, u32[]{:S(2)}) collective-permute-start(bf16[1,128,128]{2,1,0:T(8,128)(2,1)S(1)} %get-tuple-element.295), channel_id=1, source_target_pairs={{0,24},{1,25},{2,26},{3,27},{4,28},{5,29},{6,30},{7,31},{8,16},{9,... | collective-permute-start | bytes 98312 | tf_op jit(solution)/shard_map/ppermute | solution.py:55
  67.7 3.0 %shard_map.286 = (bf16[128,2304]{1,0:T(8,128)(2,1)S(1)}, f32[12,128]{1,0:T(8,128)S(1)}) custom-call(bf16[256,768]{1,0:T(8,128)(2,1)S(1)} %get-tuple-element.183.query_ref, bf16[640,768]{1,0:T(8,128)(2,1)S(1)} %get-tuple-element.184.key_ref, bf16[640,768]{1,0:T(8,128)(2,1)S(1)} %get-tuple-element.185.value_ref, ...), custom_call_target="tpu_custom_call" | custom-call | flops 4400000000 | tf_op jit(solution)/shard_map/pallas_call | solution.py:115
  70.8 4.5 %shard_map.287 = (bf16[128,5760]{1,0:T(8,128)(2,1)S(1)}, f32[128,768]{1,0:T(8,128)S(1)}, bf16[128,768]{1,0:T(8,128)(2,1)S(1)}) custom-call(bf16[1,128,128]{2,1,0:T(8,128)(2,1)S(1)} %get-tuple-element.298.refs_0_, bf16[1,128,128]{2,1,0:T(8,128)(2,1)S(1)} %collective-permute-done.14.refs_1_, bf16[1,128,128]{2,1,0:T(8,128)(2,1)S(1)} %collective-permute-done.15.refs_2_, ...), custom_call_target="tpu_custom_call" | custom-call | flops 7699999744 | tf_op jit(solution)/shard_map/pallas_call | solution.py:115
  75.4 5.1 %shard_map.288 = (bf16[576,1536]{1,0:T(8,128)(2,1)S(1)}, bf16[16,128]{1,0:T(8,128)(2,1)S(1)}) custom-call(s32[1]{0:T(128)} %bitcast.rank_ref, bf16[256,768]{1,0:T(8,128)(2,1)S(1)} %get-tuple-element.183.query_ref, bf16[640,768]{1,0:T(8,128)(2,1)S(1)} %get-tuple-element.184.key_ref, bf16[640,768]{1,0:T(8,128)(2,1)S(1)} %get-tuple-element.185.value_ref, ...), custom_call_target="tpu_custom_call" | custom-call | flops 3300000000 | tf_op jit(solution)/shard_map/pallas_call | solution.py:115
  81.6 2.7 %shard_map.289 = (bf16[192,2816]{1,0:T(8,128)(2,1)S(1)}, bf16[192,2816]{1,0:T(8,128)(2,1)S(1)}) custom-call(bf16[256,2944]{1,0:T(8,128)(2,1)S(1)} %get-tuple-element.229.kept_any, bf16[256,2944]{1,0:T(8,128)(2,1)S(1)} %collective-permute-done.18.came_any, bf16[128,5760]{1,0:T(8,128)(2,1)S(1)} %get-tuple-element.231.slot_any, ...), custom_call_target="tpu_custom_call" | custom-call | flops 3300000000 | tf_op jit(solution)/shard_map/pallas_call | solution.py:115
  84.3 0.6 collective-permute-start.24
  85.3 3.4 %shard_map.290 = (bf16[192,2304]{1,0:T(8,128)(2,1)S(1)}, bf16[208,2304]{1,0:T(8,128)(2,1)S(1)}, bf16[128,1536]{1,0:T(8,128)(2,1)S(1)}, bf16[128,1536]{1,0:T(8,128)(2,1)S(1)}) custom-call(bf16[512,384]{1,0:T(8,128)(2,1)S(1)} %get-tuple-element.204.doc_ref, bf16[256,2944]{1,0:T(8,128)(2,1)S(1)} %get-tuple-element.229.kept_any, ...), custom_call_target="tpu_custom_call" | custom-call | flops 3300000000 | tf_op jit(solution)/shard_map/pallas_call | solution.py:115
  88.6 0.9 collective-permute-start.23
  89.5 2.4 %shard_map.291 = (bf16[192,2176]{1,0:T(8,128)(2,1)S(1)}, bf16[192,2176]{1,0:T(8,128)(2,1)S(1)}) custom-call(bf16[256,2944]{1,0:T(8,128)(2,1)S(1)} %get-tuple-element.229.kept_any, bf16[256,2944]{1,0:T(8,128)(2,1)S(1)} %collective-permute-done.18.came_any, bf16[128,5760]{1,0:T(8,128)(2,1)S(1)} %get-tuple-element.231.slot_any, ...), custom_call_target="tpu_custom_call" | custom-call | flops 3300000000 | tf_op jit(solution)/shard_map/pallas_call | solution.py:115
  92.1 2.2 %shard_map.292 = (bf16[512,768]{1,0:T(8,128)(2,1)S(1)}, bf16[512,768]{1,0:T(8,128)(2,1)}) custom-call(bf16[256,2944]{1,0:T(8,128)(2,1)S(1)} %get-tuple-element.229.kept_any, bf16[256,2944]{1,0:T(8,128)(2,1)S(1)} %collective-permute-done.18.came_any, bf16[128,5760]{1,0:T(8,128)(2,1)S(1)} %get-tuple-element.231.slot_any, ...), custom_call_target="tpu_custom_call" | custom-call | flops 3300000000 | tf_op jit(solution)/shard_map/pallas_call | solution.py:115
  94.3 2.7 %shard_map.293 = f32[128,768]{1,0:T(8,128)} custom-call(s32[1]{0:T(128)} %bitcast.rank_ref, bf16[16,32,768]{2,1,0:T(8,128)(2,1)S(1)} %copy-done.19, f32[768]{0:T(1024)S(1)} %copy-done.11, f32[128,768]{1,0:T(8,128)S(1)} %get-tuple-element.179.after_ref, bf16[128,2304]{1,0:T(8,128)(2,1)S(1)} %get-tuple-element.236.slot_any.grads_ref, ...), custom_call_target="tpu_custom_call" | custom-call | flops 3300000000 | tf_op jit(solution)/shard_map/pallas_call | solution.py:115
  96.9 13.2 %collective-permute-done.24.came_ref = bf16[192,2816]{1,0:T(8,128)(2,1)S(1)} collective-permute-done((bf16[192,2816]{1,0:T(8,128)(2,1)S(1)}, bf16[192,2816]{1,0:T(8,128)(2,1)S(1)}, u32[]{:S(2)}, u32[]{:S(2)}) %collective-permute-start.24) | collective-permute-done | bytes 1081376 | tf_op jit(solution)/shard_map/ppermute | solution.py:55
  110.4 0.6 collective-permute-start.27
  111.0 1.2 collective-permute-start.26
  112.2 0.9 shard_map.295
  113.2 0.9 shard_map.296
  114.1 0.8 collective-permute-start.33
  114.9 10.8 %collective-permute-done.27.came_ref = bf16[96,2816]{1,0:T(8,128)(2,1)S(1)} collective-permute-done((bf16[96,2816]{1,0:T(8,128)(2,1)S(1)}, bf16[96,2816]{1,0:T(8,128)(2,1)S(1)}, u32[]{:S(2)}, u32[]{:S(2)}) %collective-permute-start.27) | collective-permute-done | bytes 540704 | tf_op jit(solution)/shard_map/ppermute | solution.py:55
  125.7 0.8 shard_map.297
  126.5 0.7 copy-done
  127.2 0.6 slice_reduce_fusion
  127.8 1.8 %collective-permute-done.26.came_ref = bf16[512,768]{1,0:T(8,128)(2,1)S(1)} collective-permute-done((bf16[512,768]{1,0:T(8,128)(2,1)}, bf16[512,768]{1,0:T(8,128)(2,1)S(1)}, u32[]{:S(2)}, u32[]{:S(2)}) %collective-permute-start.26) | collective-permute-done | bytes 786464 | tf_op jit(solution)/shard_map/ppermute | solution.py:55
  129.8 1.6 collective-permute-start.30
  131.5 3.1 %collective-permute-done.33.came_ref = bf16[96,2176]{1,0:T(8,128)(2,1)S(1)} collective-permute-done((bf16[96,2176]{1,0:T(8,128)(2,1)}, bf16[96,2176]{1,0:T(8,128)(2,1)S(1)}, u32[]{:S(2)}, u32[]{:S(2)}) %collective-permute-start.33) | collective-permute-done | bytes 417824 | tf_op jit(solution)/shard_map/ppermute | solution.py:55
  135.1 1.7 %collective-permute-start.35 = (bf16[48,2176]{1,0:T(8,128)(2,1)S(1)}, bf16[48,2176]{1,0:T(8,128)(2,1)S(1)}, u32[]{:S(2)}, u32[]{:S(2)}) collective-permute-start(bf16[48,2176]{1,0:T(8,128)(2,1)S(1)} %get-tuple-element.266), channel_id=1, source_target_pairs={{0,4},{1,5},{2,6},{3,7},{4,0},{5,1},{6,2},{7,3},{8,12},{9,13},{10,... | collective-permute-start | bytes 626696 | tf_op jit(solution)/shard_map/ppermute | solution.py:55
  136.9 1.1 add_convert_fusion
  138.1 4.5 %collective-permute-done.31 = bf16[64,2304]{1,0:T(8,128)(2,1)S(1)} collective-permute-done((bf16[64,2304]{1,0:T(8,128)(2,1)S(1)}, bf16[64,2304]{1,0:T(8,128)(2,1)S(1)}, u32[]{:S(2)}, u32[]{:S(2)}) %collective-permute-start.31) | collective-permute-done | bytes 294944 | tf_op jit(solution)/shard_map/ppermute | solution.py:55
  143.2 1.7 %collective-permute-done.35 = bf16[48,2176]{1,0:T(8,128)(2,1)S(1)} collective-permute-done((bf16[48,2176]{1,0:T(8,128)(2,1)S(1)}, bf16[48,2176]{1,0:T(8,128)(2,1)S(1)}, u32[]{:S(2)}, u32[]{:S(2)}) %collective-permute-start.35) | collective-permute-done | bytes 208928 | tf_op jit(solution)/shard_map/ppermute | solution.py:55
  144.8 1.3 collective-permute-start.34
  146.2 1.9 %collective-permute-start.37 = (bf16[24,2176]{1,0:T(8,128)(2,1)S(1)}, bf16[24,2176]{1,0:T(8,128)(2,1)S(1)}, u32[]{:S(2)}, u32[]{:S(2)}) collective-permute-start(bf16[24,2176]{1,0:T(8,128)(2,1)S(1)} %get-tuple-element.301), channel_id=1, source_target_pairs={{0,16},{1,17},{2,18},{3,19},{4,20},{5,21},{6,22},{7,23},{8,24},{9,... | collective-permute-start | bytes 313352 | tf_op jit(solution)/shard_map/ppermute | solution.py:55
  148.2 4.5 %collective-permute-done.34.came_ref = bf16[128,768]{1,0:T(8,128)(2,1)S(1)} collective-permute-done((bf16[128,768]{1,0:T(8,128)(2,1)S(1)}, bf16[128,768]{1,0:T(8,128)(2,1)S(1)}, u32[]{:S(2)}, u32[]{:S(2)}) %collective-permute-start.34) | collective-permute-done | bytes 196640 | tf_op jit(solution)/shard_map/ppermute | solution.py:55
  152.8 2.2 %shard_map.303 = f32[128,768]{1,0:T(8,128)} custom-call(bf16[128,768]{1,0:T(8,128)(2,1)S(1)} %bitcast.15, f32[768]{0:T(1024)S(1)} %copy-done.11, f32[128,768]{1,0:T(8,128)S(1)} %copy-done.30, bf16[576,1536]{1,0:T(8,128)(2,1)S(1)} %copy-done.16, bf16[128,1536]{1,0:T(8,128)(2,1)S(1)} %copy-done.28, bf16[128,1536]{1,0:T(8,128)(2,1)S(1)} %collective-permute-done.29.came_ref, ...), custom_call_target="tpu_custom_call" | custom-call | flops 3300000000 | tf_op jit(solution)/shard_map/pallas_call | solution.py:115
  155.0 1.4 collective-permute-done.37
  156.5 1.8 %multiply_reduce_fusion = (f32[24]{0:T(128)S(1)}, f32[24,2048]{1,0:T(8,128)}, f32[24]{0:T(128)S(1)}, f32[24,2048]{1,0:T(8,128)}) fusion(bf16[768,2048]{1,0:T(8,128)(2,1)} %refs_14_.1, s32[]{:T(128)S(6)} %select_n.2, f32[24,2176]{1,0:T(8,128)S(1)} %convert_add_fusion.2, f32[24,2816]{1,0:T(8,128)S(1)} %convert_add_fusion, bf16[768,2048]{1,0:T(8,128)(2,1)} %refs_13_.1), kind=kLoop, calls=%fused_computation.14 | loop fusion | flops 294864 | bytes 983236 | tf_op jit(solution)/shard_map/reduce_sum | solution.py:1054
  158.3 1.4 multiply_reduce_fusion.5
  159.7 2.5 %collective-permute-start.39 = (bf16[64,768]{1,0:T(8,128)(2,1)S(1)}, bf16[64,768]{1,0:T(8,128)(2,1)S(1)}, u32[]{:S(2)}, u32[]{:S(2)}) collective-permute-start(bf16[64,768]{1,0:T(8,128)(2,1)S(1)} %get-tuple-element.275), channel_id=1, source_target_pairs={{0,16},{1,17},{2,18},{3,19},{4,20},{5,21},{6,22},{7,23},{8,24},{9,... | collective-permute-start | bytes 294920 | tf_op jit(solution)/shard_map/ppermute | solution.py:55
  162.2 0.6 convert_bitcast_fusion
  162.8 0.8 multiply_reduce_fusion.3
  163.6 0.6 dynamic-slice_divide_fusion
  164.2 0.6 dynamic-slice_divide_fusion.1
  164.8 0.6 slice.210
  165.4 0.7 convert_add_fusion.3
  (132 shorter events, 6.1 us)
Async XLA Ops:
  0.6 11.6 %collective-permute-start.1 = (bf16[128,768]{1,0:T(8,128)(2,1)}, bf16[128,768]{1,0:T(8,128)(2,1)S(1)}, u32[]{:S(2)}, u32[]{:S(2)}) collective-permute-start(bf16[128,768]{1,0:T(8,128)(2,1)} %bitcast.12), channel_id=1, source_target_pairs={{0,2},{1,3},{2,0},{3,1},{4,6},{5,7},{6,4},{7,5},{8,10},{9,11},{10,... | collective-permute-start | bytes 589832 | tf_op jit(solution)/shard_map/ppermute | solution.py:55
  3.7 9.2 %collective-permute-start = (bf16[128,768]{1,0:T(8,128)(2,1)}, bf16[128,768]{1,0:T(8,128)(2,1)S(1)}, u32[]{:S(2)}, u32[]{:S(2)}) collective-permute-start(bf16[128,768]{1,0:T(8,128)(2,1)} %bitcast.13), channel_id=1, source_target_pairs={{0,1},{1,0},{2,3},{3,2},{4,5},{5,4},{6,7},{7,6},{8,9},{9,8},{10,11... | collective-permute-start | bytes 589832 | tf_op jit(solution)/shard_map/ppermute | solution.py:55
  7.2 6.7 %copy-start.2 = (bf16[768,2048]{1,0:T(8,128)(2,1)S(1)}, bf16[768,2048]{1,0:T(8,128)(2,1)}, u32[]{:S(2)}) copy-start(bf16[768,2048]{1,0:T(8,128)(2,1)} %refs_13_.1) | copy-start | bytes 9437188
  7.2 6.7 %copy-start.3 = (bf16[768,2048]{1,0:T(8,128)(2,1)S(1)}, bf16[768,2048]{1,0:T(8,128)(2,1)}, u32[]{:S(2)}) copy-start(bf16[768,2048]{1,0:T(8,128)(2,1)} %refs_14_.1) | copy-start | bytes 9437188
  7.2 6.7 %copy-start.4 = (bf16[768,768]{1,0:T(8,128)(2,1)S(1)}, bf16[768,768]{1,0:T(8,128)(2,1)}, u32[]{:S(2)}) copy-start(bf16[768,768]{1,0:T(8,128)(2,1)} %wq_ref.5) | copy-start | bytes 3538948
  7.2 6.7 %copy-start.6 = (bf16[768,768]{1,0:T(8,128)(2,1)S(1)}, bf16[768,768]{1,0:T(8,128)(2,1)}, u32[]{:S(2)}) copy-start(bf16[768,768]{1,0:T(8,128)(2,1)} %wk_ref.5) | copy-start | bytes 3538948
  7.2 6.7 %copy-start.8 = (bf16[768,768]{1,0:T(8,128)(2,1)S(1)}, bf16[768,768]{1,0:T(8,128)(2,1)}, u32[]{:S(2)}) copy-start(bf16[768,768]{1,0:T(8,128)(2,1)} %wv_ref.5) | copy-start | bytes 3538948
  7.3 6.7 %copy-start.10 = (bf16[768,128]{1,0:T(8,128)(2,1)S(1)}, bf16[768,128]{1,0:T(8,128)(2,1)}, u32[]{:S(2)}) copy-start(bf16[768,128]{1,0:T(8,128)(2,1)} %refs_11_.1) | copy-start | bytes 589828
  7.3 6.7 %copy-start.11 = (f32[768]{0:T(1024)S(1)}, f32[768]{0:T(1024)}, u32[]{:S(2)}) copy-start(f32[768]{0:T(1024)} %gain_ref.3) | copy-start | bytes 9220
  7.3 6.7 %copy-start.12 = (f32[768]{0:T(1024)S(1)}, f32[768]{0:T(1024)}, u32[]{:S(2)}) copy-start(f32[768]{0:T(1024)} %refs_10_.1) | copy-start | bytes 9220
  7.3 6.7 %copy-start.13 = (f32[768]{0:T(1024)S(1)}, f32[768]{0:T(1024)}, u32[]{:S(2)}) copy-start(f32[768]{0:T(1024)} %refs_9_.1) | copy-start | bytes 9220
  7.3 6.7 %copy-start.14 = (bf16[2048,768]{1,0:T(8,128)(2,1)S(1)}, bf16[2048,768]{1,0:T(8,128)(2,1)}, u32[]{:S(2)}) copy-start(bf16[2048,768]{1,0:T(8,128)(2,1)} %refs_12_.1) | copy-start | bytes 9437188
  7.3 6.7 %copy-start.17 = (bf16[768,768]{1,0:T(8,128)(2,1)S(1)}, bf16[768,768]{1,0:T(8,128)(2,1)}, u32[]{:S(2)}) copy-start(bf16[768,768]{1,0:T(8,128)(2,1)} %refs_15_.1) | copy-start | bytes 3538948
  7.3 6.7 %copy-start.18 = (bf16[16,32,768]{2,1,0:T(8,128)(2,1)S(1)}, bf16[16,32,768]{2,1,0:T(8,128)(2,1)}, u32[]{:S(2)}) copy-start(bf16[16,32,768]{2,1,0:T(8,128)(2,1)} %tokens_any.1) | copy-start | bytes 2359300
  7.3 6.7 %copy-start.23 = (bf16[1,128,768]{2,1,0:T(8,128)(2,1)S(1)}, bf16[1,128,768]{2,1,0:T(8,128)(2,1)}, u32[]{:S(2)}) copy-start(bf16[1,128,768]{2,1,0:T(8,128)(2,1)} %param.17) | copy-start | bytes 589828
  7.4 6.7 %copy-start.25 = (s32[16]{0:T(128)S(1)}, s32[16]{0:T(128)}, u32[]{:S(2)}) copy-start(s32[16]{0:T(128)} %lengths_ref.3) | copy-start | bytes 196
  12.3 1.6 collective-permute-start.2
  27.1 4.5 %collective-permute-start.3 = (bf16[1,128,128]{2,1,0:T(8,128)(2,1)S(1)}, bf16[1,128,128]{2,1,0:T(8,128)(2,1)S(1)}, u32[]{:S(2)}, u32[]{:S(2)}) collective-permute-start(bf16[1,128,128]{2,1,0:T(8,128)(2,1)S(1)} %bitcast.8), channel_id=1, source_target_pairs={{0,8},{1,9},{2,10},{3,11},{4,12},{5,13},{6,14},{7,15},{8,0},{9,1},... | collective-permute-start | bytes 98312 | tf_op jit(solution)/shard_map/ppermute | solution.py:55
  28.8 5.4 %collective-permute-start.4 = (bf16[1,128,128]{2,1,0:T(8,128)(2,1)S(1)}, bf16[1,128,128]{2,1,0:T(8,128)(2,1)S(1)}, u32[]{:S(2)}, u32[]{:S(2)}) collective-permute-start(bf16[1,128,128]{2,1,0:T(8,128)(2,1)S(1)} %bitcast.9), channel_id=1, source_target_pairs={{0,16},{1,17},{2,18},{3,19},{4,20},{5,21},{6,22},{7,23},{8,24},{9,... | collective-permute-start | bytes 98312 | tf_op jit(solution)/shard_map/ppermute | solution.py:55
  31.4 5.7 %collective-permute-start.5 = (bf16[1,128,128]{2,1,0:T(8,128)(2,1)S(1)}, bf16[1,128,128]{2,1,0:T(8,128)(2,1)S(1)}, u32[]{:S(2)}, u32[]{:S(2)}) collective-permute-start(bf16[1,128,128]{2,1,0:T(8,128)(2,1)S(1)} %bitcast.10), channel_id=1, source_target_pairs={{0,24},{1,25},{2,26},{3,27},{4,28},{5,29},{6,30},{7,31},{8,16},{9,... | collective-permute-start | bytes 98312 | tf_op jit(solution)/shard_map/ppermute | solution.py:55
  37.1 8.4 %collective-permute-start.6 = (bf16[4,128,128]{2,1,0:T(8,128)(2,1)S(1)}, bf16[4,128,128]{2,1,0:T(8,128)(2,1)S(1)}, u32[]{:S(2)}, u32[]{:S(2)}) collective-permute-start(bf16[4,128,128]{2,1,0:T(8,128)(2,1)S(1)} %pad_maximum_fusion.1), channel_id=1, source_target_pairs={{0,2},{1,3},{2,0},{3,1},{4,6},{5,7},{6,4},{7,5},{8,10},{9,11},{10,... | collective-permute-start | bytes 393224 | tf_op jit(solution)/shard_map/ppermute | solution.py:55
  37.7 7.9 %collective-permute-start.7 = (bf16[4,128,128]{2,1,0:T(8,128)(2,1)S(1)}, bf16[4,128,128]{2,1,0:T(8,128)(2,1)S(1)}, u32[]{:S(2)}, u32[]{:S(2)}) collective-permute-start(bf16[4,128,128]{2,1,0:T(8,128)(2,1)S(1)} %pad_maximum_fusion.1), channel_id=1, source_target_pairs={{0,4},{1,5},{2,6},{3,7},{4,0},{5,1},{6,2},{7,3},{8,12},{9,13},{10,... | collective-permute-start | bytes 393224 | tf_op jit(solution)/shard_map/ppermute | solution.py:55
  39.2 6.4 %collective-permute-start.8 = (bf16[4,128,128]{2,1,0:T(8,128)(2,1)S(1)}, bf16[4,128,128]{2,1,0:T(8,128)(2,1)S(1)}, u32[]{:S(2)}, u32[]{:S(2)}) collective-permute-start(bf16[4,128,128]{2,1,0:T(8,128)(2,1)S(1)} %pad_maximum_fusion.1), channel_id=1, source_target_pairs={{0,6},{1,7},{2,4},{3,5},{4,2},{5,3},{6,0},{7,1},{8,14},{9,15},{10,... | collective-permute-start | bytes 393224 | tf_op jit(solution)/shard_map/ppermute | solution.py:55
  40.7 7.0 %copy-start.26 = (s32[16]{0:T(128)S(1)}, s32[16]{0:T(128)}, u32[]{:S(2)}) copy-start(s32[16]{0:T(128)} %positives_ref.1) | copy-start | bytes 196
  45.7 2.0 %collective-permute-start.9 = (bf16[16,128,128]{2,1,0:T(8,128)(2,1)S(1)}, bf16[16,128,128]{2,1,0:T(8,128)(2,1)S(1)}, u32[]{:S(2)}, u32[]{:S(2)}) collective-permute-start(bf16[16,128,128]{2,1,0:T(8,128)(2,1)S(1)} %constant_dynamic-update-slice_fusion.near_ref), channel_id=1, source_target_pairs={{0,1},{1,0},{2,3},{3,2},{4,5},{5,4},{6,7},{7,6},{8,9},{9,8},{10,11... | collective-permute-start | bytes 1572872 | tf_op jit(solution)/shard_map/ppermute | solution.py:55
  50.9 2.0 %collective-permute-start.10 = (bf16[16,128,128]{2,1,0:T(8,128)(2,1)S(1)}, bf16[16,128,128]{2,1,0:T(8,128)(2,1)S(1)}, u32[]{:S(2)}, u32[]{:S(2)}) collective-permute-start(bf16[16,128,128]{2,1,0:T(8,128)(2,1)S(1)} %get-tuple-element.171), channel_id=1, source_target_pairs={{0,1},{1,0},{2,3},{3,2},{4,5},{5,4},{6,7},{7,6},{8,9},{9,8},{10,11... | collective-permute-start | bytes 1572872 | tf_op jit(solution)/shard_map/ppermute | solution.py:55
  53.0 8.2 %collective-permute-start.11 = (bf16[4,128,128]{2,1,0:T(8,128)(2,1)S(1)}, bf16[4,128,128]{2,1,0:T(8,128)(2,1)S(1)}, u32[]{:S(2)}, u32[]{:S(2)}) collective-permute-start(bf16[4,128,128]{2,1,0:T(8,128)(2,1)S(1)} %get-tuple-element.291), channel_id=1, source_target_pairs={{0,4},{1,5},{2,6},{3,7},{4,0},{5,1},{6,2},{7,3},{8,12},{9,13},{10,... | collective-permute-start | bytes 393224 | tf_op jit(solution)/shard_map/ppermute | solution.py:55
  54.6 8.1 %collective-permute-start.12 = (bf16[4,128,128]{2,1,0:T(8,128)(2,1)S(1)}, bf16[4,128,128]{2,1,0:T(8,128)(2,1)S(1)}, u32[]{:S(2)}, u32[]{:S(2)}) collective-permute-start(bf16[4,128,128]{2,1,0:T(8,128)(2,1)S(1)} %get-tuple-element.290), channel_id=1, source_target_pairs={{0,2},{1,3},{2,0},{3,1},{4,6},{5,7},{6,4},{7,5},{8,10},{9,11},{10,... | collective-permute-start | bytes 393224 | tf_op jit(solution)/shard_map/ppermute | solution.py:55
  55.1 7.6 %collective-permute-start.13 = (bf16[4,128,128]{2,1,0:T(8,128)(2,1)S(1)}, bf16[4,128,128]{2,1,0:T(8,128)(2,1)S(1)}, u32[]{:S(2)}, u32[]{:S(2)}) collective-permute-start(bf16[4,128,128]{2,1,0:T(8,128)(2,1)S(1)} %get-tuple-element.289), channel_id=1, source_target_pairs={{0,6},{1,7},{2,4},{3,5},{4,2},{5,3},{6,0},{7,1},{8,14},{9,15},{10,... | collective-permute-start | bytes 393224 | tf_op jit(solution)/shard_map/ppermute | solution.py:55
  62.7 8.0 %collective-permute-start.18 = (bf16[256,2944]{1,0:T(8,128)(2,1)S(1)}, bf16[256,2944]{1,0:T(8,128)(2,1)S(1)}, u32[]{:S(2)}, u32[]{:S(2)}) collective-permute-start(bf16[256,2944]{1,0:T(8,128)(2,1)S(1)} %get-tuple-element.196), channel_id=1, source_target_pairs={{0,1},{1,0},{2,3},{3,2},{4,5},{5,4},{6,7},{7,6},{8,9},{9,8},{10,11... | collective-permute-start | bytes 4521992 | tf_op jit(solution)/shard_map/ppermute | solution.py:55
  62.8 7.9 %collective-permute-start.17 = (bf16[128,5760]{1,0:T(8,128)(2,1)S(1)}, bf16[128,5760]{1,0:T(8,128)(2,1)S(1)}, u32[]{:S(2)}, u32[]{:S(2)}) collective-permute-start(bf16[128,5760]{1,0:T(8,128)(2,1)S(1)} %get-tuple-element.231.slot_any), channel_id=1, source_target_pairs={{0,1},{1,0},{2,3},{3,2},{4,5},{5,4},{6,7},{7,6},{8,9},{9,8},{10,11... | collective-permute-start | bytes 4423688 | tf_op jit(solution)/shard_map/ppermute | solution.py:55
  63.3 7.4 %collective-permute-start.14 = (bf16[1,128,128]{2,1,0:T(8,128)(2,1)S(1)}, bf16[1,128,128]{2,1,0:T(8,128)(2,1)S(1)}, u32[]{:S(2)}, u32[]{:S(2)}) collective-permute-start(bf16[1,128,128]{2,1,0:T(8,128)(2,1)S(1)} %get-tuple-element.297), channel_id=1, source_target_pairs={{0,16},{1,17},{2,18},{3,19},{4,20},{5,21},{6,22},{7,23},{8,24},{9,... | collective-permute-start | bytes 98312 | tf_op jit(solution)/shard_map/ppermute | solution.py:55
  63.3 7.4 %collective-permute-start.15 = (bf16[1,128,128]{2,1,0:T(8,128)(2,1)S(1)}, bf16[1,128,128]{2,1,0:T(8,128)(2,1)S(1)}, u32[]{:S(2)}, u32[]{:S(2)}) collective-permute-start(bf16[1,128,128]{2,1,0:T(8,128)(2,1)S(1)} %get-tuple-element.296), channel_id=1, source_target_pairs={{0,8},{1,9},{2,10},{3,11},{4,12},{5,13},{6,14},{7,15},{8,0},{9,1},... | collective-permute-start | bytes 98312 | tf_op jit(solution)/shard_map/ppermute | solution.py:55
  64.2 6.5 %collective-permute-start.16 = (bf16[1,128,128]{2,1,0:T(8,128)(2,1)S(1)}, bf16[1,128,128]{2,1,0:T(8,128)(2,1)S(1)}, u32[]{:S(2)}, u32[]{:S(2)}) collective-permute-start(bf16[1,128,128]{2,1,0:T(8,128)(2,1)S(1)} %get-tuple-element.295), channel_id=1, source_target_pairs={{0,24},{1,25},{2,26},{3,27},{4,28},{5,29},{6,30},{7,31},{8,16},{9,... | collective-permute-start | bytes 98312 | tf_op jit(solution)/shard_map/ppermute | solution.py:55
  75.3 6.3 %collective-permute-start.21 = (bf16[128,5760]{1,0:T(8,128)(2,1)S(1)}, bf16[128,5760]{1,0:T(8,128)(2,1)S(1)}, u32[]{:S(2)}, u32[]{:S(2)}) collective-permute-start(bf16[128,5760]{1,0:T(8,128)(2,1)S(1)} %get-tuple-element.233.doc_any), channel_id=1, source_target_pairs={{0,1},{1,0},{2,3},{3,2},{4,5},{5,4},{6,7},{7,6},{8,9},{9,8},{10,11... | collective-permute-start | bytes 4423688 | tf_op jit(solution)/shard_map/ppermute | solution.py:55
  80.5 4.7 %collective-permute-start.20 = (bf16[576,1536]{1,0:T(8,128)(2,1)S(1)}, bf16[576,1536]{1,0:T(8,128)(2,1)S(1)}, u32[]{:S(2)}, u32[]{:S(2)}) collective-permute-start(bf16[576,1536]{1,0:T(8,128)(2,1)S(1)} %get-tuple-element.203.grads_ref), channel_id=1, source_target_pairs={{0,1},{1,0},{2,3},{3,2},{4,5},{5,4},{6,7},{7,6},{8,9},{9,8},{10,11... | collective-permute-start | bytes 5308424 | tf_op jit(solution)/shard_map/ppermute | solution.py:55
  81.1 4.2 %collective-permute-start.19 = (bf16[128,2304]{1,0:T(8,128)(2,1)S(1)}, bf16[128,2304]{1,0:T(8,128)(2,1)S(1)}, u32[]{:S(2)}, u32[]{:S(2)}) collective-permute-start(bf16[128,2304]{1,0:T(8,128)(2,1)S(1)} %get-tuple-element.236.slot_any.grads_ref), channel_id=1, source_target_pairs={{0,1},{1,0},{2,3},{3,2},{4,5},{5,4},{6,7},{7,6},{8,9},{9,8},{10,11... | collective-permute-start | bytes 1769480 | tf_op jit(solution)/shard_map/ppermute | solution.py:55
  81.2 4.1 %collective-permute-start.22 = (bf16[16,128]{1,0:T(8,128)(2,1)S(1)}, bf16[16,128]{1,0:T(8,128)(2,1)S(1)}, u32[]{:S(2)}, u32[]{:S(2)}) collective-permute-start(bf16[16,128]{1,0:T(8,128)(2,1)S(1)} %get-tuple-element.216.table_ref), channel_id=1, source_target_pairs={{0,1},{1,0},{2,3},{3,2},{4,5},{5,4},{6,7},{7,6},{8,9},{9,8},{10,11... | collective-permute-start | bytes 12296 | tf_op jit(solution)/shard_map/ppermute | solution.py:55
  84.3 25.9 %collective-permute-start.24 = (bf16[192,2816]{1,0:T(8,128)(2,1)S(1)}, bf16[192,2816]{1,0:T(8,128)(2,1)S(1)}, u32[]{:S(2)}, u32[]{:S(2)}) collective-permute-start(bf16[192,2816]{1,0:T(8,128)(2,1)S(1)} %get-tuple-element.221), channel_id=1, source_target_pairs={{0,4},{1,5},{2,6},{3,7},{4,0},{5,1},{6,2},{7,3},{8,12},{9,13},{10,... | collective-permute-start | bytes 3244040 | tf_op jit(solution)/shard_map/ppermute | solution.py:55
  88.6 23.6 %collective-permute-start.23 = (bf16[208,2304]{1,0:T(8,128)(2,1)S(1)}, bf16[208,2304]{1,0:T(8,128)(2,1)S(1)}, u32[]{:S(2)}, u32[]{:S(2)}) collective-permute-start(bf16[208,2304]{1,0:T(8,128)(2,1)S(1)} %get-tuple-element.220), channel_id=1, source_target_pairs={{0,2},{1,3},{2,0},{3,1},{4,6},{5,7},{6,4},{7,5},{8,10},{9,11},{10,... | collective-permute-start | bytes 2875400 | tf_op jit(solution)/shard_map/ppermute | solution.py:55
  92.0 21.2 %collective-permute-start.28 = (bf16[192,2176]{1,0:T(8,128)(2,1)S(1)}, bf16[192,2176]{1,0:T(8,128)(2,1)S(1)}, u32[]{:S(2)}, u32[]{:S(2)}) collective-permute-start(bf16[192,2176]{1,0:T(8,128)(2,1)S(1)} %get-tuple-element.244), channel_id=1, source_target_pairs={{0,8},{1,9},{2,10},{3,11},{4,12},{5,13},{6,14},{7,15},{8,0},{9,1},... | collective-permute-start | bytes 2506760 | tf_op jit(solution)/shard_map/ppermute | solution.py:55
  110.4 15.3 %collective-permute-start.27 = (bf16[96,2816]{1,0:T(8,128)(2,1)S(1)}, bf16[96,2816]{1,0:T(8,128)(2,1)S(1)}, u32[]{:S(2)}, u32[]{:S(2)}) collective-permute-start(bf16[96,2816]{1,0:T(8,128)(2,1)S(1)} %get-tuple-element.243), channel_id=1, source_target_pairs={{0,2},{1,3},{2,0},{3,1},{4,6},{5,7},{6,4},{7,5},{8,10},{9,11},{10,... | collective-permute-start | bytes 1622024 | tf_op jit(solution)/shard_map/ppermute | solution.py:55
  111.0 18.6 %collective-permute-start.26 = (bf16[512,768]{1,0:T(8,128)(2,1)}, bf16[512,768]{1,0:T(8,128)(2,1)S(1)}, u32[]{:S(2)}, u32[]{:S(2)}) collective-permute-start(bf16[512,768]{1,0:T(8,128)(2,1)} %get-tuple-element.242), channel_id=1, source_target_pairs={{0,4},{1,5},{2,6},{3,7},{4,0},{5,1},{6,2},{7,3},{8,12},{9,13},{10,... | collective-permute-start | bytes 2359304 | tf_op jit(solution)/shard_map/ppermute | solution.py:55
  113.2 18.2 %collective-permute-start.25 = (bf16[112,2304]{1,0:T(8,128)(2,1)}, bf16[112,2304]{1,0:T(8,128)(2,1)S(1)}, u32[]{:S(2)}, u32[]{:S(2)}) collective-permute-start(bf16[112,2304]{1,0:T(8,128)(2,1)} %get-tuple-element.241), channel_id=1, source_target_pairs={{0,8},{1,9},{2,10},{3,11},{4,12},{5,13},{6,14},{7,15},{8,0},{9,1},... | collective-permute-start | bytes 1548296 | tf_op jit(solution)/shard_map/ppermute | solution.py:55
  114.1 20.6 %collective-permute-start.33 = (bf16[96,2176]{1,0:T(8,128)(2,1)}, bf16[96,2176]{1,0:T(8,128)(2,1)S(1)}, u32[]{:S(2)}, u32[]{:S(2)}) collective-permute-start(bf16[96,2176]{1,0:T(8,128)(2,1)} %get-tuple-element.258), channel_id=1, source_target_pairs={{0,2},{1,3},{2,0},{3,1},{4,6},{5,7},{6,4},{7,5},{8,10},{9,11},{10,... | collective-permute-start | bytes 1253384 | tf_op jit(solution)/shard_map/ppermute | solution.py:55
  127.2 9.7 %collective-permute-start.32 = (bf16[48,2816]{1,0:T(8,128)(2,1)}, bf16[48,2816]{1,0:T(8,128)(2,1)}, u32[]{:S(2)}, u32[]{:S(2)}) collective-permute-start(bf16[48,2816]{1,0:T(8,128)(2,1)} %get-tuple-element.257), channel_id=1, source_target_pairs={{0,8},{1,9},{2,10},{3,11},{4,12},{5,13},{6,14},{7,15},{8,0},{9,1},... | collective-permute-start | bytes 811016 | tf_op jit(solution)/shard_map/ppermute | solution.py:55
  129.6 7.2 %copy-start.21 = (bf16[128,1536]{1,0:T(8,128)(2,1)S(1)}, bf16[128,1536]{1,0:T(8,128)(2,1)}, u32[]{:S(2)}) copy-start(bf16[128,1536]{1,0:T(8,128)(2,1)} %copy-done.20) | copy-start | bytes 1179652
  129.6 7.2 %copy-start.1 = (bf16[48,2816]{1,0:T(8,128)(2,1)S(1)}, bf16[48,2816]{1,0:T(8,128)(2,1)}, u32[]{:S(2)}) copy-start(bf16[48,2816]{1,0:T(8,128)(2,1)} %copy-done) | copy-start | bytes 811012
  129.6 23.1 %copy-start.28 = (bf16[128,1536]{1,0:T(8,128)(2,1)S(1)}, bf16[128,1536]{1,0:T(8,128)(2,1)}, u32[]{:S(2)}) copy-start(bf16[128,1536]{1,0:T(8,128)(2,1)} %copy-done.27) | copy-start | bytes 1179652
  129.6 23.1 %copy-start.30 = (f32[128,768]{1,0:T(8,128)S(1)}, f32[128,768]{1,0:T(8,128)}, u32[]{:S(2)}) copy-start(f32[128,768]{1,0:T(8,128)} %copy-done.29) | copy-start | bytes 1179652
  129.8 13.3 %collective-permute-start.30 = (bf16[256,768]{1,0:T(8,128)(2,1)S(1)}, bf16[256,768]{1,0:T(8,128)(2,1)S(1)}, u32[]{:S(2)}, u32[]{:S(2)}) collective-permute-start(bf16[256,768]{1,0:T(8,128)(2,1)S(1)} %get-tuple-element.255), channel_id=1, source_target_pairs={{0,2},{1,3},{2,0},{3,1},{4,6},{5,7},{6,4},{7,5},{8,10},{9,11},{10,... | collective-permute-start | bytes 1179656 | tf_op jit(solution)/shard_map/ppermute | solution.py:55
  131.4 21.3 %copy-start.16 = (bf16[576,1536]{1,0:T(8,128)(2,1)S(1)}, bf16[576,1536]{1,0:T(8,128)(2,1)}, u32[]{:S(2)}) copy-start(bf16[576,1536]{1,0:T(8,128)(2,1)} %copy-done.15) | copy-start | bytes 5308420
  134.8 7.9 %collective-permute-start.31 = (bf16[64,2304]{1,0:T(8,128)(2,1)S(1)}, bf16[64,2304]{1,0:T(8,128)(2,1)S(1)}, u32[]{:S(2)}, u32[]{:S(2)}) collective-permute-start(bf16[64,2304]{1,0:T(8,128)(2,1)S(1)} %get-tuple-element.256), channel_id=1, source_target_pairs={{0,4},{1,5},{2,6},{3,7},{4,0},{5,1},{6,2},{7,3},{8,12},{9,13},{10,... | collective-permute-start | bytes 884744 | tf_op jit(solution)/shard_map/ppermute | solution.py:55
  135.1 9.7 %collective-permute-start.35 = (bf16[48,2176]{1,0:T(8,128)(2,1)S(1)}, bf16[48,2176]{1,0:T(8,128)(2,1)S(1)}, u32[]{:S(2)}, u32[]{:S(2)}) collective-permute-start(bf16[48,2176]{1,0:T(8,128)(2,1)S(1)} %get-tuple-element.266), channel_id=1, source_target_pairs={{0,4},{1,5},{2,6},{3,7},{4,0},{5,1},{6,2},{7,3},{8,12},{9,13},{10,... | collective-permute-start | bytes 626696 | tf_op jit(solution)/shard_map/ppermute | solution.py:55
  136.9 15.8 %collective-permute-start.29 = (bf16[128,1536]{1,0:T(8,128)(2,1)S(1)}, bf16[128,1536]{1,0:T(8,128)(2,1)S(1)}, u32[]{:S(2)}, u32[]{:S(2)}) collective-permute-start(bf16[128,1536]{1,0:T(8,128)(2,1)S(1)} %copy-done.21), channel_id=1, source_target_pairs={{0,2},{1,3},{2,0},{3,1},{4,6},{5,7},{6,4},{7,5},{8,10},{9,11},{10,... | collective-permute-start | bytes 1179656 | tf_op jit(solution)/shard_map/ppermute | solution.py:55
  136.9 15.9 %copy-start.9 = (bf16[768,768]{1,0:T(8,128)(2,1)S(1)}, bf16[768,768]{1,0:T(8,128)(2,1)}, u32[]{:S(2)}) copy-start(bf16[768,768]{1,0:T(8,128)(2,1)} %wv_ref.5) | copy-start | bytes 3538948
  138.0 16.9 %collective-permute-start.38 = (bf16[24,2816]{1,0:T(8,128)(2,1)S(1)}, bf16[24,2816]{1,0:T(8,128)(2,1)S(1)}, u32[]{:S(2)}, u32[]{:S(2)}) collective-permute-start(bf16[24,2816]{1,0:T(8,128)(2,1)S(1)} %get-tuple-element.293), channel_id=1, source_target_pairs={{0,16},{1,17},{2,18},{3,19},{4,20},{5,21},{6,22},{7,23},{8,24},{9,... | collective-permute-start | bytes 405512 | tf_op jit(solution)/shard_map/ppermute | solution.py:55
  142.6 10.1 %copy-start.5 = (bf16[768,768]{1,0:T(8,128)(2,1)S(1)}, bf16[768,768]{1,0:T(8,128)(2,1)}, u32[]{:S(2)}) copy-start(bf16[768,768]{1,0:T(8,128)(2,1)} %wq_ref.5) | copy-start | bytes 3538948
  142.6 10.1 %copy-start.7 = (bf16[768,768]{1,0:T(8,128)(2,1)S(1)}, bf16[768,768]{1,0:T(8,128)(2,1)}, u32[]{:S(2)}) copy-start(bf16[768,768]{1,0:T(8,128)(2,1)} %wk_ref.5) | copy-start | bytes 3538948
  142.6 10.1 %copy-start.24 = (bf16[1,128,768]{2,1,0:T(8,128)(2,1)S(1)}, bf16[1,128,768]{2,1,0:T(8,128)(2,1)}, u32[]{:S(2)}) copy-start(bf16[1,128,768]{2,1,0:T(8,128)(2,1)} %param.17) | copy-start | bytes 589828
  142.7 13.7 %collective-permute-start.36 = (bf16[40,2304]{1,0:T(8,128)(2,1)S(1)}, bf16[40,2304]{1,0:T(8,128)(2,1)S(1)}, u32[]{:S(2)}, u32[]{:S(2)}) collective-permute-start(bf16[40,2304]{1,0:T(8,128)(2,1)S(1)} %pad_maximum_fusion), channel_id=1, source_target_pairs={{0,16},{1,17},{2,18},{3,19},{4,20},{5,21},{6,22},{7,23},{8,24},{9,... | collective-permute-start | bytes 552968 | tf_op jit(solution)/shard_map/ppermute | solution.py:55
  144.8 7.8 %collective-permute-start.34 = (bf16[128,768]{1,0:T(8,128)(2,1)S(1)}, bf16[128,768]{1,0:T(8,128)(2,1)S(1)}, u32[]{:S(2)}, u32[]{:S(2)}) collective-permute-start(bf16[128,768]{1,0:T(8,128)(2,1)S(1)} %get-tuple-element.265), channel_id=1, source_target_pairs={{0,8},{1,9},{2,10},{3,11},{4,12},{5,13},{6,14},{7,15},{8,0},{9,1},... | collective-permute-start | bytes 589832 | tf_op jit(solution)/shard_map/ppermute | solution.py:55
  146.2 10.1 %collective-permute-start.37 = (bf16[24,2176]{1,0:T(8,128)(2,1)S(1)}, bf16[24,2176]{1,0:T(8,128)(2,1)S(1)}, u32[]{:S(2)}, u32[]{:S(2)}) collective-permute-start(bf16[24,2176]{1,0:T(8,128)(2,1)S(1)} %get-tuple-element.301), channel_id=1, source_target_pairs={{0,16},{1,17},{2,18},{3,19},{4,20},{5,21},{6,22},{7,23},{8,24},{9,... | collective-permute-start | bytes 313352 | tf_op jit(solution)/shard_map/ppermute | solution.py:55
  159.7 5.7 %collective-permute-start.39 = (bf16[64,768]{1,0:T(8,128)(2,1)S(1)}, bf16[64,768]{1,0:T(8,128)(2,1)S(1)}, u32[]{:S(2)}, u32[]{:S(2)}) collective-permute-start(bf16[64,768]{1,0:T(8,128)(2,1)S(1)} %get-tuple-element.275), channel_id=1, source_target_pairs={{0,16},{1,17},{2,18},{3,19},{4,20},{5,21},{6,22},{7,23},{8,24},{9,... | collective-permute-start | bytes 294920 | tf_op jit(solution)/shard_map/ppermute | solution.py:55
  (7 other events, 22.4 us)

commit v8 on v7

--- a/solution.py
+++ b/solution.py
@@ -1054,7 +1054,7 @@
         return sum(jnp.sum(own_rows(weight) * grad, 1) for weight, grad in pairs) / own_rows(gain)
 
     streams = {"A": first, "B": second, "C": third, "D": fourth}
-    plan = "JADBACDpBADCBCIABDCfa"
+    plan = "JADBACDpBADCBICABDCfa"
     if bits != 5:
         plan = "J" + "ADBC" + "p" + "ADBC" * (bits - 3) + "I" + "ABfDaC"
     done = third.kept

time: 166 us -> 166 us (level)
  starting transfers between devices: 35.2 us -> 33 us
    ppermute x40, starting transfers between devices: 35.2 us -> 33 us  [swap(): return lax.ppermute(values, ('wide', 'narrow'), pairs)]
  transfers between devices with their start and end apart: 40 -> 40, of which waited for: 16 -> 17; matrix products, arithmetic and copies ran while one was open for 4% -> 4% of each run, Pallas kernels for 27% -> 26%
where the time goes in v8:
time: 166 us
  Pallas kernels  64.9 us (39%)
  waiting for transfers between devices  54.9 us (33%)
  starting transfers between devices  33 us (20%)
  other arithmetic  8.08 us (5%)
  local copies, waits for them, and re-layouts  3.99 us (2%)
    pallas_call x24, Pallas kernels, call(): pl.pallas_call(kernel, out_shape=tuple(outs), in_specs=specs[:len(args)],...  64.9 us
    ppermute x40, waiting for transfers between devices, swap(): return lax.ppermute(values, ('wide', 'narrow'), pairs)  54.9 us
    ppermute x40, starting transfers between devices, swap(): return lax.ppermute(values, ('wide', 'narrow'), pairs)  33 us
    reduce_sum x3, other arithmetic, gain_grad(): jnp.sum(own_rows(weight) * grad, 1)  4.07 us
  transfers between devices with their start and end apart: 40, of which 17 were waited for; matrix products, arithmetic and copies ran while one was open for 4% of the time, Pallas kernels for 26%

profile of v8, /device:TPU:0, one launch (start us, length us, event | category | flops | bytes accessed | tf_op | source)
XLA Modules:
  0.0 166.2 jit_solution(6640962691140116686)
XLA Ops:
  0.6 3.0 %collective-permute-start.1 = (bf16[128,768]{1,0:T(8,128)(2,1)}, bf16[128,768]{1,0:T(8,128)(2,1)S(1)}, u32[]{:S(2)}, u32[]{:S(2)}) collective-permute-start(bf16[128,768]{1,0:T(8,128)(2,1)} %bitcast.12), channel_id=1, source_target_pairs={{0,2},{1,3},{2,0},{3,1},{4,6},{5,7},{6,4},{7,5},{8,10},{9,11},{10,... | collective-permute-start | bytes 589832 | tf_op jit(solution)/shard_map/ppermute | solution.py:55
  3.7 0.8 copy.33.table_ref
  4.5 2.7 %shard_map.280 = (f32[6,256,512]{2,1,0:T(8,128)S(1)}, f32[6,256,128]{2,1,0:T(8,128)S(1)}) custom-call(s32[1]{0:T(128)} %bitcast.rank_ref, f32[32,12]{1,0:T(8,128)S(1)} %copy.33.table_ref), custom_call_target="tpu_custom_call" | custom-call | flops 3300000000 | tf_op jit(solution)/shard_map/pallas_call | solution.py:115
  7.4 4.9 %shard_map.281 = (bf16[32,128,128]{2,1,0:T(8,128)(2,1)S(1)}, f32[128,128]{1,0:T(8,128)S(1)}) custom-call(s32[1]{0:T(128)} %bitcast.rank_ref, s32[16,32,128]{2,1,0:T(8,128)S(1)} %copy-done.22), custom_call_target="tpu_custom_call" | custom-call | flops 5500000256 | tf_op jit(solution)/shard_map/pallas_call | solution.py:115
  12.3 0.6 collective-permute-start.2
  12.8 1.1 collective-permute-done.2.last_ref
  14.0 13.1 %shard_map.282 = (bf16[640,768]{1,0:T(8,128)(2,1)S(1)}, bf16[256,768]{1,0:T(8,128)(2,1)S(1)}, bf16[640,768]{1,0:T(8,128)(2,1)S(1)}, bf16[640,768]{1,0:T(8,128)(2...) custom-call(s32[1]{0:T(128)} %bitcast.rank_ref, ...), custom_call_target="tpu_custom_call" | custom-call | flops 19800000512 | tf_op jit(solution)/shard_map/pallas_call | solution.py:115
  27.1 1.7 collective-permute-start.3
  28.8 2.6 %collective-permute-start.4 = (bf16[1,128,128]{2,1,0:T(8,128)(2,1)S(1)}, bf16[1,128,128]{2,1,0:T(8,128)(2,1)S(1)}, u32[]{:S(2)}, u32[]{:S(2)}) collective-permute-start(bf16[1,128,128]{2,1,0:T(8,128)(2,1)S(1)} %bitcast.9), channel_id=1, source_target_pairs={{0,16},{1,17},{2,18},{3,19},{4,20},{5,21},{6,22},{7,23},{8,24},{9,... | collective-permute-start | bytes 98312 | tf_op jit(solution)/shard_map/ppermute | solution.py:55
  31.6 2.6 %collective-permute-done.4 = bf16[1,128,128]{2,1,0:T(8,128)(2,1)S(1)} collective-permute-done((bf16[1,128,128]{2,1,0:T(8,128)(2,1)S(1)}, bf16[1,128,128]{2,1,0:T(8,128)(2,1)S(1)}, u32[]{:S(2)}, u32[]{:S(2)}) %collective-permute-start.4) | collective-permute-done | bytes 32800 | tf_op jit(solution)/shard_map/ppermute | solution.py:55
  34.2 2.9 %collective-permute-done.5 = bf16[1,128,128]{2,1,0:T(8,128)(2,1)S(1)} collective-permute-done((bf16[1,128,128]{2,1,0:T(8,128)(2,1)S(1)}, bf16[1,128,128]{2,1,0:T(8,128)(2,1)S(1)}, u32[]{:S(2)}, u32[]{:S(2)}) %collective-permute-start.5) | collective-permute-done | bytes 32800 | tf_op jit(solution)/shard_map/ppermute | solution.py:55
  37.7 1.5 collective-permute-start.7
  39.2 1.5 collective-permute-start.8
  40.7 4.8 %shard_map.283 = (bf16[256,2944]{1,0:T(8,128)(2,1)S(1)}, bf16[256,2944]{1,0:T(8,128)(2,1)S(1)}, bf16[512,384]{1,0:T(8,128)(2,1)S(1)}) custom-call(s32[1]{0:T(128)} %bitcast.rank_ref, bf16[640,768]{1,0:T(8,128)(2,1)S(1)} %get-tuple-element.159.all_ref, bf16[256,768]{1,0:T(8,128)(2,1)S(1)} %get-tuple-element.160.normed_feed_ref, ...), custom_call_target="tpu_custom_call" | custom-call | flops 5500000256 | tf_op jit(solution)/shard_map/pallas_call | solution.py:115
  45.7 1.9 %collective-permute-done.9.far_ref = bf16[16,128,128]{2,1,0:T(8,128)(2,1)S(1)} collective-permute-done((bf16[16,128,128]{2,1,0:T(8,128)(2,1)S(1)}, bf16[16,128,128]{2,1,0:T(8,128)(2,1)S(1)}, u32[]{:S(2)}, u32[]{:S(2)}) %collective-permute-start.9) | collective-permute-done | bytes 524320 | tf_op jit(solution)/shard_map/ppermute | solution.py:55
  47.6 3.2 %shard_map.284 = (f32[4,128]{1,0:T(4,128)S(1)}, f32[128,128]{1,0:T(8,128)S(1)}, bf16[16,128,128]{2,1,0:T(8,128)(2,1)S(1)}, bf16[16,128,128]{2,1,0:T(8,128)(2,1)S(1)}) custom-call(s32[1]{0:T(128)} %bitcast.rank_ref, s32[16]{0:T(128)S(1)} %copy-done.25, s32[16]{0:T(128)S(1)} %copy-done.26, bf16[32,128,128]{2,1,0:T(8,128)(2,1)S(1)} %get-tuple-element.148.counts_ref, ...), custom_call_target="tpu_custom_call" | custom-call | flops 3300000000 | tf_op jit(solution)/shard_map/pallas_call | solution.py:115
  51.1 1.8 %collective-permute-done.10 = bf16[16,128,128]{2,1,0:T(8,128)(2,1)S(1)} collective-permute-done((bf16[16,128,128]{2,1,0:T(8,128)(2,1)S(1)}, bf16[16,128,128]{2,1,0:T(8,128)(2,1)S(1)}, u32[]{:S(2)}, u32[]{:S(2)}) %collective-permute-start.10) | collective-permute-done | bytes 524320 | tf_op jit(solution)/shard_map/ppermute | solution.py:55
  53.0 1.6 collective-permute-start.11
  55.1 1.5 collective-permute-start.13
  56.6 4.6 %shard_map.285 = (bf16[128,5760]{1,0:T(8,128)(2,1)S(1)}, f32[128,768]{1,0:T(8,128)S(1)}, bf16[128,768]{1,0:T(8,128)(2,1)S(1)}) custom-call(f32[128,128]{1,0:T(8,128)S(1)} %get-tuple-element.173.grad_unit_ref, f32[256,128]{1,0:T(8,128)S(1)} %get-tuple-element.174.embed_ref.refs_4_, f32[256,768]{1,0:T(8,128)S(1)} %get-tuple-element.175.after_feed_ref.refs_5_, ...), custom_call_target="tpu_custom_call" | custom-call | flops 7699999744 | tf_op jit(solution)/shard_map/pallas_call | solution.py:115
  61.2 1.5 collective-permute-done.12
  63.3 0.9 collective-permute-start.15
  64.2 3.5 %collective-permute-start.16 = (bf16[1,128,128]{2,1,0:T(8,128)(2,1)S(1)}, bf16[1,128,128]{2,1,0:T(8,128)(2,1)S(1)}, u32[]{:S(2)}, u32[]{:S(2)}) collective-permute-start(bf16[1,128,128]{2,1,0:T(8,128)(2,1)S(1)} %get-tuple-element.295), channel_id=1, source_target_pairs={{0,24},{1,25},{2,26},{3,27},{4,28},{5,29},{6,30},{7,31},{8,16},{9,... | collective-permute-start | bytes 98312 | tf_op jit(solution)/shard_map/ppermute | solution.py:55
  67.7 3.0 %shard_map.286 = (bf16[128,2304]{1,0:T(8,128)(2,1)S(1)}, f32[12,128]{1,0:T(8,128)S(1)}) custom-call(bf16[256,768]{1,0:T(8,128)(2,1)S(1)} %get-tuple-element.183.query_ref, bf16[640,768]{1,0:T(8,128)(2,1)S(1)} %get-tuple-element.184.key_ref, bf16[640,768]{1,0:T(8,128)(2,1)S(1)} %get-tuple-element.185.value_ref, ...), custom_call_target="tpu_custom_call" | custom-call | flops 4400000000 | tf_op jit(solution)/shard_map/pallas_call | solution.py:115
  70.8 4.5 %shard_map.287 = (bf16[128,5760]{1,0:T(8,128)(2,1)S(1)}, f32[128,768]{1,0:T(8,128)S(1)}, bf16[128,768]{1,0:T(8,128)(2,1)S(1)}) custom-call(bf16[1,128,128]{2,1,0:T(8,128)(2,1)S(1)} %get-tuple-element.298.refs_0_, bf16[1,128,128]{2,1,0:T(8,128)(2,1)S(1)} %collective-permute-done.14.refs_1_, bf16[1,128,128]{2,1,0:T(8,128)(2,1)S(1)} %collective-permute-done.15.refs_2_, ...), custom_call_target="tpu_custom_call" | custom-call | flops 7699999744 | tf_op jit(solution)/shard_map/pallas_call | solution.py:115
  75.4 5.1 %shard_map.288 = (bf16[576,1536]{1,0:T(8,128)(2,1)S(1)}, bf16[16,128]{1,0:T(8,128)(2,1)S(1)}) custom-call(s32[1]{0:T(128)} %bitcast.rank_ref, bf16[256,768]{1,0:T(8,128)(2,1)S(1)} %get-tuple-element.183.query_ref, bf16[640,768]{1,0:T(8,128)(2,1)S(1)} %get-tuple-element.184.key_ref, bf16[640,768]{1,0:T(8,128)(2,1)S(1)} %get-tuple-element.185.value_ref, ...), custom_call_target="tpu_custom_call" | custom-call | flops 3300000000 | tf_op jit(solution)/shard_map/pallas_call | solution.py:115
  81.6 2.7 %shard_map.289 = (bf16[192,2816]{1,0:T(8,128)(2,1)S(1)}, bf16[192,2816]{1,0:T(8,128)(2,1)S(1)}) custom-call(bf16[256,2944]{1,0:T(8,128)(2,1)S(1)} %get-tuple-element.229.kept_any, bf16[256,2944]{1,0:T(8,128)(2,1)S(1)} %collective-permute-done.18.came_any, bf16[128,5760]{1,0:T(8,128)(2,1)S(1)} %get-tuple-element.231.slot_any, ...), custom_call_target="tpu_custom_call" | custom-call | flops 3300000000 | tf_op jit(solution)/shard_map/pallas_call | solution.py:115
  84.3 0.6 collective-permute-start.24
  85.3 3.4 %shard_map.290 = (bf16[192,2304]{1,0:T(8,128)(2,1)S(1)}, bf16[208,2304]{1,0:T(8,128)(2,1)S(1)}, bf16[128,1536]{1,0:T(8,128)(2,1)S(1)}, bf16[128,1536]{1,0:T(8,128)(2,1)S(1)}) custom-call(bf16[512,384]{1,0:T(8,128)(2,1)S(1)} %get-tuple-element.204.doc_ref, bf16[256,2944]{1,0:T(8,128)(2,1)S(1)} %get-tuple-element.229.kept_any, ...), custom_call_target="tpu_custom_call" | custom-call | flops 3300000000 | tf_op jit(solution)/shard_map/pallas_call | solution.py:115
  88.6 0.9 collective-permute-start.23
  89.5 2.4 %shard_map.291 = (bf16[192,2176]{1,0:T(8,128)(2,1)S(1)}, bf16[192,2176]{1,0:T(8,128)(2,1)S(1)}) custom-call(bf16[256,2944]{1,0:T(8,128)(2,1)S(1)} %get-tuple-element.229.kept_any, bf16[256,2944]{1,0:T(8,128)(2,1)S(1)} %collective-permute-done.18.came_any, bf16[128,5760]{1,0:T(8,128)(2,1)S(1)} %get-tuple-element.231.slot_any, ...), custom_call_target="tpu_custom_call" | custom-call | flops 3300000000 | tf_op jit(solution)/shard_map/pallas_call | solution.py:115
  92.1 2.2 %shard_map.292 = (bf16[512,768]{1,0:T(8,128)(2,1)S(1)}, bf16[512,768]{1,0:T(8,128)(2,1)}) custom-call(bf16[256,2944]{1,0:T(8,128)(2,1)S(1)} %get-tuple-element.229.kept_any, bf16[256,2944]{1,0:T(8,128)(2,1)S(1)} %collective-permute-done.18.came_any, bf16[128,5760]{1,0:T(8,128)(2,1)S(1)} %get-tuple-element.231.slot_any, ...), custom_call_target="tpu_custom_call" | custom-call | flops 3300000000 | tf_op jit(solution)/shard_map/pallas_call | solution.py:115
  94.3 2.7 %shard_map.293 = f32[128,768]{1,0:T(8,128)} custom-call(s32[1]{0:T(128)} %bitcast.rank_ref, bf16[16,32,768]{2,1,0:T(8,128)(2,1)S(1)} %copy-done.19, f32[768]{0:T(1024)S(1)} %copy-done.11, f32[128,768]{1,0:T(8,128)S(1)} %get-tuple-element.179.after_ref, bf16[128,2304]{1,0:T(8,128)(2,1)S(1)} %get-tuple-element.236.slot_any.grads_ref, ...), custom_call_target="tpu_custom_call" | custom-call | flops 3300000000 | tf_op jit(solution)/shard_map/pallas_call | solution.py:115
  96.9 13.2 %collective-permute-done.24.came_ref = bf16[192,2816]{1,0:T(8,128)(2,1)S(1)} collective-permute-done((bf16[192,2816]{1,0:T(8,128)(2,1)S(1)}, bf16[192,2816]{1,0:T(8,128)(2,1)S(1)}, u32[]{:S(2)}, u32[]{:S(2)}) %collective-permute-start.24) | collective-permute-done | bytes 1081376 | tf_op jit(solution)/shard_map/ppermute | solution.py:55
  111.0 1.2 collective-permute-start.26
  112.2 0.9 shard_map.295
  113.2 0.9 shard_map.296
  114.1 0.8 collective-permute-start.30
  114.9 10.8 %collective-permute-done.27.came_ref = bf16[96,2816]{1,0:T(8,128)(2,1)S(1)} collective-permute-done((bf16[96,2816]{1,0:T(8,128)(2,1)S(1)}, bf16[96,2816]{1,0:T(8,128)(2,1)S(1)}, u32[]{:S(2)}, u32[]{:S(2)}) %collective-permute-start.27) | collective-permute-done | bytes 540704 | tf_op jit(solution)/shard_map/ppermute | solution.py:55
  125.7 0.8 shard_map.297
  126.5 0.7 copy-done
  127.2 0.6 slice_reduce_fusion
  127.8 1.8 %collective-permute-done.26.came_ref = bf16[512,768]{1,0:T(8,128)(2,1)S(1)} collective-permute-done((bf16[512,768]{1,0:T(8,128)(2,1)}, bf16[512,768]{1,0:T(8,128)(2,1)S(1)}, u32[]{:S(2)}, u32[]{:S(2)}) %collective-permute-start.26) | collective-permute-done | bytes 786464 | tf_op jit(solution)/shard_map/ppermute | solution.py:55
  129.8 1.6 collective-permute-start.32
  131.5 3.1 %collective-permute-done.30.came_ref = bf16[96,2176]{1,0:T(8,128)(2,1)S(1)} collective-permute-done((bf16[96,2176]{1,0:T(8,128)(2,1)}, bf16[96,2176]{1,0:T(8,128)(2,1)S(1)}, u32[]{:S(2)}, u32[]{:S(2)}) %collective-permute-start.30) | collective-permute-done | bytes 417824 | tf_op jit(solution)/shard_map/ppermute | solution.py:55
  135.1 1.7 %collective-permute-start.31 = (bf16[48,2176]{1,0:T(8,128)(2,1)S(1)}, bf16[48,2176]{1,0:T(8,128)(2,1)S(1)}, u32[]{:S(2)}, u32[]{:S(2)}) collective-permute-start(bf16[48,2176]{1,0:T(8,128)(2,1)S(1)} %get-tuple-element.258), channel_id=1, source_target_pairs={{0,4},{1,5},{2,6},{3,7},{4,0},{5,1},{6,2},{7,3},{8,12},{9,13},{10,... | collective-permute-start | bytes 626696 | tf_op jit(solution)/shard_map/ppermute | solution.py:55
  136.9 1.0 add_convert_fusion
  138.0 4.6 %collective-permute-done.33 = bf16[64,2304]{1,0:T(8,128)(2,1)S(1)} collective-permute-done((bf16[64,2304]{1,0:T(8,128)(2,1)S(1)}, bf16[64,2304]{1,0:T(8,128)(2,1)S(1)}, u32[]{:S(2)}, u32[]{:S(2)}) %collective-permute-start.33) | collective-permute-done | bytes 294944 | tf_op jit(solution)/shard_map/ppermute | solution.py:55
  143.2 1.7 %collective-permute-done.31 = bf16[48,2176]{1,0:T(8,128)(2,1)S(1)} collective-permute-done((bf16[48,2176]{1,0:T(8,128)(2,1)S(1)}, bf16[48,2176]{1,0:T(8,128)(2,1)S(1)}, u32[]{:S(2)}, u32[]{:S(2)}) %collective-permute-start.31) | collective-permute-done | bytes 208928 | tf_op jit(solution)/shard_map/ppermute | solution.py:55
  144.9 1.3 collective-permute-start.38
  146.2 2.0 %collective-permute-start.36 = (bf16[24,2176]{1,0:T(8,128)(2,1)S(1)}, bf16[24,2176]{1,0:T(8,128)(2,1)S(1)}, u32[]{:S(2)}, u32[]{:S(2)}) collective-permute-start(bf16[24,2176]{1,0:T(8,128)(2,1)S(1)} %get-tuple-element.301), channel_id=1, source_target_pairs={{0,16},{1,17},{2,18},{3,19},{4,20},{5,21},{6,22},{7,23},{8,24},{9,... | collective-permute-start | bytes 313352 | tf_op jit(solution)/shard_map/ppermute | solution.py:55
  148.2 1.5 collective-permute-done.29.came_ref
  149.8 1.0 copy-done.30
  150.8 2.2 %shard_map.302 = f32[128,768]{1,0:T(8,128)} custom-call(bf16[128,768]{1,0:T(8,128)(2,1)S(1)} %bitcast.15, f32[768]{0:T(1024)S(1)} %copy-done.11, f32[128,768]{1,0:T(8,128)S(1)} %copy-done.30, bf16[576,1536]{1,0:T(8,128)(2,1)S(1)} %copy-done.16, bf16[128,1536]{1,0:T(8,128)(2,1)S(1)} %copy-done.28, bf16[128,1536]{1,0:T(8,128)(2,1)S(1)} %collective-permute-done.29.came_ref, ...), custom_call_target="tpu_custom_call" | custom-call | flops 3300000000 | tf_op jit(solution)/shard_map/pallas_call | solution.py:115
  153.0 3.3 %collective-permute-done.36 = bf16[24,2176]{1,0:T(8,128)(2,1)S(1)} collective-permute-done((bf16[24,2176]{1,0:T(8,128)(2,1)S(1)}, bf16[24,2176]{1,0:T(8,128)(2,1)S(1)}, u32[]{:S(2)}, u32[]{:S(2)}) %collective-permute-start.36) | collective-permute-done | bytes 104480 | tf_op jit(solution)/shard_map/ppermute | solution.py:55
  156.4 1.8 %multiply_reduce_fusion = (f32[24]{0:T(128)S(1)}, f32[24,2048]{1,0:T(8,128)}, f32[24]{0:T(128)S(1)}, f32[24,2048]{1,0:T(8,128)}) fusion(bf16[768,2048]{1,0:T(8,128)(2,1)} %refs_14_.1, s32[]{:T(128)S(6)} %select_n.2, f32[24,2176]{1,0:T(8,128)S(1)} %convert_add_fusion.2, f32[24,2816]{1,0:T(8,128)S(1)} %convert_add_fusion, bf16[768,2048]{1,0:T(8,128)(2,1)} %refs_13_.1), kind=kLoop, calls=%fused_computation.14 | loop fusion | flops 294864 | bytes 983236 | tf_op jit(solution)/shard_map/reduce_sum | solution.py:1054
  158.3 1.4 multiply_reduce_fusion.5
  159.9 0.6 convert_bitcast_fusion
  160.5 0.8 multiply_reduce_fusion.3
  161.4 0.6 dynamic-slice_divide_fusion
  162.0 0.6 dynamic-slice_divide_fusion.1
  162.6 0.6 slice.210
  163.2 2.3 %collective-permute-done.39 = bf16[64,768]{1,0:T(8,128)(2,1)S(1)} collective-permute-done((bf16[64,768]{1,0:T(8,128)(2,1)S(1)}, bf16[64,768]{1,0:T(8,128)(2,1)S(1)}, u32[]{:S(2)}, u32[]{:S(2)}) %collective-permute-start.39) | collective-permute-done | bytes 98336 | tf_op jit(solution)/shard_map/ppermute | solution.py:55
  165.5 0.7 convert_add_fusion.3
  (132 shorter events, 6.9 us)
Async XLA Ops:
  0.6 11.6 %collective-permute-start.1 = (bf16[128,768]{1,0:T(8,128)(2,1)}, bf16[128,768]{1,0:T(8,128)(2,1)S(1)}, u32[]{:S(2)}, u32[]{:S(2)}) collective-permute-start(bf16[128,768]{1,0:T(8,128)(2,1)} %bitcast.12), channel_id=1, source_target_pairs={{0,2},{1,3},{2,0},{3,1},{4,6},{5,7},{6,4},{7,5},{8,10},{9,11},{10,... | collective-permute-start | bytes 589832 | tf_op jit(solution)/shard_map/ppermute | solution.py:55
  3.7 9.2 %collective-permute-start = (bf16[128,768]{1,0:T(8,128)(2,1)}, bf16[128,768]{1,0:T(8,128)(2,1)S(1)}, u32[]{:S(2)}, u32[]{:S(2)}) collective-permute-start(bf16[128,768]{1,0:T(8,128)(2,1)} %bitcast.13), channel_id=1, source_target_pairs={{0,1},{1,0},{2,3},{3,2},{4,5},{5,4},{6,7},{7,6},{8,9},{9,8},{10,11... | collective-permute-start | bytes 589832 | tf_op jit(solution)/shard_map/ppermute | solution.py:55
  7.2 6.7 %copy-start.2 = (bf16[768,2048]{1,0:T(8,128)(2,1)S(1)}, bf16[768,2048]{1,0:T(8,128)(2,1)}, u32[]{:S(2)}) copy-start(bf16[768,2048]{1,0:T(8,128)(2,1)} %refs_13_.1) | copy-start | bytes 9437188
  7.2 6.7 %copy-start.3 = (bf16[768,2048]{1,0:T(8,128)(2,1)S(1)}, bf16[768,2048]{1,0:T(8,128)(2,1)}, u32[]{:S(2)}) copy-start(bf16[768,2048]{1,0:T(8,128)(2,1)} %refs_14_.1) | copy-start | bytes 9437188
  7.2 6.7 %copy-start.4 = (bf16[768,768]{1,0:T(8,128)(2,1)S(1)}, bf16[768,768]{1,0:T(8,128)(2,1)}, u32[]{:S(2)}) copy-start(bf16[768,768]{1,0:T(8,128)(2,1)} %wq_ref.5) | copy-start | bytes 3538948
  7.2 6.7 %copy-start.6 = (bf16[768,768]{1,0:T(8,128)(2,1)S(1)}, bf16[768,768]{1,0:T(8,128)(2,1)}, u32[]{:S(2)}) copy-start(bf16[768,768]{1,0:T(8,128)(2,1)} %wk_ref.5) | copy-start | bytes 3538948
  7.2 6.7 %copy-start.8 = (bf16[768,768]{1,0:T(8,128)(2,1)S(1)}, bf16[768,768]{1,0:T(8,128)(2,1)}, u32[]{:S(2)}) copy-start(bf16[768,768]{1,0:T(8,128)(2,1)} %wv_ref.5) | copy-start | bytes 3538948
  7.3 6.7 %copy-start.10 = (bf16[768,128]{1,0:T(8,128)(2,1)S(1)}, bf16[768,128]{1,0:T(8,128)(2,1)}, u32[]{:S(2)}) copy-start(bf16[768,128]{1,0:T(8,128)(2,1)} %refs_11_.1) | copy-start | bytes 589828
  7.3 6.7 %copy-start.11 = (f32[768]{0:T(1024)S(1)}, f32[768]{0:T(1024)}, u32[]{:S(2)}) copy-start(f32[768]{0:T(1024)} %gain_ref.3) | copy-start | bytes 9220
  7.3 6.7 %copy-start.12 = (f32[768]{0:T(1024)S(1)}, f32[768]{0:T(1024)}, u32[]{:S(2)}) copy-start(f32[768]{0:T(1024)} %refs_10_.1) | copy-start | bytes 9220
  7.3 6.7 %copy-start.13 = (f32[768]{0:T(1024)S(1)}, f32[768]{0:T(1024)}, u32[]{:S(2)}) copy-start(f32[768]{0:T(1024)} %refs_9_.1) | copy-start | bytes 9220
  7.3 6.7 %copy-start.14 = (bf16[2048,768]{1,0:T(8,128)(2,1)S(1)}, bf16[2048,768]{1,0:T(8,128)(2,1)}, u32[]{:S(2)}) copy-start(bf16[2048,768]{1,0:T(8,128)(2,1)} %refs_12_.1) | copy-start | bytes 9437188
  7.3 6.7 %copy-start.17 = (bf16[768,768]{1,0:T(8,128)(2,1)S(1)}, bf16[768,768]{1,0:T(8,128)(2,1)}, u32[]{:S(2)}) copy-start(bf16[768,768]{1,0:T(8,128)(2,1)} %refs_15_.1) | copy-start | bytes 3538948
  7.3 6.7 %copy-start.18 = (bf16[16,32,768]{2,1,0:T(8,128)(2,1)S(1)}, bf16[16,32,768]{2,1,0:T(8,128)(2,1)}, u32[]{:S(2)}) copy-start(bf16[16,32,768]{2,1,0:T(8,128)(2,1)} %tokens_any.1) | copy-start | bytes 2359300
  7.3 6.7 %copy-start.23 = (bf16[1,128,768]{2,1,0:T(8,128)(2,1)S(1)}, bf16[1,128,768]{2,1,0:T(8,128)(2,1)}, u32[]{:S(2)}) copy-start(bf16[1,128,768]{2,1,0:T(8,128)(2,1)} %param.17) | copy-start | bytes 589828
  7.4 6.7 %copy-start.25 = (s32[16]{0:T(128)S(1)}, s32[16]{0:T(128)}, u32[]{:S(2)}) copy-start(s32[16]{0:T(128)} %lengths_ref.3) | copy-start | bytes 196
  12.3 1.6 collective-permute-start.2
  27.1 4.5 %collective-permute-start.3 = (bf16[1,128,128]{2,1,0:T(8,128)(2,1)S(1)}, bf16[1,128,128]{2,1,0:T(8,128)(2,1)S(1)}, u32[]{:S(2)}, u32[]{:S(2)}) collective-permute-start(bf16[1,128,128]{2,1,0:T(8,128)(2,1)S(1)} %bitcast.8), channel_id=1, source_target_pairs={{0,8},{1,9},{2,10},{3,11},{4,12},{5,13},{6,14},{7,15},{8,0},{9,1},... | collective-permute-start | bytes 98312 | tf_op jit(solution)/shard_map/ppermute | solution.py:55
  28.8 5.4 %collective-permute-start.4 = (bf16[1,128,128]{2,1,0:T(8,128)(2,1)S(1)}, bf16[1,128,128]{2,1,0:T(8,128)(2,1)S(1)}, u32[]{:S(2)}, u32[]{:S(2)}) collective-permute-start(bf16[1,128,128]{2,1,0:T(8,128)(2,1)S(1)} %bitcast.9), channel_id=1, source_target_pairs={{0,16},{1,17},{2,18},{3,19},{4,20},{5,21},{6,22},{7,23},{8,24},{9,... | collective-permute-start | bytes 98312 | tf_op jit(solution)/shard_map/ppermute | solution.py:55
  31.4 5.7 %collective-permute-start.5 = (bf16[1,128,128]{2,1,0:T(8,128)(2,1)S(1)}, bf16[1,128,128]{2,1,0:T(8,128)(2,1)S(1)}, u32[]{:S(2)}, u32[]{:S(2)}) collective-permute-start(bf16[1,128,128]{2,1,0:T(8,128)(2,1)S(1)} %bitcast.10), channel_id=1, source_target_pairs={{0,24},{1,25},{2,26},{3,27},{4,28},{5,29},{6,30},{7,31},{8,16},{9,... | collective-permute-start | bytes 98312 | tf_op jit(solution)/shard_map/ppermute | solution.py:55
  37.1 8.4 %collective-permute-start.6 = (bf16[4,128,128]{2,1,0:T(8,128)(2,1)S(1)}, bf16[4,128,128]{2,1,0:T(8,128)(2,1)S(1)}, u32[]{:S(2)}, u32[]{:S(2)}) collective-permute-start(bf16[4,128,128]{2,1,0:T(8,128)(2,1)S(1)} %pad_maximum_fusion.1), channel_id=1, source_target_pairs={{0,2},{1,3},{2,0},{3,1},{4,6},{5,7},{6,4},{7,5},{8,10},{9,11},{10,... | collective-permute-start | bytes 393224 | tf_op jit(solution)/shard_map/ppermute | solution.py:55
  37.7 7.9 %collective-permute-start.7 = (bf16[4,128,128]{2,1,0:T(8,128)(2,1)S(1)}, bf16[4,128,128]{2,1,0:T(8,128)(2,1)S(1)}, u32[]{:S(2)}, u32[]{:S(2)}) collective-permute-start(bf16[4,128,128]{2,1,0:T(8,128)(2,1)S(1)} %pad_maximum_fusion.1), channel_id=1, source_target_pairs={{0,4},{1,5},{2,6},{3,7},{4,0},{5,1},{6,2},{7,3},{8,12},{9,13},{10,... | collective-permute-start | bytes 393224 | tf_op jit(solution)/shard_map/ppermute | solution.py:55
  39.2 6.4 %collective-permute-start.8 = (bf16[4,128,128]{2,1,0:T(8,128)(2,1)S(1)}, bf16[4,128,128]{2,1,0:T(8,128)(2,1)S(1)}, u32[]{:S(2)}, u32[]{:S(2)}) collective-permute-start(bf16[4,128,128]{2,1,0:T(8,128)(2,1)S(1)} %pad_maximum_fusion.1), channel_id=1, source_target_pairs={{0,6},{1,7},{2,4},{3,5},{4,2},{5,3},{6,0},{7,1},{8,14},{9,15},{10,... | collective-permute-start | bytes 393224 | tf_op jit(solution)/shard_map/ppermute | solution.py:55
  40.7 7.0 %copy-start.26 = (s32[16]{0:T(128)S(1)}, s32[16]{0:T(128)}, u32[]{:S(2)}) copy-start(s32[16]{0:T(128)} %positives_ref.1) | copy-start | bytes 196
  45.7 2.0 %collective-permute-start.9 = (bf16[16,128,128]{2,1,0:T(8,128)(2,1)S(1)}, bf16[16,128,128]{2,1,0:T(8,128)(2,1)S(1)}, u32[]{:S(2)}, u32[]{:S(2)}) collective-permute-start(bf16[16,128,128]{2,1,0:T(8,128)(2,1)S(1)} %constant_dynamic-update-slice_fusion.near_ref), channel_id=1, source_target_pairs={{0,1},{1,0},{2,3},{3,2},{4,5},{5,4},{6,7},{7,6},{8,9},{9,8},{10,11... | collective-permute-start | bytes 1572872 | tf_op jit(solution)/shard_map/ppermute | solution.py:55
  50.9 2.0 %collective-permute-start.10 = (bf16[16,128,128]{2,1,0:T(8,128)(2,1)S(1)}, bf16[16,128,128]{2,1,0:T(8,128)(2,1)S(1)}, u32[]{:S(2)}, u32[]{:S(2)}) collective-permute-start(bf16[16,128,128]{2,1,0:T(8,128)(2,1)S(1)} %get-tuple-element.171), channel_id=1, source_target_pairs={{0,1},{1,0},{2,3},{3,2},{4,5},{5,4},{6,7},{7,6},{8,9},{9,8},{10,11... | collective-permute-start | bytes 1572872 | tf_op jit(solution)/shard_map/ppermute | solution.py:55
  53.0 8.2 %collective-permute-start.11 = (bf16[4,128,128]{2,1,0:T(8,128)(2,1)S(1)}, bf16[4,128,128]{2,1,0:T(8,128)(2,1)S(1)}, u32[]{:S(2)}, u32[]{:S(2)}) collective-permute-start(bf16[4,128,128]{2,1,0:T(8,128)(2,1)S(1)} %get-tuple-element.291), channel_id=1, source_target_pairs={{0,4},{1,5},{2,6},{3,7},{4,0},{5,1},{6,2},{7,3},{8,12},{9,13},{10,... | collective-permute-start | bytes 393224 | tf_op jit(solution)/shard_map/ppermute | solution.py:55
  54.6 8.1 %collective-permute-start.12 = (bf16[4,128,128]{2,1,0:T(8,128)(2,1)S(1)}, bf16[4,128,128]{2,1,0:T(8,128)(2,1)S(1)}, u32[]{:S(2)}, u32[]{:S(2)}) collective-permute-start(bf16[4,128,128]{2,1,0:T(8,128)(2,1)S(1)} %get-tuple-element.290), channel_id=1, source_target_pairs={{0,2},{1,3},{2,0},{3,1},{4,6},{5,7},{6,4},{7,5},{8,10},{9,11},{10,... | collective-permute-start | bytes 393224 | tf_op jit(solution)/shard_map/ppermute | solution.py:55
  55.1 7.6 %collective-permute-start.13 = (bf16[4,128,128]{2,1,0:T(8,128)(2,1)S(1)}, bf16[4,128,128]{2,1,0:T(8,128)(2,1)S(1)}, u32[]{:S(2)}, u32[]{:S(2)}) collective-permute-start(bf16[4,128,128]{2,1,0:T(8,128)(2,1)S(1)} %get-tuple-element.289), channel_id=1, source_target_pairs={{0,6},{1,7},{2,4},{3,5},{4,2},{5,3},{6,0},{7,1},{8,14},{9,15},{10,... | collective-permute-start | bytes 393224 | tf_op jit(solution)/shard_map/ppermute | solution.py:55
  62.7 8.0 %collective-permute-start.18 = (bf16[256,2944]{1,0:T(8,128)(2,1)S(1)}, bf16[256,2944]{1,0:T(8,128)(2,1)S(1)}, u32[]{:S(2)}, u32[]{:S(2)}) collective-permute-start(bf16[256,2944]{1,0:T(8,128)(2,1)S(1)} %get-tuple-element.196), channel_id=1, source_target_pairs={{0,1},{1,0},{2,3},{3,2},{4,5},{5,4},{6,7},{7,6},{8,9},{9,8},{10,11... | collective-permute-start | bytes 4521992 | tf_op jit(solution)/shard_map/ppermute | solution.py:55
  62.8 7.9 %collective-permute-start.17 = (bf16[128,5760]{1,0:T(8,128)(2,1)S(1)}, bf16[128,5760]{1,0:T(8,128)(2,1)S(1)}, u32[]{:S(2)}, u32[]{:S(2)}) collective-permute-start(bf16[128,5760]{1,0:T(8,128)(2,1)S(1)} %get-tuple-element.231.slot_any), channel_id=1, source_target_pairs={{0,1},{1,0},{2,3},{3,2},{4,5},{5,4},{6,7},{7,6},{8,9},{9,8},{10,11... | collective-permute-start | bytes 4423688 | tf_op jit(solution)/shard_map/ppermute | solution.py:55
  63.3 7.4 %collective-permute-start.14 = (bf16[1,128,128]{2,1,0:T(8,128)(2,1)S(1)}, bf16[1,128,128]{2,1,0:T(8,128)(2,1)S(1)}, u32[]{:S(2)}, u32[]{:S(2)}) collective-permute-start(bf16[1,128,128]{2,1,0:T(8,128)(2,1)S(1)} %get-tuple-element.297), channel_id=1, source_target_pairs={{0,16},{1,17},{2,18},{3,19},{4,20},{5,21},{6,22},{7,23},{8,24},{9,... | collective-permute-start | bytes 98312 | tf_op jit(solution)/shard_map/ppermute | solution.py:55
  63.3 7.4 %collective-permute-start.15 = (bf16[1,128,128]{2,1,0:T(8,128)(2,1)S(1)}, bf16[1,128,128]{2,1,0:T(8,128)(2,1)S(1)}, u32[]{:S(2)}, u32[]{:S(2)}) collective-permute-start(bf16[1,128,128]{2,1,0:T(8,128)(2,1)S(1)} %get-tuple-element.296), channel_id=1, source_target_pairs={{0,8},{1,9},{2,10},{3,11},{4,12},{5,13},{6,14},{7,15},{8,0},{9,1},... | collective-permute-start | bytes 98312 | tf_op jit(solution)/shard_map/ppermute | solution.py:55
  64.2 6.5 %collective-permute-start.16 = (bf16[1,128,128]{2,1,0:T(8,128)(2,1)S(1)}, bf16[1,128,128]{2,1,0:T(8,128)(2,1)S(1)}, u32[]{:S(2)}, u32[]{:S(2)}) collective-permute-start(bf16[1,128,128]{2,1,0:T(8,128)(2,1)S(1)} %get-tuple-element.295), channel_id=1, source_target_pairs={{0,24},{1,25},{2,26},{3,27},{4,28},{5,29},{6,30},{7,31},{8,16},{9,... | collective-permute-start | bytes 98312 | tf_op jit(solution)/shard_map/ppermute | solution.py:55
  75.3 5.2 %copy-start.29 = (f32[128,768]{1,0:T(8,128)}, f32[128,768]{1,0:T(8,128)S(1)}, u32[]{:S(2)}) copy-start(f32[128,768]{1,0:T(8,128)S(1)} %get-tuple-element.200.after_ref) | copy-start | bytes 1179652
  75.3 6.3 %collective-permute-start.21 = (bf16[128,5760]{1,0:T(8,128)(2,1)S(1)}, bf16[128,5760]{1,0:T(8,128)(2,1)S(1)}, u32[]{:S(2)}, u32[]{:S(2)}) collective-permute-start(bf16[128,5760]{1,0:T(8,128)(2,1)S(1)} %get-tuple-element.233.doc_any), channel_id=1, source_target_pairs={{0,1},{1,0},{2,3},{3,2},{4,5},{5,4},{6,7},{7,6},{8,9},{9,8},{10,11... | collective-permute-start | bytes 4423688 | tf_op jit(solution)/shard_map/ppermute | solution.py:55
  80.5 4.7 %collective-permute-start.20 = (bf16[576,1536]{1,0:T(8,128)(2,1)S(1)}, bf16[576,1536]{1,0:T(8,128)(2,1)S(1)}, u32[]{:S(2)}, u32[]{:S(2)}) collective-permute-start(bf16[576,1536]{1,0:T(8,128)(2,1)S(1)} %get-tuple-element.203.grads_ref), channel_id=1, source_target_pairs={{0,1},{1,0},{2,3},{3,2},{4,5},{5,4},{6,7},{7,6},{8,9},{9,8},{10,11... | collective-permute-start | bytes 5308424 | tf_op jit(solution)/shard_map/ppermute | solution.py:55
  81.1 4.2 %collective-permute-start.19 = (bf16[128,2304]{1,0:T(8,128)(2,1)S(1)}, bf16[128,2304]{1,0:T(8,128)(2,1)S(1)}, u32[]{:S(2)}, u32[]{:S(2)}) collective-permute-start(bf16[128,2304]{1,0:T(8,128)(2,1)S(1)} %get-tuple-element.236.slot_any.grads_ref), channel_id=1, source_target_pairs={{0,1},{1,0},{2,3},{3,2},{4,5},{5,4},{6,7},{7,6},{8,9},{9,8},{10,11... | collective-permute-start | bytes 1769480 | tf_op jit(solution)/shard_map/ppermute | solution.py:55
  81.2 4.1 %collective-permute-start.22 = (bf16[16,128]{1,0:T(8,128)(2,1)S(1)}, bf16[16,128]{1,0:T(8,128)(2,1)S(1)}, u32[]{:S(2)}, u32[]{:S(2)}) collective-permute-start(bf16[16,128]{1,0:T(8,128)(2,1)S(1)} %get-tuple-element.216.table_ref), channel_id=1, source_target_pairs={{0,1},{1,0},{2,3},{3,2},{4,5},{5,4},{6,7},{7,6},{8,9},{9,8},{10,11... | collective-permute-start | bytes 12296 | tf_op jit(solution)/shard_map/ppermute | solution.py:55
  84.3 25.9 %collective-permute-start.24 = (bf16[192,2816]{1,0:T(8,128)(2,1)S(1)}, bf16[192,2816]{1,0:T(8,128)(2,1)S(1)}, u32[]{:S(2)}, u32[]{:S(2)}) collective-permute-start(bf16[192,2816]{1,0:T(8,128)(2,1)S(1)} %get-tuple-element.221), channel_id=1, source_target_pairs={{0,4},{1,5},{2,6},{3,7},{4,0},{5,1},{6,2},{7,3},{8,12},{9,13},{10,... | collective-permute-start | bytes 3244040 | tf_op jit(solution)/shard_map/ppermute | solution.py:55
  88.6 23.6 %collective-permute-start.23 = (bf16[208,2304]{1,0:T(8,128)(2,1)S(1)}, bf16[208,2304]{1,0:T(8,128)(2,1)S(1)}, u32[]{:S(2)}, u32[]{:S(2)}) collective-permute-start(bf16[208,2304]{1,0:T(8,128)(2,1)S(1)} %get-tuple-element.220), channel_id=1, source_target_pairs={{0,2},{1,3},{2,0},{3,1},{4,6},{5,7},{6,4},{7,5},{8,10},{9,11},{10,... | collective-permute-start | bytes 2875400 | tf_op jit(solution)/shard_map/ppermute | solution.py:55
  92.0 21.2 %collective-permute-start.28 = (bf16[192,2176]{1,0:T(8,128)(2,1)S(1)}, bf16[192,2176]{1,0:T(8,128)(2,1)S(1)}, u32[]{:S(2)}, u32[]{:S(2)}) collective-permute-start(bf16[192,2176]{1,0:T(8,128)(2,1)S(1)} %get-tuple-element.244), channel_id=1, source_target_pairs={{0,8},{1,9},{2,10},{3,11},{4,12},{5,13},{6,14},{7,15},{8,0},{9,1},... | collective-permute-start | bytes 2506760 | tf_op jit(solution)/shard_map/ppermute | solution.py:55
  110.4 15.3 %collective-permute-start.27 = (bf16[96,2816]{1,0:T(8,128)(2,1)S(1)}, bf16[96,2816]{1,0:T(8,128)(2,1)S(1)}, u32[]{:S(2)}, u32[]{:S(2)}) collective-permute-start(bf16[96,2816]{1,0:T(8,128)(2,1)S(1)} %get-tuple-element.243), channel_id=1, source_target_pairs={{0,2},{1,3},{2,0},{3,1},{4,6},{5,7},{6,4},{7,5},{8,10},{9,11},{10,... | collective-permute-start | bytes 1622024 | tf_op jit(solution)/shard_map/ppermute | solution.py:55
  111.0 18.6 %collective-permute-start.26 = (bf16[512,768]{1,0:T(8,128)(2,1)}, bf16[512,768]{1,0:T(8,128)(2,1)S(1)}, u32[]{:S(2)}, u32[]{:S(2)}) collective-permute-start(bf16[512,768]{1,0:T(8,128)(2,1)} %get-tuple-element.242), channel_id=1, source_target_pairs={{0,4},{1,5},{2,6},{3,7},{4,0},{5,1},{6,2},{7,3},{8,12},{9,13},{10,... | collective-permute-start | bytes 2359304 | tf_op jit(solution)/shard_map/ppermute | solution.py:55
  113.2 18.2 %collective-permute-start.25 = (bf16[112,2304]{1,0:T(8,128)(2,1)}, bf16[112,2304]{1,0:T(8,128)(2,1)S(1)}, u32[]{:S(2)}, u32[]{:S(2)}) collective-permute-start(bf16[112,2304]{1,0:T(8,128)(2,1)} %get-tuple-element.241), channel_id=1, source_target_pairs={{0,8},{1,9},{2,10},{3,11},{4,12},{5,13},{6,14},{7,15},{8,0},{9,1},... | collective-permute-start | bytes 1548296 | tf_op jit(solution)/shard_map/ppermute | solution.py:55
  114.1 20.6 %collective-permute-start.30 = (bf16[96,2176]{1,0:T(8,128)(2,1)}, bf16[96,2176]{1,0:T(8,128)(2,1)S(1)}, u32[]{:S(2)}, u32[]{:S(2)}) collective-permute-start(bf16[96,2176]{1,0:T(8,128)(2,1)} %get-tuple-element.255), channel_id=1, source_target_pairs={{0,2},{1,3},{2,0},{3,1},{4,6},{5,7},{6,4},{7,5},{8,10},{9,11},{10,... | collective-permute-start | bytes 1253384 | tf_op jit(solution)/shard_map/ppermute | solution.py:55
  127.2 9.7 %collective-permute-start.34 = (bf16[48,2816]{1,0:T(8,128)(2,1)}, bf16[48,2816]{1,0:T(8,128)(2,1)}, u32[]{:S(2)}, u32[]{:S(2)}) collective-permute-start(bf16[48,2816]{1,0:T(8,128)(2,1)} %get-tuple-element.261), channel_id=1, source_target_pairs={{0,8},{1,9},{2,10},{3,11},{4,12},{5,13},{6,14},{7,15},{8,0},{9,1},... | collective-permute-start | bytes 811016 | tf_op jit(solution)/shard_map/ppermute | solution.py:55
  129.6 7.2 %copy-start.21 = (bf16[128,1536]{1,0:T(8,128)(2,1)S(1)}, bf16[128,1536]{1,0:T(8,128)(2,1)}, u32[]{:S(2)}) copy-start(bf16[128,1536]{1,0:T(8,128)(2,1)} %copy-done.20) | copy-start | bytes 1179652
  129.6 7.2 %copy-start.1 = (bf16[48,2816]{1,0:T(8,128)(2,1)S(1)}, bf16[48,2816]{1,0:T(8,128)(2,1)}, u32[]{:S(2)}) copy-start(bf16[48,2816]{1,0:T(8,128)(2,1)} %copy-done) | copy-start | bytes 811012
  129.6 20.1 %copy-start.24 = (bf16[1,128,768]{2,1,0:T(8,128)(2,1)S(1)}, bf16[1,128,768]{2,1,0:T(8,128)(2,1)}, u32[]{:S(2)}) copy-start(bf16[1,128,768]{2,1,0:T(8,128)(2,1)} %param.17) | copy-start | bytes 589828
  129.6 20.1 %copy-start.28 = (bf16[128,1536]{1,0:T(8,128)(2,1)S(1)}, bf16[128,1536]{1,0:T(8,128)(2,1)}, u32[]{:S(2)}) copy-start(bf16[128,1536]{1,0:T(8,128)(2,1)} %copy-done.27) | copy-start | bytes 1179652
  129.8 13.3 %collective-permute-start.32 = (bf16[256,768]{1,0:T(8,128)(2,1)S(1)}, bf16[256,768]{1,0:T(8,128)(2,1)S(1)}, u32[]{:S(2)}, u32[]{:S(2)}) collective-permute-start(bf16[256,768]{1,0:T(8,128)(2,1)S(1)} %get-tuple-element.259), channel_id=1, source_target_pairs={{0,2},{1,3},{2,0},{3,1},{4,6},{5,7},{6,4},{7,5},{8,10},{9,11},{10,... | collective-permute-start | bytes 1179656 | tf_op jit(solution)/shard_map/ppermute | solution.py:55
  131.4 18.3 %copy-start.16 = (bf16[576,1536]{1,0:T(8,128)(2,1)S(1)}, bf16[576,1536]{1,0:T(8,128)(2,1)}, u32[]{:S(2)}) copy-start(bf16[576,1536]{1,0:T(8,128)(2,1)} %copy-done.15) | copy-start | bytes 5308420
  134.7 15.1 %copy-start.9 = (bf16[768,768]{1,0:T(8,128)(2,1)S(1)}, bf16[768,768]{1,0:T(8,128)(2,1)}, u32[]{:S(2)}) copy-start(bf16[768,768]{1,0:T(8,128)(2,1)} %wv_ref.5) | copy-start | bytes 3538948
  134.8 7.9 %collective-permute-start.33 = (bf16[64,2304]{1,0:T(8,128)(2,1)S(1)}, bf16[64,2304]{1,0:T(8,128)(2,1)S(1)}, u32[]{:S(2)}, u32[]{:S(2)}) collective-permute-start(bf16[64,2304]{1,0:T(8,128)(2,1)S(1)} %get-tuple-element.260), channel_id=1, source_target_pairs={{0,4},{1,5},{2,6},{3,7},{4,0},{5,1},{6,2},{7,3},{8,12},{9,13},{10,... | collective-permute-start | bytes 884744 | tf_op jit(solution)/shard_map/ppermute | solution.py:55
  135.1 9.7 %collective-permute-start.31 = (bf16[48,2176]{1,0:T(8,128)(2,1)S(1)}, bf16[48,2176]{1,0:T(8,128)(2,1)S(1)}, u32[]{:S(2)}, u32[]{:S(2)}) collective-permute-start(bf16[48,2176]{1,0:T(8,128)(2,1)S(1)} %get-tuple-element.258), channel_id=1, source_target_pairs={{0,4},{1,5},{2,6},{3,7},{4,0},{5,1},{6,2},{7,3},{8,12},{9,13},{10,... | collective-permute-start | bytes 626696 | tf_op jit(solution)/shard_map/ppermute | solution.py:55
  136.9 12.9 %collective-permute-start.29 = (bf16[128,1536]{1,0:T(8,128)(2,1)S(1)}, bf16[128,1536]{1,0:T(8,128)(2,1)S(1)}, u32[]{:S(2)}, u32[]{:S(2)}) collective-permute-start(bf16[128,1536]{1,0:T(8,128)(2,1)S(1)} %copy-done.21), channel_id=1, source_target_pairs={{0,2},{1,3},{2,0},{3,1},{4,6},{5,7},{6,4},{7,5},{8,10},{9,11},{10,... | collective-permute-start | bytes 1179656 | tf_op jit(solution)/shard_map/ppermute | solution.py:55
  137.9 11.8 %copy-start.5 = (bf16[768,768]{1,0:T(8,128)(2,1)S(1)}, bf16[768,768]{1,0:T(8,128)(2,1)}, u32[]{:S(2)}) copy-start(bf16[768,768]{1,0:T(8,128)(2,1)} %wq_ref.5) | copy-start | bytes 3538948
  137.9 11.8 %copy-start.7 = (bf16[768,768]{1,0:T(8,128)(2,1)S(1)}, bf16[768,768]{1,0:T(8,128)(2,1)}, u32[]{:S(2)}) copy-start(bf16[768,768]{1,0:T(8,128)(2,1)} %wk_ref.5) | copy-start | bytes 3538948
  137.9 15.0 %collective-permute-start.37 = (bf16[24,2816]{1,0:T(8,128)(2,1)S(1)}, bf16[24,2816]{1,0:T(8,128)(2,1)S(1)}, u32[]{:S(2)}, u32[]{:S(2)}) collective-permute-start(bf16[24,2816]{1,0:T(8,128)(2,1)S(1)} %get-tuple-element.293), channel_id=1, source_target_pairs={{0,16},{1,17},{2,18},{3,19},{4,20},{5,21},{6,22},{7,23},{8,24},{9,... | collective-permute-start | bytes 405512 | tf_op jit(solution)/shard_map/ppermute | solution.py:55
  142.7 13.7 %collective-permute-start.35 = (bf16[40,2304]{1,0:T(8,128)(2,1)S(1)}, bf16[40,2304]{1,0:T(8,128)(2,1)S(1)}, u32[]{:S(2)}, u32[]{:S(2)}) collective-permute-start(bf16[40,2304]{1,0:T(8,128)(2,1)S(1)} %pad_maximum_fusion), channel_id=1, source_target_pairs={{0,16},{1,17},{2,18},{3,19},{4,20},{5,21},{6,22},{7,23},{8,24},{9,... | collective-permute-start | bytes 552968 | tf_op jit(solution)/shard_map/ppermute | solution.py:55
  144.9 8.1 %collective-permute-start.38 = (bf16[128,768]{1,0:T(8,128)(2,1)S(1)}, bf16[128,768]{1,0:T(8,128)(2,1)S(1)}, u32[]{:S(2)}, u32[]{:S(2)}) collective-permute-start(bf16[128,768]{1,0:T(8,128)(2,1)S(1)} %get-tuple-element.269), channel_id=1, source_target_pairs={{0,8},{1,9},{2,10},{3,11},{4,12},{5,13},{6,14},{7,15},{8,0},{9,1},... | collective-permute-start | bytes 589832 | tf_op jit(solution)/shard_map/ppermute | solution.py:55
  146.2 10.1 %collective-permute-start.36 = (bf16[24,2176]{1,0:T(8,128)(2,1)S(1)}, bf16[24,2176]{1,0:T(8,128)(2,1)S(1)}, u32[]{:S(2)}, u32[]{:S(2)}) collective-permute-start(bf16[24,2176]{1,0:T(8,128)(2,1)S(1)} %get-tuple-element.301), channel_id=1, source_target_pairs={{0,16},{1,17},{2,18},{3,19},{4,20},{5,21},{6,22},{7,23},{8,24},{9,... | collective-permute-start | bytes 313352 | tf_op jit(solution)/shard_map/ppermute | solution.py:55
  159.7 5.8 %collective-permute-start.39 = (bf16[64,768]{1,0:T(8,128)(2,1)S(1)}, bf16[64,768]{1,0:T(8,128)(2,1)S(1)}, u32[]{:S(2)}, u32[]{:S(2)}) collective-permute-start(bf16[64,768]{1,0:T(8,128)(2,1)S(1)} %get-tuple-element.275), channel_id=1, source_target_pairs={{0,16},{1,17},{2,18},{3,19},{4,20},{5,21},{6,22},{7,23},{8,24},{9,... | collective-permute-start | bytes 294920 | tf_op jit(solution)/shard_map/ppermute | solution.py:55
  (7 other events, 18.1 us)
